TPU v7x, 32 devices: a whole 2x2x4 slice. The times are simulated.
32 devices in a mesh: row: 8 (over y, x, core), col: 4 (over z).
Axes of the slice: x: 2, y: 2, z: 4, core: 2. Of those that a mesh axis runs over, the one named last changes fastest.
Arguments:
- pair_feature_map: bfloat16 [64, 512, 512], P(None, 'row', 'col'), may hold values from -6 to 6
- conv_weight: bfloat16 [3, 3, 64, 64], replicated, may hold values from -0.25 to 0.25
- conv_bias: float32 [64], replicated, may hold values from -3 to 3
- cotangent: bfloat16 [64, 512, 512], P(None, 'row', 'col'), may hold values from -6 to 6
Outputs:
- symmetric: bfloat16 [64, 512, 512], P(None, 'row', 'col')
- grad_input: bfloat16 [64, 512, 512], P(None, 'row', 'col')
- grad_weight: float32 [3, 3, 64, 64], replicated
- grad_bias: float32 [64], replicated
All inputs are finite; a program needn't handle non-finite values.
Results may differ from a plain program's by a relative error of at most 0.0085.
Values may be sent and summed in bfloat16 or wider, within the bound.
No kernel may reach another device: no remote copies, remote signals or barrier semaphores. Data moves between devices by JAX's collectives and lax.ppermute only.
A program may use at most 128 MiB of HBM per device.

v0:
```python
import math

import jax
import jax.numpy as jnp
from jax import lax
from jax.sharding import PartitionSpec as P

DILATION_STEP = 8


def for_sending(shard):
    return jax.tree.map(lambda a: a.astype(jnp.bfloat16) if a.dtype == jnp.float32 else a, shard)


def with_halo(shard, sides, width):
    for axis, dim in sides:
        size, length = (lax.axis_size(axis), shard.shape[dim])
        up = [(i, (i + 1) % size) for i in range(size - 1)]
        down = [(j, i) for i, j in up]
        last = lax.slice_in_dim(shard, length - width, length, axis=dim)
        first = lax.slice_in_dim(shard, 0, width, axis=dim)
        before = lax.ppermute(last, axis, up)
        after = lax.ppermute(first, axis, down)
        shard = jnp.concatenate([before, shard, after], axis=dim)
    return shard


def tap_stack(padded_input, leading_row, block_row_span, tile_cols, flip):
    pieces = []
    for row_kernel_tap in range(3):
        for column_tap in range(3):
            row_offset = 2 - row_kernel_tap if flip else row_kernel_tap
            column_offset = 2 - column_tap if flip else column_tap
            top_margin = leading_row + DILATION_STEP * row_offset
            left_margin = DILATION_STEP * column_offset
            pieces.append(
                padded_input[
                    :,
                    top_margin : top_margin + block_row_span,
                    left_margin : left_margin + tile_cols,
                ]
            )
    return jnp.concatenate(pieces, axis=0)


def forward(padded_input, matrix, conv_bias, tile_cols, block_row_span):
    stacked = tap_stack(padded_input, 0, block_row_span, tile_cols, False)
    pieces = jnp.einsum("ok,khw->ohw", matrix, stacked, preferred_element_type=jnp.float32)
    return pieces + conv_bias[:, None, None]


def mirror(pair):
    channel_count, tile_rows, tile_cols = pair[0].shape
    ratio = tile_cols // tile_rows
    row_count = lax.axis_size("row")
    col_count = lax.axis_size("col")
    prepared = tuple(
        (
            jnp.swapaxes(member, 1, 2).reshape(channel_count, ratio, tile_rows, tile_rows)
            for member in pair
        )
    )
    second = jax.tree.map(
        lambda part, own: part.astype(own.dtype),
        lax.all_to_all(
            lax.all_to_all(for_sending(prepared), "row", split_axis=2, concat_axis=3, tiled=True),
            "col",
            split_axis=3,
            concat_axis=2,
            tiled=True,
        ),
        prepared,
    )
    reordered = tuple(
        (
            jnp.transpose(
                member.reshape(
                    channel_count, ratio, col_count, tile_rows // row_count, ratio * tile_rows
                ),
                (0, 2, 1, 3, 4),
            ).reshape(channel_count, tile_rows, tile_cols)
            for member in second
        )
    )
    return jax.tree.map(
        lambda part, own: part.astype(own.dtype),
        lax.all_to_all(for_sending(reordered), "row", split_axis=1, concat_axis=1, tiled=True),
        reordered,
    )


def shards(pair_feature_map, conv_weight, conv_bias, cotangent):
    channel_count, tile_rows, tile_cols = pair_feature_map.shape
    map_side = tile_rows * lax.axis_size("row")
    block_row_span = math.gcd(tile_rows, 64)
    w_front = jnp.transpose(conv_weight, (2, 0, 1, 3)).reshape(channel_count, 9 * channel_count)
    w_swapped = jnp.transpose(conv_weight, (2, 1, 0, 3)).reshape(channel_count, 9 * channel_count)
    w_back = jnp.transpose(conv_weight, (3, 0, 1, 2)).reshape(channel_count, 9 * channel_count)
    padded_input = with_halo(pair_feature_map, (("row", 1), ("col", 2)), DILATION_STEP)
    pre_act = forward(padded_input, w_front, conv_bias, tile_cols, block_row_span)
    mixed_map = (pair_feature_map.astype(jnp.float32) + jax.nn.elu(pre_act)).astype(jnp.bfloat16)
    flipped, cot_flip = mirror((pair_feature_map, cotangent))
    flip_padded = with_halo(flipped, (("row", 1), ("col", 2)), DILATION_STEP)
    pre_flip = forward(flip_padded, w_swapped, conv_bias, tile_cols, block_row_span)
    mixed_flip = (flipped.astype(jnp.float32) + jax.nn.elu(pre_flip)).astype(jnp.bfloat16)
    symmetric = (mixed_map.astype(jnp.float32) + mixed_flip.astype(jnp.float32)).astype(
        jnp.bfloat16
    )
    grad_mixed = cotangent.astype(jnp.float32) + cot_flip.astype(jnp.float32)
    elu_slope = jnp.where(
        pre_act > 0, jnp.float32(1.0), jnp.exp(jnp.minimum(pre_act, jnp.float32(0.0)))
    )
    gradient_preactivation = (grad_mixed * elu_slope).astype(jnp.bfloat16)
    gradient_padded = with_halo(gradient_preactivation, (("row", 1), ("col", 2)), DILATION_STEP)
    stacked = tap_stack(gradient_padded, 0, block_row_span, tile_cols, True)
    back_pieces = jnp.einsum("ik,khw->ihw", w_back, stacked, preferred_element_type=jnp.float32)
    weight_acc = jnp.einsum(
        "khw,ihw->ki", stacked, pair_feature_map, preferred_element_type=jnp.float32
    )
    grad_input = (grad_mixed + back_pieces).astype(jnp.bfloat16)
    local_bias = jnp.sum(gradient_preactivation.astype(jnp.float32), axis=(1, 2))
    weight_total, grad_bias = lax.psum(
        (weight_acc / map_side, local_bias / map_side), ("row", "col")
    )
    grad_weight = weight_total.reshape(3, 3, channel_count, channel_count)
    return (symmetric, grad_input, grad_weight, grad_bias)


def solution(mesh):
    placed = (P(None, "row", "col"), P(), P(), P(None, "row", "col"))
    return jax.shard_map(
        shards,
        mesh=mesh,
        in_specs=placed,
        out_specs=(P(None, "row", "col"), P(None, "row", "col"), P(), P()),
        check_vma=False,
    )
```

profile of v0, /device:TPU:12, one launch (start us, length us, event | category | flops | bytes accessed | tf_op | source)
XLA Modules:
  0.0 429.8 jit_solution(7574218158948743427)
XLA Ops:
  7.2 5.0 %reshape.41 = bf16[64,2,64,64]{2,1,3,0:T(2,128)(2,1)} reshape(bf16[64,128,64]{1,2,0:T(8,128)(2,1)} %bitcast.91) | data formatting | bytes 2097152 | tf_op jit(solution)/shard_map/reshape | solution.py:59
  12.1 7.0 %copy.150 = bf16[64,2,64,64]{3,1,0,2:T(2,128)(2,1)S(1)} copy(bf16[64,2,64,64]{2,1,3,0:T(2,128)(2,1)} %reshape.41) | data formatting | bytes 2097152 | tf_op jit(solution)/shard_map/reshape | solution.py:59
  19.2 2.7 reshape.53
  21.8 4.7 %all-to-all-start.3 = ((bf16[8,2,32768]{2,1,0:T(2,128)(2,1)}), bf16[8,2,32768]{2,1,0:T(2,128)(2,1)}, u32[]{:S(2)}, u32[]{:S(2)}) async-start(bf16[8,2,32768]{2,1,0:T(2,128)(2,1)} %reshape.53), calls=%async_computation.3 | async-start | bytes 2097152 | tf_op jit(solution)/shard_map/all_to_all | solution.py:66
  28.3 7.0 %copy.137 = bf16[64,2,64,64]{3,1,0,2:T(2,128)(2,1)S(1)} copy(bf16[64,2,64,64]{2,1,3,0:T(2,128)(2,1)} %reshape.38) | data formatting | bytes 2097152 | tf_op jit(solution)/shard_map/reshape | solution.py:59
  35.3 2.7 reshape.49
  38.0 2.5 all-to-all-done.3
  40.5 5.6 %all-to-all-start = ((bf16[8,2,32768]{2,1,0:T(2,128)(2,1)}), bf16[8,2,32768]{2,1,0:T(2,128)(2,1)}, u32[]{:S(2)}, u32[]{:S(2)}) async-start(bf16[8,2,32768]{2,1,0:T(2,128)(2,1)} %reshape.49), calls=%async_computation | async-start | bytes 2097152 | tf_op jit(solution)/shard_map/all_to_all | solution.py:66
  46.2 3.1 reshape.54
  49.3 3.8 copy.185
  53.1 4.8 %copy.171 = bf16[64,2,8,8,64]{0,2,1,4,3:T(8,128)(2,1)S(1)} copy(bf16[64,2,8,8,64]{4,2,3,1,0:T(8,128)(2,1)} %bitcast.86) | data formatting | bytes 2097152 | tf_op jit(solution)/shard_map/all_to_all | solution.py:66
  57.8 2.7 reshape.55
  60.5 5.6 %all-to-all-start.4 = ((bf16[4,2,65536]{2,1,0:T(2,128)(2,1)}), bf16[4,2,65536]{2,1,0:T(2,128)(2,1)S(1)}, u32[]{:S(2)}, u32[]{:S(2)}) async-start(bf16[4,2,65536]{2,1,0:T(2,128)(2,1)} %reshape.55), calls=%async_computation.4 | async-start | bytes 2097152 | tf_op jit(solution)/shard_map/all_to_all | solution.py:65
  66.8 4.3 %reshape.50 = bf16[64,64,2,64]{3,2,1,0:T(2,128)(2,1)} reshape(bf16[8,2,32768]{2,1,0:T(2,128)(2,1)} %all-to-all-done) | data formatting | bytes 2097152
  71.1 5.4 %copy.186 = bf16[64,2,64,64]{3,2,1,0:T(8,128)(2,1)} copy(bf16[64,2,64,64]{3,1,0,2:T(2,128)(2,1)} %bitcast.88) | data formatting | bytes 2097152 | tf_op jit(solution)/shard_map/all_to_all | solution.py:66
  76.5 5.4 %copy.169 = bf16[64,2,8,8,64]{0,2,1,4,3:T(8,128)(2,1)} copy(bf16[64,2,8,8,64]{4,2,3,1,0:T(8,128)(2,1)} %bitcast.89) | data formatting | bytes 2097152 | tf_op jit(solution)/shard_map/all_to_all | solution.py:66
  81.9 4.4 %reshape.51 = bf16[4,2,65536]{2,1,0:T(2,128)(2,1)} reshape(bf16[512,2,8,64]{3,2,1,0:T(8,128)(2,1)} %bitcast.90) | data formatting | bytes 2097152
  86.2 2.6 all-to-all-done.4
  88.9 7.5 %all-to-all-start.1 = ((bf16[4,2,65536]{2,1,0:T(2,128)(2,1)}), bf16[4,2,65536]{2,1,0:T(2,128)(2,1)}, u32[]{:S(2)}, u32[]{:S(2)}) async-start(bf16[4,2,65536]{2,1,0:T(2,128)(2,1)} %reshape.51), calls=%async_computation.1 | async-start | bytes 2097152 | tf_op jit(solution)/shard_map/all_to_all | solution.py:65
  98.3 4.5 %collective-permute-start.1 = (bf16[64,8,128]{2,0,1:T(8,128)(2,1)S(1)}, bf16[64,8,128]{2,0,1:T(8,128)(2,1)S(1)}, u32[]{:S(2)}, u32[]{:S(2)}) collective-permute-start(bf16[64,8,128]{2,0,1:T(8,128)(2,1)S(1)} %get-tuple-element.36), channel_id=1, source_target_pairs={{4,0},{8,4},{12,8},{16,12},{20,16},{24,20},{28,24},{5,1},{9,5},{13... | collective-permute-start | bytes 393224 | tf_op jit(solution)/shard_map/ppermute | solution.py:23
  106.0 2.0 fusion.40
  108.1 3.2 copy.128
  111.3 3.4 collective-permute-start.2
  114.7 3.2 copy.131
  117.9 3.6 collective-permute-start.3
  123.1 3.8 copy.129
  126.9 3.7 copy.132
  130.6 2.9 fusion.26
  136.5 4.3 %reshape.56 = bf16[512,2,8,64]{3,2,1,0:T(8,128)(2,1)} reshape(bf16[4,2,65536]{2,1,0:T(2,128)(2,1)} %copy-done.11) | data formatting | bytes 2097152
  140.8 4.2 copy.154
  145.1 2.9 copy.155
  148.0 4.4 %all-to-all-start.5 = ((bf16[64,64,128]{2,0,1:T(8,128)(2,1)}), bf16[64,64,128]{2,0,1:T(8,128)(2,1)}, u32[]{:S(2)}, u32[]{:S(2)}) async-start(bf16[64,64,128]{2,0,1:T(8,128)(2,1)} %bitcast.94), calls=%async_computation.5 | async-start | bytes 2097152 | tf_op jit(solution)/shard_map/all_to_all | solution.py:87
  152.4 2.9 fusion.24
  163.3 3.1 reshape.52
  166.4 3.5 copy.141
  170.0 3.0 copy.142
  172.9 4.1 all-to-all-start.2
  177.1 8.1 %convert_reduce_fusion = (f32[64]{0:T(128)S(1)}, bf16[64,64,128]{2,0,1:T(8,128)(2,1)S(1)}, f32[64,128,64]{1,2,0:T(8,128)}) fusion(f32[64]{0:T(128)S(1)} %copy-done.23, bf16[64,64,128]{2,0,1:T(8,128)(2,1)} %all-to-all-done.5, bf16[64,64,128]{2,1,0:T(8,128)(2,1)S(1)} %copy-done.9, bf16[576,64,128]{2,0,1:T(8,128)(2,1)} %fusion.33, ...), kind=kOutput, calls=%fused_computation.37 | convolution fusion | flops 609746880 | bytes 14754304 | tf_op jit(solution)/shard_map/ok,khw->ohw/dot_general | solution.py:48
  185.2 2.1 collective-permute-start.8
  187.2 4.4 %collective-permute-start.9 = (bf16[64,8,128]{2,0,1:T(8,128)(2,1)S(1)}, bf16[64,8,128]{2,0,1:T(8,128)(2,1)S(1)}, u32[]{:S(2)}, u32[]{:S(2)}) collective-permute-start(bf16[64,8,128]{2,0,1:T(8,128)(2,1)S(1)} %get-tuple-element.35), channel_id=1, source_target_pairs={{4,0},{8,4},{12,8},{16,12},{20,16},{24,20},{28,24},{5,1},{9,5},{13... | collective-permute-start | bytes 393224 | tf_op jit(solution)/shard_map/ppermute | solution.py:23
  194.3 4.5 %collective-permute-start.5 = (bf16[64,8,128]{2,0,1:T(8,128)(2,1)}, bf16[64,8,128]{2,0,1:T(8,128)(2,1)}, u32[]{:S(2)}, u32[]{:S(2)}) collective-permute-start(bf16[64,8,128]{2,0,1:T(8,128)(2,1)} %get-tuple-element.38), channel_id=1, source_target_pairs={{4,0},{8,4},{12,8},{16,12},{20,16},{24,20},{28,24},{5,1},{9,5},{13... | collective-permute-start | bytes 393224 | tf_op jit(solution)/shard_map/ppermute | solution.py:23
  198.8 40.1 %psum.15 = f32[64]{0:T(128)} all-reduce(f32[64]{0:T(128)S(1)} %broadcast_multiply_fusion), channel_id=1, replica_groups=mesh['row'=8,'col'=4] {'row','col'}, use_global_device_ids=true, to_apply=%region_2.3 | all-reduce | flops 64 | bytes 512 | tf_op jit(solution)/shard_map/psum | solution.py:122
  242.1 3.2 copy.156
  245.3 2.7 collective-permute-start.10
  248.0 2.1 copy.158
  250.1 3.3 collective-permute-start.11
  257.5 3.2 copy.143
  260.7 3.9 collective-permute-start.6
  264.6 3.2 copy.145
  267.8 2.6 collective-permute-start.7
  270.4 3.8 copy.157
  274.1 3.7 copy.159
  277.8 4.4 %maximum_maximum_fusion = (bf16[64,80,136]{2,0,1:T(8,128)(2,1)S(1)}, bf16[64,80,136]{2,0,1:T(8,128)(2,1)S(1)}) fusion(bf16[64,8,128]{2,0,1:T(8,128)(2,1)} %copy-done.15, bf16[64,64,128]{2,0,1:T(8,128)(2,1)S(1)} %get-tuple-element.25, bf16[64,8,128]{2,0,1:T(8,128)(2,1)} %copy-done.13, bf16[64,80,8]{2,0,1:T(8,128)(2,1)} %copy.159, bf16[64,80,8]{2,0,1:T(8,128)(2,1)} %copy.157), kind=kLoop, calls=%fused_computation.22 | loop fusion | flops 11141120 | bytes 4259840 | tf_op jit(solution)/shard_map/concatenate | solution.py:24
  285.6 3.6 copy-done
  289.3 2.9 fusion.10
  293.0 3.7 copy.144
  296.8 2.8 fusion.18
  299.6 2.1 fusion.32
  301.7 3.7 copy.146
  305.4 3.1 fusion.14
  314.5 2.3 fusion.30
  318.8 7.8 %add_convert_fusion = bf16[64,64,128]{2,0,1:T(8,128)(2,1)S(1)} fusion(bf16[576,64,128]{2,0,1:T(8,128)(2,1)} %fusion.29, bf16[64,576,1]{0,1,2:T(8,128)(2,1)S(1)} %bitcast.99, bf16[64,64,128]{2,0,1:T(8,128)(2,1)S(1)} %all-to-all-done.2, f32[64,128,64]{1,2,0:T(8,128)S(1)} %copy-done.25, f32[64]{0:T(128)S(1)} %copy-done.24, bf16[64,64,128]{2,1,0:T(8,128)(2,1)S(1)} %copy-done.3), kind=kOutput, calls=%fused_computation.39 | convolution fusion | flops 613416960 | bytes 14754048 | tf_op jit(solution)/shard_map/ok,khw->ohw/dot_general | solution.py:48
  326.6 3.6 fusion.8
  333.5 87.5 %all-reduce.2.cloned.1.call-done = f32[3,3,64,64]{3,2,1,0:T(8,128)} async-done(((f32[3,3,64,64]{3,2,1,0:T(8,128)}), f32[3,3,64,64]{3,2,1,0:T(8,128)}) %all-reduce.2.cloned.1.call-update) | async-done | bytes 147472 | tf_op jit(solution)/shard_map/psum | solution.py:122
  (120 shorter events, 47.3 us)
Async XLA Ops:
  19.2 7.3 %copy-start.1 = (bf16[64,64,128]{2,1,0:T(8,128)(2,1)S(1)}, bf16[64,64,128]{2,1,0:T(8,128)(2,1)}, u32[]{:S(2)}) copy-start(bf16[64,64,128]{2,1,0:T(8,128)(2,1)} %param.4) | copy-start | bytes 3145732
  21.8 18.7 %all-to-all-start.3 = ((bf16[8,2,32768]{2,1,0:T(2,128)(2,1)}), bf16[8,2,32768]{2,1,0:T(2,128)(2,1)}, u32[]{:S(2)}, u32[]{:S(2)}) async-start(bf16[8,2,32768]{2,1,0:T(2,128)(2,1)} %reshape.53), calls=%async_computation.3 | async-start | bytes 2097152 | tf_op jit(solution)/shard_map/all_to_all | solution.py:66
  40.5 20.0 %all-to-all-start = ((bf16[8,2,32768]{2,1,0:T(2,128)(2,1)}), bf16[8,2,32768]{2,1,0:T(2,128)(2,1)}, u32[]{:S(2)}, u32[]{:S(2)}) async-start(bf16[8,2,32768]{2,1,0:T(2,128)(2,1)} %reshape.49), calls=%async_computation | async-start | bytes 2097152 | tf_op jit(solution)/shard_map/all_to_all | solution.py:66
  60.5 28.4 %all-to-all-start.4 = ((bf16[4,2,65536]{2,1,0:T(2,128)(2,1)}), bf16[4,2,65536]{2,1,0:T(2,128)(2,1)S(1)}, u32[]{:S(2)}, u32[]{:S(2)}) async-start(bf16[4,2,65536]{2,1,0:T(2,128)(2,1)} %reshape.55), calls=%async_computation.4 | async-start | bytes 2097152 | tf_op jit(solution)/shard_map/all_to_all | solution.py:65
  88.9 14.0 %copy-start.11 = (bf16[4,2,65536]{2,1,0:T(2,128)(2,1)}, bf16[4,2,65536]{2,1,0:T(2,128)(2,1)S(1)}, u32[]{:S(2)}) copy-start(bf16[4,2,65536]{2,1,0:T(2,128)(2,1)S(1)} %all-to-all-done.4) | copy-start | bytes 3145732
  88.9 59.1 %all-to-all-start.1 = ((bf16[4,2,65536]{2,1,0:T(2,128)(2,1)}), bf16[4,2,65536]{2,1,0:T(2,128)(2,1)}, u32[]{:S(2)}, u32[]{:S(2)}) async-start(bf16[4,2,65536]{2,1,0:T(2,128)(2,1)} %reshape.51), calls=%async_computation.1 | async-start | bytes 2097152 | tf_op jit(solution)/shard_map/all_to_all | solution.py:65
  96.4 7.2 %collective-permute-start = (bf16[64,8,128]{2,0,1:T(8,128)(2,1)S(1)}, bf16[64,8,128]{2,0,1:T(8,128)(2,1)S(1)}, u32[]{:S(2)}, u32[]{:S(2)}) collective-permute-start(bf16[64,8,128]{2,0,1:T(8,128)(2,1)S(1)} %get-tuple-element.37), channel_id=1, source_target_pairs={{0,4},{4,8},{8,12},{12,16},{16,20},{20,24},{24,28},{1,5},{5,9},{9,... | collective-permute-start | bytes 393224 | tf_op jit(solution)/shard_map/ppermute | solution.py:22
  98.3 7.0 %collective-permute-start.1 = (bf16[64,8,128]{2,0,1:T(8,128)(2,1)S(1)}, bf16[64,8,128]{2,0,1:T(8,128)(2,1)S(1)}, u32[]{:S(2)}, u32[]{:S(2)}) collective-permute-start(bf16[64,8,128]{2,0,1:T(8,128)(2,1)S(1)} %get-tuple-element.36), channel_id=1, source_target_pairs={{4,0},{8,4},{12,8},{16,12},{20,16},{24,20},{28,24},{5,1},{9,5},{13... | collective-permute-start | bytes 393224 | tf_op jit(solution)/shard_map/ppermute | solution.py:23
  103.6 0.6 copy-start.19
  105.4 0.7 copy-start.17
  108.1 13.4 %copy-start.12 = (bf16[3,3,64,64]{3,2,1,0:T(8,128)(2,1)S(1)}, bf16[3,3,64,64]{3,2,1,0:T(8,128)(2,1)}, u32[]{:S(2)}) copy-start(bf16[3,3,64,64]{3,2,1,0:T(8,128)(2,1)} %param.5) | copy-start | bytes 221188
  111.3 11.8 %collective-permute-start.2 = (bf16[64,80,8]{1,2,0:T(8,128)(2,1)}, bf16[64,80,8]{1,2,0:T(8,128)(2,1)}, u32[]{:S(2)}, u32[]{:S(2)}) collective-permute-start(bf16[64,80,8]{1,2,0:T(8,128)(2,1)} %copy.128), channel_id=1, source_target_pairs={{0,1},{1,2},{2,3},{4,5},{5,6},{6,7},{8,9},{9,10},{10,11},{12,13},{... | collective-permute-start | bytes 245768 | tf_op jit(solution)/shard_map/ppermute | solution.py:22
  117.9 9.1 %collective-permute-start.3 = (bf16[64,80,8]{1,2,0:T(8,128)(2,1)}, bf16[64,80,8]{1,2,0:T(8,128)(2,1)}, u32[]{:S(2)}, u32[]{:S(2)}) collective-permute-start(bf16[64,80,8]{1,2,0:T(8,128)(2,1)} %copy.131), channel_id=1, source_target_pairs={{1,0},{2,1},{3,2},{5,4},{6,5},{7,6},{9,8},{10,9},{11,10},{13,12},{... | collective-permute-start | bytes 245768 | tf_op jit(solution)/shard_map/ppermute | solution.py:23
  130.6 2.9 copy-start.20
  130.6 4.1 copy-start.4
  148.0 25.0 %all-to-all-start.5 = ((bf16[64,64,128]{2,0,1:T(8,128)(2,1)}), bf16[64,64,128]{2,0,1:T(8,128)(2,1)}, u32[]{:S(2)}, u32[]{:S(2)}) async-start(bf16[64,64,128]{2,0,1:T(8,128)(2,1)} %bitcast.94), calls=%async_computation.5 | async-start | bytes 2097152 | tf_op jit(solution)/shard_map/all_to_all | solution.py:87
  152.3 4.6 %copy-start.5 = (bf16[64,80,8]{2,0,1:T(8,128)(2,1)S(1)}, bf16[64,80,8]{2,0,1:T(8,128)(2,1)}, u32[]{:S(2)}) copy-start(bf16[64,80,8]{2,0,1:T(8,128)(2,1)} %copy.132) | copy-start | bytes 245764
  156.9 1.9 copy-start.6
  158.8 1.6 copy-start.18
  170.0 7.1 %copy-start.9 = (bf16[64,64,128]{2,1,0:T(8,128)(2,1)S(1)}, bf16[64,64,128]{2,1,0:T(8,128)(2,1)}, u32[]{:S(2)}) copy-start(bf16[64,64,128]{2,1,0:T(8,128)(2,1)} %param.7) | copy-start | bytes 3145732
  170.0 7.1 %copy-start.22 = (bf16[64,3,3,64]{0,3,2,1:T(8,128)(2,1)S(1)}, bf16[64,3,3,64]{0,3,2,1:T(8,128)(2,1)}, u32[]{:S(2)}) copy-start(bf16[64,3,3,64]{0,3,2,1:T(8,128)(2,1)} %copy.135) | copy-start | bytes 221188
  170.0 7.1 %copy-start.23 = (f32[64]{0:T(128)S(1)}, f32[64]{0:T(128)}, u32[]{:S(2)}) copy-start(f32[64]{0:T(128)} %param.6) | copy-start | bytes 772
  172.9 18.7 %all-to-all-start.2 = ((bf16[64,64,128]{2,0,1:T(8,128)(2,1)}), bf16[64,64,128]{2,0,1:T(8,128)(2,1)S(1)}, u32[]{:S(2)}, u32[]{:S(2)}) async-start(bf16[64,64,128]{2,0,1:T(8,128)(2,1)} %bitcast.10), calls=%async_computation.2 | async-start | bytes 2097152 | tf_op jit(solution)/shard_map/all_to_all | solution.py:87
  177.0 244.0 %all-reduce.2.cloned.1.call-start = ((), (), s32[]{:S(2)}) async-start(), calls=%async_computation.6 | async-start | bytes 589824 | tf_op jit(solution)/shard_map/psum | solution.py:122
  185.2 53.8 %collective-permute-start.8 = (bf16[64,8,128]{2,0,1:T(8,128)(2,1)S(1)}, bf16[64,8,128]{2,0,1:T(8,128)(2,1)S(1)}, u32[]{:S(2)}, u32[]{:S(2)}) collective-permute-start(bf16[64,8,128]{2,0,1:T(8,128)(2,1)S(1)} %get-tuple-element.34), channel_id=1, source_target_pairs={{0,4},{4,8},{8,12},{12,16},{16,20},{20,24},{24,28},{1,5},{5,9},{9,... | collective-permute-start | bytes 393224 | tf_op jit(solution)/shard_map/ppermute | solution.py:22
  187.2 51.8 %collective-permute-start.9 = (bf16[64,8,128]{2,0,1:T(8,128)(2,1)S(1)}, bf16[64,8,128]{2,0,1:T(8,128)(2,1)S(1)}, u32[]{:S(2)}, u32[]{:S(2)}) collective-permute-start(bf16[64,8,128]{2,0,1:T(8,128)(2,1)S(1)} %get-tuple-element.35), channel_id=1, source_target_pairs={{4,0},{8,4},{12,8},{16,12},{20,16},{24,20},{28,24},{5,1},{9,5},{13... | collective-permute-start | bytes 393224 | tf_op jit(solution)/shard_map/ppermute | solution.py:23
  192.4 61.1 %collective-permute-start.4 = (bf16[64,8,128]{2,0,1:T(8,128)(2,1)}, bf16[64,8,128]{2,0,1:T(8,128)(2,1)}, u32[]{:S(2)}, u32[]{:S(2)}) collective-permute-start(bf16[64,8,128]{2,0,1:T(8,128)(2,1)} %get-tuple-element.39), channel_id=1, source_target_pairs={{0,4},{4,8},{8,12},{12,16},{16,20},{20,24},{24,28},{1,5},{5,9},{9,... | collective-permute-start | bytes 393224 | tf_op jit(solution)/shard_map/ppermute | solution.py:22
  194.3 60.2 %collective-permute-start.5 = (bf16[64,8,128]{2,0,1:T(8,128)(2,1)}, bf16[64,8,128]{2,0,1:T(8,128)(2,1)}, u32[]{:S(2)}, u32[]{:S(2)}) collective-permute-start(bf16[64,8,128]{2,0,1:T(8,128)(2,1)} %get-tuple-element.38), channel_id=1, source_target_pairs={{4,0},{8,4},{12,8},{16,12},{20,16},{24,20},{28,24},{5,1},{9,5},{13... | collective-permute-start | bytes 393224 | tf_op jit(solution)/shard_map/ppermute | solution.py:23
  239.0 0.7 copy-start.13
  239.6 0.6 copy-start.15
  245.3 25.1 %collective-permute-start.10 = (bf16[64,80,8]{1,2,0:T(8,128)(2,1)}, bf16[64,80,8]{1,2,0:T(8,128)(2,1)}, u32[]{:S(2)}, u32[]{:S(2)}) collective-permute-start(bf16[64,80,8]{1,2,0:T(8,128)(2,1)} %copy.156), channel_id=1, source_target_pairs={{1,0},{2,1},{3,2},{5,4},{6,5},{7,6},{9,8},{10,9},{11,10},{13,12},{... | collective-permute-start | bytes 245768 | tf_op jit(solution)/shard_map/ppermute | solution.py:23
  250.1 24.0 %collective-permute-start.11 = (bf16[64,80,8]{1,2,0:T(8,128)(2,1)}, bf16[64,80,8]{1,2,0:T(8,128)(2,1)}, u32[]{:S(2)}, u32[]{:S(2)}) collective-permute-start(bf16[64,80,8]{1,2,0:T(8,128)(2,1)} %copy.158), channel_id=1, source_target_pairs={{0,1},{1,2},{2,3},{4,5},{5,6},{6,7},{8,9},{9,10},{10,11},{12,13},{... | collective-permute-start | bytes 245768 | tf_op jit(solution)/shard_map/ppermute | solution.py:22
  260.7 32.4 %collective-permute-start.6 = (bf16[64,80,8]{1,2,0:T(8,128)(2,1)}, bf16[64,80,8]{1,2,0:T(8,128)(2,1)}, u32[]{:S(2)}, u32[]{:S(2)}) collective-permute-start(bf16[64,80,8]{1,2,0:T(8,128)(2,1)} %copy.143), channel_id=1, source_target_pairs={{0,1},{1,2},{2,3},{4,5},{5,6},{6,7},{8,9},{9,10},{10,11},{12,13},{... | collective-permute-start | bytes 245768 | tf_op jit(solution)/shard_map/ppermute | solution.py:22
  267.8 33.9 %collective-permute-start.7 = (bf16[64,80,8]{1,2,0:T(8,128)(2,1)}, bf16[64,80,8]{1,2,0:T(8,128)(2,1)}, u32[]{:S(2)}, u32[]{:S(2)}) collective-permute-start(bf16[64,80,8]{1,2,0:T(8,128)(2,1)} %copy.145), channel_id=1, source_target_pairs={{1,0},{2,1},{3,2},{5,4},{6,5},{7,6},{9,8},{10,9},{11,10},{13,12},{... | collective-permute-start | bytes 245768 | tf_op jit(solution)/shard_map/ppermute | solution.py:23
  282.2 0.9 copy-start.16
  284.3 0.9 copy-start.14
  285.2 4.1 copy-start.2
  285.6 3.6 copy-start
  305.4 3.1 copy-start.7
  308.5 2.8 copy-start.8
  314.5 4.2 copy-start.3
  314.5 4.2 copy-start.21
  314.5 4.2 copy-start.24
  314.5 4.2 copy-start.25
  316.8 9.8 %slice-start = ((s8[9437184]{0:T(1024)(128)(4,1)}), s8[4194304]{0:T(1024)(128)(4,1)S(1)}, s32[]{:S(2)}) async-start(s8[9437184]{0:T(1024)(128)(4,1)} %bitcast.78), calls=%async_computation.7 | async-start | bytes 8388608
  318.8 7.8 %slice-start.1 = ((s8[9437184]{0:T(1024)(128)(4,1)}), s8[4194304]{0:T(1024)(128)(4,1)S(1)}, s32[]{:S(2)}) async-start(s8[9437184]{0:T(1024)(128)(4,1)} %bitcast.78), calls=%async_computation.8 | async-start | bytes 8388608
  318.8 7.8 %slice-start.2 = ((s8[9437184]{0:T(1024)(128)(4,1)}), s8[1048576]{0:T(1024)(128)(4,1)S(1)}, s32[]{:S(2)}) async-start(s8[9437184]{0:T(1024)(128)(4,1)} %bitcast.78), calls=%async_computation.9 | async-start | bytes 2097152
  318.8 7.8 %copy-start.10 = (bf16[64,64,128]{2,1,0:T(8,128)(2,1)S(1)}, bf16[64,64,128]{2,1,0:T(8,128)(2,1)}, u32[]{:S(2)}) copy-start(bf16[64,64,128]{2,1,0:T(8,128)(2,1)} %param.7) | copy-start | bytes 3145732
Sparse Core Ops, SparseCore 0:
  293.2 127.8 all-reduce.1
where the time goes:
time: 438 us; the launch traced here: 430 us
  local copies, waits for them, and re-layouts  151 us (34%)
  waiting for transfers between devices  93.8 us (21%)
  starting transfers between devices  70.8 us (16%)
  blocking collectives  40.1 us (9%)
  other arithmetic  37 us (8%)
  matrix products  22.3 us (5%)
  between operations  14.8 us (3%)
    psum x1, waiting for transfers between devices, shards(): lax.psum((weight_acc / map_side, local_bias / map_side), ('row', 'col'))  87.5 us
    unnamed x82, local copies, waits for them, and re-layouts  46.6 us
    psum x1, blocking collectives, shards(): lax.psum((weight_acc / map_side, local_bias / map_side), ('row', 'col'))  40.1 us
    unnamed x17, other arithmetic  28.7 us
    ppermute x6, starting transfers between devices, with_halo(): after = lax.ppermute(first, axis, down)  22.4 us
    reshape x4, local copies, waits for them, and re-layouts, mirror(): jnp.swapaxes(member, 1, 2)  20.8 us
    all_to_all x4, local copies, waits for them, and re-layouts, mirror(): lax.all_to_all(for_sending(prepared), 'row', split_axis=2, concat_axis=3,...  19.3 us
    ppermute x6, starting transfers between devices, with_halo(): before = lax.ppermute(last, axis, up)  16.5 us
  transfers between devices with their start and end apart: 19, of which 5 were waited for; matrix products, arithmetic and copies ran while one was open for 44% of the time, Pallas kernels for 0%

commit v1 on v0

v1 whole, which is shorter than its diff:
```python
import functools

import jax
import jax.numpy as jnp
from jax import lax
from jax.experimental import pallas as pl
from jax.experimental.pallas import tpu as pltpu
from jax.sharding import PartitionSpec as P

DILATION_STEP = 8
STEP = DILATION_STEP
BF16, F32 = jnp.bfloat16, jnp.float32
VMEM_LIMIT = 40 * 1024 * 1024


def call(kernel, out_shape, *args, scratch=(), flops=0, name=None):
    out_bytes = sum(o.size * o.dtype.itemsize for o in jax.tree.leaves(out_shape))
    in_bytes = sum(a.size * a.dtype.itemsize for a in args)
    return pl.pallas_call(
        kernel,
        out_shape=out_shape,
        scratch_shapes=scratch,
        name=name,
        compiler_params=pltpu.CompilerParams(vmem_limit_bytes=VMEM_LIMIT),
        cost_estimate=pl.CostEstimate(
            flops=flops, bytes_accessed=in_bytes + out_bytes, transcendentals=0
        ),
    )(*args)


def shape(dims, dtype):
    return jax.ShapeDtypeStruct(tuple(dims), dtype)


def columns_of(rows, first):
    picked = [r[:, :STEP] if first else r[:, -STEP:] for r in rows]
    return jnp.concatenate(picked, axis=1)


def write_edges(tile, up_ref, down_ref, left_ref, right_ref):
    tile_rows, _, tile_cols = tile.shape
    span = tile_cols // STEP
    for group in range(tile_rows // span):
        rows = [tile[group * span + k] for k in range(span)]
        left_ref[group] = columns_of(rows, True)
        right_ref[group] = columns_of(rows, False)
    top = [tile[k] for k in range(STEP)]
    bottom = [tile[tile_rows - STEP + k] for k in range(STEP)]
    for k in range(STEP):
        up_ref[k] = bottom[k]
        down_ref[k] = top[k]
    up_ref[STEP] = jnp.concatenate([columns_of(bottom, True), columns_of(bottom, False)], axis=1)
    down_ref[STEP] = jnp.concatenate([columns_of(top, False), columns_of(top, True)], axis=1)


def edge_shapes(channels, tile_rows, tile_cols):
    message = shape((STEP + 1, channels, tile_cols), BF16)
    strips = shape((tile_rows * STEP // tile_cols, channels, tile_cols), BF16)
    return [message, message, strips, strips]


def exchange_edges(up, down, left, right):
    half = up.shape[2] // 2
    rows, cols = lax.axis_size("row"), lax.axis_size("col")
    up_row = [(i, i + 1) for i in range(rows - 1)]
    up_col = [(i, i + 1) for i in range(cols - 1)]
    before = lax.ppermute(up, "row", up_row)
    after = lax.ppermute(down, "row", [(j, i) for i, j in up_row])
    lower = lax.broadcasted_iota(jnp.int32, (1, 1, up.shape[2]), 2) < half
    corner_left = jnp.where(lower, before[STEP:], after[STEP:])
    corner_right = jnp.where(lower, after[STEP:], before[STEP:])
    from_right = lax.ppermute(
        jnp.concatenate([left, corner_left]), "col", [(j, i) for i, j in up_col]
    )
    from_left = lax.ppermute(jnp.concatenate([right, corner_right]), "col", up_col)
    return before, after, from_left, from_right


def write_shifted(tile, before, after, from_left, from_right, stack):
    tile_rows, channels, tile_cols = tile.shape
    span = tile_cols // STEP
    corner = tile_rows // span
    half = tile_cols // 2
    for row in range(tile_rows + 2 * STEP):
        own = row - STEP
        if own < 0:
            middle, group, at_left, at_right = before[row], corner, half + STEP * row, STEP * row
        elif own >= tile_rows:
            k = own - tile_rows
            middle, group, at_left, at_right = after[k], corner, STEP * k, half + STEP * k
        else:
            middle, group = tile[own], own // span
            at_left = at_right = STEP * (own % span)
        left = from_left[group][:, at_left : at_left + STEP]
        right = from_right[group][:, at_right : at_right + STEP]
        stack[row, :channels] = jnp.concatenate([left, middle[:, :-STEP]], axis=1)
        stack[row, channels : 2 * channels] = middle
        stack[row, 2 * channels :] = jnp.concatenate([middle[:, STEP:], right], axis=1)


def convolve(stack, matrix, tile_rows, emit):
    channels = matrix.shape[0] // 3
    cols = stack.shape[2]
    weights = matrix[...]
    for pair in range(STEP // 2):
        products = []
        for k in range(tile_rows // STEP + 2):
            row = STEP * k + 2 * pair
            both = jnp.concatenate([stack[row], stack[row + 1]], axis=1)
            products.append(jnp.dot(weights, both, preferred_element_type=F32))
            if k >= 2:
                total = (
                    products[k - 2][:channels]
                    + products[k - 1][channels : 2 * channels]
                    + products[k][2 * channels :]
                )
                out_row = STEP * (k - 2) + 2 * pair
                emit(out_row, total[:, :cols])
                emit(out_row + 1, total[:, cols:])


def split_kernel(x, tile, up, down, left, right):
    rows = x.shape[1]
    for a in range(0, rows, 16):
        tile[a : a + 16] = jnp.swapaxes(x[:, a : a + 16], 0, 1)
    write_edges(tile, up, down, left, right)


def forward_kernel(
    tile, before, after, from_left, from_right, matrix, bias, stack, mixed, slope, kept
):
    tile_rows = tile.shape[0]
    write_shifted(tile, before, after, from_left, from_right, stack)
    offset = bias[...]

    def emit(row, total):
        pre_act = total + offset
        rise = jnp.exp(jnp.minimum(pre_act, 0.0))
        slope[row] = rise
        elu = jnp.where(pre_act > 0, pre_act, rise - 1.0)
        kept[row] = (tile[row].astype(F32) + elu).astype(BF16)

    convolve(stack, matrix, tile_rows, emit)
    for a in range(0, tile_rows, 16):
        mixed[:, a : a + 16] = jnp.swapaxes(kept[a : a + 16], 0, 1)


def grad_pre_kernel(cot, mirrored, slope, tile, up, down, left, right):
    rows = cot.shape[1]
    for a in range(0, rows, 16):
        grad_mixed = cot[:, a : a + 16].astype(F32) + mirrored[:, a : a + 16].astype(F32)
        tile[a : a + 16] = (jnp.swapaxes(grad_mixed, 0, 1) * slope[a : a + 16]).astype(BF16)
    write_edges(tile, up, down, left, right)


def weight_kernel(side, grad, stack, packed):
    tile_rows, channels, cols = grad.shape
    nothing = jnp.zeros((channels, cols), BF16)

    def taps(row):
        own = [row - STEP * p for p in range(3)]
        return jnp.concatenate([grad[a] if 0 <= a < tile_rows else nothing for a in own], axis=0)

    total = jnp.zeros((3 * channels, 3 * channels), F32)
    for row in range(0, tile_rows + 2 * STEP, 2):
        total = total + lax.dot_general(
            jnp.concatenate([taps(row), taps(row + 1)], axis=1),
            jnp.concatenate([stack[row], stack[row + 1]], axis=1),
            (((1,), (1,)), ((), ())),
            preferred_element_type=F32,
        )
    cells = jnp.zeros((channels, cols), F32)
    for row in range(tile_rows):
        cells = cells + grad[row].astype(F32)
    bias = jnp.broadcast_to(jnp.sum(cells, axis=1, keepdims=True), (channels, channels))
    blocks = [
        total[p * channels : (p + 1) * channels, q * channels : (q + 1) * channels]
        for p in range(3)
        for q in range(3)
    ] + [bias]
    for k in range(0, len(blocks), 2):
        packed[k // 2] = jnp.concatenate(blocks[k : k + 2], axis=1) * (1.0 / side)


def unpack_kernel(mine, other, weight, bias):
    channels = mine.shape[1]
    for k in range(9):
        at = channels * (k % 2)
        block = mine[k // 2] + other[k // 2]
        weight[k // 3, k % 3] = block[:, at : at + channels]
    last = mine[4][:, channels:] + other[4][:, channels:]
    line = lax.broadcasted_iota(jnp.int32, last.shape, 0)
    lane = lax.broadcasted_iota(jnp.int32, last.shape, 1)
    bias[...] = jnp.sum(jnp.where(line == lane, last, 0.0), axis=0, keepdims=True)


def input_grad_kernel(
    tile, before, after, from_left, from_right, matrix, cot, mirrored, out, stack, kept
):
    tile_rows = tile.shape[0]
    write_shifted(tile, before, after, from_left, from_right, stack)

    def emit(row, total):
        kept[row] = total

    convolve(stack, matrix, tile_rows, emit)
    for a in range(0, tile_rows, 16):
        grad_mixed = cot[:, a : a + 16].astype(F32) + mirrored[:, a : a + 16].astype(F32)
        out[:, a : a + 16] = (grad_mixed + jnp.swapaxes(kept[a : a + 16], 0, 1)).astype(BF16)


def turn_kernel(add, *refs):
    if add:
        source, own, out = refs
    else:
        source, out = refs
    cols_of, ratio, channels, tile_rows, tile_cols = source.shape
    for z in range(cols_of):
        for c in range(channels):
            square = jnp.concatenate([source[z, e, c] for e in range(ratio)], axis=0)
            turned = square.T
            for h in range(ratio):
                part = turned[h * tile_rows : (h + 1) * tile_rows]
                if add:
                    part = (part.astype(F32) + own[z, h, c].astype(F32)).astype(BF16)
                out[z, h, c] = part


def mirror(x, add):
    channels, tile_rows, tile_cols = x.shape
    rows, cols = lax.axis_size("row"), lax.axis_size("col")
    ratio = tile_cols // tile_rows
    blocks = (cols, ratio, channels // rows, tile_rows, tile_cols)
    dealt = lax.all_to_all(x, "row", split_axis=0, concat_axis=0, tiled=True)
    moved = lax.all_to_all(dealt, "col", split_axis=0, concat_axis=0, tiled=True)
    args = [moved.reshape(blocks)] + ([dealt.reshape(blocks)] if add else [])
    turned = call(
        functools.partial(turn_kernel, add),
        shape(blocks, BF16),
        *args,
        name="turn_and_add" if add else "turn",
    )
    return lax.all_to_all(turned.reshape(x.shape), "row", split_axis=0, concat_axis=0, tiled=True)


def summed(part):
    hops = []
    for axis in ("row", "col"):
        size, reach = lax.axis_size(axis), 1
        while reach < size:
            hops.append((axis, [(i, i ^ reach) for i in range(size)]))
            reach *= 2
    for axis, pairs in hops[:-1]:
        part = part + lax.ppermute(part, axis, pairs)
    axis, pairs = hops[-1]
    return part, lax.ppermute(part, axis, pairs)


def shards(pair_feature_map, conv_weight, conv_bias, cotangent):
    channels, tile_rows, tile_cols = pair_feature_map.shape
    side = tile_rows * lax.axis_size("row")
    tile_shape = shape((tile_rows, channels, tile_cols), BF16)
    edges = edge_shapes(channels, tile_rows, tile_cols)
    stack_dims = (tile_rows + 2 * STEP, 3 * channels, tile_cols)
    conv_flops = 2 * 9 * channels * channels * tile_rows * tile_cols
    w_front = jnp.transpose(conv_weight, (0, 2, 1, 3)).reshape(3 * channels, 3 * channels)
    w_back = jnp.transpose(conv_weight[::-1, ::-1], (0, 3, 1, 2)).reshape(
        3 * channels, 3 * channels
    )

    mirrored = mirror(cotangent, False)

    tile, *edge = call(split_kernel, [tile_shape] + edges, pair_feature_map, name="split")
    halo = exchange_edges(*edge)
    stack, mixed, slope = call(
        forward_kernel,
        [
            shape(stack_dims, BF16),
            shape(pair_feature_map.shape, BF16),
            shape((tile_rows, channels, tile_cols), F32),
        ],
        tile,
        *halo,
        w_front,
        conv_bias[:, None],
        scratch=[pltpu.VMEM((tile_rows, channels, tile_cols), BF16)],
        flops=conv_flops,
        name="forward",
    )
    symmetric = mirror(mixed, True)

    grad, *edge = call(
        grad_pre_kernel, [tile_shape] + edges, cotangent, mirrored, slope, name="grad_pre"
    )
    packed = call(
        functools.partial(weight_kernel, side),
        shape((5, channels, 2 * channels), F32),
        grad,
        stack,
        flops=conv_flops,
        name="weight_terms",
    )
    halo = exchange_edges(*edge)
    grad_input = call(
        input_grad_kernel,
        shape(pair_feature_map.shape, BF16),
        grad,
        *halo,
        w_back,
        cotangent,
        mirrored,
        scratch=[
            pltpu.VMEM(stack_dims, BF16),
            pltpu.VMEM((tile_rows, channels, tile_cols), F32),
        ],
        flops=conv_flops,
        name="input_grad",
    )
    grad_weight, grad_bias = call(
        unpack_kernel,
        [shape((3, 3, channels, channels), F32), shape((1, channels), F32)],
        *summed(packed),
        name="unpack",
    )
    return symmetric, grad_input, grad_weight, grad_bias.reshape(channels)


def solution(mesh):
    placed = (P(None, "row", "col"), P(), P(), P(None, "row", "col"))
    return jax.shard_map(
        shards,
        mesh=mesh,
        in_specs=placed,
        out_specs=(P(None, "row", "col"), P(None, "row", "col"), P(), P()),
        check_vma=False,
    )
```

time: 438 us -> 182 us (0.42)
  the two profiles are of different devices: /device:TPU:12 before, /device:TPU:0 now
where the time goes in v1:
time: 182 us; the launch traced here: 181 us
  waiting for transfers between devices  60.7 us (33%)
  starting transfers between devices  48 us (26%)
  blocking collectives  38.6 us (21%)
  Pallas kernels  16.5 us (9%)
  local copies, waits for them, and re-layouts  13.6 us (7%)
  other arithmetic  2.92 us (2%)
    all_to_all x1, blocking collectives, mirror(): dealt = lax.all_to_all(x, 'row', split_axis=0, concat_axis=0, tiled=True)  20.8 us
    all_to_all x2, waiting for transfers between devices, mirror(): lax.all_to_all(dealt, 'col', split_axis=0, concat_axis=0, tiled=True)  20.4 us
    all_to_all x1, blocking collectives, mirror(): lax.all_to_all(turned.reshape(x.shape), 'row', split_axis=0, concat_axis=...  17.8 us
    ppermute x4, waiting for transfers between devices, summed(): part = part + lax.ppermute(part, axis, pairs)  16.9 us
    pallas_call x8, Pallas kernels, call(): pl.pallas_call(kernel, out_shape=out_shape, scratch_shapes=scratch, name=...  16.5 us
    all_to_all x2, starting transfers between devices, mirror(): lax.all_to_all(dealt, 'col', split_axis=0, concat_axis=0, tiled=True)  15.2 us
    all_to_all x1, waiting for transfers between devices, mirror(): dealt = lax.all_to_all(x, 'row', split_axis=0, concat_axis=0, tiled=True)  15.1 us
    ppermute x2, starting transfers between devices, exchange_edges(): lax.ppermute(jnp.concatenate([right, corner_right]), 'col', up_col)  9.73 us
  transfers between devices with their start and end apart: 17, of which 8 were waited for; matrix products, arithmetic and copies ran while one was open for 4% of the time, Pallas kernels for 8%

profile of v1, /device:TPU:0, one launch (start us, length us, event | category | flops | bytes accessed | tf_op | source)
XLA Modules:
  0.0 181.2 jit_solution(2403426123575507530)
XLA Ops:
  0.6 0.0 copy-start.13
  0.7 0.0 copy-start.15
  0.7 20.8 %all_to_all.30 = bf16[64,64,128]{2,1,0:T(8,128)(2,1)} all-to-all(bf16[64,64,128]{2,1,0:T(8,128)(2,1)} %cot.3), channel_id=1, replica_groups=mesh['row'=8,'col'=4] {'row'}, dimensions={0} | all-to-all | bytes 2097152 | tf_op jit(solution)/shard_map/all_to_all | solution.py:234
  21.4 5.3 %all-to-all-start.4 = ((bf16[64,64,128]{2,1,0:T(8,128)(2,1)}), bf16[64,64,128]{2,1,0:T(8,128)(2,1)S(1)}, u32[]{:S(2)}, u32[]{:S(2)}) async-start(bf16[64,64,128]{2,1,0:T(8,128)(2,1)} %all_to_all.30), calls=%async_computation.4 | async-start | bytes 2097152 | tf_op jit(solution)/shard_map/all_to_all | solution.py:235
  26.7 0.9 split.1
  27.6 1.3 collective-permute-start
  28.9 1.3 collective-permute-start.1
  30.3 0.0 copy-start.14
  30.3 0.0 collective-permute-done.before
  30.3 2.7 %collective-permute-done.1.after = bf16[9,64,128]{2,1,0:T(8,128)(2,1)S(1)} collective-permute-done((bf16[9,64,128]{2,1,0:T(8,128)(2,1)S(1)}, bf16[9,64,128]{2,1,0:T(8,128)(2,1)S(1)}, u32[]{:S(2)}, u32[]{:S(2)}) %collective-permute-start.1) | collective-permute-done | bytes 147488 | tf_op jit(solution)/shard_map/ppermute | solution.py:68
  33.0 1.3 collective-permute-start.3
  34.3 4.6 %collective-permute-start.2 = (bf16[5,64,128]{2,1,0:T(8,128)(2,1)S(1)}, bf16[5,64,128]{2,1,0:T(8,128)(2,1)S(1)}, u32[]{:S(2)}, u32[]{:S(2)}) collective-permute-start(bf16[5,64,128]{2,1,0:T(8,128)(2,1)S(1)} %pad_maximum_fusion), channel_id=1, source_target_pairs={{0,1},{1,2},{2,3},{4,5},{5,6},{6,7},{8,9},{9,10},{10,11},{12,13},{... | collective-permute-start | bytes 245768 | tf_op jit(solution)/shard_map/ppermute | solution.py:75
  38.9 0.1 copy.11
  39.1 0.2 reshape.39.matrix
  39.2 0.1 copy.12.bias
  39.3 1.5 collective-permute-done.3.from_right
  40.9 4.0 %collective-permute-done.2.from_left = bf16[5,64,128]{2,1,0:T(8,128)(2,1)S(1)} collective-permute-done((bf16[5,64,128]{2,1,0:T(8,128)(2,1)S(1)}, bf16[5,64,128]{2,1,0:T(8,128)(2,1)S(1)}, u32[]{:S(2)}, u32[]{:S(2)}) %collective-permute-start.2) | collective-permute-done | bytes 81952 | tf_op jit(solution)/shard_map/ppermute | solution.py:75
  44.9 4.0 %forward.1 = (bf16[80,192,128]{2,1,0:T(8,128)(2,1)S(1)}, bf16[64,64,128]{2,1,0:T(8,128)(2,1)}, f32[64,64,128]{2,1,0:T(8,128)S(1)}) custom-call(bf16[64,64,128]{2,1,0:T(8,128)(2,1)S(1)} %get-tuple-element.19.tile, bf16[9,64,128]{2,1,0:T(8,128)(2,1)S(1)} %collective-permute-done.before, bf16[9,64,128]{2,1,0:T(8,128)(2,1)S(1)} %collective-permute-done.1.after, ...), custom_call_target="tpu_custom_call" | custom-call | flops 603979776 | bytes 8659200 | tf_op jit(solution)/shard_map/forward/pallas_call | solution.py:19
  48.9 1.9 %copy-done.3 = bf16[80,192,128]{2,1,0:T(8,128)(2,1)} copy-done((bf16[80,192,128]{2,1,0:T(8,128)(2,1)}, bf16[80,192,128]{2,1,0:T(8,128)(2,1)S(1)}, u32[]{:S(2)}) %copy-start.3) | copy-done | bytes 3932184
  50.8 1.4 copy-done.5
  52.1 0.5 all-to-all-done.4
  52.7 4.4 %all-to-all-start = ((bf16[64,64,128]{2,1,0:T(8,128)(2,1)}), bf16[64,64,128]{2,1,0:T(8,128)(2,1)}, u32[]{:S(2)}, u32[]{:S(2)}) async-start(bf16[64,64,128]{2,1,0:T(8,128)(2,1)} %get-tuple-element.24), calls=%async_computation | async-start | bytes 2097152 | tf_op jit(solution)/shard_map/all_to_all | solution.py:234
  57.1 0.3 turn.1
  57.4 15.1 %all-to-all-done = bf16[64,64,128]{2,1,0:T(8,128)(2,1)} async-done(((bf16[64,64,128]{2,1,0:T(8,128)(2,1)}), bf16[64,64,128]{2,1,0:T(8,128)(2,1)}, u32[]{:S(2)}, u32[]{:S(2)}) %all-to-all-start) | async-done | bytes 1048608 | tf_op jit(solution)/shard_map/all_to_all | solution.py:234
  72.5 17.8 %all_to_all.31.mirrored = bf16[64,64,128]{2,1,0:T(8,128)(2,1)S(1)} all-to-all(bf16[64,64,128]{2,1,0:T(8,128)(2,1)S(1)} %bitcast.12), channel_id=1, replica_groups=mesh['row'=8,'col'=4] {'row'}, dimensions={0} | all-to-all | bytes 2097152 | tf_op jit(solution)/shard_map/all_to_all | solution.py:243
  90.3 10.0 %all-to-all-start.1 = ((bf16[64,64,128]{2,1,0:T(8,128)(2,1)}), bf16[64,64,128]{2,1,0:T(8,128)(2,1)S(1)}, u32[]{:S(2)}, u32[]{:S(2)}) async-start(bf16[64,64,128]{2,1,0:T(8,128)(2,1)} %all-to-all-done), calls=%async_computation.1 | async-start | bytes 2097152 | tf_op jit(solution)/shard_map/all_to_all | solution.py:235
  100.2 1.7 copy-done.6
  102.0 1.4 grad_pre.1
  103.3 0.0 copy-start.12
  103.3 0.0 copy-start.1
  103.4 0.6 copy-done.12
  104.0 1.3 weight_terms.1
  105.3 0.1 collective-permute-start.8
  105.4 19.9 %all-to-all-done.1 = bf16[64,64,128]{2,1,0:T(8,128)(2,1)S(1)} async-done(((bf16[64,64,128]{2,1,0:T(8,128)(2,1)}), bf16[64,64,128]{2,1,0:T(8,128)(2,1)S(1)}, u32[]{:S(2)}, u32[]{:S(2)}) %all-to-all-start.1) | async-done | bytes 1048608 | tf_op jit(solution)/shard_map/all_to_all | solution.py:235
  125.3 2.5 %turn_and_add.1 = bf16[4,2,8,64,128]{4,3,2,1,0:T(8,128)(2,1)} custom-call(bf16[4,2,8,64,128]{4,3,2,1,0:T(8,128)(2,1)S(1)} %bitcast.10, bf16[4,2,8,64,128]{4,3,2,1,0:T(8,128)(2,1)} %bitcast.3.refs_1_), custom_call_target="tpu_custom_call" | custom-call | bytes 3145728 | tf_op jit(solution)/shard_map/turn_and_add/pallas_call | solution.py:19
  127.8 4.4 %all-to-all-start.2 = ((bf16[64,64,128]{2,1,0:T(8,128)(2,1)}), bf16[64,64,128]{2,1,0:T(8,128)(2,1)}, u32[]{:S(2)}, u32[]{:S(2)}) async-start(bf16[64,64,128]{2,1,0:T(8,128)(2,1)} %bitcast.4), calls=%async_computation.2 | async-start | bytes 2097152 | tf_op jit(solution)/shard_map/all_to_all | solution.py:243
  132.2 0.0 collective-permute-done.8
  132.2 2.0 %collective-permute-start.9 = (f32[5,64,128]{2,1,0:T(8,128)S(1)}, f32[5,64,128]{2,1,0:T(8,128)S(1)}, u32[]{:S(2)}, u32[]{:S(2)}) collective-permute-start(f32[5,64,128]{2,1,0:T(8,128)S(1)} %add.12), channel_id=1, source_target_pairs={{0,8},{4,12},{8,0},{12,4},{16,24},{20,28},{24,16},{28,20},{1,9},{5... | collective-permute-start | bytes 491528 | tf_op jit(solution)/shard_map/ppermute | solution.py:254
  134.2 1.8 collective-permute-start.4
  136.0 1.3 collective-permute-start.5
  137.3 13.3 %collective-permute-done.9 = f32[5,64,128]{2,1,0:T(8,128)S(1)} collective-permute-done((f32[5,64,128]{2,1,0:T(8,128)S(1)}, f32[5,64,128]{2,1,0:T(8,128)S(1)}, u32[]{:S(2)}, u32[]{:S(2)}) %collective-permute-start.9) | collective-permute-done | bytes 163872 | tf_op jit(solution)/shard_map/ppermute | solution.py:254
  150.6 1.1 collective-permute-start.10
  151.7 0.0 collective-permute-done.4.before
  151.7 0.0 collective-permute-done.5.after
  151.7 0.7 broadcast_select_fusion
  152.4 3.6 %collective-permute-done.10 = f32[5,64,128]{2,1,0:T(8,128)S(1)} collective-permute-done((f32[5,64,128]{2,1,0:T(8,128)S(1)}, f32[5,64,128]{2,1,0:T(8,128)S(1)}, u32[]{:S(2)}, u32[]{:S(2)}) %collective-permute-start.10) | collective-permute-done | bytes 163872 | tf_op jit(solution)/shard_map/ppermute | solution.py:254
  156.0 0.1 collective-permute-start.11
  156.1 1.5 pad_maximum_fusion.3
  157.5 1.3 collective-permute-start.7
  158.8 0.6 pad_maximum_fusion.2
  159.5 5.2 %collective-permute-start.6 = (bf16[5,64,128]{2,1,0:T(8,128)(2,1)}, bf16[5,64,128]{2,1,0:T(8,128)(2,1)}, u32[]{:S(2)}, u32[]{:S(2)}) collective-permute-start(bf16[5,64,128]{2,1,0:T(8,128)(2,1)} %pad_maximum_fusion.2), channel_id=1, source_target_pairs={{0,1},{1,2},{2,3},{4,5},{5,6},{6,7},{8,9},{9,10},{10,11},{12,13},{... | collective-permute-start | bytes 245768 | tf_op jit(solution)/shard_map/ppermute | solution.py:75
  164.6 0.0 collective-permute-done.11
  164.7 2.8 %collective-permute-start.12 = (f32[5,64,128]{2,1,0:T(8,128)S(1)}, f32[5,64,128]{2,1,0:T(8,128)}, u32[]{:S(2)}, u32[]{:S(2)}) collective-permute-start(f32[5,64,128]{2,1,0:T(8,128)S(1)} %add.15.mine), channel_id=1, source_target_pairs={{0,2},{1,3},{2,0},{3,1},{4,6},{5,7},{6,4},{7,5},{8,10},{9,11},{10,... | collective-permute-start | bytes 491528 | tf_op jit(solution)/shard_map/ppermute | solution.py:256
  167.5 1.6 reverse_bitcast_fusion
  169.1 1.7 copy.13
  170.8 1.1 reshape.45.matrix
  171.9 0.0 collective-permute-done.7.from_right
  171.9 0.0 collective-permute-done.6.from_left
  172.0 0.9 copy-done.9
  172.9 4.4 %input_grad.1 = bf16[64,64,128]{2,1,0:T(8,128)(2,1)} custom-call(bf16[64,64,128]{2,1,0:T(8,128)(2,1)S(1)} %copy-done.2, bf16[9,64,128]{2,1,0:T(8,128)(2,1)S(1)} %collective-permute-done.4.before, bf16[9,64,128]{2,1,0:T(8,128)(2,1)S(1)} %copy-done.9, bf16[5,64,128]{2,1,0:T(8,128)(2,1)} %collective-permute-done.6.from_left, ...), custom_call_target="tpu_custom_call" | custom-call | flops 603979776 | bytes 4726784 | tf_op jit(solution)/shard_map/input_grad/pallas_call | solution.py:19
  177.2 0.0 all-to-all-done.2
  177.2 0.0 collective-permute-done.12.other
  177.2 1.7 unpack.1
  179.0 2.3 %copy.15 = bf16[64,64,128]{2,1,0:T(8,128)(2,1)} copy(bf16[64,64,128]{2,1,0:T(8,128)(2,1)} %all-to-all-done.2) | data formatting | bytes 2097152
  (30 shorter events, 0.2 us)
Async XLA Ops:
  0.6 26.1 %copy-start.7 = (bf16[64,64,128]{2,1,0:T(8,128)(2,1)S(1)}, bf16[64,64,128]{2,1,0:T(8,128)(2,1)}, u32[]{:S(2)}) copy-start(bf16[64,64,128]{2,1,0:T(8,128)(2,1)} %x.1) | copy-start | bytes 3145732
  0.6 38.3 %copy-start.13 = (bf16[3,3,64,64]{3,2,1,0:T(8,128)(2,1)S(1)}, bf16[3,3,64,64]{3,2,1,0:T(8,128)(2,1)}, u32[]{:S(2)}) copy-start(bf16[3,3,64,64]{3,2,1,0:T(8,128)(2,1)} %param.5) | copy-start | bytes 221188
  0.7 38.6 %copy-start.15 = (f32[64]{0:T(128)S(1)}, f32[64]{0:T(128)}, u32[]{:S(2)}) copy-start(f32[64]{0:T(128)} %param.6) | copy-start | bytes 772
  21.4 31.2 %all-to-all-start.4 = ((bf16[64,64,128]{2,1,0:T(8,128)(2,1)}), bf16[64,64,128]{2,1,0:T(8,128)(2,1)S(1)}, u32[]{:S(2)}, u32[]{:S(2)}) async-start(bf16[64,64,128]{2,1,0:T(8,128)(2,1)} %all_to_all.30), calls=%async_computation.4 | async-start | bytes 2097152 | tf_op jit(solution)/shard_map/all_to_all | solution.py:235
  27.6 2.6 %collective-permute-start = (bf16[9,64,128]{2,1,0:T(8,128)(2,1)S(1)}, bf16[9,64,128]{2,1,0:T(8,128)(2,1)S(1)}, u32[]{:S(2)}, u32[]{:S(2)}) collective-permute-start(bf16[9,64,128]{2,1,0:T(8,128)(2,1)S(1)} %get-tuple-element.20), channel_id=1, source_target_pairs={{0,4},{4,8},{8,12},{12,16},{16,20},{20,24},{24,28},{1,5},{5,9},{9,... | collective-permute-start | bytes 442376 | tf_op jit(solution)/shard_map/ppermute | solution.py:67
  28.9 4.0 %collective-permute-start.1 = (bf16[9,64,128]{2,1,0:T(8,128)(2,1)S(1)}, bf16[9,64,128]{2,1,0:T(8,128)(2,1)S(1)}, u32[]{:S(2)}, u32[]{:S(2)}) collective-permute-start(bf16[9,64,128]{2,1,0:T(8,128)(2,1)S(1)} %get-tuple-element.21), channel_id=1, source_target_pairs={{4,0},{8,4},{12,8},{16,12},{20,16},{24,20},{28,24},{5,1},{9,5},{13... | collective-permute-start | bytes 442376 | tf_op jit(solution)/shard_map/ppermute | solution.py:68
  30.3 4.1 %copy-start.14 = (pred[128]{0:T(512)(128)(4,1)}, pred[128]{0:T(512)(128)(4,1)S(1)}, u32[]{:S(2)}) copy-start(pred[128]{0:T(512)(128)(4,1)S(1)} %iota_compare_fusion) | copy-start | bytes 388
  33.0 7.8 %collective-permute-start.3 = (bf16[5,64,128]{2,1,0:T(8,128)(2,1)S(1)}, bf16[5,64,128]{2,1,0:T(8,128)(2,1)S(1)}, u32[]{:S(2)}, u32[]{:S(2)}) collective-permute-start(bf16[5,64,128]{2,1,0:T(8,128)(2,1)S(1)} %pad_maximum_fusion.1), channel_id=1, source_target_pairs={{1,0},{2,1},{3,2},{5,4},{6,5},{7,6},{9,8},{10,9},{11,10},{13,12},{... | collective-permute-start | bytes 245768 | tf_op jit(solution)/shard_map/ppermute | solution.py:72
  34.3 10.5 %collective-permute-start.2 = (bf16[5,64,128]{2,1,0:T(8,128)(2,1)S(1)}, bf16[5,64,128]{2,1,0:T(8,128)(2,1)S(1)}, u32[]{:S(2)}, u32[]{:S(2)}) collective-permute-start(bf16[5,64,128]{2,1,0:T(8,128)(2,1)S(1)} %pad_maximum_fusion), channel_id=1, source_target_pairs={{0,1},{1,2},{2,3},{4,5},{5,6},{6,7},{8,9},{9,10},{10,11},{12,13},{... | collective-permute-start | bytes 245768 | tf_op jit(solution)/shard_map/ppermute | solution.py:75
  48.9 1.9 %copy-start.3 = (bf16[80,192,128]{2,1,0:T(8,128)(2,1)}, bf16[80,192,128]{2,1,0:T(8,128)(2,1)S(1)}, u32[]{:S(2)}) copy-start(bf16[80,192,128]{2,1,0:T(8,128)(2,1)S(1)} %get-tuple-element.31.stack) | copy-start | bytes 11796484
  50.8 1.4 copy-start.5
  52.7 47.5 %copy-start = (bf16[64,64,128]{2,1,0:T(8,128)(2,1)S(1)}, bf16[64,64,128]{2,1,0:T(8,128)(2,1)}, u32[]{:S(2)}) copy-start(bf16[64,64,128]{2,1,0:T(8,128)(2,1)} %cot.3) | copy-start | bytes 3145732
  52.7 19.8 %all-to-all-start = ((bf16[64,64,128]{2,1,0:T(8,128)(2,1)}), bf16[64,64,128]{2,1,0:T(8,128)(2,1)}, u32[]{:S(2)}, u32[]{:S(2)}) async-start(bf16[64,64,128]{2,1,0:T(8,128)(2,1)} %get-tuple-element.24), calls=%async_computation | async-start | bytes 2097152 | tf_op jit(solution)/shard_map/all_to_all | solution.py:234
  90.3 35.0 %all-to-all-start.1 = ((bf16[64,64,128]{2,1,0:T(8,128)(2,1)}), bf16[64,64,128]{2,1,0:T(8,128)(2,1)S(1)}, u32[]{:S(2)}, u32[]{:S(2)}) async-start(bf16[64,64,128]{2,1,0:T(8,128)(2,1)} %all-to-all-done), calls=%async_computation.1 | async-start | bytes 2097152 | tf_op jit(solution)/shard_map/all_to_all | solution.py:235
  100.2 3.8 %copy-start.4 = (bf16[80,192,128]{2,1,0:T(8,128)(2,1)S(1)}, bf16[80,192,128]{2,1,0:T(8,128)(2,1)}, u32[]{:S(2)}) copy-start(bf16[80,192,128]{2,1,0:T(8,128)(2,1)} %copy-done.3) | copy-start | bytes 11796484
  100.2 1.7 copy-start.6
  103.3 0.7 copy-start.12
  103.3 1.9 %copy-start.1 = (bf16[64,64,128]{2,1,0:T(8,128)(2,1)}, bf16[64,64,128]{2,1,0:T(8,128)(2,1)S(1)}, u32[]{:S(2)}) copy-start(bf16[64,64,128]{2,1,0:T(8,128)(2,1)S(1)} %get-tuple-element.26.tile.grad) | copy-start | bytes 3145732
  103.4 1.9 %copy-start.10 = (bf16[4,64,128]{2,1,0:T(8,128)(2,1)}, bf16[4,64,128]{2,1,0:T(8,128)(2,1)S(1)}, u32[]{:S(2)}) copy-start(bf16[4,64,128]{2,1,0:T(8,128)(2,1)S(1)} %get-tuple-element.30) | copy-start | bytes 196612
  103.4 1.9 %copy-start.11 = (bf16[9,64,128]{2,1,0:T(8,128)(2,1)}, bf16[9,64,128]{2,1,0:T(8,128)(2,1)S(1)}, u32[]{:S(2)}) copy-start(bf16[9,64,128]{2,1,0:T(8,128)(2,1)S(1)} %get-tuple-element.28) | copy-start | bytes 442372
  105.3 26.9 %collective-permute-start.8 = (f32[5,64,128]{2,1,0:T(8,128)S(1)}, f32[5,64,128]{2,1,0:T(8,128)S(1)}, u32[]{:S(2)}, u32[]{:S(2)}) collective-permute-start(f32[5,64,128]{2,1,0:T(8,128)S(1)} %weight_terms.1), channel_id=1, source_target_pairs={{0,4},{4,0},{8,12},{12,8},{16,20},{20,16},{24,28},{28,24},{1,5},{5... | collective-permute-start | bytes 491528 | tf_op jit(solution)/shard_map/ppermute | solution.py:254
  127.8 44.1 %copy-start.2 = (bf16[64,64,128]{2,1,0:T(8,128)(2,1)S(1)}, bf16[64,64,128]{2,1,0:T(8,128)(2,1)}, u32[]{:S(2)}) copy-start(bf16[64,64,128]{2,1,0:T(8,128)(2,1)} %copy-done.1) | copy-start | bytes 3145732
  127.8 49.4 %all-to-all-start.2 = ((bf16[64,64,128]{2,1,0:T(8,128)(2,1)}), bf16[64,64,128]{2,1,0:T(8,128)(2,1)}, u32[]{:S(2)}, u32[]{:S(2)}) async-start(bf16[64,64,128]{2,1,0:T(8,128)(2,1)} %bitcast.4), calls=%async_computation.2 | async-start | bytes 2097152 | tf_op jit(solution)/shard_map/all_to_all | solution.py:243
  132.2 18.3 %collective-permute-start.9 = (f32[5,64,128]{2,1,0:T(8,128)S(1)}, f32[5,64,128]{2,1,0:T(8,128)S(1)}, u32[]{:S(2)}, u32[]{:S(2)}) collective-permute-start(f32[5,64,128]{2,1,0:T(8,128)S(1)} %add.12), channel_id=1, source_target_pairs={{0,8},{4,12},{8,0},{12,4},{16,24},{20,28},{24,16},{28,20},{1,9},{5... | collective-permute-start | bytes 491528 | tf_op jit(solution)/shard_map/ppermute | solution.py:254
  134.2 17.5 %collective-permute-start.4 = (bf16[9,64,128]{2,1,0:T(8,128)(2,1)}, bf16[9,64,128]{2,1,0:T(8,128)(2,1)S(1)}, u32[]{:S(2)}, u32[]{:S(2)}) collective-permute-start(bf16[9,64,128]{2,1,0:T(8,128)(2,1)} %copy-done.12), channel_id=1, source_target_pairs={{0,4},{4,8},{8,12},{12,16},{16,20},{20,24},{24,28},{1,5},{5,9},{9,... | collective-permute-start | bytes 442376 | tf_op jit(solution)/shard_map/ppermute | solution.py:67
  136.0 15.7 %collective-permute-start.5 = (bf16[9,64,128]{2,1,0:T(8,128)(2,1)}, bf16[9,64,128]{2,1,0:T(8,128)(2,1)S(1)}, u32[]{:S(2)}, u32[]{:S(2)}) collective-permute-start(bf16[9,64,128]{2,1,0:T(8,128)(2,1)} %copy-done.11), channel_id=1, source_target_pairs={{4,0},{8,4},{12,8},{16,12},{20,16},{24,20},{28,24},{5,1},{9,5},{13... | collective-permute-start | bytes 442376 | tf_op jit(solution)/shard_map/ppermute | solution.py:68
  150.6 5.4 %collective-permute-start.10 = (f32[5,64,128]{2,1,0:T(8,128)S(1)}, f32[5,64,128]{2,1,0:T(8,128)S(1)}, u32[]{:S(2)}, u32[]{:S(2)}) collective-permute-start(f32[5,64,128]{2,1,0:T(8,128)S(1)} %add.13), channel_id=1, source_target_pairs={{0,16},{4,20},{8,24},{12,28},{16,0},{20,4},{24,8},{28,12},{1,17},{... | collective-permute-start | bytes 491528 | tf_op jit(solution)/shard_map/ppermute | solution.py:254
  151.7 13.0 %copy-start.8 = (bf16[9,64,128]{2,1,0:T(8,128)(2,1)}, bf16[9,64,128]{2,1,0:T(8,128)(2,1)S(1)}, u32[]{:S(2)}) copy-start(bf16[9,64,128]{2,1,0:T(8,128)(2,1)S(1)} %collective-permute-done.5.after) | copy-start | bytes 442372
  156.0 8.7 %collective-permute-start.11 = (f32[5,64,128]{2,1,0:T(8,128)S(1)}, f32[5,64,128]{2,1,0:T(8,128)S(1)}, u32[]{:S(2)}, u32[]{:S(2)}) collective-permute-start(f32[5,64,128]{2,1,0:T(8,128)S(1)} %add.14), channel_id=1, source_target_pairs={{0,1},{1,0},{2,3},{3,2},{4,5},{5,4},{6,7},{7,6},{8,9},{9,8},{10,11... | collective-permute-start | bytes 491528 | tf_op jit(solution)/shard_map/ppermute | solution.py:254
  157.5 14.4 %collective-permute-start.7 = (bf16[5,64,128]{2,1,0:T(8,128)(2,1)}, bf16[5,64,128]{2,1,0:T(8,128)(2,1)}, u32[]{:S(2)}, u32[]{:S(2)}) collective-permute-start(bf16[5,64,128]{2,1,0:T(8,128)(2,1)} %pad_maximum_fusion.3), channel_id=1, source_target_pairs={{1,0},{2,1},{3,2},{5,4},{6,5},{7,6},{9,8},{10,9},{11,10},{13,12},{... | collective-permute-start | bytes 245768 | tf_op jit(solution)/shard_map/ppermute | solution.py:72
  159.5 12.5 %collective-permute-start.6 = (bf16[5,64,128]{2,1,0:T(8,128)(2,1)}, bf16[5,64,128]{2,1,0:T(8,128)(2,1)}, u32[]{:S(2)}, u32[]{:S(2)}) collective-permute-start(bf16[5,64,128]{2,1,0:T(8,128)(2,1)} %pad_maximum_fusion.2), channel_id=1, source_target_pairs={{0,1},{1,2},{2,3},{4,5},{5,6},{6,7},{8,9},{9,10},{10,11},{12,13},{... | collective-permute-start | bytes 245768 | tf_op jit(solution)/shard_map/ppermute | solution.py:75
  164.7 12.6 %collective-permute-start.12 = (f32[5,64,128]{2,1,0:T(8,128)S(1)}, f32[5,64,128]{2,1,0:T(8,128)}, u32[]{:S(2)}, u32[]{:S(2)}) collective-permute-start(f32[5,64,128]{2,1,0:T(8,128)S(1)} %add.15.mine), channel_id=1, source_target_pairs={{0,2},{1,3},{2,0},{3,1},{4,6},{5,7},{6,4},{7,5},{8,10},{9,11},{10,... | collective-permute-start | bytes 491528 | tf_op jit(solution)/shard_map/ppermute | solution.py:256
  172.0 0.9 copy-start.9

commit v2 on v1

--- a/solution.py
+++ b/solution.py
@@ -16,9 +16,13 @@
 def call(kernel, out_shape, *args, scratch=(), flops=0, name=None):
     out_bytes = sum(o.size * o.dtype.itemsize for o in jax.tree.leaves(out_shape))
     in_bytes = sum(a.size * a.dtype.itemsize for a in args)
+    in_specs = [
+        pl.BlockSpec(memory_space=pltpu.SMEM if a.dtype == jnp.int32 else pltpu.VMEM) for a in args
+    ]
     return pl.pallas_call(
         kernel,
         out_shape=out_shape,
+        in_specs=in_specs,
         scratch_shapes=scratch,
         name=name,
         compiler_params=pltpu.CompilerParams(vmem_limit_bytes=VMEM_LIMIT),
@@ -98,10 +102,21 @@
         stack[row, 2 * channels :] = jnp.concatenate([middle[:, STEP:], right], axis=1)
 
 
-def convolve(stack, matrix, tile_rows, emit):
-    channels = matrix.shape[0] // 3
+def forward_taps(weight):
+    lines = [jnp.concatenate([weight[p, q] for q in range(3)], axis=1) for p in range(3)]
+    return jnp.concatenate(lines, axis=0)
+
+
+def backward_taps(weight):
+    lines = [
+        jnp.concatenate([weight[2 - p, 2 - q].T for q in range(3)], axis=1) for p in range(3)
+    ]
+    return jnp.concatenate(lines, axis=0)
+
+
+def convolve(stack, weights, tile_rows, emit):
+    channels = weights.shape[0] // 3
     cols = stack.shape[2]
-    weights = matrix[...]
     for pair in range(STEP // 2):
         products = []
         for k in range(tile_rows // STEP + 2):
@@ -127,8 +142,9 @@
 
 
 def forward_kernel(
-    tile, before, after, from_left, from_right, matrix, bias, stack, mixed, slope, kept
+    place, tile, before, after, from_left, from_right, weight, bias, stack, mixed, slope, *rest
 ):
+    pieces, kept = rest[:-1], rest[-1]
     tile_rows = tile.shape[0]
     write_shifted(tile, before, after, from_left, from_right, stack)
     offset = bias[...]
@@ -140,15 +156,20 @@
         elu = jnp.where(pre_act > 0, pre_act, rise - 1.0)
         kept[row] = (tile[row].astype(F32) + elu).astype(BF16)
 
-    convolve(stack, matrix, tile_rows, emit)
+    convolve(stack, forward_taps(weight), tile_rows, emit)
     for a in range(0, tile_rows, 16):
         mixed[:, a : a + 16] = jnp.swapaxes(kept[a : a + 16], 0, 1)
-
-
-def grad_pre_kernel(cot, mirrored, slope, tile, up, down, left, right):
+    deal_kernel(place, mixed, *pieces)
+
+
+def grad_pre_kernel(
+    groups, place, cot, keep, got, slope, tile, up, down, left, right, mirrored
+):
     rows = cot.shape[1]
     for a in range(0, rows, 16):
-        grad_mixed = cot[:, a : a + 16].astype(F32) + mirrored[:, a : a + 16].astype(F32)
+        turned = joined(place[1], keep[:, a : a + 16], got[:, a : a + 16], groups)
+        mirrored[:, a : a + 16] = turned.astype(BF16)
+        grad_mixed = cot[:, a : a + 16].astype(F32) + turned
         tile[a : a + 16] = (jnp.swapaxes(grad_mixed, 0, 1) * slope[a : a + 16]).astype(BF16)
     write_edges(tile, up, down, left, right)
 
@@ -195,7 +216,7 @@
 
 
 def input_grad_kernel(
-    tile, before, after, from_left, from_right, matrix, cot, mirrored, out, stack, kept
+    tile, before, after, from_left, from_right, weight, cot, mirrored, out, stack, kept
 ):
     tile_rows = tile.shape[0]
     write_shifted(tile, before, after, from_left, from_right, stack)
@@ -203,44 +224,84 @@
     def emit(row, total):
         kept[row] = total
 
-    convolve(stack, matrix, tile_rows, emit)
+    convolve(stack, backward_taps(weight), tile_rows, emit)
     for a in range(0, tile_rows, 16):
         grad_mixed = cot[:, a : a + 16].astype(F32) + mirrored[:, a : a + 16].astype(F32)
         out[:, a : a + 16] = (grad_mixed + jnp.swapaxes(kept[a : a + 16], 0, 1)).astype(BF16)
 
 
-def turn_kernel(add, *refs):
-    if add:
-        source, own, out = refs
-    else:
-        source, out = refs
-    cols_of, ratio, channels, tile_rows, tile_cols = source.shape
-    for z in range(cols_of):
-        for c in range(channels):
-            square = jnp.concatenate([source[z, e, c] for e in range(ratio)], axis=0)
-            turned = square.T
-            for h in range(ratio):
-                part = turned[h * tile_rows : (h + 1) * tile_rows]
-                if add:
-                    part = (part.astype(F32) + own[z, h, c].astype(F32)).astype(BF16)
-                out[z, h, c] = part
-
-
-def mirror(x, add):
-    channels, tile_rows, tile_cols = x.shape
-    rows, cols = lax.axis_size("row"), lax.axis_size("col")
-    ratio = tile_cols // tile_rows
-    blocks = (cols, ratio, channels // rows, tile_rows, tile_cols)
-    dealt = lax.all_to_all(x, "row", split_axis=0, concat_axis=0, tiled=True)
-    moved = lax.all_to_all(dealt, "col", split_axis=0, concat_axis=0, tiled=True)
-    args = [moved.reshape(blocks)] + ([dealt.reshape(blocks)] if add else [])
-    turned = call(
-        functools.partial(turn_kernel, add),
-        shape(blocks, BF16),
-        *args,
-        name="turn_and_add" if add else "turn",
-    )
-    return lax.all_to_all(turned.reshape(x.shape), "row", split_axis=0, concat_axis=0, tiled=True)
+def deal_kernel(place, x, *pieces):
+    group = x.shape[0] // len(pieces)
+    for j, piece in enumerate(pieces):
+        piece[...] = x[pl.ds((place[0] ^ j) * group, group)]
+
+
+def turn_kernel(place, *refs):
+    pieces, (keep, give) = refs[:-2], refs[-2:]
+    group, tile_rows, tile_cols = pieces[0].shape
+    half = group // 2
+    core = place[1]
+    for j, piece in enumerate(pieces):
+        at = (place[2] ^ j) * half
+        for c in range(half):
+            low, high = piece[c].T, piece[c + half].T
+            first = jnp.concatenate([low[:tile_rows], high[:tile_rows]], axis=1)
+            second = jnp.concatenate([low[tile_rows:], high[tile_rows:]], axis=1)
+            keep[at + c] = jnp.where(core == 0, first, second)
+            give[at + c] = jnp.where(core == 0, second, first)
+
+
+def joined(core, keep, got, groups):
+    keep, got = keep.astype(F32), got.astype(F32)
+    pairs, rows, cols = keep.shape
+    lower = lax.broadcasted_iota(jnp.int32, (1, 1, cols), 2) < cols // 2
+    first, second = jnp.where(core == 0, keep, got), jnp.where(core == 0, got, keep)
+    low = jnp.where(lower, first, swap_lanes(second))
+    high = jnp.where(lower, swap_lanes(first), second)
+    shaped = [v.reshape(groups, pairs // groups, rows, cols) for v in (low, high)]
+    return jnp.concatenate(shaped, axis=1).reshape(2 * pairs, rows, cols)
+
+
+def swap_lanes(x):
+    half = x.shape[2] // 2
+    return jnp.concatenate([x[:, :, half:], x[:, :, :half]], axis=2)
+
+
+def places():
+    row = lax.axis_index("row")
+    return jnp.stack([row // 2, row % 2, lax.axis_index("col")]).astype(jnp.int32)
+
+
+def dealt(x, place):
+    rounds = lax.axis_size("col")
+    piece = shape((x.shape[0] // rounds,) + x.shape[1:], x.dtype)
+    return call(deal_kernel, [piece] * rounds, place, x, name="deal")
+
+
+def mirror(pieces, place):
+    rounds, size = lax.axis_size("col"), lax.axis_size("row")
+    arrived = []
+    for j, piece in enumerate(pieces):
+        if j:
+            piece = lax.ppermute(piece, "row", [(r, r ^ (2 * j)) for r in range(size)])
+        owners = [
+            (r * rounds + z, (z * 2 + r % 2) * rounds + ((r // 2) ^ j))
+            for r in range(size)
+            for z in range(rounds)
+        ]
+        arrived.append(lax.ppermute(piece, ("row", "col"), owners))
+    group, tile_rows, tile_cols = pieces[0].shape
+    half = shape((group * rounds // 2, tile_rows, tile_cols), BF16)
+    keep, give = call(turn_kernel, [half, half], place, *arrived, name="turn")
+    got = lax.ppermute(give, "row", [(r, r ^ 1) for r in range(size)])
+    return keep, got
+
+
+def join_kernel(groups, place, own, keep, got, out):
+    for a in range(0, own.shape[1], 16):
+        rows = slice(a, a + 16)
+        turned = joined(place[1], keep[:, rows], got[:, rows], groups)
+        out[:, rows] = (own[:, rows].astype(F32) + turned).astype(BF16)
 
 
 def summed(part):
@@ -263,34 +324,51 @@
     edges = edge_shapes(channels, tile_rows, tile_cols)
     stack_dims = (tile_rows + 2 * STEP, 3 * channels, tile_cols)
     conv_flops = 2 * 9 * channels * channels * tile_rows * tile_cols
-    w_front = jnp.transpose(conv_weight, (0, 2, 1, 3)).reshape(3 * channels, 3 * channels)
-    w_back = jnp.transpose(conv_weight[::-1, ::-1], (0, 3, 1, 2)).reshape(
-        3 * channels, 3 * channels
-    )
-
-    mirrored = mirror(cotangent, False)
+    rounds = lax.axis_size("col")
+    place = places()
+
+    keep, got = mirror(dealt(cotangent, place), place)
 
     tile, *edge = call(split_kernel, [tile_shape] + edges, pair_feature_map, name="split")
     halo = exchange_edges(*edge)
-    stack, mixed, slope = call(
+    piece = shape((channels // rounds, tile_rows, tile_cols), BF16)
+    stack, mixed, slope, *pieces = call(
         forward_kernel,
         [
             shape(stack_dims, BF16),
             shape(pair_feature_map.shape, BF16),
             shape((tile_rows, channels, tile_cols), F32),
-        ],
+        ]
+        + [piece] * rounds,
+        place,
         tile,
         *halo,
-        w_front,
+        conv_weight,
         conv_bias[:, None],
         scratch=[pltpu.VMEM((tile_rows, channels, tile_cols), BF16)],
         flops=conv_flops,
         name="forward",
     )
-    symmetric = mirror(mixed, True)
-
-    grad, *edge = call(
-        grad_pre_kernel, [tile_shape] + edges, cotangent, mirrored, slope, name="grad_pre"
+    mixed_keep, mixed_got = mirror(pieces, place)
+    symmetric = call(
+        functools.partial(join_kernel, rounds),
+        shape(mixed.shape, BF16),
+        place,
+        mixed,
+        mixed_keep,
+        mixed_got,
+        name="join",
+    )
+
+    grad, *edge, mirrored = call(
+        functools.partial(grad_pre_kernel, rounds),
+        [tile_shape] + edges + [shape(cotangent.shape, BF16)],
+        place,
+        cotangent,
+        keep,
+        got,
+        slope,
+        name="grad_pre",
     )
     packed = call(
         functools.partial(weight_kernel, side),
@@ -306,7 +384,7 @@
         shape(pair_feature_map.shape, BF16),
         grad,
         *halo,
-        w_back,
+        conv_weight,
         cotangent,
         mirrored,
         scratch=[

time: 182 us -> 126 us (0.69)
  the two profiles are of different devices: /device:TPU:0 before, /device:TPU:12 now
where the time goes in v2:
time: 126 us
  starting transfers between devices  58.4 us (46%)
  waiting for transfers between devices  41.4 us (33%)
  Pallas kernels  19.4 us (15%)
  local copies, waits for them, and re-layouts  4.12 us (3%)
  other arithmetic  1.49 us (1%)
    ppermute x8, starting transfers between devices, mirror(): arrived.append(lax.ppermute(piece, ('row', 'col'), owners))  21.3 us
    pallas_call x10, Pallas kernels, call(): pl.pallas_call(kernel, out_shape=out_shape, in_specs=in_specs, scratch_sh...  19.4 us
    ppermute x8, waiting for transfers between devices, mirror(): arrived.append(lax.ppermute(piece, ('row', 'col'), owners))  14.8 us
    ppermute x6, waiting for transfers between devices, mirror(): piece = lax.ppermute(piece, 'row', [(r, r ^ 2 * j) for r in range(size)])  11.6 us
    ppermute x2, waiting for transfers between devices, exchange_edges(): lax.ppermute(jnp.concatenate([left, corner_left]), 'col', [(j, i) for i,...  8.58 us
    ppermute x4, starting transfers between devices, summed(): part = part + lax.ppermute(part, axis, pairs)  8.51 us
    ppermute x6, starting transfers between devices, mirror(): piece = lax.ppermute(piece, 'row', [(r, r ^ 2 * j) for r in range(size)])  7.11 us
    ppermute x2, starting transfers between devices, exchange_edges(): lax.ppermute(jnp.concatenate([left, corner_left]), 'col', [(j, i) for i,...  6.9 us
  transfers between devices with their start and end apart: 29, of which 11 were waited for; matrix products, arithmetic and copies ran while one was open for 2% of the time, Pallas kernels for 14%

profile of v2, /device:TPU:12, one launch (start us, length us, event | category | flops | bytes accessed | tf_op | source)
XLA Modules:
  0.0 125.7 jit_solution(16714374804761955722)
XLA Ops:
  0.6 0.1 pad_add_fusion.place
  0.7 1.2 copy-done
  2.0 0.6 deal.1
  2.6 1.6 %collective-permute-start.13 = (bf16[16,64,128]{2,1,0:T(8,128)(2,1)S(1)}, bf16[16,64,128]{2,1,0:T(8,128)(2,1)S(1)}, u32[]{:S(2)}, u32[]{:S(2)}) collective-permute-start(bf16[16,64,128]{2,1,0:T(8,128)(2,1)S(1)} %get-tuple-element.45), channel_id=1, source_target_pairs={{0,8},{4,12},{8,0},{12,4},{16,24},{20,28},{24,16},{28,20},{1,9},{5... | collective-permute-start | bytes 786440 | tf_op jit(solution)/shard_map/ppermute | solution.py:286
  4.1 0.5 collective-permute-start.15
  4.6 1.5 %collective-permute-start.17 = (bf16[16,64,128]{2,1,0:T(8,128)(2,1)S(1)}, bf16[16,64,128]{2,1,0:T(8,128)(2,1)S(1)}, u32[]{:S(2)}, u32[]{:S(2)}) collective-permute-start(bf16[16,64,128]{2,1,0:T(8,128)(2,1)S(1)} %get-tuple-element.47), channel_id=1, source_target_pairs={{0,24},{4,28},{8,16},{12,20},{16,8},{20,12},{24,0},{28,4},{1,25},{... | collective-permute-start | bytes 786440 | tf_op jit(solution)/shard_map/ppermute | solution.py:286
  6.1 4.3 %collective-permute-start.12 = (bf16[16,64,128]{2,1,0:T(8,128)(2,1)S(1)}, bf16[16,64,128]{2,1,0:T(8,128)(2,1)S(1)}, u32[]{:S(2)}, u32[]{:S(2)}) collective-permute-start(bf16[16,64,128]{2,1,0:T(8,128)(2,1)S(1)} %get-tuple-element.44), channel_id=1, source_target_pairs={{0,0},{1,8},{2,16},{3,24},{4,4},{5,12},{6,20},{7,28},{8,1},{9,9},{... | collective-permute-start | bytes 786440 | tf_op jit(solution)/shard_map/ppermute | solution.py:292
  10.5 1.4 %collective-permute-done.13 = bf16[16,64,128]{2,1,0:T(8,128)(2,1)S(1)} collective-permute-done((bf16[16,64,128]{2,1,0:T(8,128)(2,1)S(1)}, bf16[16,64,128]{2,1,0:T(8,128)(2,1)S(1)}, u32[]{:S(2)}, u32[]{:S(2)}) %collective-permute-start.13) | collective-permute-done | bytes 262176 | tf_op jit(solution)/shard_map/ppermute | solution.py:286
  11.8 3.5 %collective-permute-start.14 = (bf16[16,64,128]{2,1,0:T(8,128)(2,1)S(1)}, bf16[16,64,128]{2,1,0:T(8,128)(2,1)S(1)}, u32[]{:S(2)}, u32[]{:S(2)}) collective-permute-start(bf16[16,64,128]{2,1,0:T(8,128)(2,1)S(1)} %collective-permute-done.13), channel_id=1, source_target_pairs={{0,1},{1,9},{2,17},{3,25},{4,5},{5,13},{6,21},{7,29},{8,0},{9,8},{... | collective-permute-start | bytes 786440 | tf_op jit(solution)/shard_map/ppermute | solution.py:292
  15.3 10.2 %collective-permute-done.17 = bf16[16,64,128]{2,1,0:T(8,128)(2,1)S(1)} collective-permute-done((bf16[16,64,128]{2,1,0:T(8,128)(2,1)S(1)}, bf16[16,64,128]{2,1,0:T(8,128)(2,1)S(1)}, u32[]{:S(2)}, u32[]{:S(2)}) %collective-permute-start.17) | collective-permute-done | bytes 262176 | tf_op jit(solution)/shard_map/ppermute | solution.py:286
  25.5 2.0 %collective-permute-start.18 = (bf16[16,64,128]{2,1,0:T(8,128)(2,1)S(1)}, bf16[16,64,128]{2,1,0:T(8,128)(2,1)S(1)}, u32[]{:S(2)}, u32[]{:S(2)}) collective-permute-start(bf16[16,64,128]{2,1,0:T(8,128)(2,1)S(1)} %collective-permute-done.17), channel_id=1, source_target_pairs={{0,3},{1,11},{2,19},{3,27},{4,7},{5,15},{6,23},{7,31},{8,2},{9,10}... | collective-permute-start | bytes 786440 | tf_op jit(solution)/shard_map/ppermute | solution.py:292
  27.4 1.2 copy-done.2
  28.7 0.9 split.1
  29.6 1.9 %collective-permute-start = (bf16[9,64,128]{2,1,0:T(8,128)(2,1)S(1)}, bf16[9,64,128]{2,1,0:T(8,128)(2,1)S(1)}, u32[]{:S(2)}, u32[]{:S(2)}) collective-permute-start(bf16[9,64,128]{2,1,0:T(8,128)(2,1)S(1)} %get-tuple-element.33), channel_id=1, source_target_pairs={{0,4},{4,8},{8,12},{12,16},{16,20},{20,24},{24,28},{1,5},{5,9},{9,... | collective-permute-start | bytes 442376 | tf_op jit(solution)/shard_map/ppermute | solution.py:71
  31.5 0.0 collective-permute-done.12.refs_0_
  31.6 4.5 %collective-permute-start.1 = (bf16[9,64,128]{2,1,0:T(8,128)(2,1)S(1)}, bf16[9,64,128]{2,1,0:T(8,128)(2,1)S(1)}, u32[]{:S(2)}, u32[]{:S(2)}) collective-permute-start(bf16[9,64,128]{2,1,0:T(8,128)(2,1)S(1)} %get-tuple-element.34), channel_id=1, source_target_pairs={{4,0},{8,4},{12,8},{16,12},{20,16},{24,20},{28,24},{5,1},{9,5},{13... | collective-permute-start | bytes 442376 | tf_op jit(solution)/shard_map/ppermute | solution.py:72
  36.1 0.0 collective-permute-done.14.refs_1_
  36.1 0.0 collective-permute-done.16.refs_2_
  36.1 6.4 %collective-permute-done.18.refs_3_ = bf16[16,64,128]{2,1,0:T(8,128)(2,1)S(1)} collective-permute-done((bf16[16,64,128]{2,1,0:T(8,128)(2,1)S(1)}, bf16[16,64,128]{2,1,0:T(8,128)(2,1)S(1)}, u32[]{:S(2)}, u32[]{:S(2)}) %collective-permute-start.18) | collective-permute-done | bytes 262176 | tf_op jit(solution)/shard_map/ppermute | solution.py:292
  42.5 2.2 %turn.3 = (bf16[32,64,128]{2,1,0:T(8,128)(2,1)S(1)}, bf16[32,64,128]{2,1,0:T(8,128)(2,1)}) custom-call(s32[3]{0:T(128)S(1)} %pad_add_fusion.place, bf16[16,64,128]{2,1,0:T(8,128)(2,1)S(1)} %collective-permute-done.12.refs_0_, bf16[16,64,128]{2,1,0:T(8,128)(2,1)S(1)} %collective-permute-done.14.refs_1_, ...), custom_call_target="tpu_custom_call" | custom-call | bytes 2097164 | tf_op jit(solution)/shard_map/turn/pallas_call | solution.py:22
  44.8 0.0 collective-permute-start.19
  44.8 0.0 collective-permute-done.before
  44.8 0.0 collective-permute-done.1.after
  44.8 0.6 pad_maximum_fusion
  45.4 2.2 %collective-permute-start.2 = (bf16[5,64,128]{2,1,0:T(8,128)(2,1)}, bf16[5,64,128]{2,1,0:T(8,128)(2,1)}, u32[]{:S(2)}, u32[]{:S(2)}) collective-permute-start(bf16[5,64,128]{2,1,0:T(8,128)(2,1)} %pad_maximum_fusion), channel_id=1, source_target_pairs={{0,1},{1,2},{2,3},{4,5},{5,6},{6,7},{8,9},{9,10},{10,11},{12,13},{... | collective-permute-start | bytes 245768 | tf_op jit(solution)/shard_map/ppermute | solution.py:79
  47.7 0.6 pad_maximum_fusion.1
  48.3 4.2 %collective-permute-start.3 = (bf16[5,64,128]{2,1,0:T(8,128)(2,1)}, bf16[5,64,128]{2,1,0:T(8,128)(2,1)}, u32[]{:S(2)}, u32[]{:S(2)}) collective-permute-start(bf16[5,64,128]{2,1,0:T(8,128)(2,1)} %pad_maximum_fusion.1), channel_id=1, source_target_pairs={{1,0},{2,1},{3,2},{5,4},{6,5},{7,6},{9,8},{10,9},{11,10},{13,12},{... | collective-permute-start | bytes 245768 | tf_op jit(solution)/shard_map/ppermute | solution.py:76
  52.5 0.7 copy.8.bias
  53.3 0.0 collective-permute-done.2.from_left
  53.3 2.6 %collective-permute-done.3.from_right = bf16[5,64,128]{2,1,0:T(8,128)(2,1)} collective-permute-done((bf16[5,64,128]{2,1,0:T(8,128)(2,1)}, bf16[5,64,128]{2,1,0:T(8,128)(2,1)}, u32[]{:S(2)}, u32[]{:S(2)}) %collective-permute-start.3) | collective-permute-done | bytes 81952 | tf_op jit(solution)/shard_map/ppermute | solution.py:76
  55.9 0.9 copy-done.3
  56.8 4.0 %forward.1 = (bf16[80,192,128]{2,1,0:T(8,128)(2,1)S(1)}, bf16[64,64,128]{2,1,0:T(8,128)(2,1)S(1)}, f32[64,64,128]{2,1,0:T(8,128)S(1)}, bf16[16,64,128]{2,1,0:T(8...) custom-call(s32[3]{0:T(128)S(1)} %pad_add_fusion.place, ...), custom_call_target="tpu_custom_call" | custom-call | flops 603979776 | bytes 9707788 | tf_op jit(solution)/shard_map/forward/pallas_call | solution.py:22
  60.9 0.6 collective-permute-start.5
  61.4 1.5 %collective-permute-start.7 = (bf16[16,64,128]{2,1,0:T(8,128)(2,1)S(1)}, bf16[16,64,128]{2,1,0:T(8,128)(2,1)S(1)}, u32[]{:S(2)}, u32[]{:S(2)}) collective-permute-start(bf16[16,64,128]{2,1,0:T(8,128)(2,1)S(1)} %get-tuple-element.40), channel_id=1, source_target_pairs={{0,16},{4,20},{8,24},{12,28},{16,0},{20,4},{24,8},{28,12},{1,17},{... | collective-permute-start | bytes 786440 | tf_op jit(solution)/shard_map/ppermute | solution.py:286
  62.9 1.5 %collective-permute-start.9 = (bf16[16,64,128]{2,1,0:T(8,128)(2,1)S(1)}, bf16[16,64,128]{2,1,0:T(8,128)(2,1)S(1)}, u32[]{:S(2)}, u32[]{:S(2)}) collective-permute-start(bf16[16,64,128]{2,1,0:T(8,128)(2,1)S(1)} %get-tuple-element.41), channel_id=1, source_target_pairs={{0,24},{4,28},{8,16},{12,20},{16,8},{20,12},{24,0},{28,4},{1,25},{... | collective-permute-start | bytes 786440 | tf_op jit(solution)/shard_map/ppermute | solution.py:286
  64.4 0.0 collective-permute-done.19.got
  64.4 2.3 %grad_pre.1 = (bf16[64,64,128]{2,1,0:T(8,128)(2,1)S(1)}, bf16[9,64,128]{2,1,0:T(8,128)(2,1)S(1)}, bf16[9,64,128]{2,1,0:T(8,128)(2,1)S(1)}, bf16[4,64,128]{2,1,0:...) custom-call(s32[3]{0:T(128)S(1)} %pad_add_fusion.place, ...), custom_call_target="tpu_custom_call" | custom-call | bytes 6717452 | tf_op jit(solution)/shard_map/grad_pre/pallas_call | solution.py:22
  66.8 1.3 %weight_terms.1 = f32[5,64,128]{2,1,0:T(8,128)S(1)} custom-call(bf16[64,64,128]{2,1,0:T(8,128)(2,1)S(1)} %get-tuple-element.51.tile.grad, bf16[80,192,128]{2,1,0:T(8,128)(2,1)S(1)} %get-tuple-element.57.stack), custom_call_target="tpu_custom_call" | custom-call | flops 603979776 | bytes 5144576 | tf_op jit(solution)/shard_map/weight_terms/pallas_call | solution.py:22
  68.1 0.0 copy-start.4
  68.1 0.1 collective-permute-start.24
  68.2 3.1 %collective-permute-start.4 = (bf16[16,64,128]{2,1,0:T(8,128)(2,1)S(1)}, bf16[16,64,128]{2,1,0:T(8,128)(2,1)S(1)}, u32[]{:S(2)}, u32[]{:S(2)}) collective-permute-start(bf16[16,64,128]{2,1,0:T(8,128)(2,1)S(1)} %get-tuple-element.38), channel_id=1, source_target_pairs={{0,0},{1,8},{2,16},{3,24},{4,4},{5,12},{6,20},{7,28},{8,1},{9,9},{... | collective-permute-start | bytes 786440 | tf_op jit(solution)/shard_map/ppermute | solution.py:292
  71.3 2.6 %collective-permute-start.6 = (bf16[16,64,128]{2,1,0:T(8,128)(2,1)S(1)}, bf16[16,64,128]{2,1,0:T(8,128)(2,1)S(1)}, u32[]{:S(2)}, u32[]{:S(2)}) collective-permute-start(bf16[16,64,128]{2,1,0:T(8,128)(2,1)S(1)} %collective-permute-done.5), channel_id=1, source_target_pairs={{0,1},{1,9},{2,17},{3,25},{4,5},{5,13},{6,21},{7,29},{8,0},{9,8},{... | collective-permute-start | bytes 786440 | tf_op jit(solution)/shard_map/ppermute | solution.py:292
  73.9 0.7 collective-permute-start.25
  74.6 0.1 collective-permute-done.7
  74.7 3.2 %collective-permute-start.8 = (bf16[16,64,128]{2,1,0:T(8,128)(2,1)S(1)}, bf16[16,64,128]{2,1,0:T(8,128)(2,1)S(1)}, u32[]{:S(2)}, u32[]{:S(2)}) collective-permute-start(bf16[16,64,128]{2,1,0:T(8,128)(2,1)S(1)} %collective-permute-done.7), channel_id=1, source_target_pairs={{0,2},{1,10},{2,18},{3,26},{4,6},{5,14},{6,22},{7,30},{8,3},{9,11}... | collective-permute-start | bytes 786440 | tf_op jit(solution)/shard_map/ppermute | solution.py:292
  77.9 2.6 %collective-permute-start.10 = (bf16[16,64,128]{2,1,0:T(8,128)(2,1)S(1)}, bf16[16,64,128]{2,1,0:T(8,128)(2,1)S(1)}, u32[]{:S(2)}, u32[]{:S(2)}) collective-permute-start(bf16[16,64,128]{2,1,0:T(8,128)(2,1)S(1)} %collective-permute-done.9), channel_id=1, source_target_pairs={{0,3},{1,11},{2,19},{3,27},{4,7},{5,15},{6,23},{7,31},{8,2},{9,10}... | collective-permute-start | bytes 786440 | tf_op jit(solution)/shard_map/ppermute | solution.py:292
  80.5 2.0 %collective-permute-done.25 = f32[5,64,128]{2,1,0:T(8,128)S(1)} collective-permute-done((f32[5,64,128]{2,1,0:T(8,128)S(1)}, f32[5,64,128]{2,1,0:T(8,128)S(1)}, u32[]{:S(2)}, u32[]{:S(2)}) %collective-permute-start.25) | collective-permute-done | bytes 163872 | tf_op jit(solution)/shard_map/ppermute | solution.py:315
  82.5 7.0 %collective-permute-start.26 = (f32[5,64,128]{2,1,0:T(8,128)S(1)}, f32[5,64,128]{2,1,0:T(8,128)S(1)}, u32[]{:S(2)}, u32[]{:S(2)}) collective-permute-start(f32[5,64,128]{2,1,0:T(8,128)S(1)} %add.19), channel_id=1, source_target_pairs={{0,16},{4,20},{8,24},{12,28},{16,0},{20,4},{24,8},{28,12},{1,17},{... | collective-permute-start | bytes 491528 | tf_op jit(solution)/shard_map/ppermute | solution.py:315
  89.5 2.3 %collective-permute-done.4.refs_0_ = bf16[16,64,128]{2,1,0:T(8,128)(2,1)S(1)} collective-permute-done((bf16[16,64,128]{2,1,0:T(8,128)(2,1)S(1)}, bf16[16,64,128]{2,1,0:T(8,128)(2,1)S(1)}, u32[]{:S(2)}, u32[]{:S(2)}) %collective-permute-start.4) | collective-permute-done | bytes 262176 | tf_op jit(solution)/shard_map/ppermute | solution.py:292
  91.8 1.9 %collective-permute-start.20 = (bf16[9,64,128]{2,1,0:T(8,128)(2,1)S(1)}, bf16[9,64,128]{2,1,0:T(8,128)(2,1)S(1)}, u32[]{:S(2)}, u32[]{:S(2)}) collective-permute-start(bf16[9,64,128]{2,1,0:T(8,128)(2,1)S(1)} %get-tuple-element.52), channel_id=1, source_target_pairs={{0,4},{4,8},{8,12},{12,16},{16,20},{20,24},{24,28},{1,5},{5,9},{9,... | collective-permute-start | bytes 442376 | tf_op jit(solution)/shard_map/ppermute | solution.py:71
  93.7 4.3 %collective-permute-done.6.refs_1_ = bf16[16,64,128]{2,1,0:T(8,128)(2,1)S(1)} collective-permute-done((bf16[16,64,128]{2,1,0:T(8,128)(2,1)S(1)}, bf16[16,64,128]{2,1,0:T(8,128)(2,1)S(1)}, u32[]{:S(2)}, u32[]{:S(2)}) %collective-permute-start.6) | collective-permute-done | bytes 262176 | tf_op jit(solution)/shard_map/ppermute | solution.py:292
  98.0 1.9 %collective-permute-start.21 = (bf16[9,64,128]{2,1,0:T(8,128)(2,1)S(1)}, bf16[9,64,128]{2,1,0:T(8,128)(2,1)S(1)}, u32[]{:S(2)}, u32[]{:S(2)}) collective-permute-start(bf16[9,64,128]{2,1,0:T(8,128)(2,1)S(1)} %get-tuple-element.53), channel_id=1, source_target_pairs={{4,0},{8,4},{12,8},{16,12},{20,16},{24,20},{28,24},{5,1},{9,5},{13... | collective-permute-start | bytes 442376 | tf_op jit(solution)/shard_map/ppermute | solution.py:72
  100.0 1.8 %collective-permute-done.10.refs_3_ = bf16[16,64,128]{2,1,0:T(8,128)(2,1)S(1)} collective-permute-done((bf16[16,64,128]{2,1,0:T(8,128)(2,1)S(1)}, bf16[16,64,128]{2,1,0:T(8,128)(2,1)S(1)}, u32[]{:S(2)}, u32[]{:S(2)}) %collective-permute-start.10) | collective-permute-done | bytes 262176 | tf_op jit(solution)/shard_map/ppermute | solution.py:292
  101.8 1.4 %turn.2 = (bf16[32,64,128]{2,1,0:T(8,128)(2,1)S(1)}, bf16[32,64,128]{2,1,0:T(8,128)(2,1)S(1)}) custom-call(s32[3]{0:T(128)S(1)} %pad_add_fusion.place, bf16[16,64,128]{2,1,0:T(8,128)(2,1)S(1)} %collective-permute-done.4.refs_0_, bf16[16,64,128]{2,1,0:T(8,128)(2,1)S(1)} %collective-permute-done.6.refs_1_, ...), custom_call_target="tpu_custom_call" | custom-call | bytes 2097164 | tf_op jit(solution)/shard_map/turn/pallas_call | solution.py:22
  103.2 0.1 collective-permute-start.11
  103.4 0.8 collective-permute-start.27
  104.2 1.9 %collective-permute-start.22 = (bf16[5,64,128]{2,1,0:T(8,128)(2,1)S(1)}, bf16[5,64,128]{2,1,0:T(8,128)(2,1)S(1)}, u32[]{:S(2)}, u32[]{:S(2)}) collective-permute-start(bf16[5,64,128]{2,1,0:T(8,128)(2,1)S(1)} %pad_maximum_fusion.2), channel_id=1, source_target_pairs={{0,1},{1,2},{2,3},{4,5},{5,6},{6,7},{8,9},{9,10},{10,11},{12,13},{... | collective-permute-start | bytes 245768 | tf_op jit(solution)/shard_map/ppermute | solution.py:79
  106.1 4.3 %collective-permute-done.27 = f32[5,64,128]{2,1,0:T(8,128)S(1)} collective-permute-done((f32[5,64,128]{2,1,0:T(8,128)S(1)}, f32[5,64,128]{2,1,0:T(8,128)S(1)}, u32[]{:S(2)}, u32[]{:S(2)}) %collective-permute-start.27) | collective-permute-done | bytes 163872 | tf_op jit(solution)/shard_map/ppermute | solution.py:315
  110.5 0.1 collective-permute-start.28
  110.5 2.7 %collective-permute-start.23 = (bf16[5,64,128]{2,1,0:T(8,128)(2,1)S(1)}, bf16[5,64,128]{2,1,0:T(8,128)(2,1)S(1)}, u32[]{:S(2)}, u32[]{:S(2)}) collective-permute-start(bf16[5,64,128]{2,1,0:T(8,128)(2,1)S(1)} %pad_maximum_fusion.3), channel_id=1, source_target_pairs={{1,0},{2,1},{3,2},{5,4},{6,5},{7,6},{9,8},{10,9},{11,10},{13,12},{... | collective-permute-start | bytes 245768 | tf_op jit(solution)/shard_map/ppermute | solution.py:76
  113.2 2.1 %join.1 = bf16[64,64,128]{2,1,0:T(8,128)(2,1)} custom-call(s32[3]{0:T(128)S(1)} %pad_add_fusion.place, bf16[64,64,128]{2,1,0:T(8,128)(2,1)S(1)} %get-tuple-element.37.own, bf16[32,64,128]{2,1,0:T(8,128)(2,1)S(1)} %get-tuple-element.42.keep, bf16[32,64,128]{2,1,0:T(8,128)(2,1)S(1)} %collective-permute-done.11.got), custom_call_target="tpu_custom_call" | custom-call | bytes 3145740 | tf_op jit(solution)/shard_map/join/pallas_call | solution.py:22
  115.4 6.0 %collective-permute-done.23.from_right = bf16[5,64,128]{2,1,0:T(8,128)(2,1)S(1)} collective-permute-done((bf16[5,64,128]{2,1,0:T(8,128)(2,1)S(1)}, bf16[5,64,128]{2,1,0:T(8,128)(2,1)S(1)}, u32[]{:S(2)}, u32[]{:S(2)}) %collective-permute-start.23) | collective-permute-done | bytes 81952 | tf_op jit(solution)/shard_map/ppermute | solution.py:76
  121.3 3.6 %input_grad.1 = bf16[64,64,128]{2,1,0:T(8,128)(2,1)} custom-call(bf16[64,64,128]{2,1,0:T(8,128)(2,1)S(1)} %get-tuple-element.51.tile.grad, bf16[9,64,128]{2,1,0:T(8,128)(2,1)S(1)} %collective-permute-done.20.before, bf16[9,64,128]{2,1,0:T(8,128)(2,1)S(1)} %collective-permute-done.21.after, bf16[5,64,128]{2,1,0:T(8,128)(2,1)S(1)} %collective-permute-done.22.from_left, ...), custom_call_target="tpu_custom_call" | custom-call | flops 603979776 | bytes 4726784 | tf_op jit(solution)/shard_map/input_grad/pallas_call | solution.py:22
  124.9 0.8 unpack.1
  (27 shorter events, 0.2 us)
Async XLA Ops:
  0.7 1.2 copy-start
  2.0 62.5 %copy-start.1 = (bf16[64,64,128]{2,1,0:T(8,128)(2,1)S(1)}, bf16[64,64,128]{2,1,0:T(8,128)(2,1)}, u32[]{:S(2)}) copy-start(bf16[64,64,128]{2,1,0:T(8,128)(2,1)} %cot.3) | copy-start | bytes 3145732
  2.6 9.3 %collective-permute-start.13 = (bf16[16,64,128]{2,1,0:T(8,128)(2,1)S(1)}, bf16[16,64,128]{2,1,0:T(8,128)(2,1)S(1)}, u32[]{:S(2)}, u32[]{:S(2)}) collective-permute-start(bf16[16,64,128]{2,1,0:T(8,128)(2,1)S(1)} %get-tuple-element.45), channel_id=1, source_target_pairs={{0,8},{4,12},{8,0},{12,4},{16,24},{20,28},{24,16},{28,20},{1,9},{5... | collective-permute-start | bytes 786440 | tf_op jit(solution)/shard_map/ppermute | solution.py:286
  4.1 11.2 %collective-permute-start.15 = (bf16[16,64,128]{2,1,0:T(8,128)(2,1)S(1)}, bf16[16,64,128]{2,1,0:T(8,128)(2,1)S(1)}, u32[]{:S(2)}, u32[]{:S(2)}) collective-permute-start(bf16[16,64,128]{2,1,0:T(8,128)(2,1)S(1)} %get-tuple-element.46), channel_id=1, source_target_pairs={{0,16},{4,20},{8,24},{12,28},{16,0},{20,4},{24,8},{28,12},{1,17},{... | collective-permute-start | bytes 786440 | tf_op jit(solution)/shard_map/ppermute | solution.py:286
  4.6 20.8 %collective-permute-start.17 = (bf16[16,64,128]{2,1,0:T(8,128)(2,1)S(1)}, bf16[16,64,128]{2,1,0:T(8,128)(2,1)S(1)}, u32[]{:S(2)}, u32[]{:S(2)}) collective-permute-start(bf16[16,64,128]{2,1,0:T(8,128)(2,1)S(1)} %get-tuple-element.47), channel_id=1, source_target_pairs={{0,24},{4,28},{8,16},{12,20},{16,8},{20,12},{24,0},{28,4},{1,25},{... | collective-permute-start | bytes 786440 | tf_op jit(solution)/shard_map/ppermute | solution.py:286
  6.1 25.4 %collective-permute-start.12 = (bf16[16,64,128]{2,1,0:T(8,128)(2,1)S(1)}, bf16[16,64,128]{2,1,0:T(8,128)(2,1)S(1)}, u32[]{:S(2)}, u32[]{:S(2)}) collective-permute-start(bf16[16,64,128]{2,1,0:T(8,128)(2,1)S(1)} %get-tuple-element.44), channel_id=1, source_target_pairs={{0,0},{1,8},{2,16},{3,24},{4,4},{5,12},{6,20},{7,28},{8,1},{9,9},{... | collective-permute-start | bytes 786440 | tf_op jit(solution)/shard_map/ppermute | solution.py:292
  11.8 24.3 %collective-permute-start.14 = (bf16[16,64,128]{2,1,0:T(8,128)(2,1)S(1)}, bf16[16,64,128]{2,1,0:T(8,128)(2,1)S(1)}, u32[]{:S(2)}, u32[]{:S(2)}) collective-permute-start(bf16[16,64,128]{2,1,0:T(8,128)(2,1)S(1)} %collective-permute-done.13), channel_id=1, source_target_pairs={{0,1},{1,9},{2,17},{3,25},{4,5},{5,13},{6,21},{7,29},{8,0},{9,8},{... | collective-permute-start | bytes 786440 | tf_op jit(solution)/shard_map/ppermute | solution.py:292
  15.3 20.8 %collective-permute-start.16 = (bf16[16,64,128]{2,1,0:T(8,128)(2,1)S(1)}, bf16[16,64,128]{2,1,0:T(8,128)(2,1)S(1)}, u32[]{:S(2)}, u32[]{:S(2)}) collective-permute-start(bf16[16,64,128]{2,1,0:T(8,128)(2,1)S(1)} %collective-permute-done.15), channel_id=1, source_target_pairs={{0,2},{1,10},{2,18},{3,26},{4,6},{5,14},{6,22},{7,30},{8,3},{9,11}... | collective-permute-start | bytes 786440 | tf_op jit(solution)/shard_map/ppermute | solution.py:292
  25.5 17.0 %collective-permute-start.18 = (bf16[16,64,128]{2,1,0:T(8,128)(2,1)S(1)}, bf16[16,64,128]{2,1,0:T(8,128)(2,1)S(1)}, u32[]{:S(2)}, u32[]{:S(2)}) collective-permute-start(bf16[16,64,128]{2,1,0:T(8,128)(2,1)S(1)} %collective-permute-done.17), channel_id=1, source_target_pairs={{0,3},{1,11},{2,19},{3,27},{4,7},{5,15},{6,23},{7,31},{8,2},{9,10}... | collective-permute-start | bytes 786440 | tf_op jit(solution)/shard_map/ppermute | solution.py:292
  27.4 1.2 copy-start.2
  29.6 15.2 %collective-permute-start = (bf16[9,64,128]{2,1,0:T(8,128)(2,1)S(1)}, bf16[9,64,128]{2,1,0:T(8,128)(2,1)S(1)}, u32[]{:S(2)}, u32[]{:S(2)}) collective-permute-start(bf16[9,64,128]{2,1,0:T(8,128)(2,1)S(1)} %get-tuple-element.33), channel_id=1, source_target_pairs={{0,4},{4,8},{8,12},{12,16},{16,20},{20,24},{24,28},{1,5},{5,9},{9,... | collective-permute-start | bytes 442376 | tf_op jit(solution)/shard_map/ppermute | solution.py:71
  31.6 13.2 %collective-permute-start.1 = (bf16[9,64,128]{2,1,0:T(8,128)(2,1)S(1)}, bf16[9,64,128]{2,1,0:T(8,128)(2,1)S(1)}, u32[]{:S(2)}, u32[]{:S(2)}) collective-permute-start(bf16[9,64,128]{2,1,0:T(8,128)(2,1)S(1)} %get-tuple-element.34), channel_id=1, source_target_pairs={{4,0},{8,4},{12,8},{16,12},{20,16},{24,20},{28,24},{5,1},{9,5},{13... | collective-permute-start | bytes 442376 | tf_op jit(solution)/shard_map/ppermute | solution.py:72
  44.8 19.7 %collective-permute-start.19 = (bf16[32,64,128]{2,1,0:T(8,128)(2,1)}, bf16[32,64,128]{2,1,0:T(8,128)(2,1)S(1)}, u32[]{:S(2)}, u32[]{:S(2)}) collective-permute-start(bf16[32,64,128]{2,1,0:T(8,128)(2,1)} %get-tuple-element.49), channel_id=1, source_target_pairs={{0,4},{4,0},{8,12},{12,8},{16,20},{20,16},{24,28},{28,24},{1,5},{5... | collective-permute-start | bytes 1572872 | tf_op jit(solution)/shard_map/ppermute | solution.py:296
  45.4 7.8 %collective-permute-start.2 = (bf16[5,64,128]{2,1,0:T(8,128)(2,1)}, bf16[5,64,128]{2,1,0:T(8,128)(2,1)}, u32[]{:S(2)}, u32[]{:S(2)}) collective-permute-start(bf16[5,64,128]{2,1,0:T(8,128)(2,1)} %pad_maximum_fusion), channel_id=1, source_target_pairs={{0,1},{1,2},{2,3},{4,5},{5,6},{6,7},{8,9},{9,10},{10,11},{12,13},{... | collective-permute-start | bytes 245768 | tf_op jit(solution)/shard_map/ppermute | solution.py:79
  48.3 7.6 %collective-permute-start.3 = (bf16[5,64,128]{2,1,0:T(8,128)(2,1)}, bf16[5,64,128]{2,1,0:T(8,128)(2,1)}, u32[]{:S(2)}, u32[]{:S(2)}) collective-permute-start(bf16[5,64,128]{2,1,0:T(8,128)(2,1)} %pad_maximum_fusion.1), channel_id=1, source_target_pairs={{1,0},{2,1},{3,2},{5,4},{6,5},{7,6},{9,8},{10,9},{11,10},{13,12},{... | collective-permute-start | bytes 245768 | tf_op jit(solution)/shard_map/ppermute | solution.py:76
  55.9 0.9 copy-start.3
  60.9 10.4 %collective-permute-start.5 = (bf16[16,64,128]{2,1,0:T(8,128)(2,1)S(1)}, bf16[16,64,128]{2,1,0:T(8,128)(2,1)S(1)}, u32[]{:S(2)}, u32[]{:S(2)}) collective-permute-start(bf16[16,64,128]{2,1,0:T(8,128)(2,1)S(1)} %get-tuple-element.39), channel_id=1, source_target_pairs={{0,8},{4,12},{8,0},{12,4},{16,24},{20,28},{24,16},{28,20},{1,9},{5... | collective-permute-start | bytes 786440 | tf_op jit(solution)/shard_map/ppermute | solution.py:286
  61.4 13.3 %collective-permute-start.7 = (bf16[16,64,128]{2,1,0:T(8,128)(2,1)S(1)}, bf16[16,64,128]{2,1,0:T(8,128)(2,1)S(1)}, u32[]{:S(2)}, u32[]{:S(2)}) collective-permute-start(bf16[16,64,128]{2,1,0:T(8,128)(2,1)S(1)} %get-tuple-element.40), channel_id=1, source_target_pairs={{0,16},{4,20},{8,24},{12,28},{16,0},{20,4},{24,8},{28,12},{1,17},{... | collective-permute-start | bytes 786440 | tf_op jit(solution)/shard_map/ppermute | solution.py:286
  62.9 15.0 %collective-permute-start.9 = (bf16[16,64,128]{2,1,0:T(8,128)(2,1)S(1)}, bf16[16,64,128]{2,1,0:T(8,128)(2,1)S(1)}, u32[]{:S(2)}, u32[]{:S(2)}) collective-permute-start(bf16[16,64,128]{2,1,0:T(8,128)(2,1)S(1)} %get-tuple-element.41), channel_id=1, source_target_pairs={{0,24},{4,28},{8,16},{12,20},{16,8},{20,12},{24,0},{28,4},{1,25},{... | collective-permute-start | bytes 786440 | tf_op jit(solution)/shard_map/ppermute | solution.py:286
  68.1 53.2 %copy-start.4 = (bf16[3,3,64,64]{3,2,1,0:T(8,128)(2,1)S(1)}, bf16[3,3,64,64]{3,2,1,0:T(8,128)(2,1)}, u32[]{:S(2)}) copy-start(bf16[3,3,64,64]{3,2,1,0:T(8,128)(2,1)} %weight.3) | copy-start | bytes 221188
  68.1 5.8 %collective-permute-start.24 = (f32[5,64,128]{2,1,0:T(8,128)S(1)}, f32[5,64,128]{2,1,0:T(8,128)S(1)}, u32[]{:S(2)}, u32[]{:S(2)}) collective-permute-start(f32[5,64,128]{2,1,0:T(8,128)S(1)} %weight_terms.1), channel_id=1, source_target_pairs={{0,4},{4,0},{8,12},{12,8},{16,20},{20,16},{24,28},{28,24},{1,5},{5... | collective-permute-start | bytes 491528 | tf_op jit(solution)/shard_map/ppermute | solution.py:315
  68.2 23.7 %collective-permute-start.4 = (bf16[16,64,128]{2,1,0:T(8,128)(2,1)S(1)}, bf16[16,64,128]{2,1,0:T(8,128)(2,1)S(1)}, u32[]{:S(2)}, u32[]{:S(2)}) collective-permute-start(bf16[16,64,128]{2,1,0:T(8,128)(2,1)S(1)} %get-tuple-element.38), channel_id=1, source_target_pairs={{0,0},{1,8},{2,16},{3,24},{4,4},{5,12},{6,20},{7,28},{8,1},{9,9},{... | collective-permute-start | bytes 786440 | tf_op jit(solution)/shard_map/ppermute | solution.py:292
  71.3 26.8 %collective-permute-start.6 = (bf16[16,64,128]{2,1,0:T(8,128)(2,1)S(1)}, bf16[16,64,128]{2,1,0:T(8,128)(2,1)S(1)}, u32[]{:S(2)}, u32[]{:S(2)}) collective-permute-start(bf16[16,64,128]{2,1,0:T(8,128)(2,1)S(1)} %collective-permute-done.5), channel_id=1, source_target_pairs={{0,1},{1,9},{2,17},{3,25},{4,5},{5,13},{6,21},{7,29},{8,0},{9,8},{... | collective-permute-start | bytes 786440 | tf_op jit(solution)/shard_map/ppermute | solution.py:292
  73.9 8.6 %collective-permute-start.25 = (f32[5,64,128]{2,1,0:T(8,128)S(1)}, f32[5,64,128]{2,1,0:T(8,128)S(1)}, u32[]{:S(2)}, u32[]{:S(2)}) collective-permute-start(f32[5,64,128]{2,1,0:T(8,128)S(1)} %add.18), channel_id=1, source_target_pairs={{0,8},{4,12},{8,0},{12,4},{16,24},{20,28},{24,16},{28,20},{1,9},{5... | collective-permute-start | bytes 491528 | tf_op jit(solution)/shard_map/ppermute | solution.py:315
  74.7 25.2 %collective-permute-start.8 = (bf16[16,64,128]{2,1,0:T(8,128)(2,1)S(1)}, bf16[16,64,128]{2,1,0:T(8,128)(2,1)S(1)}, u32[]{:S(2)}, u32[]{:S(2)}) collective-permute-start(bf16[16,64,128]{2,1,0:T(8,128)(2,1)S(1)} %collective-permute-done.7), channel_id=1, source_target_pairs={{0,2},{1,10},{2,18},{3,26},{4,6},{5,14},{6,22},{7,30},{8,3},{9,11}... | collective-permute-start | bytes 786440 | tf_op jit(solution)/shard_map/ppermute | solution.py:292
  77.9 23.9 %collective-permute-start.10 = (bf16[16,64,128]{2,1,0:T(8,128)(2,1)S(1)}, bf16[16,64,128]{2,1,0:T(8,128)(2,1)S(1)}, u32[]{:S(2)}, u32[]{:S(2)}) collective-permute-start(bf16[16,64,128]{2,1,0:T(8,128)(2,1)S(1)} %collective-permute-done.9), channel_id=1, source_target_pairs={{0,3},{1,11},{2,19},{3,27},{4,7},{5,15},{6,23},{7,31},{8,2},{9,10}... | collective-permute-start | bytes 786440 | tf_op jit(solution)/shard_map/ppermute | solution.py:292
  82.5 20.8 %collective-permute-start.26 = (f32[5,64,128]{2,1,0:T(8,128)S(1)}, f32[5,64,128]{2,1,0:T(8,128)S(1)}, u32[]{:S(2)}, u32[]{:S(2)}) collective-permute-start(f32[5,64,128]{2,1,0:T(8,128)S(1)} %add.19), channel_id=1, source_target_pairs={{0,16},{4,20},{8,24},{12,28},{16,0},{20,4},{24,8},{28,12},{1,17},{... | collective-permute-start | bytes 491528 | tf_op jit(solution)/shard_map/ppermute | solution.py:315
  91.8 12.3 %collective-permute-start.20 = (bf16[9,64,128]{2,1,0:T(8,128)(2,1)S(1)}, bf16[9,64,128]{2,1,0:T(8,128)(2,1)S(1)}, u32[]{:S(2)}, u32[]{:S(2)}) collective-permute-start(bf16[9,64,128]{2,1,0:T(8,128)(2,1)S(1)} %get-tuple-element.52), channel_id=1, source_target_pairs={{0,4},{4,8},{8,12},{12,16},{16,20},{20,24},{24,28},{1,5},{5,9},{9,... | collective-permute-start | bytes 442376 | tf_op jit(solution)/shard_map/ppermute | solution.py:71
  98.0 6.1 %collective-permute-start.21 = (bf16[9,64,128]{2,1,0:T(8,128)(2,1)S(1)}, bf16[9,64,128]{2,1,0:T(8,128)(2,1)S(1)}, u32[]{:S(2)}, u32[]{:S(2)}) collective-permute-start(bf16[9,64,128]{2,1,0:T(8,128)(2,1)S(1)} %get-tuple-element.53), channel_id=1, source_target_pairs={{4,0},{8,4},{12,8},{16,12},{20,16},{24,20},{28,24},{5,1},{9,5},{13... | collective-permute-start | bytes 442376 | tf_op jit(solution)/shard_map/ppermute | solution.py:72
  103.2 10.0 %collective-permute-start.11 = (bf16[32,64,128]{2,1,0:T(8,128)(2,1)S(1)}, bf16[32,64,128]{2,1,0:T(8,128)(2,1)S(1)}, u32[]{:S(2)}, u32[]{:S(2)}) collective-permute-start(bf16[32,64,128]{2,1,0:T(8,128)(2,1)S(1)} %get-tuple-element.43), channel_id=1, source_target_pairs={{0,4},{4,0},{8,12},{12,8},{16,20},{20,16},{24,28},{28,24},{1,5},{5... | collective-permute-start | bytes 1572872 | tf_op jit(solution)/shard_map/ppermute | solution.py:296
  103.4 7.1 %collective-permute-start.27 = (f32[5,64,128]{2,1,0:T(8,128)S(1)}, f32[5,64,128]{2,1,0:T(8,128)S(1)}, u32[]{:S(2)}, u32[]{:S(2)}) collective-permute-start(f32[5,64,128]{2,1,0:T(8,128)S(1)} %add.20), channel_id=1, source_target_pairs={{0,1},{1,0},{2,3},{3,2},{4,5},{5,4},{6,7},{7,6},{8,9},{9,8},{10,11... | collective-permute-start | bytes 491528 | tf_op jit(solution)/shard_map/ppermute | solution.py:315
  104.2 11.2 %collective-permute-start.22 = (bf16[5,64,128]{2,1,0:T(8,128)(2,1)S(1)}, bf16[5,64,128]{2,1,0:T(8,128)(2,1)S(1)}, u32[]{:S(2)}, u32[]{:S(2)}) collective-permute-start(bf16[5,64,128]{2,1,0:T(8,128)(2,1)S(1)} %pad_maximum_fusion.2), channel_id=1, source_target_pairs={{0,1},{1,2},{2,3},{4,5},{5,6},{6,7},{8,9},{9,10},{10,11},{12,13},{... | collective-permute-start | bytes 245768 | tf_op jit(solution)/shard_map/ppermute | solution.py:79
  110.5 14.4 %collective-permute-start.28 = (f32[5,64,128]{2,1,0:T(8,128)S(1)}, f32[5,64,128]{2,1,0:T(8,128)S(1)}, u32[]{:S(2)}, u32[]{:S(2)}) collective-permute-start(f32[5,64,128]{2,1,0:T(8,128)S(1)} %add.21.mine), channel_id=1, source_target_pairs={{0,2},{1,3},{2,0},{3,1},{4,6},{5,7},{6,4},{7,5},{8,10},{9,11},{10,... | collective-permute-start | bytes 491528 | tf_op jit(solution)/shard_map/ppermute | solution.py:317
  110.5 10.8 %collective-permute-start.23 = (bf16[5,64,128]{2,1,0:T(8,128)(2,1)S(1)}, bf16[5,64,128]{2,1,0:T(8,128)(2,1)S(1)}, u32[]{:S(2)}, u32[]{:S(2)}) collective-permute-start(bf16[5,64,128]{2,1,0:T(8,128)(2,1)S(1)} %pad_maximum_fusion.3), channel_id=1, source_target_pairs={{1,0},{2,1},{3,2},{5,4},{6,5},{7,6},{9,8},{10,9},{11,10},{13,12},{... | collective-permute-start | bytes 245768 | tf_op jit(solution)/shard_map/ppermute | solution.py:76

commit v3 on v2

v3 whole, which is shorter than its diff:
```python
import functools

import jax
import jax.numpy as jnp
from jax import lax
from jax.experimental import pallas as pl
from jax.experimental.pallas import tpu as pltpu
from jax.sharding import PartitionSpec as P

DILATION_STEP = 8
STEP = DILATION_STEP
BF16, F32 = jnp.bfloat16, jnp.float32
VMEM_LIMIT = 24 * 1024 * 1024


def call(kernel, out_shape, *args, scratch=(), flops=0, in_hbm=(), out_hbm=0, name=None):
    out_bytes = sum(o.size * o.dtype.itemsize for o in jax.tree.leaves(out_shape))
    in_bytes = sum(a.size * a.dtype.itemsize for a in args)
    in_specs = [
        pl.BlockSpec(memory_space=pltpu.SMEM if a.dtype == jnp.int32 else pltpu.VMEM) for a in args
    ]
    for k in in_hbm:
        in_specs[k] = pl.BlockSpec(memory_space=pl.ANY)
    out_specs = [pl.BlockSpec(memory_space=pltpu.VMEM)] * len(jax.tree.leaves(out_shape))
    if out_hbm:
        out_specs[-out_hbm:] = [pl.BlockSpec(memory_space=pl.ANY)] * out_hbm
    if not isinstance(out_shape, list):
        out_specs = out_specs[0]
    return pl.pallas_call(
        kernel,
        out_shape=out_shape,
        in_specs=in_specs,
        out_specs=out_specs,
        scratch_shapes=scratch,
        name=name,
        compiler_params=pltpu.CompilerParams(vmem_limit_bytes=VMEM_LIMIT),
        cost_estimate=pl.CostEstimate(
            flops=flops, bytes_accessed=in_bytes + out_bytes, transcendentals=0
        ),
    )(*args)


def shape(dims, dtype):
    return jax.ShapeDtypeStruct(tuple(dims), dtype)


def columns_of(rows, first):
    picked = [r[:, :STEP] if first else r[:, -STEP:] for r in rows]
    return jnp.concatenate(picked, axis=1)


def write_edges(tile, top_ref, bottom_ref, left_ref, right_ref):
    tile_rows, _, tile_cols = tile.shape
    span = tile_cols // STEP
    for group in range(tile_rows // span):
        rows = [tile[group * span + k] for k in range(span)]
        left_ref[group] = columns_of(rows, True)
        right_ref[group] = columns_of(rows, False)
    for k in range(STEP):
        top_ref[k] = tile[k]
        bottom_ref[k] = tile[tile_rows - STEP + k]


def edge_shapes(channels, tile_rows, tile_cols):
    rows = shape((STEP, channels, tile_cols), BF16)
    strips = shape((tile_rows * STEP // tile_cols, channels, tile_cols), BF16)
    return [rows, rows, strips, strips]


def shift(x, axis, forward):
    pairs = [(i, i + 1) for i in range(lax.axis_size(axis) - 1)]
    return lax.ppermute(x, axis, pairs if forward else [(j, i) for i, j in pairs])


def columns_first(top, bottom, left, right):
    from_left, from_right = shift(right, "col", True), shift(left, "col", False)
    last = left.shape[0] - 1
    down = jnp.concatenate([top, from_left[:1], from_right[:1]])
    up = jnp.concatenate([bottom, from_left[last:], from_right[last:]])
    return shift(up, "row", True), shift(down, "row", False), from_left, from_right


def corner_kernel(before, after, left, right, left_out, right_out):
    groups = left.shape[0]
    rows = [edge[k] for edge in (before, after) for k in range(STEP)]
    for first, strips, out in ((True, left, left_out), (False, right, right_out)):
        out[:groups] = strips[...]
        out[groups] = columns_of(rows, first)


def rows_first(top, bottom, left, right):
    before, after = shift(bottom, "row", True), shift(top, "row", False)
    whole = shape((left.shape[0] + 1,) + left.shape[1:], BF16)
    left, right = call(
        corner_kernel, [whole, whole], before, after, left, right, name="corners"
    )
    from_right, from_left = shift(left, "col", False), shift(right, "col", True)
    return before, after, from_left, from_right


def write_shifted(tile, before, after, from_left, from_right, stack):
    tile_rows, channels, tile_cols = tile.shape
    span = tile_cols // STEP
    groups = tile_rows // span
    rows_carry_corners = before.shape[0] > STEP
    for row in range(tile_rows + 2 * STEP):
        own = row - STEP
        if 0 <= own < tile_rows:
            middle, lane = tile[own], STEP * (own % span)
            left, right = from_left[own // span], from_right[own // span]
        else:
            edge, k = (before, row) if own < 0 else (after, own - tile_rows)
            middle = edge[k]
            if rows_carry_corners:
                left, right = edge[STEP], edge[STEP + 1]
                lane = STEP * (k + span - STEP if own < 0 else k)
            else:
                left, right = from_left[groups], from_right[groups]
                lane = STEP * (k if own < 0 else k + STEP)
        left, right = left[:, lane : lane + STEP], right[:, lane : lane + STEP]
        stack[row, :channels] = jnp.concatenate([left, middle[:, :-STEP]], axis=1)
        stack[row, channels : 2 * channels] = middle
        stack[row, 2 * channels :] = jnp.concatenate([middle[:, STEP:], right], axis=1)


def forward_taps(weight):
    lines = [jnp.concatenate([weight[p, q] for q in range(3)], axis=1) for p in range(3)]
    return jnp.concatenate(lines, axis=0)


def backward_taps(weight):
    lines = [
        jnp.concatenate([weight[2 - p, 2 - q].T for q in range(3)], axis=1) for p in range(3)
    ]
    return jnp.concatenate(lines, axis=0)


def convolve(stack, weights, tile_rows, emit):
    channels = weights.shape[0] // 3
    cols = stack.shape[2]
    for pair in range(STEP // 2):
        products = []
        for k in range(tile_rows // STEP + 2):
            row = STEP * k + 2 * pair
            both = jnp.concatenate([stack[row], stack[row + 1]], axis=1)
            products.append(jnp.dot(weights, both, preferred_element_type=F32))
            if k >= 2:
                total = (
                    products[k - 2][:channels]
                    + products[k - 1][channels : 2 * channels]
                    + products[k][2 * channels :]
                )
                out_row = STEP * (k - 2) + 2 * pair
                emit(out_row, total[:, :cols])
                emit(out_row + 1, total[:, cols:])


def open_kernel(cot, x, tile, top, bottom, left, right, *rest):
    pieces, done = rest[:-1], rest[-1]
    group = pieces[0].shape[0]
    copies = [
        pltpu.make_async_copy(cot.at[pl.ds(j * group, group)], piece, done.at[j])
        for j, piece in enumerate(pieces)
    ]
    for copy in copies:
        copy.start()
    rows = x.shape[1]
    for a in range(0, rows, 16):
        tile[a : a + 16] = jnp.swapaxes(x[:, a : a + 16], 0, 1)
    write_edges(tile, top, bottom, left, right)
    for copy in copies:
        copy.wait()


def forward_kernel(
    tile, before, after, from_left, from_right, weight, bias, token, stack, slope, *refs
):
    pieces, kept = refs[:-1], refs[-1]
    token[...] = jnp.zeros_like(token)
    group = pieces[0].shape[0]
    tile_rows = tile.shape[0]
    write_shifted(tile, before, after, from_left, from_right, stack)
    offset = bias[...]

    def emit(row, total):
        pre_act = total + offset
        rise = jnp.exp(jnp.minimum(pre_act, 0.0))
        slope[row] = rise
        elu = jnp.where(pre_act > 0, pre_act, rise - 1.0)
        kept[row] = (tile[row].astype(F32) + elu).astype(BF16)

    convolve(stack, forward_taps(weight), tile_rows, emit)
    for a in range(0, tile_rows, 16):
        mixed = jnp.swapaxes(kept[a : a + 16], 0, 1)
        for j, piece in enumerate(pieces):
            piece[:, a : a + 16] = mixed[j * group : (j + 1) * group]


def grad_pre_kernel(place, cot, keep, got, slope, token, tile, top, bottom, left, right, mirrored):
    token[...] = jnp.zeros_like(token)
    rows = cot.shape[1]
    for a in range(0, rows, 16):
        turned = joined(place[0], keep[:, a : a + 16], got[:, a : a + 16])
        mirrored[:, a : a + 16] = turned.astype(BF16)
        grad_mixed = cot[:, a : a + 16].astype(F32) + turned
        tile[a : a + 16] = (jnp.swapaxes(grad_mixed, 0, 1) * slope[a : a + 16]).astype(BF16)
    write_edges(tile, top, bottom, left, right)


def weight_kernel(side, place, grad, stack, token, keep, give, packed):
    token[...] = jnp.zeros_like(token)
    tile_rows, channels, cols = grad.shape
    nothing = jnp.zeros((channels, cols), BF16)

    def taps(row):
        own = [row - STEP * p for p in range(3)]
        return jnp.concatenate([grad[a] if 0 <= a < tile_rows else nothing for a in own], axis=0)

    total = jnp.zeros((3 * channels, 3 * channels), F32)
    for row in range(0, tile_rows + 2 * STEP, 2):
        total = total + lax.dot_general(
            jnp.concatenate([taps(row), taps(row + 1)], axis=1),
            jnp.concatenate([stack[row], stack[row + 1]], axis=1),
            (((1,), (1,)), ((), ())),
            preferred_element_type=F32,
        )
    cells = jnp.zeros((channels, cols), F32)
    for row in range(tile_rows):
        cells = cells + grad[row].astype(F32)
    bias = jnp.broadcast_to(jnp.sum(cells, axis=1, keepdims=True), (channels, channels))
    blocks = [
        total[p * channels : (p + 1) * channels, q * channels : (q + 1) * channels]
        for p in range(3)
        for q in range(3)
    ] + [bias]
    for k in range(0, len(blocks), 2):
        at = k // 2 * channels
        packed[at : at + channels] = jnp.concatenate(blocks[k : k + 2], axis=1) * (1.0 / side)
    half = keep.shape[0]
    keep[...] = packed[pl.ds(place[0] * half, half)]
    give[...] = packed[pl.ds((1 - place[0]) * half, half)]


def unpack_kernel(place, mine, other, weight, bias, packed):
    half, channels = mine.shape[0], weight.shape[2]
    packed[pl.ds(place[0] * half, half)] = mine[...]
    packed[pl.ds((1 - place[0]) * half, half)] = other[...]
    for k in range(9):
        row, col = k // 2 * channels, k % 2 * channels
        weight[k // 3, k % 3] = packed[row : row + channels, col : col + channels]
    last = packed[4 * channels :, channels:]
    line = lax.broadcasted_iota(jnp.int32, last.shape, 0)
    lane = lax.broadcasted_iota(jnp.int32, last.shape, 1)
    bias[...] = jnp.sum(jnp.where(line == lane, last, 0.0), axis=0, keepdims=True)


def input_grad_kernel(
    tile, before, after, from_left, from_right, weight, cot, mirrored, out, stack, kept
):
    tile_rows = tile.shape[0]
    write_shifted(tile, before, after, from_left, from_right, stack)

    def emit(row, total):
        kept[row] = total

    convolve(stack, backward_taps(weight), tile_rows, emit)
    for a in range(0, tile_rows, 16):
        grad_mixed = cot[:, a : a + 16].astype(F32) + mirrored[:, a : a + 16].astype(F32)
        out[:, a : a + 16] = (grad_mixed + jnp.swapaxes(kept[a : a + 16], 0, 1)).astype(BF16)


def turn_kernel(place, *refs):
    pieces, (keep, give) = refs[:-2], refs[-2:]
    tile_rows = pieces[0].shape[1]
    core = place[0]
    group, near = pieces[0].shape[0], len(pieces) // 2
    for j in range(near):
        for c in range(group):
            low, high = pieces[j][c].T, pieces[j + near][c].T
            first = jnp.concatenate([low[:tile_rows], high[:tile_rows]], axis=1)
            second = jnp.concatenate([low[tile_rows:], high[tile_rows:]], axis=1)
            keep[j * group + c] = jnp.where(core == 0, first, second)
            give[j * group + c] = jnp.where(core == 0, second, first)


def joined(core, keep, got):
    keep, got = keep.astype(F32), got.astype(F32)
    lower = lax.broadcasted_iota(jnp.int32, (1, 1, keep.shape[2]), 2) < keep.shape[2] // 2
    first, second = jnp.where(core == 0, keep, got), jnp.where(core == 0, got, keep)
    low = jnp.where(lower, first, swap_lanes(second))
    high = jnp.where(lower, swap_lanes(first), second)
    return jnp.concatenate([low, high], axis=0)


def swap_lanes(x):
    half = x.shape[2] // 2
    return jnp.concatenate([x[:, :, half:], x[:, :, :half]], axis=2)


def detour(piece, far):
    if far == 0:
        return piece
    return lax.ppermute(piece, "row", [(r, r ^ (2 * far)) for r in range(lax.axis_size("row"))])


def cross(piece, far):
    size, blocks = lax.axis_size("row"), lax.axis_size("col")
    owners = [
        (r * blocks + z, (z * 2 + r % 2) * blocks + ((r // 2) ^ far))
        for r in range(size)
        for z in range(blocks)
    ]
    return lax.ppermute(piece, ("row", "col"), owners)


def turn(pieces, place):
    group, tile_rows, tile_cols = pieces[0].shape
    half = shape((group * len(pieces) // 2, tile_rows, tile_cols), BF16)
    return call(turn_kernel, [half, half], place, *pieces, name="turn")


def swapped(give):
    return lax.ppermute(give, "row", [(r, r ^ 1) for r in range(lax.axis_size("row"))])


def held(pieces, *until):
    return lax.optimization_barrier((pieces, until))[0]


def join_kernel(place, keep, got, *refs):
    pieces, out = refs[:-1], refs[-1]
    for a in range(0, out.shape[1], 16):
        rows = slice(a, a + 16)
        turned = joined(place[0], keep[:, rows], got[:, rows])
        own = jnp.concatenate([piece[:, rows] for piece in pieces], axis=0)
        out[:, rows] = (own.astype(F32) + turned).astype(BF16)


def summed(part, axis, reach):
    size = lax.axis_size(axis)
    while reach < size:
        part = part + lax.ppermute(part, axis, [(i, i ^ reach) for i in range(size)])
        reach *= 2
    return part


def shards(pair_feature_map, conv_weight, conv_bias, cotangent):
    channels, tile_rows, tile_cols = pair_feature_map.shape
    side = tile_rows * lax.axis_size("row")
    tile_shape = shape((tile_rows, channels, tile_cols), BF16)
    edges = edge_shapes(channels, tile_rows, tile_cols)
    stack_dims = (tile_rows + 2 * STEP, 3 * channels, tile_cols)
    conv_flops = 2 * 9 * channels * channels * tile_rows * tile_cols
    rounds = lax.axis_size("col")
    place = jnp.full((1,), lax.axis_index("row") % 2, jnp.int32)
    piece = shape((channels // rounds, tile_rows, tile_cols), BF16)

    tile, *opened = call(
        open_kernel,
        [tile_shape] + edges + [piece] * rounds,
        cotangent,
        pair_feature_map,
        scratch=[pltpu.SemaphoreType.DMA((rounds,))],
        in_hbm=[0],
        out_hbm=rounds,
        name="open",
    )
    token = shape((8, 128), F32)
    halo = columns_first(*opened[:4])
    dealt = [detour(p, j) for j, p in enumerate(opened[4:])]
    forwarded, stack, slope, *mixed = call(
        forward_kernel,
        [token, shape(stack_dims, BF16), shape((tile_rows, channels, tile_cols), F32)]
        + [piece] * rounds,
        tile,
        *halo,
        conv_weight,
        conv_bias[:, None],
        scratch=[pltpu.VMEM((tile_rows, channels, tile_cols), BF16)],
        flops=conv_flops,
        name="forward",
    )
    arrived = [cross(held(p, *halo[2:]), j) for j, p in enumerate(dealt)]
    mixed_dealt = [detour(p, j) for j, p in enumerate(mixed)]
    keep, give = turn(held(arrived, slope), place)
    ready, grad, *edge, mirrored = call(
        grad_pre_kernel,
        [token, tile_shape] + edges + [shape(cotangent.shape, BF16)],
        place,
        cotangent,
        keep,
        swapped(give),
        slope,
        name="grad_pre",
    )
    packed = pltpu.VMEM((5 * channels, 2 * channels), F32)
    half = shape((5 * channels // 2, 2 * channels), F32)
    weighed, *terms = call(
        functools.partial(weight_kernel, side),
        [token, half, half],
        place,
        grad,
        stack,
        scratch=[packed],
        flops=conv_flops,
        name="weight_terms",
    )
    halo = columns_first(*edge)
    part = summed(terms[0] + swapped(terms[1]), "col", 1)
    mixed_arrived = [cross(held(p, part, *halo[2:]), j) for j, p in enumerate(mixed_dealt)]
    part = summed(part, "row", 2)
    mixed_keep, mixed_give = turn(held(mixed_arrived, part, *halo[:2]), place)
    symmetric = call(
        join_kernel,
        shape(pair_feature_map.shape, BF16),
        place,
        mixed_keep,
        swapped(mixed_give),
        *mixed,
        name="join",
    )
    grad_input = call(
        input_grad_kernel,
        shape(pair_feature_map.shape, BF16),
        grad,
        *halo,
        conv_weight,
        cotangent,
        mirrored,
        scratch=[
            pltpu.VMEM(stack_dims, BF16),
            pltpu.VMEM((tile_rows, channels, tile_cols), F32),
        ],
        flops=conv_flops,
        name="input_grad",
    )
    grad_weight, grad_bias = call(
        unpack_kernel,
        [shape((3, 3, channels, channels), F32), shape((1, channels), F32)],
        place,
        part,
        swapped(part),
        scratch=[packed],
        name="unpack",
    )
    return symmetric, grad_input, grad_weight, grad_bias.reshape(channels)


def solution(mesh):
    placed = (P(None, "row", "col"), P(), P(), P(None, "row", "col"))
    return jax.shard_map(
        shards,
        mesh=mesh,
        in_specs=placed,
        out_specs=(P(None, "row", "col"), P(None, "row", "col"), P(), P()),
        check_vma=False,
    )
```

time: 126 us -> 118 us (0.937); the launches traced: 126 us -> 116 us
  waiting for transfers between devices: 41.4 us -> 32.7 us
  Pallas kernels: 19.4 us -> 17.1 us
  starting transfers between devices: 58.4 us -> 60.1 us
    ppermute x29 -> x30, waiting for transfers between devices: 41.4 us -> 32.7 us  [the longest x8 15.4 us: shift(): lax.ppermute(x, axis, pairs if forward else [(j, i) for i, j in pairs])]
    pallas_call x10 -> x9, Pallas kernels: 19.4 us -> 17.1 us  [call(): pl.pallas_call(kernel, out_shape=out_shape, in_specs=in_specs, out_specs=...]
    ppermute x29 -> x30, starting transfers between devices: 58.4 us -> 60.1 us  [the longest x8 27.3 us: cross(): return lax.ppermute(piece, ('row', 'col'), owners)]
  transfers between devices with their start and end apart: 29 -> 30, of which waited for: 11 -> 12; matrix products, arithmetic and copies ran while one was open for 2% -> 1% of each run, Pallas kernels for 14% -> 9%
where the time goes in v3:
time: 118 us; the launch traced here: 116 us
  starting transfers between devices  60.1 us (51%)
  waiting for transfers between devices  32.7 us (28%)
  Pallas kernels  17.1 us (14%)
  local copies, waits for them, and re-layouts  4.12 us (3%)
    ppermute x8, starting transfers between devices, cross(): return lax.ppermute(piece, ('row', 'col'), owners)  27.3 us
    ppermute x8, starting transfers between devices, shift(): lax.ppermute(x, axis, pairs if forward else [(j, i) for i, j in pairs])  19.7 us
    pallas_call x9, Pallas kernels, call(): pl.pallas_call(kernel, out_shape=out_shape, in_specs=in_specs, out_specs=...  17.1 us
    ppermute x8, waiting for transfers between devices, shift(): lax.ppermute(x, axis, pairs if forward else [(j, i) for i, j in pairs])  15.4 us
    ppermute x4, waiting for transfers between devices, summed(): lax.ppermute(part, axis, [(i, i ^ reach) for i in range(size)])  8.2 us
    ppermute x6, starting transfers between devices, detour(): lax.ppermute(piece, 'row', [(r, r ^ 2 * far) for r in range(lax.axis_size...  7.11 us
    ppermute x8, waiting for transfers between devices, cross(): return lax.ppermute(piece, ('row', 'col'), owners)  5 us
    ppermute x4, starting transfers between devices, summed(): lax.ppermute(part, axis, [(i, i ^ reach) for i in range(size)])  4.61 us
  transfers between devices with their start and end apart: 30, of which 12 were waited for; matrix products, arithmetic and copies ran while one was open for 1% of the time, Pallas kernels for 9%

profile of v3, /device:TPU:12, one launch (start us, length us, event | category | flops | bytes accessed | tf_op | source)
XLA Modules:
  0.0 115.7 jit_solution(12825346347738667755)
XLA Ops:
  0.6 1.2 %copy-done = bf16[64,64,128]{2,1,0:T(8,128)(2,1)S(1)} copy-done((bf16[64,64,128]{2,1,0:T(8,128)(2,1)S(1)}, bf16[64,64,128]{2,1,0:T(8,128)(2,1)}, u32[]{:S(2)}) %copy-start) | copy-done | bytes 1048600
  1.9 1.2 %copy-done.2 = bf16[64,64,128]{2,1,0:T(8,128)(2,1)S(1)} copy-done((bf16[64,64,128]{2,1,0:T(8,128)(2,1)S(1)}, bf16[64,64,128]{2,1,0:T(8,128)(2,1)}, u32[]{:S(2)}) %copy-start.2) | copy-done | bytes 1048600
  3.1 0.9 open.1
  3.9 2.4 %collective-permute-start.1 = (bf16[4,64,128]{2,1,0:T(8,128)(2,1)S(1)}, bf16[4,64,128]{2,1,0:T(8,128)(2,1)S(1)}, u32[]{:S(2)}, u32[]{:S(2)}) collective-permute-start(bf16[4,64,128]{2,1,0:T(8,128)(2,1)S(1)} %get-tuple-element.52), channel_id=1, source_target_pairs={{1,0},{2,1},{3,2},{5,4},{6,5},{7,6},{9,8},{10,9},{11,10},{13,12},{... | collective-permute-start | bytes 196616 | tf_op jit(solution)/shard_map/ppermute | solution.py:72
  6.3 3.5 %collective-permute-start = (bf16[4,64,128]{2,1,0:T(8,128)(2,1)S(1)}, bf16[4,64,128]{2,1,0:T(8,128)(2,1)S(1)}, u32[]{:S(2)}, u32[]{:S(2)}) collective-permute-start(bf16[4,64,128]{2,1,0:T(8,128)(2,1)S(1)} %get-tuple-element.51), channel_id=1, source_target_pairs={{0,1},{1,2},{2,3},{4,5},{5,6},{6,7},{8,9},{9,10},{10,11},{12,13},{... | collective-permute-start | bytes 196616 | tf_op jit(solution)/shard_map/ppermute | solution.py:72
  9.8 1.5 %collective-permute-start.9 = (bf16[16,64,128]{2,1,0:T(8,128)(2,1)S(1)}, bf16[16,64,128]{2,1,0:T(8,128)(2,1)}, u32[]{:S(2)}, u32[]{:S(2)}) collective-permute-start(bf16[16,64,128]{2,1,0:T(8,128)(2,1)S(1)} %get-tuple-element.61), channel_id=1, source_target_pairs={{0,24},{4,28},{8,16},{12,20},{16,8},{20,12},{24,0},{28,4},{1,25},{... | collective-permute-start | bytes 786440 | tf_op jit(solution)/shard_map/ppermute | solution.py:303
  11.3 0.5 collective-permute-start.5
  11.8 1.5 %collective-permute-start.7 = (bf16[16,64,128]{2,1,0:T(8,128)(2,1)S(1)}, bf16[16,64,128]{2,1,0:T(8,128)(2,1)}, u32[]{:S(2)}, u32[]{:S(2)}) collective-permute-start(bf16[16,64,128]{2,1,0:T(8,128)(2,1)S(1)} %get-tuple-element.59), channel_id=1, source_target_pairs={{0,16},{4,20},{8,24},{12,28},{16,0},{20,4},{24,8},{28,12},{1,17},{... | collective-permute-start | bytes 786440 | tf_op jit(solution)/shard_map/ppermute | solution.py:303
  13.4 0.0 collective-permute-done.1.from_right
  13.4 0.0 collective-permute-done.from_left
  13.4 1.9 %collective-permute-start.3 = (bf16[10,64,128]{2,1,0:T(8,128)(2,1)S(1)}, bf16[10,64,128]{2,1,0:T(8,128)(2,1)S(1)}, u32[]{:S(2)}, u32[]{:S(2)}) collective-permute-start(bf16[10,64,128]{2,1,0:T(8,128)(2,1)S(1)} %pad_maximum_fusion.1), channel_id=1, source_target_pairs={{4,0},{8,4},{12,8},{16,12},{20,16},{24,20},{28,24},{5,1},{9,5},{13... | collective-permute-start | bytes 491528 | tf_op jit(solution)/shard_map/ppermute | solution.py:72
  15.3 4.4 %collective-permute-start.4 = (bf16[16,64,128]{2,1,0:T(8,128)(2,1)}, bf16[16,64,128]{2,1,0:T(8,128)(2,1)S(1)}, u32[]{:S(2)}, u32[]{:S(2)}) collective-permute-start(bf16[16,64,128]{2,1,0:T(8,128)(2,1)} %get-tuple-element.56), channel_id=1, source_target_pairs={{0,0},{1,8},{2,16},{3,24},{4,4},{5,12},{6,20},{7,28},{8,1},{9,9},{... | collective-permute-start | bytes 786440 | tf_op jit(solution)/shard_map/ppermute | solution.py:313
  19.7 0.5 collective-permute-done.9
  20.2 1.4 %collective-permute-start.10 = (bf16[16,64,128]{2,1,0:T(8,128)(2,1)}, bf16[16,64,128]{2,1,0:T(8,128)(2,1)S(1)}, u32[]{:S(2)}, u32[]{:S(2)}) collective-permute-start(bf16[16,64,128]{2,1,0:T(8,128)(2,1)} %collective-permute-done.9), channel_id=1, source_target_pairs={{0,3},{1,11},{2,19},{3,27},{4,7},{5,15},{6,23},{7,31},{8,2},{9,10}... | collective-permute-start | bytes 786440 | tf_op jit(solution)/shard_map/ppermute | solution.py:313
  21.6 1.7 %collective-permute-done.5 = bf16[16,64,128]{2,1,0:T(8,128)(2,1)} collective-permute-done((bf16[16,64,128]{2,1,0:T(8,128)(2,1)S(1)}, bf16[16,64,128]{2,1,0:T(8,128)(2,1)}, u32[]{:S(2)}, u32[]{:S(2)}) %collective-permute-start.5) | collective-permute-done | bytes 262176 | tf_op jit(solution)/shard_map/ppermute | solution.py:303
  23.3 3.1 %collective-permute-start.6 = (bf16[16,64,128]{2,1,0:T(8,128)(2,1)}, bf16[16,64,128]{2,1,0:T(8,128)(2,1)S(1)}, u32[]{:S(2)}, u32[]{:S(2)}) collective-permute-start(bf16[16,64,128]{2,1,0:T(8,128)(2,1)} %collective-permute-done.5), channel_id=1, source_target_pairs={{0,1},{1,9},{2,17},{3,25},{4,5},{5,13},{6,21},{7,29},{8,0},{9,8},{... | collective-permute-start | bytes 786440 | tf_op jit(solution)/shard_map/ppermute | solution.py:313
  26.4 0.0 collective-permute-done.7
  26.4 9.8 %collective-permute-start.8 = (bf16[16,64,128]{2,1,0:T(8,128)(2,1)}, bf16[16,64,128]{2,1,0:T(8,128)(2,1)S(1)}, u32[]{:S(2)}, u32[]{:S(2)}) collective-permute-start(bf16[16,64,128]{2,1,0:T(8,128)(2,1)} %collective-permute-done.7), channel_id=1, source_target_pairs={{0,2},{1,10},{2,18},{3,26},{4,6},{5,14},{6,22},{7,30},{8,3},{9,11}... | collective-permute-start | bytes 786440 | tf_op jit(solution)/shard_map/ppermute | solution.py:313
  36.2 0.7 pad_maximum_fusion
  36.9 0.0 collective-permute-done.3.after
  36.9 1.9 %collective-permute-start.2 = (bf16[10,64,128]{2,1,0:T(8,128)(2,1)}, bf16[10,64,128]{2,1,0:T(8,128)(2,1)}, u32[]{:S(2)}, u32[]{:S(2)}) collective-permute-start(bf16[10,64,128]{2,1,0:T(8,128)(2,1)} %pad_maximum_fusion), channel_id=1, source_target_pairs={{0,4},{4,8},{8,12},{12,16},{16,20},{20,24},{24,28},{1,5},{5,9},{9,... | collective-permute-start | bytes 491528 | tf_op jit(solution)/shard_map/ppermute | solution.py:72
  38.8 0.7 copy.8.bias
  39.6 6.1 %collective-permute-done.2.before = bf16[10,64,128]{2,1,0:T(8,128)(2,1)} collective-permute-done((bf16[10,64,128]{2,1,0:T(8,128)(2,1)}, bf16[10,64,128]{2,1,0:T(8,128)(2,1)}, u32[]{:S(2)}, u32[]{:S(2)}) %collective-permute-start.2) | collective-permute-done | bytes 163872 | tf_op jit(solution)/shard_map/ppermute | solution.py:72
  45.7 0.9 copy-done.3
  46.6 4.5 %forward.1 = (f32[8,128]{1,0:T(8,128)}, bf16[80,192,128]{2,1,0:T(8,128)(2,1)S(1)}, f32[64,64,128]{2,1,0:T(8,128)S(1)}, bf16[16,64,128]{2,1,0:T(8,128)(2,1)S(1)},...) custom-call(bf16[64,64,128]{2,1,0:T(8,128)(2,1)S(1)} %get-tuple-element.49.tile, ...), custom_call_target="tpu_custom_call" | custom-call | flops 603979776 | bytes 8663296 | tf_op jit(solution)/shard_map/forward/pallas_call | solution.py:29
  51.2 0.0 collective-permute-done.4.refs_0_
  51.2 0.0 collective-permute-done.8.refs_2_
  51.2 0.9 turn.2
  52.1 0.1 collective-permute-start.11
  52.2 1.9 %collective-permute-done.11.got = bf16[32,64,128]{2,1,0:T(8,128)(2,1)S(1)} collective-permute-done((bf16[32,64,128]{2,1,0:T(8,128)(2,1)S(1)}, bf16[32,64,128]{2,1,0:T(8,128)(2,1)S(1)}, u32[]{:S(2)}, u32[]{:S(2)}) %collective-permute-start.11) | collective-permute-done | bytes 524320 | tf_op jit(solution)/shard_map/ppermute | solution.py:323
  54.1 2.1 %grad_pre.1 = (f32[8,128]{1,0:T(8,128)}, bf16[64,64,128]{2,1,0:T(8,128)(2,1)S(1)}, bf16[8,64,128]{2,1,0:T(8,128)(2,1)S(1)}, bf16[8,64,128]{2,1,0:T(8,128)(2,1)S(...) custom-call(s32[1]{0:T(128)} %bitcast.place, ...), custom_call_target="tpu_custom_call" | custom-call | bytes 6688772 | tf_op jit(solution)/shard_map/grad_pre/pallas_call | solution.py:29
  56.2 1.9 %collective-permute-start.15 = (bf16[4,64,128]{2,1,0:T(8,128)(2,1)S(1)}, bf16[4,64,128]{2,1,0:T(8,128)(2,1)S(1)}, u32[]{:S(2)}, u32[]{:S(2)}) collective-permute-start(bf16[4,64,128]{2,1,0:T(8,128)(2,1)S(1)} %get-tuple-element.74), channel_id=1, source_target_pairs={{0,1},{1,2},{2,3},{4,5},{5,6},{6,7},{8,9},{9,10},{10,11},{12,13},{... | collective-permute-start | bytes 196616 | tf_op jit(solution)/shard_map/ppermute | solution.py:72
  58.1 2.1 %collective-permute-start.22 = (bf16[16,64,128]{2,1,0:T(8,128)(2,1)S(1)}, bf16[16,64,128]{2,1,0:T(8,128)(2,1)S(1)}, u32[]{:S(2)}, u32[]{:S(2)}) collective-permute-start(bf16[16,64,128]{2,1,0:T(8,128)(2,1)S(1)} %get-tuple-element.81.refs_3_), channel_id=1, source_target_pairs={{0,24},{4,28},{8,16},{12,20},{16,8},{20,12},{24,0},{28,4},{1,25},{... | collective-permute-start | bytes 786440 | tf_op jit(solution)/shard_map/ppermute | solution.py:303
  60.2 0.0 collective-permute-start.20
  60.2 1.5 %collective-permute-start.18 = (bf16[16,64,128]{2,1,0:T(8,128)(2,1)S(1)}, bf16[16,64,128]{2,1,0:T(8,128)(2,1)S(1)}, u32[]{:S(2)}, u32[]{:S(2)}) collective-permute-start(bf16[16,64,128]{2,1,0:T(8,128)(2,1)S(1)} %get-tuple-element.77.refs_1_), channel_id=1, source_target_pairs={{0,8},{4,12},{8,0},{12,4},{16,24},{20,28},{24,16},{28,20},{1,9},{5... | collective-permute-start | bytes 786440 | tf_op jit(solution)/shard_map/ppermute | solution.py:303
  61.6 1.8 %weight_terms.1 = (f32[8,128]{1,0:T(8,128)}, f32[160,128]{1,0:T(8,128)S(1)}, f32[160,128]{1,0:T(8,128)S(1)}) custom-call(s32[1]{0:T(128)} %bitcast.place, bf16[64,64,128]{2,1,0:T(8,128)(2,1)S(1)} %get-tuple-element.70.grad.tile, bf16[80,192,128]{2,1,0:T(8,128)(2,1)S(1)} %get-tuple-element.71.stack), custom_call_target="tpu_custom_call" | custom-call | flops 603979776 | bytes 5148676 | tf_op jit(solution)/shard_map/weight_terms/pallas_call | solution.py:29
  63.5 3.9 %collective-permute-start.16 = (bf16[4,64,128]{2,1,0:T(8,128)(2,1)S(1)}, bf16[4,64,128]{2,1,0:T(8,128)(2,1)S(1)}, u32[]{:S(2)}, u32[]{:S(2)}) collective-permute-start(bf16[4,64,128]{2,1,0:T(8,128)(2,1)S(1)} %get-tuple-element.75), channel_id=1, source_target_pairs={{1,0},{2,1},{3,2},{5,4},{6,5},{7,6},{9,8},{10,9},{11,10},{13,12},{... | collective-permute-start | bytes 196616 | tf_op jit(solution)/shard_map/ppermute | solution.py:72
  67.4 0.0 collective-permute-done.12
  67.5 0.1 collective-permute-start.13
  67.5 3.3 %collective-permute-done.16.from_right = bf16[4,64,128]{2,1,0:T(8,128)(2,1)S(1)} collective-permute-done((bf16[4,64,128]{2,1,0:T(8,128)(2,1)S(1)}, bf16[4,64,128]{2,1,0:T(8,128)(2,1)S(1)}, u32[]{:S(2)}, u32[]{:S(2)}) %collective-permute-start.16) | collective-permute-done | bytes 65568 | tf_op jit(solution)/shard_map/ppermute | solution.py:72
  70.8 1.3 %collective-permute-done.13 = f32[160,128]{1,0:T(8,128)S(1)} collective-permute-done((f32[160,128]{1,0:T(8,128)S(1)}, f32[160,128]{1,0:T(8,128)S(1)}, u32[]{:S(2)}, u32[]{:S(2)}) %collective-permute-start.13) | collective-permute-done | bytes 81952 | tf_op jit(solution)/shard_map/ppermute | solution.py:342
  72.1 2.2 %collective-permute-start.14 = (f32[160,128]{1,0:T(8,128)S(1)}, f32[160,128]{1,0:T(8,128)S(1)}, u32[]{:S(2)}, u32[]{:S(2)}) collective-permute-start(f32[160,128]{1,0:T(8,128)S(1)} %add.21), channel_id=1, source_target_pairs={{0,2},{1,3},{2,0},{3,1},{4,6},{5,7},{6,4},{7,5},{8,10},{9,11},{10,... | collective-permute-start | bytes 245768 | tf_op jit(solution)/shard_map/ppermute | solution.py:342
  74.3 2.1 %collective-permute-start.27 = (bf16[10,64,128]{2,1,0:T(8,128)(2,1)S(1)}, bf16[10,64,128]{2,1,0:T(8,128)(2,1)S(1)}, u32[]{:S(2)}, u32[]{:S(2)}) collective-permute-start(bf16[10,64,128]{2,1,0:T(8,128)(2,1)S(1)} %pad_maximum_fusion.3), channel_id=1, source_target_pairs={{4,0},{8,4},{12,8},{16,12},{20,16},{24,20},{28,24},{5,1},{9,5},{13... | collective-permute-start | bytes 491528 | tf_op jit(solution)/shard_map/ppermute | solution.py:72
  76.4 1.4 %collective-permute-done.14 = f32[160,128]{1,0:T(8,128)S(1)} collective-permute-done((f32[160,128]{1,0:T(8,128)S(1)}, f32[160,128]{1,0:T(8,128)S(1)}, u32[]{:S(2)}, u32[]{:S(2)}) %collective-permute-start.14) | collective-permute-done | bytes 81952 | tf_op jit(solution)/shard_map/ppermute | solution.py:342
  77.8 2.1 %collective-permute-start.24 = (f32[160,128]{1,0:T(8,128)S(1)}, f32[160,128]{1,0:T(8,128)S(1)}, u32[]{:S(2)}, u32[]{:S(2)}) collective-permute-start(f32[160,128]{1,0:T(8,128)S(1)} %add.22), channel_id=1, source_target_pairs={{0,8},{4,12},{8,0},{12,4},{16,24},{20,28},{24,16},{28,20},{1,9},{5... | collective-permute-start | bytes 245768 | tf_op jit(solution)/shard_map/ppermute | solution.py:342
  79.9 0.0 collective-permute-done.22
  79.9 0.1 collective-permute-start.23
  80.0 3.7 %collective-permute-start.21 = (bf16[16,64,128]{2,1,0:T(8,128)(2,1)S(1)}, bf16[16,64,128]{2,1,0:T(8,128)(2,1)S(1)}, u32[]{:S(2)}, u32[]{:S(2)}) collective-permute-start(bf16[16,64,128]{2,1,0:T(8,128)(2,1)S(1)} %collective-permute-done.20), channel_id=1, source_target_pairs={{0,2},{1,10},{2,18},{3,26},{4,6},{5,14},{6,22},{7,30},{8,3},{9,11}... | collective-permute-start | bytes 786440 | tf_op jit(solution)/shard_map/ppermute | solution.py:313
  83.6 0.0 collective-permute-done.18
  83.6 1.8 %collective-permute-start.19 = (bf16[16,64,128]{2,1,0:T(8,128)(2,1)S(1)}, bf16[16,64,128]{2,1,0:T(8,128)(2,1)S(1)}, u32[]{:S(2)}, u32[]{:S(2)}) collective-permute-start(bf16[16,64,128]{2,1,0:T(8,128)(2,1)S(1)} %collective-permute-done.18), channel_id=1, source_target_pairs={{0,1},{1,9},{2,17},{3,25},{4,5},{5,13},{6,21},{7,29},{8,0},{9,8},{... | collective-permute-start | bytes 786440 | tf_op jit(solution)/shard_map/ppermute | solution.py:313
  85.4 1.4 %collective-permute-done.24 = f32[160,128]{1,0:T(8,128)S(1)} collective-permute-done((f32[160,128]{1,0:T(8,128)S(1)}, f32[160,128]{1,0:T(8,128)S(1)}, u32[]{:S(2)}, u32[]{:S(2)}) %collective-permute-start.24) | collective-permute-done | bytes 81952 | tf_op jit(solution)/shard_map/ppermute | solution.py:342
  86.8 3.1 %collective-permute-start.17 = (bf16[16,64,128]{2,1,0:T(8,128)(2,1)S(1)}, bf16[16,64,128]{2,1,0:T(8,128)(2,1)S(1)}, u32[]{:S(2)}, u32[]{:S(2)}) collective-permute-start(bf16[16,64,128]{2,1,0:T(8,128)(2,1)S(1)} %get-tuple-element.76.refs_0_), channel_id=1, source_target_pairs={{0,0},{1,8},{2,16},{3,24},{4,4},{5,12},{6,20},{7,28},{8,1},{9,9},{... | collective-permute-start | bytes 786440 | tf_op jit(solution)/shard_map/ppermute | solution.py:313
  89.9 0.3 collective-permute-start.25
  90.2 4.2 %collective-permute-done.25 = f32[160,128]{1,0:T(8,128)S(1)} collective-permute-done((f32[160,128]{1,0:T(8,128)S(1)}, f32[160,128]{1,0:T(8,128)S(1)}, u32[]{:S(2)}, u32[]{:S(2)}) %collective-permute-start.25) | collective-permute-done | bytes 81952 | tf_op jit(solution)/shard_map/ppermute | solution.py:342
  94.4 2.1 %collective-permute-start.26 = (bf16[10,64,128]{2,1,0:T(8,128)(2,1)S(1)}, bf16[10,64,128]{2,1,0:T(8,128)(2,1)S(1)}, u32[]{:S(2)}, u32[]{:S(2)}) collective-permute-start(bf16[10,64,128]{2,1,0:T(8,128)(2,1)S(1)} %pad_maximum_fusion.2), channel_id=1, source_target_pairs={{0,4},{4,8},{8,12},{12,16},{16,20},{20,24},{24,28},{1,5},{5,9},{9,... | collective-permute-start | bytes 491528 | tf_op jit(solution)/shard_map/ppermute | solution.py:72
  96.5 6.0 %collective-permute-done.26.before = bf16[10,64,128]{2,1,0:T(8,128)(2,1)S(1)} collective-permute-done((bf16[10,64,128]{2,1,0:T(8,128)(2,1)S(1)}, bf16[10,64,128]{2,1,0:T(8,128)(2,1)S(1)}, u32[]{:S(2)}, u32[]{:S(2)}) %collective-permute-start.26) | collective-permute-done | bytes 163872 | tf_op jit(solution)/shard_map/ppermute | solution.py:72
  102.6 3.7 %collective-permute-done.21.refs_2_ = bf16[16,64,128]{2,1,0:T(8,128)(2,1)S(1)} collective-permute-done((bf16[16,64,128]{2,1,0:T(8,128)(2,1)S(1)}, bf16[16,64,128]{2,1,0:T(8,128)(2,1)S(1)}, u32[]{:S(2)}, u32[]{:S(2)}) %collective-permute-start.21) | collective-permute-done | bytes 262176 | tf_op jit(solution)/shard_map/ppermute | solution.py:313
  106.3 1.2 %collective-permute-done.17.refs_0_ = bf16[16,64,128]{2,1,0:T(8,128)(2,1)S(1)} collective-permute-done((bf16[16,64,128]{2,1,0:T(8,128)(2,1)S(1)}, bf16[16,64,128]{2,1,0:T(8,128)(2,1)S(1)}, u32[]{:S(2)}, u32[]{:S(2)}) %collective-permute-start.17) | collective-permute-done | bytes 262176 | tf_op jit(solution)/shard_map/ppermute | solution.py:313
  107.5 0.9 turn.3
  108.5 1.2 %collective-permute-start.28 = (bf16[32,64,128]{2,1,0:T(8,128)(2,1)S(1)}, bf16[32,64,128]{2,1,0:T(8,128)(2,1)S(1)}, u32[]{:S(2)}, u32[]{:S(2)}) collective-permute-start(bf16[32,64,128]{2,1,0:T(8,128)(2,1)S(1)} %get-tuple-element.90), channel_id=1, source_target_pairs={{0,4},{4,0},{8,12},{12,8},{16,20},{20,16},{24,28},{28,24},{1,5},{5... | collective-permute-start | bytes 1572872 | tf_op jit(solution)/shard_map/ppermute | solution.py:323
  109.7 0.1 collective-permute-start.29
  109.8 3.5 %input_grad.1 = bf16[64,64,128]{2,1,0:T(8,128)(2,1)} custom-call(bf16[64,64,128]{2,1,0:T(8,128)(2,1)S(1)} %get-tuple-element.70.grad.tile, bf16[10,64,128]{2,1,0:T(8,128)(2,1)S(1)} %collective-permute-done.26.before, bf16[10,64,128]{2,1,0:T(8,128)(2,1)S(1)} %collective-permute-done.27.after, bf16[4,64,128]{2,1,0:T(8,128)(2,1)S(1)} %collective-permute-done.15.from_left, ...), custom_call_target="tpu_custom_call" | custom-call | flops 603979776 | bytes 4726784 | tf_op jit(solution)/shard_map/input_grad/pallas_call | solution.py:29
  113.3 0.8 unpack.1
  114.1 1.6 %join.1 = bf16[64,64,128]{2,1,0:T(8,128)(2,1)} custom-call(s32[1]{0:T(128)} %bitcast.place, bf16[32,64,128]{2,1,0:T(8,128)(2,1)S(1)} %get-tuple-element.89.keep, bf16[32,64,128]{2,1,0:T(8,128)(2,1)S(1)} %collective-permute-done.28.got, bf16[16,64,128]{2,1,0:T(8,128)(2,1)S(1)} %get-tuple-element.76.refs_0_, ...), custom_call_target="tpu_custom_call" | custom-call | bytes 3145732 | tf_op jit(solution)/shard_map/join/pallas_call | solution.py:29
  (29 shorter events, 0.2 us)
Async XLA Ops:
  0.6 1.2 %copy-start = (bf16[64,64,128]{2,1,0:T(8,128)(2,1)S(1)}, bf16[64,64,128]{2,1,0:T(8,128)(2,1)}, u32[]{:S(2)}) copy-start(bf16[64,64,128]{2,1,0:T(8,128)(2,1)} %cot.5) | copy-start | bytes 3145732
  1.9 1.2 %copy-start.2 = (bf16[64,64,128]{2,1,0:T(8,128)(2,1)S(1)}, bf16[64,64,128]{2,1,0:T(8,128)(2,1)}, u32[]{:S(2)}) copy-start(bf16[64,64,128]{2,1,0:T(8,128)(2,1)} %x.1) | copy-start | bytes 3145732
  3.1 51.0 %copy-start.1 = (bf16[64,64,128]{2,1,0:T(8,128)(2,1)S(1)}, bf16[64,64,128]{2,1,0:T(8,128)(2,1)}, u32[]{:S(2)}) copy-start(bf16[64,64,128]{2,1,0:T(8,128)(2,1)} %cot.5) | copy-start | bytes 3145732
  3.9 9.4 %collective-permute-start.1 = (bf16[4,64,128]{2,1,0:T(8,128)(2,1)S(1)}, bf16[4,64,128]{2,1,0:T(8,128)(2,1)S(1)}, u32[]{:S(2)}, u32[]{:S(2)}) collective-permute-start(bf16[4,64,128]{2,1,0:T(8,128)(2,1)S(1)} %get-tuple-element.52), channel_id=1, source_target_pairs={{1,0},{2,1},{3,2},{5,4},{6,5},{7,6},{9,8},{10,9},{11,10},{13,12},{... | collective-permute-start | bytes 196616 | tf_op jit(solution)/shard_map/ppermute | solution.py:72
  6.3 7.1 %collective-permute-start = (bf16[4,64,128]{2,1,0:T(8,128)(2,1)S(1)}, bf16[4,64,128]{2,1,0:T(8,128)(2,1)S(1)}, u32[]{:S(2)}, u32[]{:S(2)}) collective-permute-start(bf16[4,64,128]{2,1,0:T(8,128)(2,1)S(1)} %get-tuple-element.51), channel_id=1, source_target_pairs={{0,1},{1,2},{2,3},{4,5},{5,6},{6,7},{8,9},{9,10},{10,11},{12,13},{... | collective-permute-start | bytes 196616 | tf_op jit(solution)/shard_map/ppermute | solution.py:72
  9.8 10.4 %collective-permute-start.9 = (bf16[16,64,128]{2,1,0:T(8,128)(2,1)S(1)}, bf16[16,64,128]{2,1,0:T(8,128)(2,1)}, u32[]{:S(2)}, u32[]{:S(2)}) collective-permute-start(bf16[16,64,128]{2,1,0:T(8,128)(2,1)S(1)} %get-tuple-element.61), channel_id=1, source_target_pairs={{0,24},{4,28},{8,16},{12,20},{16,8},{20,12},{24,0},{28,4},{1,25},{... | collective-permute-start | bytes 786440 | tf_op jit(solution)/shard_map/ppermute | solution.py:303
  11.3 12.0 %collective-permute-start.5 = (bf16[16,64,128]{2,1,0:T(8,128)(2,1)S(1)}, bf16[16,64,128]{2,1,0:T(8,128)(2,1)}, u32[]{:S(2)}, u32[]{:S(2)}) collective-permute-start(bf16[16,64,128]{2,1,0:T(8,128)(2,1)S(1)} %get-tuple-element.57), channel_id=1, source_target_pairs={{0,8},{4,12},{8,0},{12,4},{16,24},{20,28},{24,16},{28,20},{1,9},{5... | collective-permute-start | bytes 786440 | tf_op jit(solution)/shard_map/ppermute | solution.py:303
  11.8 14.5 %collective-permute-start.7 = (bf16[16,64,128]{2,1,0:T(8,128)(2,1)S(1)}, bf16[16,64,128]{2,1,0:T(8,128)(2,1)}, u32[]{:S(2)}, u32[]{:S(2)}) collective-permute-start(bf16[16,64,128]{2,1,0:T(8,128)(2,1)S(1)} %get-tuple-element.59), channel_id=1, source_target_pairs={{0,16},{4,20},{8,24},{12,28},{16,0},{20,4},{24,8},{28,12},{1,17},{... | collective-permute-start | bytes 786440 | tf_op jit(solution)/shard_map/ppermute | solution.py:303
  13.4 23.5 %collective-permute-start.3 = (bf16[10,64,128]{2,1,0:T(8,128)(2,1)S(1)}, bf16[10,64,128]{2,1,0:T(8,128)(2,1)S(1)}, u32[]{:S(2)}, u32[]{:S(2)}) collective-permute-start(bf16[10,64,128]{2,1,0:T(8,128)(2,1)S(1)} %pad_maximum_fusion.1), channel_id=1, source_target_pairs={{4,0},{8,4},{12,8},{16,12},{20,16},{24,20},{28,24},{5,1},{9,5},{13... | collective-permute-start | bytes 491528 | tf_op jit(solution)/shard_map/ppermute | solution.py:72
  15.3 35.8 %collective-permute-start.4 = (bf16[16,64,128]{2,1,0:T(8,128)(2,1)}, bf16[16,64,128]{2,1,0:T(8,128)(2,1)S(1)}, u32[]{:S(2)}, u32[]{:S(2)}) collective-permute-start(bf16[16,64,128]{2,1,0:T(8,128)(2,1)} %get-tuple-element.56), channel_id=1, source_target_pairs={{0,0},{1,8},{2,16},{3,24},{4,4},{5,12},{6,20},{7,28},{8,1},{9,9},{... | collective-permute-start | bytes 786440 | tf_op jit(solution)/shard_map/ppermute | solution.py:313
  20.2 31.0 %collective-permute-start.10 = (bf16[16,64,128]{2,1,0:T(8,128)(2,1)}, bf16[16,64,128]{2,1,0:T(8,128)(2,1)S(1)}, u32[]{:S(2)}, u32[]{:S(2)}) collective-permute-start(bf16[16,64,128]{2,1,0:T(8,128)(2,1)} %collective-permute-done.9), channel_id=1, source_target_pairs={{0,3},{1,11},{2,19},{3,27},{4,7},{5,15},{6,23},{7,31},{8,2},{9,10}... | collective-permute-start | bytes 786440 | tf_op jit(solution)/shard_map/ppermute | solution.py:313
  23.3 27.9 %collective-permute-start.6 = (bf16[16,64,128]{2,1,0:T(8,128)(2,1)}, bf16[16,64,128]{2,1,0:T(8,128)(2,1)S(1)}, u32[]{:S(2)}, u32[]{:S(2)}) collective-permute-start(bf16[16,64,128]{2,1,0:T(8,128)(2,1)} %collective-permute-done.5), channel_id=1, source_target_pairs={{0,1},{1,9},{2,17},{3,25},{4,5},{5,13},{6,21},{7,29},{8,0},{9,8},{... | collective-permute-start | bytes 786440 | tf_op jit(solution)/shard_map/ppermute | solution.py:313
  26.4 24.8 %collective-permute-start.8 = (bf16[16,64,128]{2,1,0:T(8,128)(2,1)}, bf16[16,64,128]{2,1,0:T(8,128)(2,1)S(1)}, u32[]{:S(2)}, u32[]{:S(2)}) collective-permute-start(bf16[16,64,128]{2,1,0:T(8,128)(2,1)} %collective-permute-done.7), channel_id=1, source_target_pairs={{0,2},{1,10},{2,18},{3,26},{4,6},{5,14},{6,22},{7,30},{8,3},{9,11}... | collective-permute-start | bytes 786440 | tf_op jit(solution)/shard_map/ppermute | solution.py:313
  36.9 8.8 %collective-permute-start.2 = (bf16[10,64,128]{2,1,0:T(8,128)(2,1)}, bf16[10,64,128]{2,1,0:T(8,128)(2,1)}, u32[]{:S(2)}, u32[]{:S(2)}) collective-permute-start(bf16[10,64,128]{2,1,0:T(8,128)(2,1)} %pad_maximum_fusion), channel_id=1, source_target_pairs={{0,4},{4,8},{8,12},{12,16},{16,20},{20,24},{24,28},{1,5},{5,9},{9,... | collective-permute-start | bytes 491528 | tf_op jit(solution)/shard_map/ppermute | solution.py:72
  45.7 0.9 copy-start.3
  52.1 2.0 %collective-permute-start.11 = (bf16[32,64,128]{2,1,0:T(8,128)(2,1)S(1)}, bf16[32,64,128]{2,1,0:T(8,128)(2,1)S(1)}, u32[]{:S(2)}, u32[]{:S(2)}) collective-permute-start(bf16[32,64,128]{2,1,0:T(8,128)(2,1)S(1)} %get-tuple-element.69), channel_id=1, source_target_pairs={{0,4},{4,0},{8,12},{12,8},{16,20},{20,16},{24,28},{28,24},{1,5},{5... | collective-permute-start | bytes 1572872 | tf_op jit(solution)/shard_map/ppermute | solution.py:323
  56.2 7.3 %collective-permute-start.15 = (bf16[4,64,128]{2,1,0:T(8,128)(2,1)S(1)}, bf16[4,64,128]{2,1,0:T(8,128)(2,1)S(1)}, u32[]{:S(2)}, u32[]{:S(2)}) collective-permute-start(bf16[4,64,128]{2,1,0:T(8,128)(2,1)S(1)} %get-tuple-element.74), channel_id=1, source_target_pairs={{0,1},{1,2},{2,3},{4,5},{5,6},{6,7},{8,9},{9,10},{10,11},{12,13},{... | collective-permute-start | bytes 196616 | tf_op jit(solution)/shard_map/ppermute | solution.py:72
  58.1 21.8 %collective-permute-start.22 = (bf16[16,64,128]{2,1,0:T(8,128)(2,1)S(1)}, bf16[16,64,128]{2,1,0:T(8,128)(2,1)S(1)}, u32[]{:S(2)}, u32[]{:S(2)}) collective-permute-start(bf16[16,64,128]{2,1,0:T(8,128)(2,1)S(1)} %get-tuple-element.81.refs_3_), channel_id=1, source_target_pairs={{0,24},{4,28},{8,16},{12,20},{16,8},{20,12},{24,0},{28,4},{1,25},{... | collective-permute-start | bytes 786440 | tf_op jit(solution)/shard_map/ppermute | solution.py:303
  60.2 19.8 %collective-permute-start.20 = (bf16[16,64,128]{2,1,0:T(8,128)(2,1)S(1)}, bf16[16,64,128]{2,1,0:T(8,128)(2,1)S(1)}, u32[]{:S(2)}, u32[]{:S(2)}) collective-permute-start(bf16[16,64,128]{2,1,0:T(8,128)(2,1)S(1)} %get-tuple-element.79.refs_2_), channel_id=1, source_target_pairs={{0,16},{4,20},{8,24},{12,28},{16,0},{20,4},{24,8},{28,12},{1,17},{... | collective-permute-start | bytes 786440 | tf_op jit(solution)/shard_map/ppermute | solution.py:303
  60.2 23.5 %collective-permute-start.18 = (bf16[16,64,128]{2,1,0:T(8,128)(2,1)S(1)}, bf16[16,64,128]{2,1,0:T(8,128)(2,1)S(1)}, u32[]{:S(2)}, u32[]{:S(2)}) collective-permute-start(bf16[16,64,128]{2,1,0:T(8,128)(2,1)S(1)} %get-tuple-element.77.refs_1_), channel_id=1, source_target_pairs={{0,8},{4,12},{8,0},{12,4},{16,24},{20,28},{24,16},{28,20},{1,9},{5... | collective-permute-start | bytes 786440 | tf_op jit(solution)/shard_map/ppermute | solution.py:303
  61.6 48.1 %copy-start.4 = (bf16[3,3,64,64]{3,2,1,0:T(8,128)(2,1)S(1)}, bf16[3,3,64,64]{3,2,1,0:T(8,128)(2,1)}, u32[]{:S(2)}) copy-start(bf16[3,3,64,64]{3,2,1,0:T(8,128)(2,1)} %weight.3) | copy-start | bytes 221188
  63.5 3.9 %collective-permute-start.12 = (f32[160,128]{1,0:T(8,128)S(1)}, f32[160,128]{1,0:T(8,128)S(1)}, u32[]{:S(2)}, u32[]{:S(2)}) collective-permute-start(f32[160,128]{1,0:T(8,128)S(1)} %get-tuple-element.73), channel_id=1, source_target_pairs={{0,4},{4,0},{8,12},{12,8},{16,20},{20,16},{24,28},{28,24},{1,5},{5... | collective-permute-start | bytes 245768 | tf_op jit(solution)/shard_map/ppermute | solution.py:323
  63.5 7.3 %collective-permute-start.16 = (bf16[4,64,128]{2,1,0:T(8,128)(2,1)S(1)}, bf16[4,64,128]{2,1,0:T(8,128)(2,1)S(1)}, u32[]{:S(2)}, u32[]{:S(2)}) collective-permute-start(bf16[4,64,128]{2,1,0:T(8,128)(2,1)S(1)} %get-tuple-element.75), channel_id=1, source_target_pairs={{1,0},{2,1},{3,2},{5,4},{6,5},{7,6},{9,8},{10,9},{11,10},{13,12},{... | collective-permute-start | bytes 196616 | tf_op jit(solution)/shard_map/ppermute | solution.py:72
  67.5 4.6 %collective-permute-start.13 = (f32[160,128]{1,0:T(8,128)S(1)}, f32[160,128]{1,0:T(8,128)S(1)}, u32[]{:S(2)}, u32[]{:S(2)}) collective-permute-start(f32[160,128]{1,0:T(8,128)S(1)} %add.20), channel_id=1, source_target_pairs={{0,1},{1,0},{2,3},{3,2},{4,5},{5,4},{6,7},{7,6},{8,9},{9,8},{10,11... | collective-permute-start | bytes 245768 | tf_op jit(solution)/shard_map/ppermute | solution.py:342
  72.1 5.7 %collective-permute-start.14 = (f32[160,128]{1,0:T(8,128)S(1)}, f32[160,128]{1,0:T(8,128)S(1)}, u32[]{:S(2)}, u32[]{:S(2)}) collective-permute-start(f32[160,128]{1,0:T(8,128)S(1)} %add.21), channel_id=1, source_target_pairs={{0,2},{1,3},{2,0},{3,1},{4,6},{5,7},{6,4},{7,5},{8,10},{9,11},{10,... | collective-permute-start | bytes 245768 | tf_op jit(solution)/shard_map/ppermute | solution.py:342
  74.3 15.6 %collective-permute-start.27 = (bf16[10,64,128]{2,1,0:T(8,128)(2,1)S(1)}, bf16[10,64,128]{2,1,0:T(8,128)(2,1)S(1)}, u32[]{:S(2)}, u32[]{:S(2)}) collective-permute-start(bf16[10,64,128]{2,1,0:T(8,128)(2,1)S(1)} %pad_maximum_fusion.3), channel_id=1, source_target_pairs={{4,0},{8,4},{12,8},{16,12},{20,16},{24,20},{28,24},{5,1},{9,5},{13... | collective-permute-start | bytes 491528 | tf_op jit(solution)/shard_map/ppermute | solution.py:72
  77.8 9.0 %collective-permute-start.24 = (f32[160,128]{1,0:T(8,128)S(1)}, f32[160,128]{1,0:T(8,128)S(1)}, u32[]{:S(2)}, u32[]{:S(2)}) collective-permute-start(f32[160,128]{1,0:T(8,128)S(1)} %add.22), channel_id=1, source_target_pairs={{0,8},{4,12},{8,0},{12,4},{16,24},{20,28},{24,16},{28,20},{1,9},{5... | collective-permute-start | bytes 245768 | tf_op jit(solution)/shard_map/ppermute | solution.py:342
  79.9 22.7 %collective-permute-start.23 = (bf16[16,64,128]{2,1,0:T(8,128)(2,1)S(1)}, bf16[16,64,128]{2,1,0:T(8,128)(2,1)S(1)}, u32[]{:S(2)}, u32[]{:S(2)}) collective-permute-start(bf16[16,64,128]{2,1,0:T(8,128)(2,1)S(1)} %collective-permute-done.22), channel_id=1, source_target_pairs={{0,3},{1,11},{2,19},{3,27},{4,7},{5,15},{6,23},{7,31},{8,2},{9,10}... | collective-permute-start | bytes 786440 | tf_op jit(solution)/shard_map/ppermute | solution.py:313
  80.0 26.3 %collective-permute-start.21 = (bf16[16,64,128]{2,1,0:T(8,128)(2,1)S(1)}, bf16[16,64,128]{2,1,0:T(8,128)(2,1)S(1)}, u32[]{:S(2)}, u32[]{:S(2)}) collective-permute-start(bf16[16,64,128]{2,1,0:T(8,128)(2,1)S(1)} %collective-permute-done.20), channel_id=1, source_target_pairs={{0,2},{1,10},{2,18},{3,26},{4,6},{5,14},{6,22},{7,30},{8,3},{9,11}... | collective-permute-start | bytes 786440 | tf_op jit(solution)/shard_map/ppermute | solution.py:313
  83.6 22.7 %collective-permute-start.19 = (bf16[16,64,128]{2,1,0:T(8,128)(2,1)S(1)}, bf16[16,64,128]{2,1,0:T(8,128)(2,1)S(1)}, u32[]{:S(2)}, u32[]{:S(2)}) collective-permute-start(bf16[16,64,128]{2,1,0:T(8,128)(2,1)S(1)} %collective-permute-done.18), channel_id=1, source_target_pairs={{0,1},{1,9},{2,17},{3,25},{4,5},{5,13},{6,21},{7,29},{8,0},{9,8},{... | collective-permute-start | bytes 786440 | tf_op jit(solution)/shard_map/ppermute | solution.py:313
  86.8 20.8 %collective-permute-start.17 = (bf16[16,64,128]{2,1,0:T(8,128)(2,1)S(1)}, bf16[16,64,128]{2,1,0:T(8,128)(2,1)S(1)}, u32[]{:S(2)}, u32[]{:S(2)}) collective-permute-start(bf16[16,64,128]{2,1,0:T(8,128)(2,1)S(1)} %get-tuple-element.76.refs_0_), channel_id=1, source_target_pairs={{0,0},{1,8},{2,16},{3,24},{4,4},{5,12},{6,20},{7,28},{8,1},{9,9},{... | collective-permute-start | bytes 786440 | tf_op jit(solution)/shard_map/ppermute | solution.py:313
  89.9 4.5 %collective-permute-start.25 = (f32[160,128]{1,0:T(8,128)S(1)}, f32[160,128]{1,0:T(8,128)S(1)}, u32[]{:S(2)}, u32[]{:S(2)}) collective-permute-start(f32[160,128]{1,0:T(8,128)S(1)} %add.23), channel_id=1, source_target_pairs={{0,16},{4,20},{8,24},{12,28},{16,0},{20,4},{24,8},{28,12},{1,17},{... | collective-permute-start | bytes 245768 | tf_op jit(solution)/shard_map/ppermute | solution.py:342
  94.4 8.1 %collective-permute-start.26 = (bf16[10,64,128]{2,1,0:T(8,128)(2,1)S(1)}, bf16[10,64,128]{2,1,0:T(8,128)(2,1)S(1)}, u32[]{:S(2)}, u32[]{:S(2)}) collective-permute-start(bf16[10,64,128]{2,1,0:T(8,128)(2,1)S(1)} %pad_maximum_fusion.2), channel_id=1, source_target_pairs={{0,4},{4,8},{8,12},{12,16},{16,20},{20,24},{24,28},{1,5},{5,9},{9,... | collective-permute-start | bytes 491528 | tf_op jit(solution)/shard_map/ppermute | solution.py:72
  108.5 5.7 %collective-permute-start.28 = (bf16[32,64,128]{2,1,0:T(8,128)(2,1)S(1)}, bf16[32,64,128]{2,1,0:T(8,128)(2,1)S(1)}, u32[]{:S(2)}, u32[]{:S(2)}) collective-permute-start(bf16[32,64,128]{2,1,0:T(8,128)(2,1)S(1)} %get-tuple-element.90), channel_id=1, source_target_pairs={{0,4},{4,0},{8,12},{12,8},{16,20},{20,16},{24,28},{28,24},{1,5},{5... | collective-permute-start | bytes 1572872 | tf_op jit(solution)/shard_map/ppermute | solution.py:323
  109.7 3.6 %collective-permute-start.29 = (f32[160,128]{1,0:T(8,128)S(1)}, f32[160,128]{1,0:T(8,128)S(1)}, u32[]{:S(2)}, u32[]{:S(2)}) collective-permute-start(f32[160,128]{1,0:T(8,128)S(1)} %add.24.mine), channel_id=1, source_target_pairs={{0,4},{4,0},{8,12},{12,8},{16,20},{20,16},{24,28},{28,24},{1,5},{5... | collective-permute-start | bytes 245768 | tf_op jit(solution)/shard_map/ppermute | solution.py:323

commit v4 on v3

--- a/solution.py
+++ b/solution.py
@@ -49,13 +49,27 @@
     return jnp.concatenate(picked, axis=1)
 
 
-def write_edges(tile, top_ref, bottom_ref, left_ref, right_ref):
+def write_pair(parity, start, end, first, second):
+    first[...] = jnp.where(parity == 0, end, start)
+    second[...] = jnp.where(parity == 0, start, end)
+
+
+def picked(parity, first, second):
+    return jnp.where(parity == 0, second, first), jnp.where(parity == 0, first, second)
+
+
+def write_edges(row_odd, col_odd, tile, top_ref, bottom_ref, first_ref, second_ref):
     tile_rows, _, tile_cols = tile.shape
     span = tile_cols // STEP
     for group in range(tile_rows // span):
         rows = [tile[group * span + k] for k in range(span)]
-        left_ref[group] = columns_of(rows, True)
-        right_ref[group] = columns_of(rows, False)
+        write_pair(
+            col_odd[0],
+            columns_of(rows, True),
+            columns_of(rows, False),
+            first_ref.at[group],
+            second_ref.at[group],
+        )
     for k in range(STEP):
         top_ref[k] = tile[k]
         bottom_ref[k] = tile[tile_rows - STEP + k]
@@ -67,42 +81,40 @@
     return [rows, rows, strips, strips]
 
 
-def shift(x, axis, forward):
-    pairs = [(i, i + 1) for i in range(lax.axis_size(axis) - 1)]
-    return lax.ppermute(x, axis, pairs if forward else [(j, i) for i, j in pairs])
-
-
-def columns_first(top, bottom, left, right):
-    from_left, from_right = shift(right, "col", True), shift(left, "col", False)
-    last = left.shape[0] - 1
-    down = jnp.concatenate([top, from_left[:1], from_right[:1]])
-    up = jnp.concatenate([bottom, from_left[last:], from_right[last:]])
-    return shift(up, "row", True), shift(down, "row", False), from_left, from_right
-
-
-def corner_kernel(before, after, left, right, left_out, right_out):
-    groups = left.shape[0]
-    rows = [edge[k] for edge in (before, after) for k in range(STEP)]
-    for first, strips, out in ((True, left, left_out), (False, right, right_out)):
-        out[:groups] = strips[...]
-        out[groups] = columns_of(rows, first)
-
-
-def rows_first(top, bottom, left, right):
-    before, after = shift(bottom, "row", True), shift(top, "row", False)
-    whole = shape((left.shape[0] + 1,) + left.shape[1:], BF16)
-    left, right = call(
-        corner_kernel, [whole, whole], before, after, left, right, name="corners"
-    )
-    from_right, from_left = shift(left, "col", False), shift(right, "col", True)
-    return before, after, from_left, from_right
-
-
-def write_shifted(tile, before, after, from_left, from_right, stack):
+def exchanged(first, second, axis):
+    size = lax.axis_size(axis)
+    pairs = [[(i, i + 1) for i in range(k, size - 1, 2)] for k in range(2)]
+    return [
+        lax.ppermute(x, axis, pair + [(j, i) for i, j in pair])
+        for x, pair in zip((first, second), pairs)
+    ]
+
+
+def message_kernel(row_odd, col_odd, top, bottom, first, second, row_first, row_second):
+    last = first.shape[0] - 1
+    write_pair(row_odd[0], top[...], bottom[...], row_first.at[:STEP], row_second.at[:STEP])
+    starts = picked(col_odd[0], first[0], second[0])
+    ends = picked(col_odd[0], first[last], second[last])
+    for k in range(2):
+        write_pair(
+            row_odd[0], starts[k], ends[k], row_first.at[STEP + k], row_second.at[STEP + k]
+        )
+
+
+def halo_of(place, top, bottom, first, second):
+    strips = exchanged(first, second, "col")
+    message = shape((STEP + 2,) + top.shape[1:], BF16)
+    rows = call(
+        message_kernel, [message, message], *place, top, bottom, *strips, name="messages"
+    )
+    return *exchanged(*rows, "row"), *strips
+
+
+def write_shifted(row_odd, col_odd, tile, row_first, row_second, col_first, col_second, stack):
     tile_rows, channels, tile_cols = tile.shape
     span = tile_cols // STEP
-    groups = tile_rows // span
-    rows_carry_corners = before.shape[0] > STEP
+    before, after = picked(row_odd[0], row_first[...], row_second[...])
+    from_left, from_right = picked(col_odd[0], col_first[...], col_second[...])
     for row in range(tile_rows + 2 * STEP):
         own = row - STEP
         if 0 <= own < tile_rows:
@@ -110,13 +122,8 @@
             left, right = from_left[own // span], from_right[own // span]
         else:
             edge, k = (before, row) if own < 0 else (after, own - tile_rows)
-            middle = edge[k]
-            if rows_carry_corners:
-                left, right = edge[STEP], edge[STEP + 1]
-                lane = STEP * (k + span - STEP if own < 0 else k)
-            else:
-                left, right = from_left[groups], from_right[groups]
-                lane = STEP * (k if own < 0 else k + STEP)
+            middle, left, right = edge[k], edge[STEP], edge[STEP + 1]
+            lane = STEP * (k + span - STEP if own < 0 else k)
         left, right = left[:, lane : lane + STEP], right[:, lane : lane + STEP]
         stack[row, :channels] = jnp.concatenate([left, middle[:, :-STEP]], axis=1)
         stack[row, channels : 2 * channels] = middle
@@ -155,7 +162,7 @@
                 emit(out_row + 1, total[:, cols:])
 
 
-def open_kernel(cot, x, tile, top, bottom, left, right, *rest):
+def open_kernel(row_odd, col_odd, cot, x, tile, top, bottom, first, second, *rest):
     pieces, done = rest[:-1], rest[-1]
     group = pieces[0].shape[0]
     copies = [
@@ -167,19 +174,17 @@
     rows = x.shape[1]
     for a in range(0, rows, 16):
         tile[a : a + 16] = jnp.swapaxes(x[:, a : a + 16], 0, 1)
-    write_edges(tile, top, bottom, left, right)
+    write_edges(row_odd, col_odd, tile, top, bottom, first, second)
     for copy in copies:
         copy.wait()
 
 
-def forward_kernel(
-    tile, before, after, from_left, from_right, weight, bias, token, stack, slope, *refs
-):
-    pieces, kept = refs[:-1], refs[-1]
+def forward_kernel(row_odd, col_odd, tile, *refs):
+    halo, (weight, bias, token, stack, slope, *pieces, kept) = refs[:4], refs[4:]
     token[...] = jnp.zeros_like(token)
     group = pieces[0].shape[0]
     tile_rows = tile.shape[0]
-    write_shifted(tile, before, after, from_left, from_right, stack)
+    write_shifted(row_odd, col_odd, tile, *halo, stack)
     offset = bias[...]
 
     def emit(row, total):
@@ -196,18 +201,20 @@
             piece[:, a : a + 16] = mixed[j * group : (j + 1) * group]
 
 
-def grad_pre_kernel(place, cot, keep, got, slope, token, tile, top, bottom, left, right, mirrored):
+def grad_pre_kernel(
+    row_odd, col_odd, cot, keep, got, slope, token, tile, top, bottom, first, second, mirrored
+):
     token[...] = jnp.zeros_like(token)
     rows = cot.shape[1]
     for a in range(0, rows, 16):
-        turned = joined(place[0], keep[:, a : a + 16], got[:, a : a + 16])
+        turned = joined(row_odd[0], keep[:, a : a + 16], got[:, a : a + 16])
         mirrored[:, a : a + 16] = turned.astype(BF16)
         grad_mixed = cot[:, a : a + 16].astype(F32) + turned
         tile[a : a + 16] = (jnp.swapaxes(grad_mixed, 0, 1) * slope[a : a + 16]).astype(BF16)
-    write_edges(tile, top, bottom, left, right)
-
-
-def weight_kernel(side, place, grad, stack, token, keep, give, packed):
+    write_edges(row_odd, col_odd, tile, top, bottom, first, second)
+
+
+def weight_kernel(side, row_odd, grad, stack, token, keep, give, packed):
     token[...] = jnp.zeros_like(token)
     tile_rows, channels, cols = grad.shape
     nothing = jnp.zeros((channels, cols), BF16)
@@ -237,14 +244,14 @@
         at = k // 2 * channels
         packed[at : at + channels] = jnp.concatenate(blocks[k : k + 2], axis=1) * (1.0 / side)
     half = keep.shape[0]
-    keep[...] = packed[pl.ds(place[0] * half, half)]
-    give[...] = packed[pl.ds((1 - place[0]) * half, half)]
-
-
-def unpack_kernel(place, mine, other, weight, bias, packed):
+    keep[...] = packed[pl.ds(row_odd[0] * half, half)]
+    give[...] = packed[pl.ds((1 - row_odd[0]) * half, half)]
+
+
+def unpack_kernel(row_odd, mine, other, weight, bias, packed):
     half, channels = mine.shape[0], weight.shape[2]
-    packed[pl.ds(place[0] * half, half)] = mine[...]
-    packed[pl.ds((1 - place[0]) * half, half)] = other[...]
+    packed[pl.ds(row_odd[0] * half, half)] = mine[...]
+    packed[pl.ds((1 - row_odd[0]) * half, half)] = other[...]
     for k in range(9):
         row, col = k // 2 * channels, k % 2 * channels
         weight[k // 3, k % 3] = packed[row : row + channels, col : col + channels]
@@ -254,11 +261,11 @@
     bias[...] = jnp.sum(jnp.where(line == lane, last, 0.0), axis=0, keepdims=True)
 
 
-def input_grad_kernel(
-    tile, before, after, from_left, from_right, weight, cot, mirrored, out, stack, kept
-):
+def input_grad_kernel(row_odd, col_odd, tile, *refs):
+    halo, (weight, cot, mirrored, token, out, stack, kept) = refs[:4], refs[4:]
+    token[...] = jnp.zeros_like(token)
     tile_rows = tile.shape[0]
-    write_shifted(tile, before, after, from_left, from_right, stack)
+    write_shifted(row_odd, col_odd, tile, *halo, stack)
 
     def emit(row, total):
         kept[row] = total
@@ -269,10 +276,10 @@
         out[:, a : a + 16] = (grad_mixed + jnp.swapaxes(kept[a : a + 16], 0, 1)).astype(BF16)
 
 
-def turn_kernel(place, *refs):
-    pieces, (keep, give) = refs[:-2], refs[-2:]
+def turn_kernel(unread, row_odd, *refs):
+    pieces, (keep, give) = refs[unread:-2], refs[-2:]
     tile_rows = pieces[0].shape[1]
-    core = place[0]
+    core = row_odd[0]
     group, near = pieces[0].shape[0], len(pieces) // 2
     for j in range(near):
         for c in range(group):
@@ -313,10 +320,11 @@
     return lax.ppermute(piece, ("row", "col"), owners)
 
 
-def turn(pieces, place):
+def turn(pieces, place, *after):
     group, tile_rows, tile_cols = pieces[0].shape
     half = shape((group * len(pieces) // 2, tile_rows, tile_cols), BF16)
-    return call(turn_kernel, [half, half], place, *pieces, name="turn")
+    kernel = functools.partial(turn_kernel, len(after))
+    return call(kernel, [half, half], place[0], *after, *pieces, name="turn")
 
 
 def swapped(give):
@@ -327,11 +335,11 @@
     return lax.optimization_barrier((pieces, until))[0]
 
 
-def join_kernel(place, keep, got, *refs):
+def join_kernel(row_odd, keep, got, *refs):
     pieces, out = refs[:-1], refs[-1]
     for a in range(0, out.shape[1], 16):
         rows = slice(a, a + 16)
-        turned = joined(place[0], keep[:, rows], got[:, rows])
+        turned = joined(row_odd[0], keep[:, rows], got[:, rows])
         own = jnp.concatenate([piece[:, rows] for piece in pieces], axis=0)
         out[:, rows] = (own.astype(F32) + turned).astype(BF16)
 
@@ -352,26 +360,28 @@
     stack_dims = (tile_rows + 2 * STEP, 3 * channels, tile_cols)
     conv_flops = 2 * 9 * channels * channels * tile_rows * tile_cols
     rounds = lax.axis_size("col")
-    place = jnp.full((1,), lax.axis_index("row") % 2, jnp.int32)
+    place = [jnp.full((1,), lax.axis_index(axis) % 2, jnp.int32) for axis in ("row", "col")]
     piece = shape((channels // rounds, tile_rows, tile_cols), BF16)
 
     tile, *opened = call(
         open_kernel,
         [tile_shape] + edges + [piece] * rounds,
+        *place,
         cotangent,
         pair_feature_map,
         scratch=[pltpu.SemaphoreType.DMA((rounds,))],
-        in_hbm=[0],
+        in_hbm=[2],
         out_hbm=rounds,
         name="open",
     )
     token = shape((8, 128), F32)
-    halo = columns_first(*opened[:4])
     dealt = [detour(p, j) for j, p in enumerate(opened[4:])]
+    halo = halo_of(place, *opened[:4])
     forwarded, stack, slope, *mixed = call(
         forward_kernel,
         [token, shape(stack_dims, BF16), shape((tile_rows, channels, tile_cols), F32)]
         + [piece] * rounds,
+        *place,
         tile,
         *halo,
         conv_weight,
@@ -386,7 +396,7 @@
     ready, grad, *edge, mirrored = call(
         grad_pre_kernel,
         [token, tile_shape] + edges + [shape(cotangent.shape, BF16)],
-        place,
+        *place,
         cotangent,
         keep,
         swapped(give),
@@ -398,30 +408,21 @@
     weighed, *terms = call(
         functools.partial(weight_kernel, side),
         [token, half, half],
-        place,
+        place[0],
         grad,
         stack,
         scratch=[packed],
         flops=conv_flops,
         name="weight_terms",
     )
-    halo = columns_first(*edge)
     part = summed(terms[0] + swapped(terms[1]), "col", 1)
-    mixed_arrived = [cross(held(p, part, *halo[2:]), j) for j, p in enumerate(mixed_dealt)]
-    part = summed(part, "row", 2)
-    mixed_keep, mixed_give = turn(held(mixed_arrived, part, *halo[:2]), place)
-    symmetric = call(
-        join_kernel,
-        shape(pair_feature_map.shape, BF16),
-        place,
-        mixed_keep,
-        swapped(mixed_give),
-        *mixed,
-        name="join",
-    )
-    grad_input = call(
+    across = summed(part, "row", 2)
+    halo = halo_of(place, *edge)
+    mixed_arrived = [cross(held(p, part), j) for j, p in enumerate(mixed_dealt)]
+    ended, grad_input = call(
         input_grad_kernel,
-        shape(pair_feature_map.shape, BF16),
+        [token, shape(pair_feature_map.shape, BF16)],
+        *place,
         grad,
         *halo,
         conv_weight,
@@ -437,11 +438,21 @@
     grad_weight, grad_bias = call(
         unpack_kernel,
         [shape((3, 3, channels, channels), F32), shape((1, channels), F32)],
-        place,
-        part,
-        swapped(part),
+        place[0],
+        across,
+        swapped(across),
         scratch=[packed],
         name="unpack",
+    )
+    mixed_keep, mixed_give = turn(held(mixed_arrived, across, *halo[:2]), place)
+    symmetric = call(
+        join_kernel,
+        shape(pair_feature_map.shape, BF16),
+        place[0],
+        mixed_keep,
+        swapped(mixed_give),
+        *mixed,
+        name="join",
     )
     return symmetric, grad_input, grad_weight, grad_bias.reshape(channels)
 

time: 118 us -> 107 us (0.907)
  starting transfers between devices: 60.1 us -> 37.7 us
  waiting for transfers between devices: 32.7 us -> 44.5 us
    ppermute x8, waiting for transfers between devices: 15.4 us -> 30.6 us  [exchanged(): lax.ppermute(x, axis, pair + [(j, i) for i, j in pair])]
    ppermute x8, starting transfers between devices: 27.3 us -> 16.2 us  [cross(): return lax.ppermute(piece, ('row', 'col'), owners)]
    ppermute x8, starting transfers between devices: 19.7 us -> 11.4 us  [exchanged(): lax.ppermute(x, axis, pair + [(j, i) for i, j in pair])]
    ppermute x4, starting transfers between devices: 4.61 us -> 2.25 us  [summed(): lax.ppermute(part, axis, [(i, i ^ reach) for i in range(size)])]
    ppermute x6, waiting for transfers between devices: 2.14 us -> 0.02 us  [detour(): lax.ppermute(piece, 'row', [(r, r ^ 2 * far) for r in range(lax.axis_size...]
    ppermute x8, waiting for transfers between devices: 5 us -> 3.43 us  [cross(): return lax.ppermute(piece, ('row', 'col'), owners)]
    pallas_call x9 -> x11, Pallas kernels: 17.1 us -> 17.9 us  [call(): pl.pallas_call(kernel, out_shape=out_shape, in_specs=in_specs, out_specs=...]
where the time goes in v4:
time: 107 us; the launch traced here: 105 us
  waiting for transfers between devices  44.5 us (42%)
  starting transfers between devices  37.7 us (35%)
  Pallas kernels  17.9 us (17%)
  local copies, waits for them, and re-layouts  4.11 us (4%)
    ppermute x8, waiting for transfers between devices, exchanged(): lax.ppermute(x, axis, pair + [(j, i) for i, j in pair])  30.6 us
    pallas_call x11, Pallas kernels, call(): pl.pallas_call(kernel, out_shape=out_shape, in_specs=in_specs, out_specs=...  17.9 us
    ppermute x8, starting transfers between devices, cross(): return lax.ppermute(piece, ('row', 'col'), owners)  16.2 us
    ppermute x8, starting transfers between devices, exchanged(): lax.ppermute(x, axis, pair + [(j, i) for i, j in pair])  11.4 us
    ppermute x4, waiting for transfers between devices, summed(): lax.ppermute(part, axis, [(i, i ^ reach) for i in range(size)])  7.5 us
    ppermute x6, starting transfers between devices, detour(): lax.ppermute(piece, 'row', [(r, r ^ 2 * far) for r in range(lax.axis_size...  7.04 us
    ppermute x8, waiting for transfers between devices, cross(): return lax.ppermute(piece, ('row', 'col'), owners)  3.43 us
    unnamed x10, local copies, waits for them, and re-layouts  3.36 us
  transfers between devices with their start and end apart: 30, of which 12 were waited for; matrix products, arithmetic and copies ran while one was open for 1% of the time, Pallas kernels for 9%

profile of v4, /device:TPU:12, one launch (start us, length us, event | category | flops | bytes accessed | tf_op | source)
XLA Modules:
  0.0 105.2 jit_solution(12171677661406961134)
XLA Ops:
  0.7 1.2 %copy-done = bf16[64,64,128]{2,1,0:T(8,128)(2,1)S(1)} copy-done((bf16[64,64,128]{2,1,0:T(8,128)(2,1)S(1)}, bf16[64,64,128]{2,1,0:T(8,128)(2,1)}, u32[]{:S(2)}) %copy-start) | copy-done | bytes 1048600
  1.9 1.2 %copy-done.2 = bf16[64,64,128]{2,1,0:T(8,128)(2,1)S(1)} copy-done((bf16[64,64,128]{2,1,0:T(8,128)(2,1)S(1)}, bf16[64,64,128]{2,1,0:T(8,128)(2,1)}, u32[]{:S(2)}) %copy-start.2) | copy-done | bytes 1048600
  3.1 0.9 open.1
  4.0 1.5 %collective-permute-start.9 = (bf16[16,64,128]{2,1,0:T(8,128)(2,1)S(1)}, bf16[16,64,128]{2,1,0:T(8,128)(2,1)}, u32[]{:S(2)}, u32[]{:S(2)}) collective-permute-start(bf16[16,64,128]{2,1,0:T(8,128)(2,1)S(1)} %get-tuple-element.68), channel_id=1, source_target_pairs={{0,24},{4,28},{8,16},{12,20},{16,8},{20,12},{24,0},{28,4},{1,25},{... | collective-permute-start | bytes 786440 | tf_op jit(solution)/shard_map/ppermute | solution.py:310
  5.5 0.5 collective-permute-start.5
  6.0 1.5 %collective-permute-start.7 = (bf16[16,64,128]{2,1,0:T(8,128)(2,1)S(1)}, bf16[16,64,128]{2,1,0:T(8,128)(2,1)}, u32[]{:S(2)}, u32[]{:S(2)}) collective-permute-start(bf16[16,64,128]{2,1,0:T(8,128)(2,1)S(1)} %get-tuple-element.66), channel_id=1, source_target_pairs={{0,16},{4,20},{8,24},{12,28},{16,0},{20,4},{24,8},{28,12},{1,17},{... | collective-permute-start | bytes 786440 | tf_op jit(solution)/shard_map/ppermute | solution.py:310
  7.6 0.4 collective-permute-start
  8.0 4.6 %collective-permute-start.1 = (bf16[4,64,128]{2,1,0:T(8,128)(2,1)S(1)}, bf16[4,64,128]{2,1,0:T(8,128)(2,1)S(1)}, u32[]{:S(2)}, u32[]{:S(2)}) collective-permute-start(bf16[4,64,128]{2,1,0:T(8,128)(2,1)S(1)} %get-tuple-element.58), channel_id=1, source_target_pairs={{1,2},{2,1},{5,6},{6,5},{9,10},{10,9},{13,14},{14,13},{17,18},{18,... | collective-permute-start | bytes 196616 | tf_op jit(solution)/shard_map/ppermute | solution.py:88
  12.6 0.0 collective-permute-done.first.refs_2_
  12.6 2.2 %collective-permute-done.1.second.refs_3_ = bf16[4,64,128]{2,1,0:T(8,128)(2,1)S(1)} collective-permute-done((bf16[4,64,128]{2,1,0:T(8,128)(2,1)S(1)}, bf16[4,64,128]{2,1,0:T(8,128)(2,1)S(1)}, u32[]{:S(2)}, u32[]{:S(2)}) %collective-permute-start.1) | collective-permute-done | bytes 65568 | tf_op jit(solution)/shard_map/ppermute | solution.py:88
  14.8 0.7 messages.2
  15.6 4.8 %collective-permute-start.4 = (bf16[16,64,128]{2,1,0:T(8,128)(2,1)}, bf16[16,64,128]{2,1,0:T(8,128)(2,1)S(1)}, u32[]{:S(2)}, u32[]{:S(2)}) collective-permute-start(bf16[16,64,128]{2,1,0:T(8,128)(2,1)} %get-tuple-element.63), channel_id=1, source_target_pairs={{0,0},{1,8},{2,16},{3,24},{4,4},{5,12},{6,20},{7,28},{8,1},{9,9},{... | collective-permute-start | bytes 786440 | tf_op jit(solution)/shard_map/ppermute | solution.py:320
  20.4 0.0 collective-permute-done.9
  20.4 0.1 collective-permute-start.10
  20.4 0.0 collective-permute-done.5
  20.4 2.4 %collective-permute-start.6 = (bf16[16,64,128]{2,1,0:T(8,128)(2,1)}, bf16[16,64,128]{2,1,0:T(8,128)(2,1)S(1)}, u32[]{:S(2)}, u32[]{:S(2)}) collective-permute-start(bf16[16,64,128]{2,1,0:T(8,128)(2,1)} %collective-permute-done.5), channel_id=1, source_target_pairs={{0,1},{1,9},{2,17},{3,25},{4,5},{5,13},{6,21},{7,29},{8,0},{9,8},{... | collective-permute-start | bytes 786440 | tf_op jit(solution)/shard_map/ppermute | solution.py:320
  22.9 0.0 collective-permute-done.7
  22.9 2.1 %collective-permute-start.3 = (bf16[10,64,128]{2,1,0:T(8,128)(2,1)}, bf16[10,64,128]{2,1,0:T(8,128)(2,1)}, u32[]{:S(2)}, u32[]{:S(2)}) collective-permute-start(bf16[10,64,128]{2,1,0:T(8,128)(2,1)} %get-tuple-element.60), channel_id=1, source_target_pairs={{4,8},{12,16},{20,24},{8,4},{16,12},{24,20},{5,9},{13,17},{21,25},... | collective-permute-start | bytes 491528 | tf_op jit(solution)/shard_map/ppermute | solution.py:88
  24.9 0.7 copy.8.refs_5_
  25.7 10.8 %collective-permute-done.3.refs_1_ = bf16[10,64,128]{2,1,0:T(8,128)(2,1)} collective-permute-done((bf16[10,64,128]{2,1,0:T(8,128)(2,1)}, bf16[10,64,128]{2,1,0:T(8,128)(2,1)}, u32[]{:S(2)}, u32[]{:S(2)}) %collective-permute-start.3) | collective-permute-done | bytes 163872 | tf_op jit(solution)/shard_map/ppermute | solution.py:88
  36.5 0.9 copy-done.3
  37.4 4.5 %forward.1 = (f32[8,128]{1,0:T(8,128)}, bf16[80,192,128]{2,1,0:T(8,128)(2,1)S(1)}, f32[64,64,128]{2,1,0:T(8,128)S(1)}, bf16[16,64,128]{2,1,0:T(8,128)(2,1)S(1)},...) custom-call(s32[1]{0:T(128)} %bitcast.row_odd, ...), custom_call_target="tpu_custom_call" | custom-call | flops 603979776 | bytes 8663304 | tf_op jit(solution)/shard_map/forward/pallas_call | solution.py:29
  41.9 0.0 collective-permute-done.10.refs_3_
  41.9 1.9 %collective-permute-done.6.refs_1_ = bf16[16,64,128]{2,1,0:T(8,128)(2,1)S(1)} collective-permute-done((bf16[16,64,128]{2,1,0:T(8,128)(2,1)}, bf16[16,64,128]{2,1,0:T(8,128)(2,1)S(1)}, u32[]{:S(2)}, u32[]{:S(2)}) %collective-permute-start.6) | collective-permute-done | bytes 262176 | tf_op jit(solution)/shard_map/ppermute | solution.py:320
  43.8 1.5 %collective-permute-done.8.refs_2_ = bf16[16,64,128]{2,1,0:T(8,128)(2,1)S(1)} collective-permute-done((bf16[16,64,128]{2,1,0:T(8,128)(2,1)}, bf16[16,64,128]{2,1,0:T(8,128)(2,1)S(1)}, u32[]{:S(2)}, u32[]{:S(2)}) %collective-permute-start.8) | collective-permute-done | bytes 262176 | tf_op jit(solution)/shard_map/ppermute | solution.py:320
  45.3 0.9 turn.2
  46.3 0.1 collective-permute-start.11
  46.4 1.9 %collective-permute-done.11.got = bf16[32,64,128]{2,1,0:T(8,128)(2,1)S(1)} collective-permute-done((bf16[32,64,128]{2,1,0:T(8,128)(2,1)S(1)}, bf16[32,64,128]{2,1,0:T(8,128)(2,1)S(1)}, u32[]{:S(2)}, u32[]{:S(2)}) %collective-permute-start.11) | collective-permute-done | bytes 524320 | tf_op jit(solution)/shard_map/ppermute | solution.py:331
  48.2 2.1 %grad_pre.1 = (f32[8,128]{1,0:T(8,128)}, bf16[64,64,128]{2,1,0:T(8,128)(2,1)S(1)}, bf16[8,64,128]{2,1,0:T(8,128)(2,1)S(1)}, bf16[8,64,128]{2,1,0:T(8,128)(2,1)S(...) custom-call(s32[1]{0:T(128)} %bitcast.row_odd, ...), custom_call_target="tpu_custom_call" | custom-call | bytes 6688776 | tf_op jit(solution)/shard_map/grad_pre/pallas_call | solution.py:29
  50.3 1.8 %weight_terms.1 = (f32[8,128]{1,0:T(8,128)}, f32[160,128]{1,0:T(8,128)S(1)}, f32[160,128]{1,0:T(8,128)S(1)}) custom-call(s32[1]{0:T(128)} %bitcast.row_odd, bf16[64,64,128]{2,1,0:T(8,128)(2,1)S(1)} %get-tuple-element.77.grad.tile, bf16[80,192,128]{2,1,0:T(8,128)(2,1)S(1)} %get-tuple-element.78.stack), custom_call_target="tpu_custom_call" | custom-call | flops 603979776 | bytes 5148676 | tf_op jit(solution)/shard_map/weight_terms/pallas_call | solution.py:29
  52.2 0.1 collective-permute-start.12
  52.3 1.1 %collective-permute-done.12 = f32[160,128]{1,0:T(8,128)S(1)} collective-permute-done((f32[160,128]{1,0:T(8,128)S(1)}, f32[160,128]{1,0:T(8,128)S(1)}, u32[]{:S(2)}, u32[]{:S(2)}) %collective-permute-start.12) | collective-permute-done | bytes 81952 | tf_op jit(solution)/shard_map/ppermute | solution.py:331
  53.4 2.1 %collective-permute-start.13 = (f32[160,128]{1,0:T(8,128)S(1)}, f32[160,128]{1,0:T(8,128)S(1)}, u32[]{:S(2)}, u32[]{:S(2)}) collective-permute-start(f32[160,128]{1,0:T(8,128)S(1)} %add.24), channel_id=1, source_target_pairs={{0,1},{1,0},{2,3},{3,2},{4,5},{5,4},{6,7},{7,6},{8,9},{9,8},{10,11... | collective-permute-start | bytes 245768 | tf_op jit(solution)/shard_map/ppermute | solution.py:350
  55.6 0.0 collective-permute-start.20
  55.6 0.0 collective-permute-start.18
  55.6 3.5 %collective-permute-start.16 = (bf16[16,64,128]{2,1,0:T(8,128)(2,1)S(1)}, bf16[16,64,128]{2,1,0:T(8,128)(2,1)S(1)}, u32[]{:S(2)}, u32[]{:S(2)}) collective-permute-start(bf16[16,64,128]{2,1,0:T(8,128)(2,1)S(1)} %get-tuple-element.82.refs_1_), channel_id=1, source_target_pairs={{0,8},{4,12},{8,0},{12,4},{16,24},{20,28},{24,16},{28,20},{1,9},{5... | collective-permute-start | bytes 786440 | tf_op jit(solution)/shard_map/ppermute | solution.py:310
  59.0 0.1 collective-permute-start.24
  59.1 2.0 %collective-permute-start.25 = (bf16[4,64,128]{2,1,0:T(8,128)(2,1)S(1)}, bf16[4,64,128]{2,1,0:T(8,128)(2,1)S(1)}, u32[]{:S(2)}, u32[]{:S(2)}) collective-permute-start(bf16[4,64,128]{2,1,0:T(8,128)(2,1)S(1)} %get-tuple-element.91), channel_id=1, source_target_pairs={{1,2},{2,1},{5,6},{6,5},{9,10},{10,9},{13,14},{14,13},{17,18},{18,... | collective-permute-start | bytes 196616 | tf_op jit(solution)/shard_map/ppermute | solution.py:88
  61.2 2.1 %collective-permute-done.24.first.refs_2_ = bf16[4,64,128]{2,1,0:T(8,128)(2,1)S(1)} collective-permute-done((bf16[4,64,128]{2,1,0:T(8,128)(2,1)S(1)}, bf16[4,64,128]{2,1,0:T(8,128)(2,1)S(1)}, u32[]{:S(2)}, u32[]{:S(2)}) %collective-permute-start.24) | collective-permute-done | bytes 65568 | tf_op jit(solution)/shard_map/ppermute | solution.py:88
  63.3 0.0 collective-permute-start.14
  63.3 3.0 %collective-permute-done.25.second.refs_3_ = bf16[4,64,128]{2,1,0:T(8,128)(2,1)S(1)} collective-permute-done((bf16[4,64,128]{2,1,0:T(8,128)(2,1)S(1)}, bf16[4,64,128]{2,1,0:T(8,128)(2,1)S(1)}, u32[]{:S(2)}, u32[]{:S(2)}) %collective-permute-start.25) | collective-permute-done | bytes 65568 | tf_op jit(solution)/shard_map/ppermute | solution.py:88
  66.3 0.1 messages.3
  66.4 0.1 collective-permute-start.26
  66.5 2.2 %collective-permute-done.14 = f32[160,128]{1,0:T(8,128)S(1)} collective-permute-done((f32[160,128]{1,0:T(8,128)S(1)}, f32[160,128]{1,0:T(8,128)S(1)}, u32[]{:S(2)}, u32[]{:S(2)}) %collective-permute-start.14) | collective-permute-done | bytes 81952 | tf_op jit(solution)/shard_map/ppermute | solution.py:350
  68.7 0.1 collective-permute-start.22
  68.7 0.0 collective-permute-done.20
  68.8 1.4 %collective-permute-start.21 = (bf16[16,64,128]{2,1,0:T(8,128)(2,1)S(1)}, bf16[16,64,128]{2,1,0:T(8,128)(2,1)S(1)}, u32[]{:S(2)}, u32[]{:S(2)}) collective-permute-start(bf16[16,64,128]{2,1,0:T(8,128)(2,1)S(1)} %collective-permute-done.20), channel_id=1, source_target_pairs={{0,3},{1,11},{2,19},{3,27},{4,7},{5,15},{6,23},{7,31},{8,2},{9,10}... | collective-permute-start | bytes 786440 | tf_op jit(solution)/shard_map/ppermute | solution.py:320
  70.2 3.6 %collective-permute-start.19 = (bf16[16,64,128]{2,1,0:T(8,128)(2,1)S(1)}, bf16[16,64,128]{2,1,0:T(8,128)(2,1)S(1)}, u32[]{:S(2)}, u32[]{:S(2)}) collective-permute-start(bf16[16,64,128]{2,1,0:T(8,128)(2,1)S(1)} %collective-permute-done.18), channel_id=1, source_target_pairs={{0,2},{1,10},{2,18},{3,26},{4,6},{5,14},{6,22},{7,30},{8,3},{9,11}... | collective-permute-start | bytes 786440 | tf_op jit(solution)/shard_map/ppermute | solution.py:320
  73.8 0.0 collective-permute-done.16
  73.8 0.3 collective-permute-start.17
  74.1 0.9 collective-permute-done.22
  75.0 3.6 %collective-permute-start.15 = (bf16[16,64,128]{2,1,0:T(8,128)(2,1)S(1)}, bf16[16,64,128]{2,1,0:T(8,128)(2,1)S(1)}, u32[]{:S(2)}, u32[]{:S(2)}) collective-permute-start(bf16[16,64,128]{2,1,0:T(8,128)(2,1)S(1)} %get-tuple-element.81.refs_0_), channel_id=1, source_target_pairs={{0,0},{1,8},{2,16},{3,24},{4,4},{5,12},{6,20},{7,28},{8,1},{9,9},{... | collective-permute-start | bytes 786440 | tf_op jit(solution)/shard_map/ppermute | solution.py:320
  78.7 0.1 collective-permute-start.23
  78.8 4.4 %collective-permute-done.23 = f32[160,128]{1,0:T(8,128)S(1)} collective-permute-done((f32[160,128]{1,0:T(8,128)S(1)}, f32[160,128]{1,0:T(8,128)S(1)}, u32[]{:S(2)}, u32[]{:S(2)}) %collective-permute-start.23) | collective-permute-done | bytes 81952 | tf_op jit(solution)/shard_map/ppermute | solution.py:350
  83.2 2.1 %collective-permute-start.27 = (bf16[10,64,128]{2,1,0:T(8,128)(2,1)S(1)}, bf16[10,64,128]{2,1,0:T(8,128)(2,1)S(1)}, u32[]{:S(2)}, u32[]{:S(2)}) collective-permute-start(bf16[10,64,128]{2,1,0:T(8,128)(2,1)S(1)} %get-tuple-element.93), channel_id=1, source_target_pairs={{4,8},{12,16},{20,24},{8,4},{16,12},{24,20},{5,9},{13,17},{21,25},... | collective-permute-start | bytes 491528 | tf_op jit(solution)/shard_map/ppermute | solution.py:88
  85.3 12.4 %collective-permute-done.27.refs_1_ = bf16[10,64,128]{2,1,0:T(8,128)(2,1)S(1)} collective-permute-done((bf16[10,64,128]{2,1,0:T(8,128)(2,1)S(1)}, bf16[10,64,128]{2,1,0:T(8,128)(2,1)S(1)}, u32[]{:S(2)}, u32[]{:S(2)}) %collective-permute-start.27) | collective-permute-done | bytes 163872 | tf_op jit(solution)/shard_map/ppermute | solution.py:88
  97.7 0.0 collective-permute-done.21.refs_3_
  97.7 0.0 collective-permute-done.19.refs_2_
  97.7 0.9 turn.3
  98.6 0.1 collective-permute-start.28
  98.7 0.5 collective-permute-start.29
  99.2 3.6 %input_grad.1 = (f32[8,128]{1,0:T(8,128)}, bf16[64,64,128]{2,1,0:T(8,128)(2,1)}) custom-call(s32[1]{0:T(128)} %bitcast.row_odd, s32[1]{0:T(128)} %bitcast.1.col_odd, bf16[64,64,128]{2,1,0:T(8,128)(2,1)S(1)} %get-tuple-element.77.grad.tile, bf16[10,64,128]{2,1,0:T(8,128)(2,1)S(1)} %collective-permute-done.26.refs_0_, ...), custom_call_target="tpu_custom_call" | custom-call | flops 603979776 | bytes 4730888 | tf_op jit(solution)/shard_map/input_grad/pallas_call | solution.py:29
  102.8 0.8 unpack.1
  103.6 1.6 %join.1 = bf16[64,64,128]{2,1,0:T(8,128)(2,1)} custom-call(s32[1]{0:T(128)} %bitcast.row_odd, bf16[32,64,128]{2,1,0:T(8,128)(2,1)S(1)} %get-tuple-element.98.keep, bf16[32,64,128]{2,1,0:T(8,128)(2,1)S(1)} %collective-permute-done.28.got, bf16[16,64,128]{2,1,0:T(8,128)(2,1)S(1)} %get-tuple-element.81.refs_0_, ...), custom_call_target="tpu_custom_call" | custom-call | bytes 3145732 | tf_op jit(solution)/shard_map/join/pallas_call | solution.py:29
  (23 shorter events, 0.1 us)
Async XLA Ops:
  0.6 1.2 %copy-start = (bf16[64,64,128]{2,1,0:T(8,128)(2,1)S(1)}, bf16[64,64,128]{2,1,0:T(8,128)(2,1)}, u32[]{:S(2)}) copy-start(bf16[64,64,128]{2,1,0:T(8,128)(2,1)} %refs_5_.1) | copy-start | bytes 3145732
  1.9 1.2 %copy-start.2 = (bf16[64,64,128]{2,1,0:T(8,128)(2,1)S(1)}, bf16[64,64,128]{2,1,0:T(8,128)(2,1)}, u32[]{:S(2)}) copy-start(bf16[64,64,128]{2,1,0:T(8,128)(2,1)} %x.1) | copy-start | bytes 3145732
  3.1 45.1 %copy-start.1 = (bf16[64,64,128]{2,1,0:T(8,128)(2,1)S(1)}, bf16[64,64,128]{2,1,0:T(8,128)(2,1)}, u32[]{:S(2)}) copy-start(bf16[64,64,128]{2,1,0:T(8,128)(2,1)} %refs_5_.1) | copy-start | bytes 3145732
  4.0 16.4 %collective-permute-start.9 = (bf16[16,64,128]{2,1,0:T(8,128)(2,1)S(1)}, bf16[16,64,128]{2,1,0:T(8,128)(2,1)}, u32[]{:S(2)}, u32[]{:S(2)}) collective-permute-start(bf16[16,64,128]{2,1,0:T(8,128)(2,1)S(1)} %get-tuple-element.68), channel_id=1, source_target_pairs={{0,24},{4,28},{8,16},{12,20},{16,8},{20,12},{24,0},{28,4},{1,25},{... | collective-permute-start | bytes 786440 | tf_op jit(solution)/shard_map/ppermute | solution.py:310
  5.5 14.9 %collective-permute-start.5 = (bf16[16,64,128]{2,1,0:T(8,128)(2,1)S(1)}, bf16[16,64,128]{2,1,0:T(8,128)(2,1)}, u32[]{:S(2)}, u32[]{:S(2)}) collective-permute-start(bf16[16,64,128]{2,1,0:T(8,128)(2,1)S(1)} %get-tuple-element.64), channel_id=1, source_target_pairs={{0,8},{4,12},{8,0},{12,4},{16,24},{20,28},{24,16},{28,20},{1,9},{5... | collective-permute-start | bytes 786440 | tf_op jit(solution)/shard_map/ppermute | solution.py:310
  6.0 16.8 %collective-permute-start.7 = (bf16[16,64,128]{2,1,0:T(8,128)(2,1)S(1)}, bf16[16,64,128]{2,1,0:T(8,128)(2,1)}, u32[]{:S(2)}, u32[]{:S(2)}) collective-permute-start(bf16[16,64,128]{2,1,0:T(8,128)(2,1)S(1)} %get-tuple-element.66), channel_id=1, source_target_pairs={{0,16},{4,20},{8,24},{12,28},{16,0},{20,4},{24,8},{28,12},{1,17},{... | collective-permute-start | bytes 786440 | tf_op jit(solution)/shard_map/ppermute | solution.py:310
  7.6 5.1 %collective-permute-start = (bf16[4,64,128]{2,1,0:T(8,128)(2,1)S(1)}, bf16[4,64,128]{2,1,0:T(8,128)(2,1)S(1)}, u32[]{:S(2)}, u32[]{:S(2)}) collective-permute-start(bf16[4,64,128]{2,1,0:T(8,128)(2,1)S(1)} %get-tuple-element.57), channel_id=1, source_target_pairs={{0,1},{2,3},{1,0},{3,2},{4,5},{6,7},{5,4},{7,6},{8,9},{10,11},{9,8... | collective-permute-start | bytes 196616 | tf_op jit(solution)/shard_map/ppermute | solution.py:88
  8.0 6.8 %collective-permute-start.1 = (bf16[4,64,128]{2,1,0:T(8,128)(2,1)S(1)}, bf16[4,64,128]{2,1,0:T(8,128)(2,1)S(1)}, u32[]{:S(2)}, u32[]{:S(2)}) collective-permute-start(bf16[4,64,128]{2,1,0:T(8,128)(2,1)S(1)} %get-tuple-element.58), channel_id=1, source_target_pairs={{1,2},{2,1},{5,6},{6,5},{9,10},{10,9},{13,14},{14,13},{17,18},{18,... | collective-permute-start | bytes 196616 | tf_op jit(solution)/shard_map/ppermute | solution.py:88
  15.6 7.3 %collective-permute-start.2 = (bf16[10,64,128]{2,1,0:T(8,128)(2,1)S(1)}, bf16[10,64,128]{2,1,0:T(8,128)(2,1)S(1)}, u32[]{:S(2)}, u32[]{:S(2)}) collective-permute-start(bf16[10,64,128]{2,1,0:T(8,128)(2,1)S(1)} %get-tuple-element.59), channel_id=1, source_target_pairs={{0,4},{8,12},{16,20},{24,28},{4,0},{12,8},{20,16},{28,24},{1,5},{9... | collective-permute-start | bytes 491528 | tf_op jit(solution)/shard_map/ppermute | solution.py:88
  15.6 26.4 %collective-permute-start.4 = (bf16[16,64,128]{2,1,0:T(8,128)(2,1)}, bf16[16,64,128]{2,1,0:T(8,128)(2,1)S(1)}, u32[]{:S(2)}, u32[]{:S(2)}) collective-permute-start(bf16[16,64,128]{2,1,0:T(8,128)(2,1)} %get-tuple-element.63), channel_id=1, source_target_pairs={{0,0},{1,8},{2,16},{3,24},{4,4},{5,12},{6,20},{7,28},{8,1},{9,9},{... | collective-permute-start | bytes 786440 | tf_op jit(solution)/shard_map/ppermute | solution.py:320
  20.4 21.6 %collective-permute-start.10 = (bf16[16,64,128]{2,1,0:T(8,128)(2,1)}, bf16[16,64,128]{2,1,0:T(8,128)(2,1)S(1)}, u32[]{:S(2)}, u32[]{:S(2)}) collective-permute-start(bf16[16,64,128]{2,1,0:T(8,128)(2,1)} %collective-permute-done.9), channel_id=1, source_target_pairs={{0,3},{1,11},{2,19},{3,27},{4,7},{5,15},{6,23},{7,31},{8,2},{9,10}... | collective-permute-start | bytes 786440 | tf_op jit(solution)/shard_map/ppermute | solution.py:320
  20.4 23.4 %collective-permute-start.6 = (bf16[16,64,128]{2,1,0:T(8,128)(2,1)}, bf16[16,64,128]{2,1,0:T(8,128)(2,1)S(1)}, u32[]{:S(2)}, u32[]{:S(2)}) collective-permute-start(bf16[16,64,128]{2,1,0:T(8,128)(2,1)} %collective-permute-done.5), channel_id=1, source_target_pairs={{0,1},{1,9},{2,17},{3,25},{4,5},{5,13},{6,21},{7,29},{8,0},{9,8},{... | collective-permute-start | bytes 786440 | tf_op jit(solution)/shard_map/ppermute | solution.py:320
  22.9 22.5 %collective-permute-start.8 = (bf16[16,64,128]{2,1,0:T(8,128)(2,1)}, bf16[16,64,128]{2,1,0:T(8,128)(2,1)S(1)}, u32[]{:S(2)}, u32[]{:S(2)}) collective-permute-start(bf16[16,64,128]{2,1,0:T(8,128)(2,1)} %collective-permute-done.7), channel_id=1, source_target_pairs={{0,2},{1,10},{2,18},{3,26},{4,6},{5,14},{6,22},{7,30},{8,3},{9,11}... | collective-permute-start | bytes 786440 | tf_op jit(solution)/shard_map/ppermute | solution.py:320
  22.9 13.6 %collective-permute-start.3 = (bf16[10,64,128]{2,1,0:T(8,128)(2,1)}, bf16[10,64,128]{2,1,0:T(8,128)(2,1)}, u32[]{:S(2)}, u32[]{:S(2)}) collective-permute-start(bf16[10,64,128]{2,1,0:T(8,128)(2,1)} %get-tuple-element.60), channel_id=1, source_target_pairs={{4,8},{12,16},{20,24},{8,4},{16,12},{24,20},{5,9},{13,17},{21,25},... | collective-permute-start | bytes 491528 | tf_op jit(solution)/shard_map/ppermute | solution.py:88
  36.5 0.9 copy-start.3
  46.3 2.0 %collective-permute-start.11 = (bf16[32,64,128]{2,1,0:T(8,128)(2,1)S(1)}, bf16[32,64,128]{2,1,0:T(8,128)(2,1)S(1)}, u32[]{:S(2)}, u32[]{:S(2)}) collective-permute-start(bf16[32,64,128]{2,1,0:T(8,128)(2,1)S(1)} %get-tuple-element.76), channel_id=1, source_target_pairs={{0,4},{4,0},{8,12},{12,8},{16,20},{20,16},{24,28},{28,24},{1,5},{5... | collective-permute-start | bytes 1572872 | tf_op jit(solution)/shard_map/ppermute | solution.py:331
  50.3 48.9 %copy-start.4 = (bf16[3,3,64,64]{3,2,1,0:T(8,128)(2,1)S(1)}, bf16[3,3,64,64]{3,2,1,0:T(8,128)(2,1)}, u32[]{:S(2)}) copy-start(bf16[3,3,64,64]{3,2,1,0:T(8,128)(2,1)} %refs_4_.3) | copy-start | bytes 221188
  52.2 1.3 %collective-permute-start.12 = (f32[160,128]{1,0:T(8,128)S(1)}, f32[160,128]{1,0:T(8,128)S(1)}, u32[]{:S(2)}, u32[]{:S(2)}) collective-permute-start(f32[160,128]{1,0:T(8,128)S(1)} %get-tuple-element.80), channel_id=1, source_target_pairs={{0,4},{4,0},{8,12},{12,8},{16,20},{20,16},{24,28},{28,24},{1,5},{5... | collective-permute-start | bytes 245768 | tf_op jit(solution)/shard_map/ppermute | solution.py:331
  53.4 5.7 %collective-permute-start.13 = (f32[160,128]{1,0:T(8,128)S(1)}, f32[160,128]{1,0:T(8,128)S(1)}, u32[]{:S(2)}, u32[]{:S(2)}) collective-permute-start(f32[160,128]{1,0:T(8,128)S(1)} %add.24), channel_id=1, source_target_pairs={{0,1},{1,0},{2,3},{3,2},{4,5},{5,4},{6,7},{7,6},{8,9},{9,8},{10,11... | collective-permute-start | bytes 245768 | tf_op jit(solution)/shard_map/ppermute | solution.py:350
  55.6 13.2 %collective-permute-start.20 = (bf16[16,64,128]{2,1,0:T(8,128)(2,1)S(1)}, bf16[16,64,128]{2,1,0:T(8,128)(2,1)S(1)}, u32[]{:S(2)}, u32[]{:S(2)}) collective-permute-start(bf16[16,64,128]{2,1,0:T(8,128)(2,1)S(1)} %get-tuple-element.86.refs_3_), channel_id=1, source_target_pairs={{0,24},{4,28},{8,16},{12,20},{16,8},{20,12},{24,0},{28,4},{1,25},{... | collective-permute-start | bytes 786440 | tf_op jit(solution)/shard_map/ppermute | solution.py:310
  55.6 14.6 %collective-permute-start.18 = (bf16[16,64,128]{2,1,0:T(8,128)(2,1)S(1)}, bf16[16,64,128]{2,1,0:T(8,128)(2,1)S(1)}, u32[]{:S(2)}, u32[]{:S(2)}) collective-permute-start(bf16[16,64,128]{2,1,0:T(8,128)(2,1)S(1)} %get-tuple-element.84.refs_2_), channel_id=1, source_target_pairs={{0,16},{4,20},{8,24},{12,28},{16,0},{20,4},{24,8},{28,12},{1,17},{... | collective-permute-start | bytes 786440 | tf_op jit(solution)/shard_map/ppermute | solution.py:310
  55.6 18.2 %collective-permute-start.16 = (bf16[16,64,128]{2,1,0:T(8,128)(2,1)S(1)}, bf16[16,64,128]{2,1,0:T(8,128)(2,1)S(1)}, u32[]{:S(2)}, u32[]{:S(2)}) collective-permute-start(bf16[16,64,128]{2,1,0:T(8,128)(2,1)S(1)} %get-tuple-element.82.refs_1_), channel_id=1, source_target_pairs={{0,8},{4,12},{8,0},{12,4},{16,24},{20,28},{24,16},{28,20},{1,9},{5... | collective-permute-start | bytes 786440 | tf_op jit(solution)/shard_map/ppermute | solution.py:310
  59.0 4.3 %collective-permute-start.24 = (bf16[4,64,128]{2,1,0:T(8,128)(2,1)S(1)}, bf16[4,64,128]{2,1,0:T(8,128)(2,1)S(1)}, u32[]{:S(2)}, u32[]{:S(2)}) collective-permute-start(bf16[4,64,128]{2,1,0:T(8,128)(2,1)S(1)} %get-tuple-element.90), channel_id=1, source_target_pairs={{0,1},{2,3},{1,0},{3,2},{4,5},{6,7},{5,4},{7,6},{8,9},{10,11},{9,8... | collective-permute-start | bytes 196616 | tf_op jit(solution)/shard_map/ppermute | solution.py:88
  59.1 7.2 %collective-permute-start.25 = (bf16[4,64,128]{2,1,0:T(8,128)(2,1)S(1)}, bf16[4,64,128]{2,1,0:T(8,128)(2,1)S(1)}, u32[]{:S(2)}, u32[]{:S(2)}) collective-permute-start(bf16[4,64,128]{2,1,0:T(8,128)(2,1)S(1)} %get-tuple-element.91), channel_id=1, source_target_pairs={{1,2},{2,1},{5,6},{6,5},{9,10},{10,9},{13,14},{14,13},{17,18},{18,... | collective-permute-start | bytes 196616 | tf_op jit(solution)/shard_map/ppermute | solution.py:88
  63.3 5.3 %collective-permute-start.14 = (f32[160,128]{1,0:T(8,128)S(1)}, f32[160,128]{1,0:T(8,128)S(1)}, u32[]{:S(2)}, u32[]{:S(2)}) collective-permute-start(f32[160,128]{1,0:T(8,128)S(1)} %add.25), channel_id=1, source_target_pairs={{0,2},{1,3},{2,0},{3,1},{4,6},{5,7},{6,4},{7,5},{8,10},{9,11},{10,... | collective-permute-start | bytes 245768 | tf_op jit(solution)/shard_map/ppermute | solution.py:350
  66.4 12.3 %collective-permute-start.26 = (bf16[10,64,128]{2,1,0:T(8,128)(2,1)S(1)}, bf16[10,64,128]{2,1,0:T(8,128)(2,1)S(1)}, u32[]{:S(2)}, u32[]{:S(2)}) collective-permute-start(bf16[10,64,128]{2,1,0:T(8,128)(2,1)S(1)} %get-tuple-element.92), channel_id=1, source_target_pairs={{0,4},{8,12},{16,20},{24,28},{4,0},{12,8},{20,16},{28,24},{1,5},{9... | collective-permute-start | bytes 491528 | tf_op jit(solution)/shard_map/ppermute | solution.py:88
  68.7 6.3 %collective-permute-start.22 = (f32[160,128]{1,0:T(8,128)S(1)}, f32[160,128]{1,0:T(8,128)S(1)}, u32[]{:S(2)}, u32[]{:S(2)}) collective-permute-start(f32[160,128]{1,0:T(8,128)S(1)} %add.26), channel_id=1, source_target_pairs={{0,8},{4,12},{8,0},{12,4},{16,24},{20,28},{24,16},{28,20},{1,9},{5... | collective-permute-start | bytes 245768 | tf_op jit(solution)/shard_map/ppermute | solution.py:350
  68.8 29.0 %collective-permute-start.21 = (bf16[16,64,128]{2,1,0:T(8,128)(2,1)S(1)}, bf16[16,64,128]{2,1,0:T(8,128)(2,1)S(1)}, u32[]{:S(2)}, u32[]{:S(2)}) collective-permute-start(bf16[16,64,128]{2,1,0:T(8,128)(2,1)S(1)} %collective-permute-done.20), channel_id=1, source_target_pairs={{0,3},{1,11},{2,19},{3,27},{4,7},{5,15},{6,23},{7,31},{8,2},{9,10}... | collective-permute-start | bytes 786440 | tf_op jit(solution)/shard_map/ppermute | solution.py:320
  70.2 27.5 %collective-permute-start.19 = (bf16[16,64,128]{2,1,0:T(8,128)(2,1)S(1)}, bf16[16,64,128]{2,1,0:T(8,128)(2,1)S(1)}, u32[]{:S(2)}, u32[]{:S(2)}) collective-permute-start(bf16[16,64,128]{2,1,0:T(8,128)(2,1)S(1)} %collective-permute-done.18), channel_id=1, source_target_pairs={{0,2},{1,10},{2,18},{3,26},{4,6},{5,14},{6,22},{7,30},{8,3},{9,11}... | collective-permute-start | bytes 786440 | tf_op jit(solution)/shard_map/ppermute | solution.py:320
  73.8 24.0 %collective-permute-start.17 = (bf16[16,64,128]{2,1,0:T(8,128)(2,1)S(1)}, bf16[16,64,128]{2,1,0:T(8,128)(2,1)S(1)}, u32[]{:S(2)}, u32[]{:S(2)}) collective-permute-start(bf16[16,64,128]{2,1,0:T(8,128)(2,1)S(1)} %collective-permute-done.16), channel_id=1, source_target_pairs={{0,1},{1,9},{2,17},{3,25},{4,5},{5,13},{6,21},{7,29},{8,0},{9,8},{... | collective-permute-start | bytes 786440 | tf_op jit(solution)/shard_map/ppermute | solution.py:320
  75.0 22.7 %collective-permute-start.15 = (bf16[16,64,128]{2,1,0:T(8,128)(2,1)S(1)}, bf16[16,64,128]{2,1,0:T(8,128)(2,1)S(1)}, u32[]{:S(2)}, u32[]{:S(2)}) collective-permute-start(bf16[16,64,128]{2,1,0:T(8,128)(2,1)S(1)} %get-tuple-element.81.refs_0_), channel_id=1, source_target_pairs={{0,0},{1,8},{2,16},{3,24},{4,4},{5,12},{6,20},{7,28},{8,1},{9,9},{... | collective-permute-start | bytes 786440 | tf_op jit(solution)/shard_map/ppermute | solution.py:320
  78.7 4.5 %collective-permute-start.23 = (f32[160,128]{1,0:T(8,128)S(1)}, f32[160,128]{1,0:T(8,128)S(1)}, u32[]{:S(2)}, u32[]{:S(2)}) collective-permute-start(f32[160,128]{1,0:T(8,128)S(1)} %add.27), channel_id=1, source_target_pairs={{0,16},{4,20},{8,24},{12,28},{16,0},{20,4},{24,8},{28,12},{1,17},{... | collective-permute-start | bytes 245768 | tf_op jit(solution)/shard_map/ppermute | solution.py:350
  83.2 14.5 %collective-permute-start.27 = (bf16[10,64,128]{2,1,0:T(8,128)(2,1)S(1)}, bf16[10,64,128]{2,1,0:T(8,128)(2,1)S(1)}, u32[]{:S(2)}, u32[]{:S(2)}) collective-permute-start(bf16[10,64,128]{2,1,0:T(8,128)(2,1)S(1)} %get-tuple-element.93), channel_id=1, source_target_pairs={{4,8},{12,16},{20,24},{8,4},{16,12},{24,20},{5,9},{13,17},{21,25},... | collective-permute-start | bytes 491528 | tf_op jit(solution)/shard_map/ppermute | solution.py:88
  98.6 5.0 %collective-permute-start.28 = (bf16[32,64,128]{2,1,0:T(8,128)(2,1)S(1)}, bf16[32,64,128]{2,1,0:T(8,128)(2,1)S(1)}, u32[]{:S(2)}, u32[]{:S(2)}) collective-permute-start(bf16[32,64,128]{2,1,0:T(8,128)(2,1)S(1)} %get-tuple-element.99), channel_id=1, source_target_pairs={{0,4},{4,0},{8,12},{12,8},{16,20},{20,16},{24,28},{28,24},{1,5},{5... | collective-permute-start | bytes 1572872 | tf_op jit(solution)/shard_map/ppermute | solution.py:331
  98.7 4.1 %collective-permute-start.29 = (f32[160,128]{1,0:T(8,128)S(1)}, f32[160,128]{1,0:T(8,128)S(1)}, u32[]{:S(2)}, u32[]{:S(2)}) collective-permute-start(f32[160,128]{1,0:T(8,128)S(1)} %add.28.mine), channel_id=1, source_target_pairs={{0,4},{4,0},{8,12},{12,8},{16,20},{20,16},{24,28},{28,24},{1,5},{5... | collective-permute-start | bytes 245768 | tf_op jit(solution)/shard_map/ppermute | solution.py:331

commit v5 on v4

--- a/solution.py
+++ b/solution.py
@@ -13,7 +13,9 @@
 VMEM_LIMIT = 24 * 1024 * 1024
 
 
-def call(kernel, out_shape, *args, scratch=(), flops=0, in_hbm=(), out_hbm=0, name=None):
+def call(
+    kernel, out_shape, *args, scratch=(), flops=0, in_hbm=(), out_hbm=0, aliases=None, name=None
+):
     out_bytes = sum(o.size * o.dtype.itemsize for o in jax.tree.leaves(out_shape))
     in_bytes = sum(a.size * a.dtype.itemsize for a in args)
     in_specs = [
@@ -32,6 +34,7 @@
         in_specs=in_specs,
         out_specs=out_specs,
         scratch_shapes=scratch,
+        input_output_aliases=aliases or {},
         name=name,
         compiler_params=pltpu.CompilerParams(vmem_limit_bytes=VMEM_LIMIT),
         cost_estimate=pl.CostEstimate(
@@ -81,13 +84,10 @@
     return [rows, rows, strips, strips]
 
 
-def exchanged(first, second, axis):
+def exchanged(x, axis, turn):
     size = lax.axis_size(axis)
-    pairs = [[(i, i + 1) for i in range(k, size - 1, 2)] for k in range(2)]
-    return [
-        lax.ppermute(x, axis, pair + [(j, i) for i, j in pair])
-        for x, pair in zip((first, second), pairs)
-    ]
+    pairs = [(i, i + 1) for i in range(turn, size - 1, 2)]
+    return lax.ppermute(x, axis, pairs + [(j, i) for i, j in pairs])
 
 
 def message_kernel(row_odd, col_odd, top, bottom, first, second, row_first, row_second):
@@ -101,33 +101,50 @@
         )
 
 
-def halo_of(place, top, bottom, first, second):
-    strips = exchanged(first, second, "col")
+def columns_of_halo(place, top, bottom, first, second):
+    strips = exchanged(first, "col", 0), exchanged(second, "col", 1)
     message = shape((STEP + 2,) + top.shape[1:], BF16)
     rows = call(
         message_kernel, [message, message], *place, top, bottom, *strips, name="messages"
     )
-    return *exchanged(*rows, "row"), *strips
+    return rows, strips
+
+
+def rows_of_halo(rows, *before_far):
+    near = exchanged(rows[0], "row", 0)
+    return near, exchanged(held(rows[1], near, *before_far), "row", 1)
+
+
+def shifted(left, middle, right, lane, out):
+    channels = middle.shape[0]
+    left, right = left[:, lane : lane + STEP], right[:, lane : lane + STEP]
+    out[:channels] = jnp.concatenate([left, middle[:, :-STEP]], axis=1)
+    out[channels : 2 * channels] = middle
+    out[2 * channels :] = jnp.concatenate([middle[:, STEP:], right], axis=1)
+
+
+def write_own(col_odd, tile, col_first, col_second, stack):
+    tile_rows, _, tile_cols = tile.shape
+    span = tile_cols // STEP
+    from_left, from_right = picked(col_odd[0], col_first[...], col_second[...])
+    for row in range(tile_rows):
+        group = row // span
+        lane = STEP * (row % span)
+        shifted(from_left[group], tile[row], from_right[group], lane, stack.at[STEP + row])
+
+
+def write_ends(row_odd, row_first, row_second, before, after):
+    span = row_first.shape[2] // STEP
+    ends = picked(row_odd[0], row_first[...], row_second[...])
+    for end, out, first in zip(ends, (before, after), (span - STEP, 0)):
+        for k in range(STEP):
+            shifted(end[STEP], end[k], end[STEP + 1], STEP * (first + k), out.at[k])
 
 
 def write_shifted(row_odd, col_odd, tile, row_first, row_second, col_first, col_second, stack):
-    tile_rows, channels, tile_cols = tile.shape
-    span = tile_cols // STEP
-    before, after = picked(row_odd[0], row_first[...], row_second[...])
-    from_left, from_right = picked(col_odd[0], col_first[...], col_second[...])
-    for row in range(tile_rows + 2 * STEP):
-        own = row - STEP
-        if 0 <= own < tile_rows:
-            middle, lane = tile[own], STEP * (own % span)
-            left, right = from_left[own // span], from_right[own // span]
-        else:
-            edge, k = (before, row) if own < 0 else (after, own - tile_rows)
-            middle, left, right = edge[k], edge[STEP], edge[STEP + 1]
-            lane = STEP * (k + span - STEP if own < 0 else k)
-        left, right = left[:, lane : lane + STEP], right[:, lane : lane + STEP]
-        stack[row, :channels] = jnp.concatenate([left, middle[:, :-STEP]], axis=1)
-        stack[row, channels : 2 * channels] = middle
-        stack[row, 2 * channels :] = jnp.concatenate([middle[:, STEP:], right], axis=1)
+    write_own(col_odd, tile, col_first, col_second, stack)
+    far = stack.shape[0] - STEP
+    write_ends(row_odd, row_first, row_second, stack.at[:STEP], stack.at[far:])
 
 
 def forward_taps(weight):
@@ -261,11 +278,13 @@
     bias[...] = jnp.sum(jnp.where(line == lane, last, 0.0), axis=0, keepdims=True)
 
 
-def input_grad_kernel(row_odd, col_odd, tile, *refs):
-    halo, (weight, cot, mirrored, token, out, stack, kept) = refs[:4], refs[4:]
+def input_grad_kernel(col_odd, tile, col_first, col_second, weight, cot, mirrored, *refs):
+    token, out, ends, stack, kept = refs
+    tile_rows = tile.shape[0]
     token[...] = jnp.zeros_like(token)
-    tile_rows = tile.shape[0]
-    write_shifted(row_odd, col_odd, tile, *halo, stack)
+    for at in (0, tile_rows + STEP):
+        stack[at : at + STEP] = jnp.zeros((STEP,) + stack.shape[1:], stack.dtype)
+    write_own(col_odd, tile, col_first, col_second, stack)
 
     def emit(row, total):
         kept[row] = total
@@ -273,7 +292,40 @@
     convolve(stack, backward_taps(weight), tile_rows, emit)
     for a in range(0, tile_rows, 16):
         grad_mixed = cot[:, a : a + 16].astype(F32) + mirrored[:, a : a + 16].astype(F32)
-        out[:, a : a + 16] = (grad_mixed + jnp.swapaxes(kept[a : a + 16], 0, 1)).astype(BF16)
+        total = grad_mixed + jnp.swapaxes(kept[a : a + 16], 0, 1)
+        if a == 0:
+            ends[0] = total
+        elif a == tile_rows - 16:
+            ends[1] = total
+        else:
+            out[:, a : a + 16] = total.astype(BF16)
+
+
+def input_grad_ends_kernel(row_odd, row_first, row_second, weight, ends, whole, out, *scratch):
+    before, after, added, rounded, done = scratch
+    channels, tile_rows = out.shape[:2]
+    taps = backward_taps(weight)
+    write_ends(row_odd, row_first, row_second, before, after)
+    added[...] = jnp.zeros_like(added)
+    for side, rows, tap, at in ((0, before, 0, 0), (1, after, 2, STEP)):
+        own = taps[tap * channels : (tap + 1) * channels]
+        for k in range(0, STEP, 2):
+            both = jnp.concatenate([rows[k], rows[k + 1]], axis=1)
+            total = jnp.dot(own, both, preferred_element_type=F32)
+            cols = total.shape[1] // 2
+            added[side, at + k] = total[:, :cols]
+            added[side, at + k + 1] = total[:, cols:]
+    copies = []
+    for side, a in ((0, 0), (1, tile_rows - 16)):
+        total = ends[side] + jnp.swapaxes(added[side], 0, 1)
+        rounded[side] = total.astype(BF16)
+        copy = pltpu.make_async_copy(
+            rounded.at[side], out.at[:, pl.ds(a, 16)], done.at[side]
+        )
+        copy.start()
+        copies.append(copy)
+    for copy in copies:
+        copy.wait()
 
 
 def turn_kernel(unread, row_odd, *refs):
@@ -291,17 +343,12 @@
 
 
 def joined(core, keep, got):
+    lower = lax.broadcasted_iota(jnp.int32, (1, 1, keep.shape[2]), 2) < keep.shape[2] // 2
     keep, got = keep.astype(F32), got.astype(F32)
-    lower = lax.broadcasted_iota(jnp.int32, (1, 1, keep.shape[2]), 2) < keep.shape[2] // 2
     first, second = jnp.where(core == 0, keep, got), jnp.where(core == 0, got, keep)
-    low = jnp.where(lower, first, swap_lanes(second))
-    high = jnp.where(lower, swap_lanes(first), second)
+    low = jnp.where(lower, first, pltpu.roll(second, keep.shape[2] // 2, 2))
+    high = jnp.where(lower, pltpu.roll(first, keep.shape[2] // 2, 2), second)
     return jnp.concatenate([low, high], axis=0)
-
-
-def swap_lanes(x):
-    half = x.shape[2] // 2
-    return jnp.concatenate([x[:, :, half:], x[:, :, :half]], axis=2)
 
 
 def detour(piece, far):
@@ -376,7 +423,8 @@
     )
     token = shape((8, 128), F32)
     dealt = [detour(p, j) for j, p in enumerate(opened[4:])]
-    halo = halo_of(place, *opened[:4])
+    rows, strips = columns_of_halo(place, *opened[:4])
+    halo = *rows_of_halo(rows), *strips
     forwarded, stack, slope, *mixed = call(
         forward_kernel,
         [token, shape(stack_dims, BF16), shape((tile_rows, channels, tile_cols), F32)]
@@ -415,16 +463,19 @@
         flops=conv_flops,
         name="weight_terms",
     )
-    part = summed(terms[0] + swapped(terms[1]), "col", 1)
+    part = held(terms[0] + swapped(terms[1]), mixed_dealt[1])
+    size = lax.axis_size("col")
+    part = part + lax.ppermute(part, "col", [(i, i ^ 1) for i in range(size)])
+    part = summed(held(part, mixed_dealt[2]), "col", 2)
     across = summed(part, "row", 2)
-    halo = halo_of(place, *edge)
+    rows, strips = columns_of_halo(place, *edge)
     mixed_arrived = [cross(held(p, part), j) for j, p in enumerate(mixed_dealt)]
-    ended, grad_input = call(
+    ended, grad_input, ends = call(
         input_grad_kernel,
-        [token, shape(pair_feature_map.shape, BF16)],
-        *place,
+        [token, shape(cotangent.shape, BF16), shape((2, channels, 16, tile_cols), F32)],
+        place[1],
         grad,
-        *halo,
+        *strips,
         conv_weight,
         cotangent,
         mirrored,
@@ -435,6 +486,28 @@
         flops=conv_flops,
         name="input_grad",
     )
+    halo = rows_of_halo(rows, ended)
+    strip = pltpu.VMEM((STEP, 3 * channels, tile_cols), BF16)
+    grad_input = call(
+        input_grad_ends_kernel,
+        shape(cotangent.shape, BF16),
+        place[0],
+        *halo,
+        conv_weight,
+        ends,
+        grad_input,
+        scratch=[
+            strip,
+            strip,
+            pltpu.VMEM((2, 16, channels, tile_cols), F32),
+            pltpu.VMEM((2, channels, 16, tile_cols), BF16),
+            pltpu.SemaphoreType.DMA((2,)),
+        ],
+        in_hbm=[5],
+        out_hbm=1,
+        aliases={5: 0},
+        name="input_grad_ends",
+    )
     grad_weight, grad_bias = call(
         unpack_kernel,
         [shape((3, 3, channels, channels), F32), shape((1, channels), F32)],
@@ -444,7 +517,7 @@
         scratch=[packed],
         name="unpack",
     )
-    mixed_keep, mixed_give = turn(held(mixed_arrived, across, *halo[:2]), place)
+    mixed_keep, mixed_give = turn(held(mixed_arrived, across, *halo), place, ended)
     symmetric = call(
         join_kernel,
         shape(pair_feature_map.shape, BF16),

time: 107 us -> 104 us (0.972)
  the two profiles are of different devices: /device:TPU:12 before, /device:TPU:29 now
where the time goes in v5:
time: 104 us
  starting transfers between devices  51 us (49%)
  waiting for transfers between devices  28.7 us (28%)
  Pallas kernels  19 us (18%)
  local copies, waits for them, and re-layouts  4.11 us (4%)
    pallas_call x12, Pallas kernels, call(): pl.pallas_call(kernel, out_shape=out_shape, in_specs=in_specs, out_specs=...  19 us
    ppermute x8, starting transfers between devices, exchanged(): return lax.ppermute(x, axis, pairs + [(j, i) for i, j in pairs])  16.1 us
    ppermute x4, starting transfers between devices, swapped(): lax.ppermute(give, 'row', [(r, r ^ 1) for r in range(lax.axis_size('row'))])  14.2 us
    ppermute x8, waiting for transfers between devices, exchanged(): return lax.ppermute(x, axis, pairs + [(j, i) for i, j in pairs])  11.7 us
    ppermute x8, starting transfers between devices, cross(): return lax.ppermute(piece, ('row', 'col'), owners)  11.6 us
    ppermute x3, waiting for transfers between devices, summed(): lax.ppermute(part, axis, [(i, i ^ reach) for i in range(size)])  7.96 us
    ppermute x8, waiting for transfers between devices, cross(): return lax.ppermute(piece, ('row', 'col'), owners)  6.13 us
    ppermute x6, starting transfers between devices, detour(): lax.ppermute(piece, 'row', [(r, r ^ 2 * far) for r in range(lax.axis_size...  5.03 us
  transfers between devices with their start and end apart: 30, of which 12 were waited for; matrix products, arithmetic and copies ran while one was open for 1% of the time, Pallas kernels for 14%

profile of v5, /device:TPU:29, one launch (start us, length us, event | category | flops | bytes accessed | tf_op | source)
XLA Modules:
  0.0 103.7 jit_solution(18297215280797377642)
XLA Ops:
  0.7 1.2 %copy-done = bf16[64,64,128]{2,1,0:T(8,128)(2,1)S(1)} copy-done((bf16[64,64,128]{2,1,0:T(8,128)(2,1)S(1)}, bf16[64,64,128]{2,1,0:T(8,128)(2,1)}, u32[]{:S(2)}) %copy-start) | copy-done | bytes 1048600
  1.9 1.2 %copy-done.2 = bf16[64,64,128]{2,1,0:T(8,128)(2,1)S(1)} copy-done((bf16[64,64,128]{2,1,0:T(8,128)(2,1)S(1)}, bf16[64,64,128]{2,1,0:T(8,128)(2,1)}, u32[]{:S(2)}) %copy-start.2) | copy-done | bytes 1048600
  3.1 0.9 open.1
  4.0 1.2 %collective-permute-start.7 = (bf16[16,64,128]{2,1,0:T(8,128)(2,1)S(1)}, bf16[16,64,128]{2,1,0:T(8,128)(2,1)}, u32[]{:S(2)}, u32[]{:S(2)}) collective-permute-start(bf16[16,64,128]{2,1,0:T(8,128)(2,1)S(1)} %get-tuple-element.68), channel_id=1, source_target_pairs={{0,24},{4,28},{8,16},{12,20},{16,8},{20,12},{24,0},{28,4},{1,25},{... | collective-permute-start | bytes 786440 | tf_op jit(solution)/shard_map/ppermute | solution.py:357
  5.2 1.2 %collective-permute-start.5 = (bf16[16,64,128]{2,1,0:T(8,128)(2,1)S(1)}, bf16[16,64,128]{2,1,0:T(8,128)(2,1)}, u32[]{:S(2)}, u32[]{:S(2)}) collective-permute-start(bf16[16,64,128]{2,1,0:T(8,128)(2,1)S(1)} %get-tuple-element.66), channel_id=1, source_target_pairs={{0,16},{4,20},{8,24},{12,28},{16,0},{20,4},{24,8},{28,12},{1,17},{... | collective-permute-start | bytes 786440 | tf_op jit(solution)/shard_map/ppermute | solution.py:357
  6.5 0.3 collective-permute-start.3
  6.7 0.2 collective-permute-start
  6.9 0.7 collective-permute-start.1
  7.5 2.7 %collective-permute-done.first.refs_2_ = bf16[4,64,128]{2,1,0:T(8,128)(2,1)S(1)} collective-permute-done((bf16[4,64,128]{2,1,0:T(8,128)(2,1)S(1)}, bf16[4,64,128]{2,1,0:T(8,128)(2,1)S(1)}, u32[]{:S(2)}, u32[]{:S(2)}) %collective-permute-start) | collective-permute-done | bytes 65568 | tf_op jit(solution)/shard_map/ppermute | solution.py:90
  10.2 0.7 messages.2
  11.0 2.3 %collective-permute-start.9 = (bf16[10,64,128]{2,1,0:T(8,128)(2,1)S(1)}, bf16[10,64,128]{2,1,0:T(8,128)(2,1)S(1)}, u32[]{:S(2)}, u32[]{:S(2)}) collective-permute-start(bf16[10,64,128]{2,1,0:T(8,128)(2,1)S(1)} %get-tuple-element.73), channel_id=1, source_target_pairs={{0,4},{8,12},{16,20},{24,28},{4,0},{12,8},{20,16},{28,24},{1,5},{9... | collective-permute-start | bytes 491528 | tf_op jit(solution)/shard_map/ppermute | solution.py:90
  13.2 6.4 %collective-permute-start.2 = (bf16[16,64,128]{2,1,0:T(8,128)(2,1)}, bf16[16,64,128]{2,1,0:T(8,128)(2,1)S(1)}, u32[]{:S(2)}, u32[]{:S(2)}) collective-permute-start(bf16[16,64,128]{2,1,0:T(8,128)(2,1)} %get-tuple-element.63), channel_id=1, source_target_pairs={{0,0},{1,8},{2,16},{3,24},{4,4},{5,12},{6,20},{7,28},{8,1},{9,9},{... | collective-permute-start | bytes 786440 | tf_op jit(solution)/shard_map/ppermute | solution.py:367
  19.7 0.0 collective-permute-done.7
  19.7 0.1 collective-permute-start.8
  19.8 0.0 collective-permute-done.5
  19.8 0.1 collective-permute-start.6
  19.8 1.0 collective-permute-start.4
  20.9 4.2 %collective-permute-start.10 = (bf16[10,64,128]{2,1,0:T(8,128)(2,1)}, bf16[10,64,128]{2,1,0:T(8,128)(2,1)}, u32[]{:S(2)}, u32[]{:S(2)}) collective-permute-start(bf16[10,64,128]{2,1,0:T(8,128)(2,1)} %get-tuple-element.75), channel_id=1, source_target_pairs={{4,8},{12,16},{20,24},{8,4},{16,12},{24,20},{5,9},{13,17},{21,25},... | collective-permute-start | bytes 491528 | tf_op jit(solution)/shard_map/ppermute | solution.py:90
  25.1 0.7 copy.9.refs_5_
  25.8 3.3 %collective-permute-done.10.refs_1_ = bf16[10,64,128]{2,1,0:T(8,128)(2,1)} collective-permute-done((bf16[10,64,128]{2,1,0:T(8,128)(2,1)}, bf16[10,64,128]{2,1,0:T(8,128)(2,1)}, u32[]{:S(2)}, u32[]{:S(2)}) %collective-permute-start.10) | collective-permute-done | bytes 163872 | tf_op jit(solution)/shard_map/ppermute | solution.py:90
  29.1 0.9 copy-done.3
  30.0 4.5 %forward.1 = (f32[8,128]{1,0:T(8,128)}, bf16[80,192,128]{2,1,0:T(8,128)(2,1)S(1)}, f32[64,64,128]{2,1,0:T(8,128)S(1)}, bf16[16,64,128]{2,1,0:T(8,128)(2,1)S(1)},...) custom-call(s32[1]{0:T(128)} %bitcast.row_odd, ...), custom_call_target="tpu_custom_call" | custom-call | flops 603979776 | bytes 8663304 | tf_op jit(solution)/shard_map/forward/pallas_call | solution.py:31
  34.5 3.0 %collective-permute-done.2.refs_0_ = bf16[16,64,128]{2,1,0:T(8,128)(2,1)S(1)} collective-permute-done((bf16[16,64,128]{2,1,0:T(8,128)(2,1)}, bf16[16,64,128]{2,1,0:T(8,128)(2,1)S(1)}, u32[]{:S(2)}, u32[]{:S(2)}) %collective-permute-start.2) | collective-permute-done | bytes 262176 | tf_op jit(solution)/shard_map/ppermute | solution.py:367
  37.5 3.1 %collective-permute-done.8.refs_3_ = bf16[16,64,128]{2,1,0:T(8,128)(2,1)S(1)} collective-permute-done((bf16[16,64,128]{2,1,0:T(8,128)(2,1)}, bf16[16,64,128]{2,1,0:T(8,128)(2,1)S(1)}, u32[]{:S(2)}, u32[]{:S(2)}) %collective-permute-start.8) | collective-permute-done | bytes 262176 | tf_op jit(solution)/shard_map/ppermute | solution.py:367
  40.6 0.9 turn.2
  41.5 6.7 %collective-permute-start.11 = (bf16[32,64,128]{2,1,0:T(8,128)(2,1)S(1)}, bf16[32,64,128]{2,1,0:T(8,128)(2,1)S(1)}, u32[]{:S(2)}, u32[]{:S(2)}) collective-permute-start(bf16[32,64,128]{2,1,0:T(8,128)(2,1)S(1)} %get-tuple-element.82), channel_id=1, source_target_pairs={{0,4},{4,0},{8,12},{12,8},{16,20},{20,16},{24,28},{28,24},{1,5},{5... | collective-permute-start | bytes 1572872 | tf_op jit(solution)/shard_map/ppermute | solution.py:378
  48.3 0.9 collective-permute-start.17
  49.2 0.6 collective-permute-done.11.got
  49.8 2.1 %grad_pre.1 = (f32[8,128]{1,0:T(8,128)}, bf16[64,64,128]{2,1,0:T(8,128)(2,1)S(1)}, bf16[8,64,128]{2,1,0:T(8,128)(2,1)S(1)}, bf16[8,64,128]{2,1,0:T(8,128)(2,1)S(...) custom-call(s32[1]{0:T(128)} %bitcast.row_odd, ...), custom_call_target="tpu_custom_call" | custom-call | bytes 6688776 | tf_op jit(solution)/shard_map/grad_pre/pallas_call | solution.py:31
  51.9 1.8 %weight_terms.1 = (f32[8,128]{1,0:T(8,128)}, f32[160,128]{1,0:T(8,128)S(1)}, f32[160,128]{1,0:T(8,128)S(1)}) custom-call(s32[1]{0:T(128)} %bitcast.row_odd, bf16[64,64,128]{2,1,0:T(8,128)(2,1)S(1)} %get-tuple-element.83.tile.grad, bf16[80,192,128]{2,1,0:T(8,128)(2,1)S(1)} %get-tuple-element.89.stack), custom_call_target="tpu_custom_call" | custom-call | flops 603979776 | bytes 5148676 | tf_op jit(solution)/shard_map/weight_terms/pallas_call | solution.py:31
  53.7 0.4 collective-permute-start.14
  54.1 1.4 %collective-permute-start.22 = (bf16[16,64,128]{2,1,0:T(8,128)(2,1)S(1)}, bf16[16,64,128]{2,1,0:T(8,128)(2,1)S(1)}, u32[]{:S(2)}, u32[]{:S(2)}) collective-permute-start(bf16[16,64,128]{2,1,0:T(8,128)(2,1)S(1)} %get-tuple-element.99.refs_3_), channel_id=1, source_target_pairs={{0,24},{4,28},{8,16},{12,20},{16,8},{20,12},{24,0},{28,4},{1,25},{... | collective-permute-start | bytes 786440 | tf_op jit(solution)/shard_map/ppermute | solution.py:357
  55.5 0.0 collective-permute-done.14
  55.5 0.6 collective-permute-done.15
  56.2 0.0 collective-permute-start.16
  56.2 1.5 %collective-permute-start.12 = (bf16[4,64,128]{2,1,0:T(8,128)(2,1)S(1)}, bf16[4,64,128]{2,1,0:T(8,128)(2,1)S(1)}, u32[]{:S(2)}, u32[]{:S(2)}) collective-permute-start(bf16[4,64,128]{2,1,0:T(8,128)(2,1)S(1)} %get-tuple-element.84), channel_id=1, source_target_pairs={{0,1},{2,3},{1,0},{3,2},{4,5},{6,7},{5,4},{7,6},{8,9},{10,11},{9,8... | collective-permute-start | bytes 196616 | tf_op jit(solution)/shard_map/ppermute | solution.py:90
  57.6 0.7 collective-permute-start.13
  58.3 1.5 %collective-permute-done.16 = f32[160,128]{1,0:T(8,128)S(1)} collective-permute-done((f32[160,128]{1,0:T(8,128)S(1)}, f32[160,128]{1,0:T(8,128)S(1)}, u32[]{:S(2)}, u32[]{:S(2)}) %collective-permute-start.16) | collective-permute-done | bytes 81952 | tf_op jit(solution)/shard_map/ppermute | solution.py:468
  59.8 1.1 %collective-permute-start.18 = (f32[160,128]{1,0:T(8,128)S(1)}, f32[160,128]{1,0:T(8,128)S(1)}, u32[]{:S(2)}, u32[]{:S(2)}) collective-permute-start(f32[160,128]{1,0:T(8,128)S(1)} %add.25), channel_id=1, source_target_pairs={{0,2},{1,3},{2,0},{3,1},{4,6},{5,7},{6,4},{7,5},{8,10},{9,11},{10,... | collective-permute-start | bytes 245768 | tf_op jit(solution)/shard_map/ppermute | solution.py:397
  60.8 0.0 collective-permute-done.12.col_first.first
  60.8 0.0 collective-permute-done.13.col_second.second
  60.9 0.1 messages.3
  60.9 1.8 %collective-permute-start.26 = (bf16[10,64,128]{2,1,0:T(8,128)(2,1)S(1)}, bf16[10,64,128]{2,1,0:T(8,128)(2,1)S(1)}, u32[]{:S(2)}, u32[]{:S(2)}) collective-permute-start(bf16[10,64,128]{2,1,0:T(8,128)(2,1)S(1)} %get-tuple-element.103), channel_id=1, source_target_pairs={{0,4},{8,12},{16,20},{24,28},{4,0},{12,8},{20,16},{28,24},{1,5},{9... | collective-permute-start | bytes 491528 | tf_op jit(solution)/shard_map/ppermute | solution.py:90
  62.7 2.6 %collective-permute-done.18 = f32[160,128]{1,0:T(8,128)S(1)} collective-permute-done((f32[160,128]{1,0:T(8,128)S(1)}, f32[160,128]{1,0:T(8,128)S(1)}, u32[]{:S(2)}, u32[]{:S(2)}) %collective-permute-start.18) | collective-permute-done | bytes 81952 | tf_op jit(solution)/shard_map/ppermute | solution.py:397
  65.3 0.3 collective-permute-start.24
  65.7 0.0 collective-permute-done.22
  65.7 0.8 collective-permute-start.23
  66.5 0.0 collective-permute-start.21
  66.5 0.4 collective-permute-start.20
  66.9 1.8 %collective-permute-done.24 = f32[160,128]{1,0:T(8,128)S(1)} collective-permute-done((f32[160,128]{1,0:T(8,128)S(1)}, f32[160,128]{1,0:T(8,128)S(1)}, u32[]{:S(2)}, u32[]{:S(2)}) %collective-permute-start.24) | collective-permute-done | bytes 81952 | tf_op jit(solution)/shard_map/ppermute | solution.py:397
  68.7 2.8 %collective-permute-start.19 = (bf16[16,64,128]{2,1,0:T(8,128)(2,1)S(1)}, bf16[16,64,128]{2,1,0:T(8,128)(2,1)S(1)}, u32[]{:S(2)}, u32[]{:S(2)}) collective-permute-start(bf16[16,64,128]{2,1,0:T(8,128)(2,1)S(1)} %get-tuple-element.96.refs_0_), channel_id=1, source_target_pairs={{0,0},{1,8},{2,16},{3,24},{4,4},{5,12},{6,20},{7,28},{8,1},{9,9},{... | collective-permute-start | bytes 786440 | tf_op jit(solution)/shard_map/ppermute | solution.py:367
  71.5 2.7 %collective-permute-start.25 = (f32[160,128]{1,0:T(8,128)S(1)}, f32[160,128]{1,0:T(8,128)S(1)}, u32[]{:S(2)}, u32[]{:S(2)}) collective-permute-start(f32[160,128]{1,0:T(8,128)S(1)} %add.27), channel_id=1, source_target_pairs={{0,16},{4,20},{8,24},{12,28},{16,0},{20,4},{24,8},{28,12},{1,17},{... | collective-permute-start | bytes 245768 | tf_op jit(solution)/shard_map/ppermute | solution.py:397
  74.2 3.2 %input_grad.1 = (f32[8,128]{1,0:T(8,128)S(1)}, bf16[64,64,128]{2,1,0:T(8,128)(2,1)}, f32[2,64,16,128]{3,2,1,0:T(8,128)S(1)}) custom-call(s32[1]{0:T(128)} %bitcast.1.col_odd, bf16[64,64,128]{2,1,0:T(8,128)(2,1)S(1)} %get-tuple-element.83.tile.grad, bf16[4,64,128]{2,1,0:T(8,128)(2,1)S(1)} %collective-permute-done.12.col_first.first, ...), custom_call_target="tpu_custom_call" | custom-call | flops 603979776 | bytes 5451780 | tf_op jit(solution)/shard_map/input_grad/pallas_call | solution.py:31
  77.4 3.6 %collective-permute-done.25 = f32[160,128]{1,0:T(8,128)S(1)} collective-permute-done((f32[160,128]{1,0:T(8,128)S(1)}, f32[160,128]{1,0:T(8,128)S(1)}, u32[]{:S(2)}, u32[]{:S(2)}) %collective-permute-start.25) | collective-permute-done | bytes 81952 | tf_op jit(solution)/shard_map/ppermute | solution.py:397
  80.9 4.9 %collective-permute-start.27 = (bf16[10,64,128]{2,1,0:T(8,128)(2,1)S(1)}, bf16[10,64,128]{2,1,0:T(8,128)(2,1)S(1)}, u32[]{:S(2)}, u32[]{:S(2)}) collective-permute-start(bf16[10,64,128]{2,1,0:T(8,128)(2,1)S(1)} %get-tuple-element.105), channel_id=1, source_target_pairs={{4,8},{12,16},{20,24},{8,4},{16,12},{24,20},{5,9},{13,17},{21,25},... | collective-permute-start | bytes 491528 | tf_op jit(solution)/shard_map/ppermute | solution.py:90
  85.9 5.8 %collective-permute-done.27.row_second = bf16[10,64,128]{2,1,0:T(8,128)(2,1)S(1)} collective-permute-done((bf16[10,64,128]{2,1,0:T(8,128)(2,1)S(1)}, bf16[10,64,128]{2,1,0:T(8,128)(2,1)S(1)}, u32[]{:S(2)}, u32[]{:S(2)}) %collective-permute-start.27) | collective-permute-done | bytes 163872 | tf_op jit(solution)/shard_map/ppermute | solution.py:90
  91.7 0.0 collective-permute-done.19.refs_1_
  91.7 0.9 turn.3
  92.6 7.0 %collective-permute-start.28 = (bf16[32,64,128]{2,1,0:T(8,128)(2,1)S(1)}, bf16[32,64,128]{2,1,0:T(8,128)(2,1)S(1)}, u32[]{:S(2)}, u32[]{:S(2)}) collective-permute-start(bf16[32,64,128]{2,1,0:T(8,128)(2,1)S(1)} %get-tuple-element.111), channel_id=1, source_target_pairs={{0,4},{4,0},{8,12},{12,8},{16,20},{20,16},{24,28},{28,24},{1,5},{5... | collective-permute-start | bytes 1572872 | tf_op jit(solution)/shard_map/ppermute | solution.py:378
  99.6 0.1 collective-permute-start.29
  99.7 1.5 %input_grad_ends.1 = bf16[64,64,128]{2,1,0:T(8,128)(2,1)} custom-call(s32[1]{0:T(128)} %bitcast.row_odd, bf16[10,64,128]{2,1,0:T(8,128)(2,1)S(1)} %collective-permute-done.26.row_first, bf16[10,64,128]{2,1,0:T(8,128)(2,1)S(1)} %collective-permute-done.27.row_second, bf16[3,3,64,64]{3,2,1,0:T(8,128)(2,1)S(1)} %copy-done.4, ...), custom_call_target="tpu_custom_call", output_to_operand_aliasing={{}: (5, {})} | custom-call | bytes 3547140 | tf_op jit(solution)/shard_map/input_grad_ends/pallas_call | solution.py:31
  101.2 0.1 collective-permute-done.29.other
  101.3 0.8 unpack.1
  102.1 1.6 %join.1 = bf16[64,64,128]{2,1,0:T(8,128)(2,1)} custom-call(s32[1]{0:T(128)} %bitcast.row_odd, bf16[32,64,128]{2,1,0:T(8,128)(2,1)S(1)} %get-tuple-element.110.keep, bf16[32,64,128]{2,1,0:T(8,128)(2,1)S(1)} %collective-permute-done.28.got, bf16[16,64,128]{2,1,0:T(8,128)(2,1)S(1)} %get-tuple-element.96.refs_0_, ...), custom_call_target="tpu_custom_call" | custom-call | bytes 3145732 | tf_op jit(solution)/shard_map/join/pallas_call | solution.py:31
  (24 shorter events, 0.1 us)
Async XLA Ops:
  0.6 1.2 %copy-start = (bf16[64,64,128]{2,1,0:T(8,128)(2,1)S(1)}, bf16[64,64,128]{2,1,0:T(8,128)(2,1)}, u32[]{:S(2)}) copy-start(bf16[64,64,128]{2,1,0:T(8,128)(2,1)} %cot.5) | copy-start | bytes 3145732
  1.9 1.2 %copy-start.2 = (bf16[64,64,128]{2,1,0:T(8,128)(2,1)S(1)}, bf16[64,64,128]{2,1,0:T(8,128)(2,1)}, u32[]{:S(2)}) copy-start(bf16[64,64,128]{2,1,0:T(8,128)(2,1)} %x.1) | copy-start | bytes 3145732
  3.1 46.7 %copy-start.1 = (bf16[64,64,128]{2,1,0:T(8,128)(2,1)S(1)}, bf16[64,64,128]{2,1,0:T(8,128)(2,1)}, u32[]{:S(2)}) copy-start(bf16[64,64,128]{2,1,0:T(8,128)(2,1)} %cot.5) | copy-start | bytes 3145732
  4.0 15.7 %collective-permute-start.7 = (bf16[16,64,128]{2,1,0:T(8,128)(2,1)S(1)}, bf16[16,64,128]{2,1,0:T(8,128)(2,1)}, u32[]{:S(2)}, u32[]{:S(2)}) collective-permute-start(bf16[16,64,128]{2,1,0:T(8,128)(2,1)S(1)} %get-tuple-element.68), channel_id=1, source_target_pairs={{0,24},{4,28},{8,16},{12,20},{16,8},{20,12},{24,0},{28,4},{1,25},{... | collective-permute-start | bytes 786440 | tf_op jit(solution)/shard_map/ppermute | solution.py:357
  5.2 14.5 %collective-permute-start.5 = (bf16[16,64,128]{2,1,0:T(8,128)(2,1)S(1)}, bf16[16,64,128]{2,1,0:T(8,128)(2,1)}, u32[]{:S(2)}, u32[]{:S(2)}) collective-permute-start(bf16[16,64,128]{2,1,0:T(8,128)(2,1)S(1)} %get-tuple-element.66), channel_id=1, source_target_pairs={{0,16},{4,20},{8,24},{12,28},{16,0},{20,4},{24,8},{28,12},{1,17},{... | collective-permute-start | bytes 786440 | tf_op jit(solution)/shard_map/ppermute | solution.py:357
  6.5 13.4 %collective-permute-start.3 = (bf16[16,64,128]{2,1,0:T(8,128)(2,1)S(1)}, bf16[16,64,128]{2,1,0:T(8,128)(2,1)}, u32[]{:S(2)}, u32[]{:S(2)}) collective-permute-start(bf16[16,64,128]{2,1,0:T(8,128)(2,1)S(1)} %get-tuple-element.64), channel_id=1, source_target_pairs={{0,8},{4,12},{8,0},{12,4},{16,24},{20,28},{24,16},{28,20},{1,9},{5... | collective-permute-start | bytes 786440 | tf_op jit(solution)/shard_map/ppermute | solution.py:357
  6.7 3.5 %collective-permute-start = (bf16[4,64,128]{2,1,0:T(8,128)(2,1)S(1)}, bf16[4,64,128]{2,1,0:T(8,128)(2,1)S(1)}, u32[]{:S(2)}, u32[]{:S(2)}) collective-permute-start(bf16[4,64,128]{2,1,0:T(8,128)(2,1)S(1)} %get-tuple-element.61), channel_id=1, source_target_pairs={{0,1},{2,3},{1,0},{3,2},{4,5},{6,7},{5,4},{7,6},{8,9},{10,11},{9,8... | collective-permute-start | bytes 196616 | tf_op jit(solution)/shard_map/ppermute | solution.py:90
  6.9 3.3 %collective-permute-start.1 = (bf16[4,64,128]{2,1,0:T(8,128)(2,1)S(1)}, bf16[4,64,128]{2,1,0:T(8,128)(2,1)S(1)}, u32[]{:S(2)}, u32[]{:S(2)}) collective-permute-start(bf16[4,64,128]{2,1,0:T(8,128)(2,1)S(1)} %get-tuple-element.62), channel_id=1, source_target_pairs={{1,2},{2,1},{5,6},{6,5},{9,10},{10,9},{13,14},{14,13},{17,18},{18,... | collective-permute-start | bytes 196616 | tf_op jit(solution)/shard_map/ppermute | solution.py:90
  11.0 9.9 %collective-permute-start.9 = (bf16[10,64,128]{2,1,0:T(8,128)(2,1)S(1)}, bf16[10,64,128]{2,1,0:T(8,128)(2,1)S(1)}, u32[]{:S(2)}, u32[]{:S(2)}) collective-permute-start(bf16[10,64,128]{2,1,0:T(8,128)(2,1)S(1)} %get-tuple-element.73), channel_id=1, source_target_pairs={{0,4},{8,12},{16,20},{24,28},{4,0},{12,8},{20,16},{28,24},{1,5},{9... | collective-permute-start | bytes 491528 | tf_op jit(solution)/shard_map/ppermute | solution.py:90
  13.2 24.3 %collective-permute-start.2 = (bf16[16,64,128]{2,1,0:T(8,128)(2,1)}, bf16[16,64,128]{2,1,0:T(8,128)(2,1)S(1)}, u32[]{:S(2)}, u32[]{:S(2)}) collective-permute-start(bf16[16,64,128]{2,1,0:T(8,128)(2,1)} %get-tuple-element.63), channel_id=1, source_target_pairs={{0,0},{1,8},{2,16},{3,24},{4,4},{5,12},{6,20},{7,28},{8,1},{9,9},{... | collective-permute-start | bytes 786440 | tf_op jit(solution)/shard_map/ppermute | solution.py:367
  19.7 20.9 %collective-permute-start.8 = (bf16[16,64,128]{2,1,0:T(8,128)(2,1)}, bf16[16,64,128]{2,1,0:T(8,128)(2,1)S(1)}, u32[]{:S(2)}, u32[]{:S(2)}) collective-permute-start(bf16[16,64,128]{2,1,0:T(8,128)(2,1)} %collective-permute-done.7), channel_id=1, source_target_pairs={{0,3},{1,11},{2,19},{3,27},{4,7},{5,15},{6,23},{7,31},{8,2},{9,10}... | collective-permute-start | bytes 786440 | tf_op jit(solution)/shard_map/ppermute | solution.py:367
  19.8 20.9 %collective-permute-start.6 = (bf16[16,64,128]{2,1,0:T(8,128)(2,1)}, bf16[16,64,128]{2,1,0:T(8,128)(2,1)S(1)}, u32[]{:S(2)}, u32[]{:S(2)}) collective-permute-start(bf16[16,64,128]{2,1,0:T(8,128)(2,1)} %collective-permute-done.5), channel_id=1, source_target_pairs={{0,2},{1,10},{2,18},{3,26},{4,6},{5,14},{6,22},{7,30},{8,3},{9,11}... | collective-permute-start | bytes 786440 | tf_op jit(solution)/shard_map/ppermute | solution.py:367
  19.8 20.8 %collective-permute-start.4 = (bf16[16,64,128]{2,1,0:T(8,128)(2,1)}, bf16[16,64,128]{2,1,0:T(8,128)(2,1)S(1)}, u32[]{:S(2)}, u32[]{:S(2)}) collective-permute-start(bf16[16,64,128]{2,1,0:T(8,128)(2,1)} %collective-permute-done.3), channel_id=1, source_target_pairs={{0,1},{1,9},{2,17},{3,25},{4,5},{5,13},{6,21},{7,29},{8,0},{9,8},{... | collective-permute-start | bytes 786440 | tf_op jit(solution)/shard_map/ppermute | solution.py:367
  20.9 8.2 %collective-permute-start.10 = (bf16[10,64,128]{2,1,0:T(8,128)(2,1)}, bf16[10,64,128]{2,1,0:T(8,128)(2,1)}, u32[]{:S(2)}, u32[]{:S(2)}) collective-permute-start(bf16[10,64,128]{2,1,0:T(8,128)(2,1)} %get-tuple-element.75), channel_id=1, source_target_pairs={{4,8},{12,16},{20,24},{8,4},{16,12},{24,20},{5,9},{13,17},{21,25},... | collective-permute-start | bytes 491528 | tf_op jit(solution)/shard_map/ppermute | solution.py:90
  29.1 0.9 copy-start.3
  41.5 8.3 %collective-permute-start.11 = (bf16[32,64,128]{2,1,0:T(8,128)(2,1)S(1)}, bf16[32,64,128]{2,1,0:T(8,128)(2,1)S(1)}, u32[]{:S(2)}, u32[]{:S(2)}) collective-permute-start(bf16[32,64,128]{2,1,0:T(8,128)(2,1)S(1)} %get-tuple-element.82), channel_id=1, source_target_pairs={{0,4},{4,0},{8,12},{12,8},{16,20},{20,16},{24,28},{28,24},{1,5},{5... | collective-permute-start | bytes 1572872 | tf_op jit(solution)/shard_map/ppermute | solution.py:378
  48.3 7.9 %collective-permute-start.15 = (bf16[16,64,128]{2,1,0:T(8,128)(2,1)S(1)}, bf16[16,64,128]{2,1,0:T(8,128)(2,1)S(1)}, u32[]{:S(2)}, u32[]{:S(2)}) collective-permute-start(bf16[16,64,128]{2,1,0:T(8,128)(2,1)S(1)} %get-tuple-element.92.refs_1_), channel_id=1, source_target_pairs={{0,8},{4,12},{8,0},{12,4},{16,24},{20,28},{24,16},{28,20},{1,9},{5... | collective-permute-start | bytes 786440 | tf_op jit(solution)/shard_map/ppermute | solution.py:357
  48.3 11.5 %collective-permute-start.17 = (bf16[16,64,128]{2,1,0:T(8,128)(2,1)S(1)}, bf16[16,64,128]{2,1,0:T(8,128)(2,1)S(1)}, u32[]{:S(2)}, u32[]{:S(2)}) collective-permute-start(bf16[16,64,128]{2,1,0:T(8,128)(2,1)S(1)} %get-tuple-element.94.refs_2_), channel_id=1, source_target_pairs={{0,16},{4,20},{8,24},{12,28},{16,0},{20,4},{24,8},{28,12},{1,17},{... | collective-permute-start | bytes 786440 | tf_op jit(solution)/shard_map/ppermute | solution.py:357
  51.9 22.3 %copy-start.4 = (bf16[3,3,64,64]{3,2,1,0:T(8,128)(2,1)S(1)}, bf16[3,3,64,64]{3,2,1,0:T(8,128)(2,1)}, u32[]{:S(2)}) copy-start(bf16[3,3,64,64]{3,2,1,0:T(8,128)(2,1)} %weight.3) | copy-start | bytes 221188
  53.7 1.8 %collective-permute-start.14 = (f32[160,128]{1,0:T(8,128)S(1)}, f32[160,128]{1,0:T(8,128)S(1)}, u32[]{:S(2)}, u32[]{:S(2)}) collective-permute-start(f32[160,128]{1,0:T(8,128)S(1)} %get-tuple-element.91), channel_id=1, source_target_pairs={{0,4},{4,0},{8,12},{12,8},{16,20},{20,16},{24,28},{28,24},{1,5},{5... | collective-permute-start | bytes 245768 | tf_op jit(solution)/shard_map/ppermute | solution.py:378
  54.1 11.6 %collective-permute-start.22 = (bf16[16,64,128]{2,1,0:T(8,128)(2,1)S(1)}, bf16[16,64,128]{2,1,0:T(8,128)(2,1)S(1)}, u32[]{:S(2)}, u32[]{:S(2)}) collective-permute-start(bf16[16,64,128]{2,1,0:T(8,128)(2,1)S(1)} %get-tuple-element.99.refs_3_), channel_id=1, source_target_pairs={{0,24},{4,28},{8,16},{12,20},{16,8},{20,12},{24,0},{28,4},{1,25},{... | collective-permute-start | bytes 786440 | tf_op jit(solution)/shard_map/ppermute | solution.py:357
  56.2 3.6 %collective-permute-start.16 = (f32[160,128]{1,0:T(8,128)S(1)}, f32[160,128]{1,0:T(8,128)S(1)}, u32[]{:S(2)}, u32[]{:S(2)}) collective-permute-start(f32[160,128]{1,0:T(8,128)S(1)} %add.24), channel_id=1, source_target_pairs={{0,1},{1,0},{2,3},{3,2},{4,5},{5,4},{6,7},{7,6},{8,9},{9,8},{10,11... | collective-permute-start | bytes 245768 | tf_op jit(solution)/shard_map/ppermute | solution.py:468
  56.2 4.7 %collective-permute-start.12 = (bf16[4,64,128]{2,1,0:T(8,128)(2,1)S(1)}, bf16[4,64,128]{2,1,0:T(8,128)(2,1)S(1)}, u32[]{:S(2)}, u32[]{:S(2)}) collective-permute-start(bf16[4,64,128]{2,1,0:T(8,128)(2,1)S(1)} %get-tuple-element.84), channel_id=1, source_target_pairs={{0,1},{2,3},{1,0},{3,2},{4,5},{6,7},{5,4},{7,6},{8,9},{10,11},{9,8... | collective-permute-start | bytes 196616 | tf_op jit(solution)/shard_map/ppermute | solution.py:90
  57.6 3.2 %collective-permute-start.13 = (bf16[4,64,128]{2,1,0:T(8,128)(2,1)S(1)}, bf16[4,64,128]{2,1,0:T(8,128)(2,1)S(1)}, u32[]{:S(2)}, u32[]{:S(2)}) collective-permute-start(bf16[4,64,128]{2,1,0:T(8,128)(2,1)S(1)} %get-tuple-element.85), channel_id=1, source_target_pairs={{1,2},{2,1},{5,6},{6,5},{9,10},{10,9},{13,14},{14,13},{17,18},{18,... | collective-permute-start | bytes 196616 | tf_op jit(solution)/shard_map/ppermute | solution.py:90
  59.8 5.6 %collective-permute-start.18 = (f32[160,128]{1,0:T(8,128)S(1)}, f32[160,128]{1,0:T(8,128)S(1)}, u32[]{:S(2)}, u32[]{:S(2)}) collective-permute-start(f32[160,128]{1,0:T(8,128)S(1)} %add.25), channel_id=1, source_target_pairs={{0,2},{1,3},{2,0},{3,1},{4,6},{5,7},{6,4},{7,5},{8,10},{9,11},{10,... | collective-permute-start | bytes 245768 | tf_op jit(solution)/shard_map/ppermute | solution.py:397
  60.9 10.6 %collective-permute-start.26 = (bf16[10,64,128]{2,1,0:T(8,128)(2,1)S(1)}, bf16[10,64,128]{2,1,0:T(8,128)(2,1)S(1)}, u32[]{:S(2)}, u32[]{:S(2)}) collective-permute-start(bf16[10,64,128]{2,1,0:T(8,128)(2,1)S(1)} %get-tuple-element.103), channel_id=1, source_target_pairs={{0,4},{8,12},{16,20},{24,28},{4,0},{12,8},{20,16},{28,24},{1,5},{9... | collective-permute-start | bytes 491528 | tf_op jit(solution)/shard_map/ppermute | solution.py:90
  65.3 3.4 %collective-permute-start.24 = (f32[160,128]{1,0:T(8,128)S(1)}, f32[160,128]{1,0:T(8,128)S(1)}, u32[]{:S(2)}, u32[]{:S(2)}) collective-permute-start(f32[160,128]{1,0:T(8,128)S(1)} %add.26), channel_id=1, source_target_pairs={{0,8},{4,12},{8,0},{12,4},{16,24},{20,28},{24,16},{28,20},{1,9},{5... | collective-permute-start | bytes 245768 | tf_op jit(solution)/shard_map/ppermute | solution.py:397
  65.7 26.0 %collective-permute-start.23 = (bf16[16,64,128]{2,1,0:T(8,128)(2,1)S(1)}, bf16[16,64,128]{2,1,0:T(8,128)(2,1)S(1)}, u32[]{:S(2)}, u32[]{:S(2)}) collective-permute-start(bf16[16,64,128]{2,1,0:T(8,128)(2,1)S(1)} %collective-permute-done.22), channel_id=1, source_target_pairs={{0,3},{1,11},{2,19},{3,27},{4,7},{5,15},{6,23},{7,31},{8,2},{9,10}... | collective-permute-start | bytes 786440 | tf_op jit(solution)/shard_map/ppermute | solution.py:367
  66.5 25.1 %collective-permute-start.21 = (bf16[16,64,128]{2,1,0:T(8,128)(2,1)S(1)}, bf16[16,64,128]{2,1,0:T(8,128)(2,1)S(1)}, u32[]{:S(2)}, u32[]{:S(2)}) collective-permute-start(bf16[16,64,128]{2,1,0:T(8,128)(2,1)S(1)} %collective-permute-done.17), channel_id=1, source_target_pairs={{0,2},{1,10},{2,18},{3,26},{4,6},{5,14},{6,22},{7,30},{8,3},{9,11}... | collective-permute-start | bytes 786440 | tf_op jit(solution)/shard_map/ppermute | solution.py:367
  66.5 25.1 %collective-permute-start.20 = (bf16[16,64,128]{2,1,0:T(8,128)(2,1)S(1)}, bf16[16,64,128]{2,1,0:T(8,128)(2,1)S(1)}, u32[]{:S(2)}, u32[]{:S(2)}) collective-permute-start(bf16[16,64,128]{2,1,0:T(8,128)(2,1)S(1)} %collective-permute-done.15), channel_id=1, source_target_pairs={{0,1},{1,9},{2,17},{3,25},{4,5},{5,13},{6,21},{7,29},{8,0},{9,8},{... | collective-permute-start | bytes 786440 | tf_op jit(solution)/shard_map/ppermute | solution.py:367
  68.7 23.0 %collective-permute-start.19 = (bf16[16,64,128]{2,1,0:T(8,128)(2,1)S(1)}, bf16[16,64,128]{2,1,0:T(8,128)(2,1)S(1)}, u32[]{:S(2)}, u32[]{:S(2)}) collective-permute-start(bf16[16,64,128]{2,1,0:T(8,128)(2,1)S(1)} %get-tuple-element.96.refs_0_), channel_id=1, source_target_pairs={{0,0},{1,8},{2,16},{3,24},{4,4},{5,12},{6,20},{7,28},{8,1},{9,9},{... | collective-permute-start | bytes 786440 | tf_op jit(solution)/shard_map/ppermute | solution.py:367
  71.5 9.4 %collective-permute-start.25 = (f32[160,128]{1,0:T(8,128)S(1)}, f32[160,128]{1,0:T(8,128)S(1)}, u32[]{:S(2)}, u32[]{:S(2)}) collective-permute-start(f32[160,128]{1,0:T(8,128)S(1)} %add.27), channel_id=1, source_target_pairs={{0,16},{4,20},{8,24},{12,28},{16,0},{20,4},{24,8},{28,12},{1,17},{... | collective-permute-start | bytes 245768 | tf_op jit(solution)/shard_map/ppermute | solution.py:397
  80.9 10.7 %collective-permute-start.27 = (bf16[10,64,128]{2,1,0:T(8,128)(2,1)S(1)}, bf16[10,64,128]{2,1,0:T(8,128)(2,1)S(1)}, u32[]{:S(2)}, u32[]{:S(2)}) collective-permute-start(bf16[10,64,128]{2,1,0:T(8,128)(2,1)S(1)} %get-tuple-element.105), channel_id=1, source_target_pairs={{4,8},{12,16},{20,24},{8,4},{16,12},{24,20},{5,9},{13,17},{21,25},... | collective-permute-start | bytes 491528 | tf_op jit(solution)/shard_map/ppermute | solution.py:90
  92.6 9.5 %collective-permute-start.28 = (bf16[32,64,128]{2,1,0:T(8,128)(2,1)S(1)}, bf16[32,64,128]{2,1,0:T(8,128)(2,1)S(1)}, u32[]{:S(2)}, u32[]{:S(2)}) collective-permute-start(bf16[32,64,128]{2,1,0:T(8,128)(2,1)S(1)} %get-tuple-element.111), channel_id=1, source_target_pairs={{0,4},{4,0},{8,12},{12,8},{16,20},{20,16},{24,28},{28,24},{1,5},{5... | collective-permute-start | bytes 1572872 | tf_op jit(solution)/shard_map/ppermute | solution.py:378
  99.6 1.7 %collective-permute-start.29 = (f32[160,128]{1,0:T(8,128)S(1)}, f32[160,128]{1,0:T(8,128)S(1)}, u32[]{:S(2)}, u32[]{:S(2)}) collective-permute-start(f32[160,128]{1,0:T(8,128)S(1)} %add.28.mine), channel_id=1, source_target_pairs={{0,4},{4,0},{8,12},{12,8},{16,20},{20,16},{24,28},{28,24},{1,5},{5... | collective-permute-start | bytes 245768 | tf_op jit(solution)/shard_map/ppermute | solution.py:378

commit v6 on v5

--- a/solution.py
+++ b/solution.py
@@ -110,9 +110,9 @@
     return rows, strips
 
 
-def rows_of_halo(rows, *before_far):
+def rows_of_halo(rows):
     near = exchanged(rows[0], "row", 0)
-    return near, exchanged(held(rows[1], near, *before_far), "row", 1)
+    return near, exchanged(held(rows[1], near), "row", 1)
 
 
 def shifted(left, middle, right, lane, out):
@@ -438,7 +438,7 @@
         flops=conv_flops,
         name="forward",
     )
-    arrived = [cross(held(p, *halo[2:]), j) for j, p in enumerate(dealt)]
+    arrived = [cross(held(p, halo[2]), j) for j, p in enumerate(dealt)]
     mixed_dealt = [detour(p, j) for j, p in enumerate(mixed)]
     keep, give = turn(held(arrived, slope), place)
     ready, grad, *edge, mirrored = call(
@@ -469,7 +469,7 @@
     part = summed(held(part, mixed_dealt[2]), "col", 2)
     across = summed(part, "row", 2)
     rows, strips = columns_of_halo(place, *edge)
-    mixed_arrived = [cross(held(p, part), j) for j, p in enumerate(mixed_dealt)]
+    mixed_arrived = [cross(held(p, part, *strips), j) for j, p in enumerate(mixed_dealt)]
     ended, grad_input, ends = call(
         input_grad_kernel,
         [token, shape(cotangent.shape, BF16), shape((2, channels, 16, tile_cols), F32)],
@@ -486,7 +486,7 @@
         flops=conv_flops,
         name="input_grad",
     )
-    halo = rows_of_halo(rows, ended)
+    halo = rows_of_halo(rows)
     strip = pltpu.VMEM((STEP, 3 * channels, tile_cols), BF16)
     grad_input = call(
         input_grad_ends_kernel,

time: 104 us -> 104 us (level)
  the two profiles are of different devices: /device:TPU:29 before, /device:TPU:12 now
where the time goes in v6:
time: 104 us; the launch traced here: 102 us
  starting transfers between devices  42.1 us (40%)
  waiting for transfers between devices  35.8 us (34%)
  Pallas kernels  19 us (18%)
  local copies, waits for them, and re-layouts  4.11 us (4%)
    pallas_call x12, Pallas kernels, call(): pl.pallas_call(kernel, out_shape=out_shape, in_specs=in_specs, out_specs=...  19 us
    ppermute x8, waiting for transfers between devices, exchanged(): return lax.ppermute(x, axis, pairs + [(j, i) for i, j in pairs])  18.6 us
    ppermute x8, starting transfers between devices, cross(): return lax.ppermute(piece, ('row', 'col'), owners)  17.1 us
    ppermute x8, starting transfers between devices, exchanged(): return lax.ppermute(x, axis, pairs + [(j, i) for i, j in pairs])  13.5 us
    ppermute x3, waiting for transfers between devices, summed(): lax.ppermute(part, axis, [(i, i ^ reach) for i in range(size)])  7.55 us
    ppermute x8, waiting for transfers between devices, cross(): return lax.ppermute(piece, ('row', 'col'), owners)  6.83 us
    ppermute x6, starting transfers between devices, detour(): lax.ppermute(piece, 'row', [(r, r ^ 2 * far) for r in range(lax.axis_size...  5.43 us
    unnamed x10, local copies, waits for them, and re-layouts  3.36 us
  transfers between devices with their start and end apart: 30, of which 13 were waited for; matrix products, arithmetic and copies ran while one was open for 1% of the time, Pallas kernels for 14%

profile of v6, /device:TPU:12, one launch (start us, length us, event | category | flops | bytes accessed | tf_op | source)
XLA Modules:
  0.0 102.0 jit_solution(11168120764872507344)
XLA Ops:
  0.7 1.2 %copy-done = bf16[64,64,128]{2,1,0:T(8,128)(2,1)S(1)} copy-done((bf16[64,64,128]{2,1,0:T(8,128)(2,1)S(1)}, bf16[64,64,128]{2,1,0:T(8,128)(2,1)}, u32[]{:S(2)}) %copy-start) | copy-done | bytes 1048600
  1.9 1.2 %copy-done.2 = bf16[64,64,128]{2,1,0:T(8,128)(2,1)S(1)} copy-done((bf16[64,64,128]{2,1,0:T(8,128)(2,1)S(1)}, bf16[64,64,128]{2,1,0:T(8,128)(2,1)}, u32[]{:S(2)}) %copy-start.2) | copy-done | bytes 1048600
  3.1 0.9 open.1
  4.0 1.5 %collective-permute-start.6 = (bf16[16,64,128]{2,1,0:T(8,128)(2,1)S(1)}, bf16[16,64,128]{2,1,0:T(8,128)(2,1)}, u32[]{:S(2)}, u32[]{:S(2)}) collective-permute-start(bf16[16,64,128]{2,1,0:T(8,128)(2,1)S(1)} %get-tuple-element.67), channel_id=1, source_target_pairs={{0,24},{4,28},{8,16},{12,20},{16,8},{20,12},{24,0},{28,4},{1,25},{... | collective-permute-start | bytes 786440 | tf_op jit(solution)/shard_map/ppermute | solution.py:357
  5.5 1.5 %collective-permute-start.4 = (bf16[16,64,128]{2,1,0:T(8,128)(2,1)S(1)}, bf16[16,64,128]{2,1,0:T(8,128)(2,1)}, u32[]{:S(2)}, u32[]{:S(2)}) collective-permute-start(bf16[16,64,128]{2,1,0:T(8,128)(2,1)S(1)} %get-tuple-element.65), channel_id=1, source_target_pairs={{0,16},{4,20},{8,24},{12,28},{16,0},{20,4},{24,8},{28,12},{1,17},{... | collective-permute-start | bytes 786440 | tf_op jit(solution)/shard_map/ppermute | solution.py:357
  7.0 0.5 collective-permute-start.2
  7.6 0.4 collective-permute-start
  8.0 4.6 %collective-permute-start.8 = (bf16[4,64,128]{2,1,0:T(8,128)(2,1)S(1)}, bf16[4,64,128]{2,1,0:T(8,128)(2,1)S(1)}, u32[]{:S(2)}, u32[]{:S(2)}) collective-permute-start(bf16[4,64,128]{2,1,0:T(8,128)(2,1)S(1)} %get-tuple-element.72), channel_id=1, source_target_pairs={{1,2},{2,1},{5,6},{6,5},{9,10},{10,9},{13,14},{14,13},{17,18},{18,... | collective-permute-start | bytes 196616 | tf_op jit(solution)/shard_map/ppermute | solution.py:90
  12.6 0.0 collective-permute-done.first.refs_2_
  12.6 2.2 %collective-permute-done.8.second.refs_3_ = bf16[4,64,128]{2,1,0:T(8,128)(2,1)S(1)} collective-permute-done((bf16[4,64,128]{2,1,0:T(8,128)(2,1)S(1)}, bf16[4,64,128]{2,1,0:T(8,128)(2,1)S(1)}, u32[]{:S(2)}, u32[]{:S(2)}) %collective-permute-start.8) | collective-permute-done | bytes 65568 | tf_op jit(solution)/shard_map/ppermute | solution.py:90
  14.8 0.7 messages.2
  15.6 4.8 %collective-permute-start.1 = (bf16[16,64,128]{2,1,0:T(8,128)(2,1)}, bf16[16,64,128]{2,1,0:T(8,128)(2,1)S(1)}, u32[]{:S(2)}, u32[]{:S(2)}) collective-permute-start(bf16[16,64,128]{2,1,0:T(8,128)(2,1)} %get-tuple-element.62), channel_id=1, source_target_pairs={{0,0},{1,8},{2,16},{3,24},{4,4},{5,12},{6,20},{7,28},{8,1},{9,9},{... | collective-permute-start | bytes 786440 | tf_op jit(solution)/shard_map/ppermute | solution.py:367
  20.4 0.0 collective-permute-done.6
  20.4 0.1 collective-permute-start.7
  20.4 0.0 collective-permute-done.4
  20.4 1.4 %collective-permute-start.5 = (bf16[16,64,128]{2,1,0:T(8,128)(2,1)}, bf16[16,64,128]{2,1,0:T(8,128)(2,1)S(1)}, u32[]{:S(2)}, u32[]{:S(2)}) collective-permute-start(bf16[16,64,128]{2,1,0:T(8,128)(2,1)} %collective-permute-done.4), channel_id=1, source_target_pairs={{0,2},{1,10},{2,18},{3,26},{4,6},{5,14},{6,22},{7,30},{8,3},{9,11}... | collective-permute-start | bytes 786440 | tf_op jit(solution)/shard_map/ppermute | solution.py:367
  21.9 1.4 %collective-permute-start.3 = (bf16[16,64,128]{2,1,0:T(8,128)(2,1)}, bf16[16,64,128]{2,1,0:T(8,128)(2,1)S(1)}, u32[]{:S(2)}, u32[]{:S(2)}) collective-permute-start(bf16[16,64,128]{2,1,0:T(8,128)(2,1)} %collective-permute-done.2), channel_id=1, source_target_pairs={{0,1},{1,9},{2,17},{3,25},{4,5},{5,13},{6,21},{7,29},{8,0},{9,8},{... | collective-permute-start | bytes 786440 | tf_op jit(solution)/shard_map/ppermute | solution.py:367
  23.2 1.9 %collective-permute-start.10 = (bf16[10,64,128]{2,1,0:T(8,128)(2,1)}, bf16[10,64,128]{2,1,0:T(8,128)(2,1)}, u32[]{:S(2)}, u32[]{:S(2)}) collective-permute-start(bf16[10,64,128]{2,1,0:T(8,128)(2,1)} %get-tuple-element.75), channel_id=1, source_target_pairs={{4,8},{12,16},{20,24},{8,4},{16,12},{24,20},{5,9},{13,17},{21,25},... | collective-permute-start | bytes 491528 | tf_op jit(solution)/shard_map/ppermute | solution.py:90
  25.2 0.7 copy.9.refs_5_
  25.9 11.5 %collective-permute-done.10.refs_1_ = bf16[10,64,128]{2,1,0:T(8,128)(2,1)} collective-permute-done((bf16[10,64,128]{2,1,0:T(8,128)(2,1)}, bf16[10,64,128]{2,1,0:T(8,128)(2,1)}, u32[]{:S(2)}, u32[]{:S(2)}) %collective-permute-start.10) | collective-permute-done | bytes 163872 | tf_op jit(solution)/shard_map/ppermute | solution.py:90
  37.4 0.9 copy-done.3
  38.3 4.5 %forward.1 = (f32[8,128]{1,0:T(8,128)}, bf16[80,192,128]{2,1,0:T(8,128)(2,1)S(1)}, f32[64,64,128]{2,1,0:T(8,128)S(1)}, bf16[16,64,128]{2,1,0:T(8,128)(2,1)S(1)},...) custom-call(s32[1]{0:T(128)} %bitcast.row_odd, ...), custom_call_target="tpu_custom_call" | custom-call | flops 603979776 | bytes 8663304 | tf_op jit(solution)/shard_map/forward/pallas_call | solution.py:31
  42.9 2.4 %collective-permute-done.5.refs_2_ = bf16[16,64,128]{2,1,0:T(8,128)(2,1)S(1)} collective-permute-done((bf16[16,64,128]{2,1,0:T(8,128)(2,1)}, bf16[16,64,128]{2,1,0:T(8,128)(2,1)S(1)}, u32[]{:S(2)}, u32[]{:S(2)}) %collective-permute-start.5) | collective-permute-done | bytes 262176 | tf_op jit(solution)/shard_map/ppermute | solution.py:367
  45.3 0.0 collective-permute-done.3.refs_1_
  45.3 0.9 turn.2
  46.2 0.1 collective-permute-start.11
  46.3 0.0 collective-permute-start.15
  46.4 0.3 collective-permute-start.17
  46.7 1.5 %collective-permute-done.11.got = bf16[32,64,128]{2,1,0:T(8,128)(2,1)S(1)} collective-permute-done((bf16[32,64,128]{2,1,0:T(8,128)(2,1)S(1)}, bf16[32,64,128]{2,1,0:T(8,128)(2,1)S(1)}, u32[]{:S(2)}, u32[]{:S(2)}) %collective-permute-start.11) | collective-permute-done | bytes 524320 | tf_op jit(solution)/shard_map/ppermute | solution.py:378
  48.2 2.1 %grad_pre.1 = (f32[8,128]{1,0:T(8,128)}, bf16[64,64,128]{2,1,0:T(8,128)(2,1)S(1)}, bf16[8,64,128]{2,1,0:T(8,128)(2,1)S(1)}, bf16[8,64,128]{2,1,0:T(8,128)(2,1)S(...) custom-call(s32[1]{0:T(128)} %bitcast.row_odd, ...), custom_call_target="tpu_custom_call" | custom-call | bytes 6688776 | tf_op jit(solution)/shard_map/grad_pre/pallas_call | solution.py:31
  50.3 1.8 %weight_terms.1 = (f32[8,128]{1,0:T(8,128)}, f32[160,128]{1,0:T(8,128)S(1)}, f32[160,128]{1,0:T(8,128)S(1)}) custom-call(s32[1]{0:T(128)} %bitcast.row_odd, bf16[64,64,128]{2,1,0:T(8,128)(2,1)S(1)} %get-tuple-element.83.tile.grad, bf16[80,192,128]{2,1,0:T(8,128)(2,1)S(1)} %get-tuple-element.89.stack), custom_call_target="tpu_custom_call" | custom-call | flops 603979776 | bytes 5148676 | tf_op jit(solution)/shard_map/weight_terms/pallas_call | solution.py:31
  52.1 0.1 collective-permute-start.14
  52.2 1.5 %collective-permute-start.22 = (bf16[16,64,128]{2,1,0:T(8,128)(2,1)S(1)}, bf16[16,64,128]{2,1,0:T(8,128)(2,1)S(1)}, u32[]{:S(2)}, u32[]{:S(2)}) collective-permute-start(bf16[16,64,128]{2,1,0:T(8,128)(2,1)S(1)} %get-tuple-element.99.refs_3_), channel_id=1, source_target_pairs={{0,24},{4,28},{8,16},{12,20},{16,8},{20,12},{24,0},{28,4},{1,25},{... | collective-permute-start | bytes 786440 | tf_op jit(solution)/shard_map/ppermute | solution.py:357
  53.8 1.2 %collective-permute-done.15 = bf16[16,64,128]{2,1,0:T(8,128)(2,1)S(1)} collective-permute-done((bf16[16,64,128]{2,1,0:T(8,128)(2,1)S(1)}, bf16[16,64,128]{2,1,0:T(8,128)(2,1)S(1)}, u32[]{:S(2)}, u32[]{:S(2)}) %collective-permute-start.15) | collective-permute-done | bytes 262176 | tf_op jit(solution)/shard_map/ppermute | solution.py:357
  55.0 2.1 %collective-permute-start.16 = (f32[160,128]{1,0:T(8,128)S(1)}, f32[160,128]{1,0:T(8,128)S(1)}, u32[]{:S(2)}, u32[]{:S(2)}) collective-permute-start(f32[160,128]{1,0:T(8,128)S(1)} %add.24), channel_id=1, source_target_pairs={{0,1},{1,0},{2,3},{3,2},{4,5},{5,4},{6,7},{7,6},{8,9},{9,8},{10,11... | collective-permute-start | bytes 245768 | tf_op jit(solution)/shard_map/ppermute | solution.py:468
  57.1 0.0 collective-permute-start.12
  57.1 4.3 %collective-permute-start.13 = (bf16[4,64,128]{2,1,0:T(8,128)(2,1)S(1)}, bf16[4,64,128]{2,1,0:T(8,128)(2,1)S(1)}, u32[]{:S(2)}, u32[]{:S(2)}) collective-permute-start(bf16[4,64,128]{2,1,0:T(8,128)(2,1)S(1)} %get-tuple-element.85), channel_id=1, source_target_pairs={{1,2},{2,1},{5,6},{6,5},{9,10},{10,9},{13,14},{14,13},{17,18},{18,... | collective-permute-start | bytes 196616 | tf_op jit(solution)/shard_map/ppermute | solution.py:90
  61.4 0.0 collective-permute-done.16
  61.5 0.0 collective-permute-done.17
  61.5 2.2 %collective-permute-start.18 = (f32[160,128]{1,0:T(8,128)S(1)}, f32[160,128]{1,0:T(8,128)S(1)}, u32[]{:S(2)}, u32[]{:S(2)}) collective-permute-start(f32[160,128]{1,0:T(8,128)S(1)} %add.25), channel_id=1, source_target_pairs={{0,2},{1,3},{2,0},{3,1},{4,6},{5,7},{6,4},{7,5},{8,10},{9,11},{10,... | collective-permute-start | bytes 245768 | tf_op jit(solution)/shard_map/ppermute | solution.py:397
  63.7 0.7 collective-permute-done.13.col_second.second
  64.4 0.1 messages.3
  64.4 0.1 collective-permute-start.26
  64.5 2.4 %collective-permute-done.18 = f32[160,128]{1,0:T(8,128)S(1)} collective-permute-done((f32[160,128]{1,0:T(8,128)S(1)}, f32[160,128]{1,0:T(8,128)S(1)}, u32[]{:S(2)}, u32[]{:S(2)}) %collective-permute-start.18) | collective-permute-done | bytes 81952 | tf_op jit(solution)/shard_map/ppermute | solution.py:397
  66.9 0.9 collective-permute-start.24
  67.8 0.7 collective-permute-start.23
  68.5 2.8 %collective-permute-start.21 = (bf16[16,64,128]{2,1,0:T(8,128)(2,1)S(1)}, bf16[16,64,128]{2,1,0:T(8,128)(2,1)S(1)}, u32[]{:S(2)}, u32[]{:S(2)}) collective-permute-start(bf16[16,64,128]{2,1,0:T(8,128)(2,1)S(1)} %collective-permute-done.17), channel_id=1, source_target_pairs={{0,2},{1,10},{2,18},{3,26},{4,6},{5,14},{6,22},{7,30},{8,3},{9,11}... | collective-permute-start | bytes 786440 | tf_op jit(solution)/shard_map/ppermute | solution.py:367
  71.3 2.2 %collective-permute-start.20 = (bf16[16,64,128]{2,1,0:T(8,128)(2,1)S(1)}, bf16[16,64,128]{2,1,0:T(8,128)(2,1)S(1)}, u32[]{:S(2)}, u32[]{:S(2)}) collective-permute-start(bf16[16,64,128]{2,1,0:T(8,128)(2,1)S(1)} %collective-permute-done.15), channel_id=1, source_target_pairs={{0,1},{1,9},{2,17},{3,25},{4,5},{5,13},{6,21},{7,29},{8,0},{9,8},{... | collective-permute-start | bytes 786440 | tf_op jit(solution)/shard_map/ppermute | solution.py:367
  73.5 0.6 collective-permute-done.24
  74.1 3.8 %collective-permute-start.19 = (bf16[16,64,128]{2,1,0:T(8,128)(2,1)S(1)}, bf16[16,64,128]{2,1,0:T(8,128)(2,1)S(1)}, u32[]{:S(2)}, u32[]{:S(2)}) collective-permute-start(bf16[16,64,128]{2,1,0:T(8,128)(2,1)S(1)} %get-tuple-element.96.refs_0_), channel_id=1, source_target_pairs={{0,0},{1,8},{2,16},{3,24},{4,4},{5,12},{6,20},{7,28},{8,1},{9,9},{... | collective-permute-start | bytes 786440 | tf_op jit(solution)/shard_map/ppermute | solution.py:367
  77.9 0.1 collective-permute-start.25
  78.0 4.6 %collective-permute-done.25 = f32[160,128]{1,0:T(8,128)S(1)} collective-permute-done((f32[160,128]{1,0:T(8,128)S(1)}, f32[160,128]{1,0:T(8,128)S(1)}, u32[]{:S(2)}, u32[]{:S(2)}) %collective-permute-start.25) | collective-permute-done | bytes 81952 | tf_op jit(solution)/shard_map/ppermute | solution.py:397
  82.6 2.1 %collective-permute-start.27 = (bf16[10,64,128]{2,1,0:T(8,128)(2,1)S(1)}, bf16[10,64,128]{2,1,0:T(8,128)(2,1)S(1)}, u32[]{:S(2)}, u32[]{:S(2)}) collective-permute-start(bf16[10,64,128]{2,1,0:T(8,128)(2,1)S(1)} %get-tuple-element.105), channel_id=1, source_target_pairs={{4,8},{12,16},{20,24},{8,4},{16,12},{24,20},{5,9},{13,17},{21,25},... | collective-permute-start | bytes 491528 | tf_op jit(solution)/shard_map/ppermute | solution.py:90
  84.7 3.2 %input_grad.1 = (f32[8,128]{1,0:T(8,128)S(1)}, bf16[64,64,128]{2,1,0:T(8,128)(2,1)}, f32[2,64,16,128]{3,2,1,0:T(8,128)S(1)}) custom-call(s32[1]{0:T(128)} %bitcast.1.col_odd, bf16[64,64,128]{2,1,0:T(8,128)(2,1)S(1)} %get-tuple-element.83.tile.grad, bf16[4,64,128]{2,1,0:T(8,128)(2,1)S(1)} %collective-permute-done.12.col_first.first, ...), custom_call_target="tpu_custom_call" | custom-call | flops 603979776 | bytes 5451780 | tf_op jit(solution)/shard_map/input_grad/pallas_call | solution.py:31
  87.9 4.2 %collective-permute-done.27.row_second = bf16[10,64,128]{2,1,0:T(8,128)(2,1)S(1)} collective-permute-done((bf16[10,64,128]{2,1,0:T(8,128)(2,1)S(1)}, bf16[10,64,128]{2,1,0:T(8,128)(2,1)S(1)}, u32[]{:S(2)}, u32[]{:S(2)}) %collective-permute-start.27) | collective-permute-done | bytes 163872 | tf_op jit(solution)/shard_map/ppermute | solution.py:90
  92.1 0.2 collective-permute-done.21.refs_3_
  92.3 4.2 %collective-permute-done.19.refs_1_ = bf16[16,64,128]{2,1,0:T(8,128)(2,1)S(1)} collective-permute-done((bf16[16,64,128]{2,1,0:T(8,128)(2,1)S(1)}, bf16[16,64,128]{2,1,0:T(8,128)(2,1)S(1)}, u32[]{:S(2)}, u32[]{:S(2)}) %collective-permute-start.19) | collective-permute-done | bytes 262176 | tf_op jit(solution)/shard_map/ppermute | solution.py:367
  96.5 0.9 turn.3
  97.4 0.1 collective-permute-start.28
  97.5 0.5 collective-permute-start.29
  98.0 1.5 %input_grad_ends.1 = bf16[64,64,128]{2,1,0:T(8,128)(2,1)} custom-call(s32[1]{0:T(128)} %bitcast.row_odd, bf16[10,64,128]{2,1,0:T(8,128)(2,1)S(1)} %collective-permute-done.26.row_first, bf16[10,64,128]{2,1,0:T(8,128)(2,1)S(1)} %collective-permute-done.27.row_second, bf16[3,3,64,64]{3,2,1,0:T(8,128)(2,1)S(1)} %copy-done.4, ...), custom_call_target="tpu_custom_call", output_to_operand_aliasing={{}: (5, {})} | custom-call | bytes 3547140 | tf_op jit(solution)/shard_map/input_grad_ends/pallas_call | solution.py:31
  99.5 0.1 collective-permute-done.29.other
  99.5 0.8 unpack.1
  100.4 1.6 %join.1 = bf16[64,64,128]{2,1,0:T(8,128)(2,1)} custom-call(s32[1]{0:T(128)} %bitcast.row_odd, bf16[32,64,128]{2,1,0:T(8,128)(2,1)S(1)} %get-tuple-element.110.keep, bf16[32,64,128]{2,1,0:T(8,128)(2,1)S(1)} %collective-permute-done.28.got, bf16[16,64,128]{2,1,0:T(8,128)(2,1)S(1)} %get-tuple-element.96.refs_0_, ...), custom_call_target="tpu_custom_call" | custom-call | bytes 3145732 | tf_op jit(solution)/shard_map/join/pallas_call | solution.py:31
  (24 shorter events, 0.1 us)
Async XLA Ops:
  0.6 1.2 %copy-start = (bf16[64,64,128]{2,1,0:T(8,128)(2,1)S(1)}, bf16[64,64,128]{2,1,0:T(8,128)(2,1)}, u32[]{:S(2)}) copy-start(bf16[64,64,128]{2,1,0:T(8,128)(2,1)} %cot.5) | copy-start | bytes 3145732
  1.9 1.2 %copy-start.2 = (bf16[64,64,128]{2,1,0:T(8,128)(2,1)S(1)}, bf16[64,64,128]{2,1,0:T(8,128)(2,1)}, u32[]{:S(2)}) copy-start(bf16[64,64,128]{2,1,0:T(8,128)(2,1)} %x.1) | copy-start | bytes 3145732
  3.1 45.1 %copy-start.1 = (bf16[64,64,128]{2,1,0:T(8,128)(2,1)S(1)}, bf16[64,64,128]{2,1,0:T(8,128)(2,1)}, u32[]{:S(2)}) copy-start(bf16[64,64,128]{2,1,0:T(8,128)(2,1)} %cot.5) | copy-start | bytes 3145732
  4.0 16.4 %collective-permute-start.6 = (bf16[16,64,128]{2,1,0:T(8,128)(2,1)S(1)}, bf16[16,64,128]{2,1,0:T(8,128)(2,1)}, u32[]{:S(2)}, u32[]{:S(2)}) collective-permute-start(bf16[16,64,128]{2,1,0:T(8,128)(2,1)S(1)} %get-tuple-element.67), channel_id=1, source_target_pairs={{0,24},{4,28},{8,16},{12,20},{16,8},{20,12},{24,0},{28,4},{1,25},{... | collective-permute-start | bytes 786440 | tf_op jit(solution)/shard_map/ppermute | solution.py:357
  5.5 14.9 %collective-permute-start.4 = (bf16[16,64,128]{2,1,0:T(8,128)(2,1)S(1)}, bf16[16,64,128]{2,1,0:T(8,128)(2,1)}, u32[]{:S(2)}, u32[]{:S(2)}) collective-permute-start(bf16[16,64,128]{2,1,0:T(8,128)(2,1)S(1)} %get-tuple-element.65), channel_id=1, source_target_pairs={{0,16},{4,20},{8,24},{12,28},{16,0},{20,4},{24,8},{28,12},{1,17},{... | collective-permute-start | bytes 786440 | tf_op jit(solution)/shard_map/ppermute | solution.py:357
  7.0 14.9 %collective-permute-start.2 = (bf16[16,64,128]{2,1,0:T(8,128)(2,1)S(1)}, bf16[16,64,128]{2,1,0:T(8,128)(2,1)}, u32[]{:S(2)}, u32[]{:S(2)}) collective-permute-start(bf16[16,64,128]{2,1,0:T(8,128)(2,1)S(1)} %get-tuple-element.63), channel_id=1, source_target_pairs={{0,8},{4,12},{8,0},{12,4},{16,24},{20,28},{24,16},{28,20},{1,9},{5... | collective-permute-start | bytes 786440 | tf_op jit(solution)/shard_map/ppermute | solution.py:357
  7.6 5.1 %collective-permute-start = (bf16[4,64,128]{2,1,0:T(8,128)(2,1)S(1)}, bf16[4,64,128]{2,1,0:T(8,128)(2,1)S(1)}, u32[]{:S(2)}, u32[]{:S(2)}) collective-permute-start(bf16[4,64,128]{2,1,0:T(8,128)(2,1)S(1)} %get-tuple-element.61), channel_id=1, source_target_pairs={{0,1},{2,3},{1,0},{3,2},{4,5},{6,7},{5,4},{7,6},{8,9},{10,11},{9,8... | collective-permute-start | bytes 196616 | tf_op jit(solution)/shard_map/ppermute | solution.py:90
  8.0 6.8 %collective-permute-start.8 = (bf16[4,64,128]{2,1,0:T(8,128)(2,1)S(1)}, bf16[4,64,128]{2,1,0:T(8,128)(2,1)S(1)}, u32[]{:S(2)}, u32[]{:S(2)}) collective-permute-start(bf16[4,64,128]{2,1,0:T(8,128)(2,1)S(1)} %get-tuple-element.72), channel_id=1, source_target_pairs={{1,2},{2,1},{5,6},{6,5},{9,10},{10,9},{13,14},{14,13},{17,18},{18,... | collective-permute-start | bytes 196616 | tf_op jit(solution)/shard_map/ppermute | solution.py:90
  15.6 7.7 %collective-permute-start.9 = (bf16[10,64,128]{2,1,0:T(8,128)(2,1)S(1)}, bf16[10,64,128]{2,1,0:T(8,128)(2,1)S(1)}, u32[]{:S(2)}, u32[]{:S(2)}) collective-permute-start(bf16[10,64,128]{2,1,0:T(8,128)(2,1)S(1)} %get-tuple-element.73), channel_id=1, source_target_pairs={{0,4},{8,12},{16,20},{24,28},{4,0},{12,8},{20,16},{28,24},{1,5},{9... | collective-permute-start | bytes 491528 | tf_op jit(solution)/shard_map/ppermute | solution.py:90
  15.6 27.3 %collective-permute-start.1 = (bf16[16,64,128]{2,1,0:T(8,128)(2,1)}, bf16[16,64,128]{2,1,0:T(8,128)(2,1)S(1)}, u32[]{:S(2)}, u32[]{:S(2)}) collective-permute-start(bf16[16,64,128]{2,1,0:T(8,128)(2,1)} %get-tuple-element.62), channel_id=1, source_target_pairs={{0,0},{1,8},{2,16},{3,24},{4,4},{5,12},{6,20},{7,28},{8,1},{9,9},{... | collective-permute-start | bytes 786440 | tf_op jit(solution)/shard_map/ppermute | solution.py:367
  20.4 22.5 %collective-permute-start.7 = (bf16[16,64,128]{2,1,0:T(8,128)(2,1)}, bf16[16,64,128]{2,1,0:T(8,128)(2,1)S(1)}, u32[]{:S(2)}, u32[]{:S(2)}) collective-permute-start(bf16[16,64,128]{2,1,0:T(8,128)(2,1)} %collective-permute-done.6), channel_id=1, source_target_pairs={{0,3},{1,11},{2,19},{3,27},{4,7},{5,15},{6,23},{7,31},{8,2},{9,10}... | collective-permute-start | bytes 786440 | tf_op jit(solution)/shard_map/ppermute | solution.py:367
  20.4 24.8 %collective-permute-start.5 = (bf16[16,64,128]{2,1,0:T(8,128)(2,1)}, bf16[16,64,128]{2,1,0:T(8,128)(2,1)S(1)}, u32[]{:S(2)}, u32[]{:S(2)}) collective-permute-start(bf16[16,64,128]{2,1,0:T(8,128)(2,1)} %collective-permute-done.4), channel_id=1, source_target_pairs={{0,2},{1,10},{2,18},{3,26},{4,6},{5,14},{6,22},{7,30},{8,3},{9,11}... | collective-permute-start | bytes 786440 | tf_op jit(solution)/shard_map/ppermute | solution.py:367
  21.9 23.4 %collective-permute-start.3 = (bf16[16,64,128]{2,1,0:T(8,128)(2,1)}, bf16[16,64,128]{2,1,0:T(8,128)(2,1)S(1)}, u32[]{:S(2)}, u32[]{:S(2)}) collective-permute-start(bf16[16,64,128]{2,1,0:T(8,128)(2,1)} %collective-permute-done.2), channel_id=1, source_target_pairs={{0,1},{1,9},{2,17},{3,25},{4,5},{5,13},{6,21},{7,29},{8,0},{9,8},{... | collective-permute-start | bytes 786440 | tf_op jit(solution)/shard_map/ppermute | solution.py:367
  23.2 14.2 %collective-permute-start.10 = (bf16[10,64,128]{2,1,0:T(8,128)(2,1)}, bf16[10,64,128]{2,1,0:T(8,128)(2,1)}, u32[]{:S(2)}, u32[]{:S(2)}) collective-permute-start(bf16[10,64,128]{2,1,0:T(8,128)(2,1)} %get-tuple-element.75), channel_id=1, source_target_pairs={{4,8},{12,16},{20,24},{8,4},{16,12},{24,20},{5,9},{13,17},{21,25},... | collective-permute-start | bytes 491528 | tf_op jit(solution)/shard_map/ppermute | solution.py:90
  37.4 0.9 copy-start.3
  46.2 2.0 %collective-permute-start.11 = (bf16[32,64,128]{2,1,0:T(8,128)(2,1)S(1)}, bf16[32,64,128]{2,1,0:T(8,128)(2,1)S(1)}, u32[]{:S(2)}, u32[]{:S(2)}) collective-permute-start(bf16[32,64,128]{2,1,0:T(8,128)(2,1)S(1)} %get-tuple-element.82), channel_id=1, source_target_pairs={{0,4},{4,0},{8,12},{12,8},{16,20},{20,16},{24,28},{28,24},{1,5},{5... | collective-permute-start | bytes 1572872 | tf_op jit(solution)/shard_map/ppermute | solution.py:378
  46.3 8.7 %collective-permute-start.15 = (bf16[16,64,128]{2,1,0:T(8,128)(2,1)S(1)}, bf16[16,64,128]{2,1,0:T(8,128)(2,1)S(1)}, u32[]{:S(2)}, u32[]{:S(2)}) collective-permute-start(bf16[16,64,128]{2,1,0:T(8,128)(2,1)S(1)} %get-tuple-element.92.refs_1_), channel_id=1, source_target_pairs={{0,8},{4,12},{8,0},{12,4},{16,24},{20,28},{24,16},{28,20},{1,9},{5... | collective-permute-start | bytes 786440 | tf_op jit(solution)/shard_map/ppermute | solution.py:357
  46.4 15.1 %collective-permute-start.17 = (bf16[16,64,128]{2,1,0:T(8,128)(2,1)S(1)}, bf16[16,64,128]{2,1,0:T(8,128)(2,1)S(1)}, u32[]{:S(2)}, u32[]{:S(2)}) collective-permute-start(bf16[16,64,128]{2,1,0:T(8,128)(2,1)S(1)} %get-tuple-element.94.refs_2_), channel_id=1, source_target_pairs={{0,16},{4,20},{8,24},{12,28},{16,0},{20,4},{24,8},{28,12},{1,17},{... | collective-permute-start | bytes 786440 | tf_op jit(solution)/shard_map/ppermute | solution.py:357
  50.3 34.4 %copy-start.4 = (bf16[3,3,64,64]{3,2,1,0:T(8,128)(2,1)S(1)}, bf16[3,3,64,64]{3,2,1,0:T(8,128)(2,1)}, u32[]{:S(2)}) copy-start(bf16[3,3,64,64]{3,2,1,0:T(8,128)(2,1)} %weight.3) | copy-start | bytes 221188
  52.1 1.7 %collective-permute-start.14 = (f32[160,128]{1,0:T(8,128)S(1)}, f32[160,128]{1,0:T(8,128)S(1)}, u32[]{:S(2)}, u32[]{:S(2)}) collective-permute-start(f32[160,128]{1,0:T(8,128)S(1)} %get-tuple-element.91), channel_id=1, source_target_pairs={{0,4},{4,0},{8,12},{12,8},{16,20},{20,16},{24,28},{28,24},{1,5},{5... | collective-permute-start | bytes 245768 | tf_op jit(solution)/shard_map/ppermute | solution.py:378
  52.2 15.6 %collective-permute-start.22 = (bf16[16,64,128]{2,1,0:T(8,128)(2,1)S(1)}, bf16[16,64,128]{2,1,0:T(8,128)(2,1)S(1)}, u32[]{:S(2)}, u32[]{:S(2)}) collective-permute-start(bf16[16,64,128]{2,1,0:T(8,128)(2,1)S(1)} %get-tuple-element.99.refs_3_), channel_id=1, source_target_pairs={{0,24},{4,28},{8,16},{12,20},{16,8},{20,12},{24,0},{28,4},{1,25},{... | collective-permute-start | bytes 786440 | tf_op jit(solution)/shard_map/ppermute | solution.py:357
  55.0 6.4 %collective-permute-start.16 = (f32[160,128]{1,0:T(8,128)S(1)}, f32[160,128]{1,0:T(8,128)S(1)}, u32[]{:S(2)}, u32[]{:S(2)}) collective-permute-start(f32[160,128]{1,0:T(8,128)S(1)} %add.24), channel_id=1, source_target_pairs={{0,1},{1,0},{2,3},{3,2},{4,5},{5,4},{6,7},{7,6},{8,9},{9,8},{10,11... | collective-permute-start | bytes 245768 | tf_op jit(solution)/shard_map/ppermute | solution.py:468
  57.1 6.6 %collective-permute-start.12 = (bf16[4,64,128]{2,1,0:T(8,128)(2,1)S(1)}, bf16[4,64,128]{2,1,0:T(8,128)(2,1)S(1)}, u32[]{:S(2)}, u32[]{:S(2)}) collective-permute-start(bf16[4,64,128]{2,1,0:T(8,128)(2,1)S(1)} %get-tuple-element.84), channel_id=1, source_target_pairs={{0,1},{2,3},{1,0},{3,2},{4,5},{6,7},{5,4},{7,6},{8,9},{10,11},{9,8... | collective-permute-start | bytes 196616 | tf_op jit(solution)/shard_map/ppermute | solution.py:90
  57.1 7.3 %collective-permute-start.13 = (bf16[4,64,128]{2,1,0:T(8,128)(2,1)S(1)}, bf16[4,64,128]{2,1,0:T(8,128)(2,1)S(1)}, u32[]{:S(2)}, u32[]{:S(2)}) collective-permute-start(bf16[4,64,128]{2,1,0:T(8,128)(2,1)S(1)} %get-tuple-element.85), channel_id=1, source_target_pairs={{1,2},{2,1},{5,6},{6,5},{9,10},{10,9},{13,14},{14,13},{17,18},{18,... | collective-permute-start | bytes 196616 | tf_op jit(solution)/shard_map/ppermute | solution.py:90
  61.5 5.4 %collective-permute-start.18 = (f32[160,128]{1,0:T(8,128)S(1)}, f32[160,128]{1,0:T(8,128)S(1)}, u32[]{:S(2)}, u32[]{:S(2)}) collective-permute-start(f32[160,128]{1,0:T(8,128)S(1)} %add.25), channel_id=1, source_target_pairs={{0,2},{1,3},{2,0},{3,1},{4,6},{5,7},{6,4},{7,5},{8,10},{9,11},{10,... | collective-permute-start | bytes 245768 | tf_op jit(solution)/shard_map/ppermute | solution.py:397
  64.4 13.4 %collective-permute-start.26 = (bf16[10,64,128]{2,1,0:T(8,128)(2,1)S(1)}, bf16[10,64,128]{2,1,0:T(8,128)(2,1)S(1)}, u32[]{:S(2)}, u32[]{:S(2)}) collective-permute-start(bf16[10,64,128]{2,1,0:T(8,128)(2,1)S(1)} %get-tuple-element.103), channel_id=1, source_target_pairs={{0,4},{8,12},{16,20},{24,28},{4,0},{12,8},{20,16},{28,24},{1,5},{9... | collective-permute-start | bytes 491528 | tf_op jit(solution)/shard_map/ppermute | solution.py:90
  66.9 7.2 %collective-permute-start.24 = (f32[160,128]{1,0:T(8,128)S(1)}, f32[160,128]{1,0:T(8,128)S(1)}, u32[]{:S(2)}, u32[]{:S(2)}) collective-permute-start(f32[160,128]{1,0:T(8,128)S(1)} %add.26), channel_id=1, source_target_pairs={{0,8},{4,12},{8,0},{12,4},{16,24},{20,28},{24,16},{28,20},{1,9},{5... | collective-permute-start | bytes 245768 | tf_op jit(solution)/shard_map/ppermute | solution.py:397
  67.8 24.3 %collective-permute-start.23 = (bf16[16,64,128]{2,1,0:T(8,128)(2,1)S(1)}, bf16[16,64,128]{2,1,0:T(8,128)(2,1)S(1)}, u32[]{:S(2)}, u32[]{:S(2)}) collective-permute-start(bf16[16,64,128]{2,1,0:T(8,128)(2,1)S(1)} %collective-permute-done.22), channel_id=1, source_target_pairs={{0,3},{1,11},{2,19},{3,27},{4,7},{5,15},{6,23},{7,31},{8,2},{9,10}... | collective-permute-start | bytes 786440 | tf_op jit(solution)/shard_map/ppermute | solution.py:367
  68.5 23.8 %collective-permute-start.21 = (bf16[16,64,128]{2,1,0:T(8,128)(2,1)S(1)}, bf16[16,64,128]{2,1,0:T(8,128)(2,1)S(1)}, u32[]{:S(2)}, u32[]{:S(2)}) collective-permute-start(bf16[16,64,128]{2,1,0:T(8,128)(2,1)S(1)} %collective-permute-done.17), channel_id=1, source_target_pairs={{0,2},{1,10},{2,18},{3,26},{4,6},{5,14},{6,22},{7,30},{8,3},{9,11}... | collective-permute-start | bytes 786440 | tf_op jit(solution)/shard_map/ppermute | solution.py:367
  71.3 21.0 %collective-permute-start.20 = (bf16[16,64,128]{2,1,0:T(8,128)(2,1)S(1)}, bf16[16,64,128]{2,1,0:T(8,128)(2,1)S(1)}, u32[]{:S(2)}, u32[]{:S(2)}) collective-permute-start(bf16[16,64,128]{2,1,0:T(8,128)(2,1)S(1)} %collective-permute-done.15), channel_id=1, source_target_pairs={{0,1},{1,9},{2,17},{3,25},{4,5},{5,13},{6,21},{7,29},{8,0},{9,8},{... | collective-permute-start | bytes 786440 | tf_op jit(solution)/shard_map/ppermute | solution.py:367
  74.1 22.4 %collective-permute-start.19 = (bf16[16,64,128]{2,1,0:T(8,128)(2,1)S(1)}, bf16[16,64,128]{2,1,0:T(8,128)(2,1)S(1)}, u32[]{:S(2)}, u32[]{:S(2)}) collective-permute-start(bf16[16,64,128]{2,1,0:T(8,128)(2,1)S(1)} %get-tuple-element.96.refs_0_), channel_id=1, source_target_pairs={{0,0},{1,8},{2,16},{3,24},{4,4},{5,12},{6,20},{7,28},{8,1},{9,9},{... | collective-permute-start | bytes 786440 | tf_op jit(solution)/shard_map/ppermute | solution.py:367
  77.9 4.7 %collective-permute-start.25 = (f32[160,128]{1,0:T(8,128)S(1)}, f32[160,128]{1,0:T(8,128)S(1)}, u32[]{:S(2)}, u32[]{:S(2)}) collective-permute-start(f32[160,128]{1,0:T(8,128)S(1)} %add.27), channel_id=1, source_target_pairs={{0,16},{4,20},{8,24},{12,28},{16,0},{20,4},{24,8},{28,12},{1,17},{... | collective-permute-start | bytes 245768 | tf_op jit(solution)/shard_map/ppermute | solution.py:397
  82.6 9.5 %collective-permute-start.27 = (bf16[10,64,128]{2,1,0:T(8,128)(2,1)S(1)}, bf16[10,64,128]{2,1,0:T(8,128)(2,1)S(1)}, u32[]{:S(2)}, u32[]{:S(2)}) collective-permute-start(bf16[10,64,128]{2,1,0:T(8,128)(2,1)S(1)} %get-tuple-element.105), channel_id=1, source_target_pairs={{4,8},{12,16},{20,24},{8,4},{16,12},{24,20},{5,9},{13,17},{21,25},... | collective-permute-start | bytes 491528 | tf_op jit(solution)/shard_map/ppermute | solution.py:90
  97.4 2.9 %collective-permute-start.28 = (bf16[32,64,128]{2,1,0:T(8,128)(2,1)S(1)}, bf16[32,64,128]{2,1,0:T(8,128)(2,1)S(1)}, u32[]{:S(2)}, u32[]{:S(2)}) collective-permute-start(bf16[32,64,128]{2,1,0:T(8,128)(2,1)S(1)} %get-tuple-element.111), channel_id=1, source_target_pairs={{0,4},{4,0},{8,12},{12,8},{16,20},{20,16},{24,28},{28,24},{1,5},{5... | collective-permute-start | bytes 1572872 | tf_op jit(solution)/shard_map/ppermute | solution.py:378
  97.5 2.0 %collective-permute-start.29 = (f32[160,128]{1,0:T(8,128)S(1)}, f32[160,128]{1,0:T(8,128)S(1)}, u32[]{:S(2)}, u32[]{:S(2)}) collective-permute-start(f32[160,128]{1,0:T(8,128)S(1)} %add.28.mine), channel_id=1, source_target_pairs={{0,4},{4,0},{8,12},{12,8},{16,20},{20,16},{24,28},{28,24},{1,5},{5... | collective-permute-start | bytes 245768 | tf_op jit(solution)/shard_map/ppermute | solution.py:378

commit v7 on v6

--- a/solution.py
+++ b/solution.py
@@ -202,7 +202,10 @@
     group = pieces[0].shape[0]
     tile_rows = tile.shape[0]
     write_shifted(row_odd, col_odd, tile, *halo, stack)
-    offset = bias[...]
+    channels = bias.shape[1]
+    line = lax.broadcasted_iota(jnp.int32, (channels, channels), 0)
+    lane = lax.broadcasted_iota(jnp.int32, (channels, channels), 1)
+    offset = jnp.sum(jnp.where(line == lane, bias[...], 0.0), axis=1, keepdims=True)
 
     def emit(row, total):
         pre_act = total + offset
@@ -433,7 +436,7 @@
         tile,
         *halo,
         conv_weight,
-        conv_bias[:, None],
+        conv_bias[None],
         scratch=[pltpu.VMEM((tile_rows, channels, tile_cols), BF16)],
         flops=conv_flops,
         name="forward",

time: 104 us -> 104 us (level)
  Pallas kernels: 19 us -> 17.5 us
  waiting for transfers between devices: 35.8 us -> 37.1 us
    ppermute x8, waiting for transfers between devices: 6.83 us -> 8.37 us  [cross(): return lax.ppermute(piece, ('row', 'col'), owners)]
    pallas_call x12, Pallas kernels: 19 us -> 17.5 us  [call(): pl.pallas_call(kernel, out_shape=out_shape, in_specs=in_specs, out_specs=...]
    unnamed x10 -> x12, local copies, waits for them, and re-layouts: 3.36 us -> 4.01 us
  transfers between devices with their start and end apart: 30 -> 30, of which waited for: 13 -> 14; matrix products, arithmetic and copies ran while one was open for 1% -> 0% of each run, Pallas kernels for 14% -> 13%
where the time goes in v7:
time: 104 us; the launch traced here: 102 us
  starting transfers between devices  42.6 us (41%)
  waiting for transfers between devices  37.1 us (36%)
  Pallas kernels  17.5 us (17%)
  local copies, waits for them, and re-layouts  4.01 us (4%)
    ppermute x8, waiting for transfers between devices, exchanged(): return lax.ppermute(x, axis, pairs + [(j, i) for i, j in pairs])  18.1 us
    pallas_call x12, Pallas kernels, call(): pl.pallas_call(kernel, out_shape=out_shape, in_specs=in_specs, out_specs=...  17.5 us
    ppermute x8, starting transfers between devices, cross(): return lax.ppermute(piece, ('row', 'col'), owners)  16.8 us
    ppermute x8, starting transfers between devices, exchanged(): return lax.ppermute(x, axis, pairs + [(j, i) for i, j in pairs])  13.2 us
    ppermute x8, waiting for transfers between devices, cross(): return lax.ppermute(piece, ('row', 'col'), owners)  8.37 us
    ppermute x3, waiting for transfers between devices, summed(): lax.ppermute(part, axis, [(i, i ^ reach) for i in range(size)])  7.65 us
    ppermute x6, starting transfers between devices, detour(): lax.ppermute(piece, 'row', [(r, r ^ 2 * far) for r in range(lax.axis_size...  5.32 us
    unnamed x12, local copies, waits for them, and re-layouts  4.01 us
  transfers between devices with their start and end apart: 30, of which 14 were waited for; matrix products, arithmetic and copies ran while one was open for 0% of the time, Pallas kernels for 13%

profile of v7, /device:TPU:12, one launch (start us, length us, event | category | flops | bytes accessed | tf_op | source)
XLA Modules:
  0.0 102.1 jit_solution(11823940934220243803)
XLA Ops:
  0.7 1.2 %copy-done = bf16[64,64,128]{2,1,0:T(8,128)(2,1)S(1)} copy-done((bf16[64,64,128]{2,1,0:T(8,128)(2,1)S(1)}, bf16[64,64,128]{2,1,0:T(8,128)(2,1)}, u32[]{:S(2)}) %copy-start) | copy-done | bytes 1048600
  1.9 1.2 %copy-done.2 = bf16[64,64,128]{2,1,0:T(8,128)(2,1)S(1)} copy-done((bf16[64,64,128]{2,1,0:T(8,128)(2,1)S(1)}, bf16[64,64,128]{2,1,0:T(8,128)(2,1)}, u32[]{:S(2)}) %copy-start.2) | copy-done | bytes 1048600
  3.1 0.9 open.1
  4.0 1.5 %collective-permute-start.6 = (bf16[16,64,128]{2,1,0:T(8,128)(2,1)S(1)}, bf16[16,64,128]{2,1,0:T(8,128)(2,1)S(1)}, u32[]{:S(2)}, u32[]{:S(2)}) collective-permute-start(bf16[16,64,128]{2,1,0:T(8,128)(2,1)S(1)} %get-tuple-element.67), channel_id=1, source_target_pairs={{0,24},{4,28},{8,16},{12,20},{16,8},{20,12},{24,0},{28,4},{1,25},{... | collective-permute-start | bytes 786440 | tf_op jit(solution)/shard_map/ppermute | solution.py:360
  5.5 1.5 %collective-permute-start.4 = (bf16[16,64,128]{2,1,0:T(8,128)(2,1)S(1)}, bf16[16,64,128]{2,1,0:T(8,128)(2,1)S(1)}, u32[]{:S(2)}, u32[]{:S(2)}) collective-permute-start(bf16[16,64,128]{2,1,0:T(8,128)(2,1)S(1)} %get-tuple-element.65), channel_id=1, source_target_pairs={{0,16},{4,20},{8,24},{12,28},{16,0},{20,4},{24,8},{28,12},{1,17},{... | collective-permute-start | bytes 786440 | tf_op jit(solution)/shard_map/ppermute | solution.py:360
  7.0 0.5 collective-permute-start.2
  7.6 0.4 collective-permute-start
  8.0 4.6 %collective-permute-start.8 = (bf16[4,64,128]{2,1,0:T(8,128)(2,1)S(1)}, bf16[4,64,128]{2,1,0:T(8,128)(2,1)S(1)}, u32[]{:S(2)}, u32[]{:S(2)}) collective-permute-start(bf16[4,64,128]{2,1,0:T(8,128)(2,1)S(1)} %get-tuple-element.72), channel_id=1, source_target_pairs={{1,2},{2,1},{5,6},{6,5},{9,10},{10,9},{13,14},{14,13},{17,18},{18,... | collective-permute-start | bytes 196616 | tf_op jit(solution)/shard_map/ppermute | solution.py:90
  12.6 0.0 collective-permute-done.first.refs_2_
  12.7 2.2 %collective-permute-done.8.second.refs_3_ = bf16[4,64,128]{2,1,0:T(8,128)(2,1)S(1)} collective-permute-done((bf16[4,64,128]{2,1,0:T(8,128)(2,1)S(1)}, bf16[4,64,128]{2,1,0:T(8,128)(2,1)S(1)}, u32[]{:S(2)}, u32[]{:S(2)}) %collective-permute-start.8) | collective-permute-done | bytes 65568 | tf_op jit(solution)/shard_map/ppermute | solution.py:90
  14.9 0.1 messages.2
  14.9 0.1 collective-permute-start.9
  15.0 4.8 %collective-permute-start.1 = (bf16[16,64,128]{2,1,0:T(8,128)(2,1)S(1)}, bf16[16,64,128]{2,1,0:T(8,128)(2,1)S(1)}, u32[]{:S(2)}, u32[]{:S(2)}) collective-permute-start(bf16[16,64,128]{2,1,0:T(8,128)(2,1)S(1)} %get-tuple-element.62), channel_id=1, source_target_pairs={{0,0},{1,8},{2,16},{3,24},{4,4},{5,12},{6,20},{7,28},{8,1},{9,9},{... | collective-permute-start | bytes 786440 | tf_op jit(solution)/shard_map/ppermute | solution.py:370
  19.8 0.1 collective-permute-start.7
  19.9 0.0 collective-permute-done.4
  19.9 1.4 %collective-permute-start.5 = (bf16[16,64,128]{2,1,0:T(8,128)(2,1)S(1)}, bf16[16,64,128]{2,1,0:T(8,128)(2,1)S(1)}, u32[]{:S(2)}, u32[]{:S(2)}) collective-permute-start(bf16[16,64,128]{2,1,0:T(8,128)(2,1)S(1)} %collective-permute-done.4), channel_id=1, source_target_pairs={{0,2},{1,10},{2,18},{3,26},{4,6},{5,14},{6,22},{7,30},{8,3},{9,11}... | collective-permute-start | bytes 786440 | tf_op jit(solution)/shard_map/ppermute | solution.py:370
  21.3 0.0 collective-permute-done.2
  21.3 1.9 %collective-permute-start.3 = (bf16[16,64,128]{2,1,0:T(8,128)(2,1)S(1)}, bf16[16,64,128]{2,1,0:T(8,128)(2,1)S(1)}, u32[]{:S(2)}, u32[]{:S(2)}) collective-permute-start(bf16[16,64,128]{2,1,0:T(8,128)(2,1)S(1)} %collective-permute-done.2), channel_id=1, source_target_pairs={{0,1},{1,9},{2,17},{3,25},{4,5},{5,13},{6,21},{7,29},{8,0},{9,8},{... | collective-permute-start | bytes 786440 | tf_op jit(solution)/shard_map/ppermute | solution.py:370
  23.2 1.9 %collective-permute-start.10 = (bf16[10,64,128]{2,1,0:T(8,128)(2,1)S(1)}, bf16[10,64,128]{2,1,0:T(8,128)(2,1)S(1)}, u32[]{:S(2)}, u32[]{:S(2)}) collective-permute-start(bf16[10,64,128]{2,1,0:T(8,128)(2,1)S(1)} %get-tuple-element.75), channel_id=1, source_target_pairs={{4,8},{12,16},{20,24},{8,4},{16,12},{24,20},{5,9},{13,17},{21,25},... | collective-permute-start | bytes 491528 | tf_op jit(solution)/shard_map/ppermute | solution.py:90
  25.2 11.3 %collective-permute-done.10.refs_1_ = bf16[10,64,128]{2,1,0:T(8,128)(2,1)S(1)} collective-permute-done((bf16[10,64,128]{2,1,0:T(8,128)(2,1)S(1)}, bf16[10,64,128]{2,1,0:T(8,128)(2,1)S(1)}, u32[]{:S(2)}, u32[]{:S(2)}) %collective-permute-start.10) | collective-permute-done | bytes 163872 | tf_op jit(solution)/shard_map/ppermute | solution.py:90
  36.5 0.9 copy-done.3
  37.4 0.7 copy-done.5
  38.0 3.7 %forward.1 = (f32[8,128]{1,0:T(8,128)}, bf16[80,192,128]{2,1,0:T(8,128)(2,1)S(1)}, f32[64,64,128]{2,1,0:T(8,128)S(1)}, bf16[16,64,128]{2,1,0:T(8,128)(2,1)S(1)},...) custom-call(s32[1]{0:T(128)} %bitcast.row_odd, ...), custom_call_target="tpu_custom_call" | custom-call | flops 603979776 | bytes 8663304 | tf_op jit(solution)/shard_map/forward/pallas_call | solution.py:31
  41.7 0.0 collective-permute-done.1.refs_0_
  41.7 2.8 %collective-permute-done.5.refs_2_ = bf16[16,64,128]{2,1,0:T(8,128)(2,1)S(1)} collective-permute-done((bf16[16,64,128]{2,1,0:T(8,128)(2,1)S(1)}, bf16[16,64,128]{2,1,0:T(8,128)(2,1)S(1)}, u32[]{:S(2)}, u32[]{:S(2)}) %collective-permute-start.5) | collective-permute-done | bytes 262176 | tf_op jit(solution)/shard_map/ppermute | solution.py:370
  44.5 0.9 turn.2
  45.4 0.1 collective-permute-start.11
  45.5 0.0 collective-permute-start.15
  45.6 0.2 collective-permute-start.17
  45.8 1.6 %collective-permute-done.11.got = bf16[32,64,128]{2,1,0:T(8,128)(2,1)S(1)} collective-permute-done((bf16[32,64,128]{2,1,0:T(8,128)(2,1)S(1)}, bf16[32,64,128]{2,1,0:T(8,128)(2,1)S(1)}, u32[]{:S(2)}, u32[]{:S(2)}) %collective-permute-start.11) | collective-permute-done | bytes 524320 | tf_op jit(solution)/shard_map/ppermute | solution.py:381
  47.4 2.1 %grad_pre.1 = (f32[8,128]{1,0:T(8,128)}, bf16[64,64,128]{2,1,0:T(8,128)(2,1)S(1)}, bf16[8,64,128]{2,1,0:T(8,128)(2,1)S(1)}, bf16[8,64,128]{2,1,0:T(8,128)(2,1)S(...) custom-call(s32[1]{0:T(128)} %bitcast.row_odd, ...), custom_call_target="tpu_custom_call" | custom-call | bytes 6688776 | tf_op jit(solution)/shard_map/grad_pre/pallas_call | solution.py:31
  49.5 1.8 %weight_terms.1 = (f32[8,128]{1,0:T(8,128)}, f32[160,128]{1,0:T(8,128)S(1)}, f32[160,128]{1,0:T(8,128)S(1)}) custom-call(s32[1]{0:T(128)} %bitcast.row_odd, bf16[64,64,128]{2,1,0:T(8,128)(2,1)S(1)} %get-tuple-element.83.tile.grad, bf16[80,192,128]{2,1,0:T(8,128)(2,1)S(1)} %get-tuple-element.89.stack), custom_call_target="tpu_custom_call" | custom-call | flops 603979776 | bytes 5148676 | tf_op jit(solution)/shard_map/weight_terms/pallas_call | solution.py:31
  51.3 0.1 collective-permute-start.14
  51.5 1.5 %collective-permute-start.22 = (bf16[16,64,128]{2,1,0:T(8,128)(2,1)S(1)}, bf16[16,64,128]{2,1,0:T(8,128)(2,1)S(1)}, u32[]{:S(2)}, u32[]{:S(2)}) collective-permute-start(bf16[16,64,128]{2,1,0:T(8,128)(2,1)S(1)} %get-tuple-element.99.refs_3_), channel_id=1, source_target_pairs={{0,24},{4,28},{8,16},{12,20},{16,8},{20,12},{24,0},{28,4},{1,25},{... | collective-permute-start | bytes 786440 | tf_op jit(solution)/shard_map/ppermute | solution.py:360
  53.0 1.2 %collective-permute-done.15 = bf16[16,64,128]{2,1,0:T(8,128)(2,1)S(1)} collective-permute-done((bf16[16,64,128]{2,1,0:T(8,128)(2,1)S(1)}, bf16[16,64,128]{2,1,0:T(8,128)(2,1)S(1)}, u32[]{:S(2)}, u32[]{:S(2)}) %collective-permute-start.15) | collective-permute-done | bytes 262176 | tf_op jit(solution)/shard_map/ppermute | solution.py:360
  54.2 2.1 %collective-permute-start.16 = (f32[160,128]{1,0:T(8,128)S(1)}, f32[160,128]{1,0:T(8,128)S(1)}, u32[]{:S(2)}, u32[]{:S(2)}) collective-permute-start(f32[160,128]{1,0:T(8,128)S(1)} %add.24), channel_id=1, source_target_pairs={{0,1},{1,0},{2,3},{3,2},{4,5},{5,4},{6,7},{7,6},{8,9},{9,8},{10,11... | collective-permute-start | bytes 245768 | tf_op jit(solution)/shard_map/ppermute | solution.py:471
  56.3 0.0 collective-permute-start.12
  56.4 4.0 %collective-permute-start.13 = (bf16[4,64,128]{2,1,0:T(8,128)(2,1)S(1)}, bf16[4,64,128]{2,1,0:T(8,128)(2,1)S(1)}, u32[]{:S(2)}, u32[]{:S(2)}) collective-permute-start(bf16[4,64,128]{2,1,0:T(8,128)(2,1)S(1)} %get-tuple-element.85), channel_id=1, source_target_pairs={{1,2},{2,1},{5,6},{6,5},{9,10},{10,9},{13,14},{14,13},{17,18},{18,... | collective-permute-start | bytes 196616 | tf_op jit(solution)/shard_map/ppermute | solution.py:90
  60.4 2.2 %collective-permute-start.18 = (f32[160,128]{1,0:T(8,128)S(1)}, f32[160,128]{1,0:T(8,128)S(1)}, u32[]{:S(2)}, u32[]{:S(2)}) collective-permute-start(f32[160,128]{1,0:T(8,128)S(1)} %add.25), channel_id=1, source_target_pairs={{0,2},{1,3},{2,0},{3,1},{4,6},{5,7},{6,4},{7,5},{8,10},{9,11},{10,... | collective-permute-start | bytes 245768 | tf_op jit(solution)/shard_map/ppermute | solution.py:400
  62.6 1.5 %collective-permute-done.13.col_second.second = bf16[4,64,128]{2,1,0:T(8,128)(2,1)S(1)} collective-permute-done((bf16[4,64,128]{2,1,0:T(8,128)(2,1)S(1)}, bf16[4,64,128]{2,1,0:T(8,128)(2,1)S(1)}, u32[]{:S(2)}, u32[]{:S(2)}) %collective-permute-start.13) | collective-permute-done | bytes 65568 | tf_op jit(solution)/shard_map/ppermute | solution.py:90
  64.2 0.1 messages.3
  64.2 0.1 collective-permute-start.26
  64.3 1.6 %collective-permute-done.18 = f32[160,128]{1,0:T(8,128)S(1)} collective-permute-done((f32[160,128]{1,0:T(8,128)S(1)}, f32[160,128]{1,0:T(8,128)S(1)}, u32[]{:S(2)}, u32[]{:S(2)}) %collective-permute-start.18) | collective-permute-done | bytes 81952 | tf_op jit(solution)/shard_map/ppermute | solution.py:400
  65.9 1.1 %collective-permute-start.24 = (f32[160,128]{1,0:T(8,128)S(1)}, f32[160,128]{1,0:T(8,128)S(1)}, u32[]{:S(2)}, u32[]{:S(2)}) collective-permute-start(f32[160,128]{1,0:T(8,128)S(1)} %add.26), channel_id=1, source_target_pairs={{0,8},{4,12},{8,0},{12,4},{16,24},{20,28},{24,16},{28,20},{1,9},{5... | collective-permute-start | bytes 245768 | tf_op jit(solution)/shard_map/ppermute | solution.py:400
  67.0 0.5 collective-permute-start.23
  67.5 3.0 %collective-permute-start.21 = (bf16[16,64,128]{2,1,0:T(8,128)(2,1)S(1)}, bf16[16,64,128]{2,1,0:T(8,128)(2,1)S(1)}, u32[]{:S(2)}, u32[]{:S(2)}) collective-permute-start(bf16[16,64,128]{2,1,0:T(8,128)(2,1)S(1)} %collective-permute-done.17), channel_id=1, source_target_pairs={{0,2},{1,10},{2,18},{3,26},{4,6},{5,14},{6,22},{7,30},{8,3},{9,11}... | collective-permute-start | bytes 786440 | tf_op jit(solution)/shard_map/ppermute | solution.py:370
  70.5 2.2 %collective-permute-start.20 = (bf16[16,64,128]{2,1,0:T(8,128)(2,1)S(1)}, bf16[16,64,128]{2,1,0:T(8,128)(2,1)S(1)}, u32[]{:S(2)}, u32[]{:S(2)}) collective-permute-start(bf16[16,64,128]{2,1,0:T(8,128)(2,1)S(1)} %collective-permute-done.15), channel_id=1, source_target_pairs={{0,1},{1,9},{2,17},{3,25},{4,5},{5,13},{6,21},{7,29},{8,0},{9,8},{... | collective-permute-start | bytes 786440 | tf_op jit(solution)/shard_map/ppermute | solution.py:370
  72.7 1.4 %collective-permute-done.24 = f32[160,128]{1,0:T(8,128)S(1)} collective-permute-done((f32[160,128]{1,0:T(8,128)S(1)}, f32[160,128]{1,0:T(8,128)S(1)}, u32[]{:S(2)}, u32[]{:S(2)}) %collective-permute-start.24) | collective-permute-done | bytes 81952 | tf_op jit(solution)/shard_map/ppermute | solution.py:400
  74.1 3.0 %collective-permute-start.19 = (bf16[16,64,128]{2,1,0:T(8,128)(2,1)S(1)}, bf16[16,64,128]{2,1,0:T(8,128)(2,1)S(1)}, u32[]{:S(2)}, u32[]{:S(2)}) collective-permute-start(bf16[16,64,128]{2,1,0:T(8,128)(2,1)S(1)} %get-tuple-element.96.refs_0_), channel_id=1, source_target_pairs={{0,0},{1,8},{2,16},{3,24},{4,4},{5,12},{6,20},{7,28},{8,1},{9,9},{... | collective-permute-start | bytes 786440 | tf_op jit(solution)/shard_map/ppermute | solution.py:370
  77.1 0.1 collective-permute-start.25
  77.2 4.6 %collective-permute-done.25 = f32[160,128]{1,0:T(8,128)S(1)} collective-permute-done((f32[160,128]{1,0:T(8,128)S(1)}, f32[160,128]{1,0:T(8,128)S(1)}, u32[]{:S(2)}, u32[]{:S(2)}) %collective-permute-start.25) | collective-permute-done | bytes 81952 | tf_op jit(solution)/shard_map/ppermute | solution.py:400
  81.8 2.1 %collective-permute-start.27 = (bf16[10,64,128]{2,1,0:T(8,128)(2,1)S(1)}, bf16[10,64,128]{2,1,0:T(8,128)(2,1)S(1)}, u32[]{:S(2)}, u32[]{:S(2)}) collective-permute-start(bf16[10,64,128]{2,1,0:T(8,128)(2,1)S(1)} %get-tuple-element.105), channel_id=1, source_target_pairs={{4,8},{12,16},{20,24},{8,4},{16,12},{24,20},{5,9},{13,17},{21,25},... | collective-permute-start | bytes 491528 | tf_op jit(solution)/shard_map/ppermute | solution.py:90
  83.9 3.2 %input_grad.1 = (f32[8,128]{1,0:T(8,128)S(1)}, bf16[64,64,128]{2,1,0:T(8,128)(2,1)}, f32[2,64,16,128]{3,2,1,0:T(8,128)S(1)}) custom-call(s32[1]{0:T(128)} %bitcast.1.col_odd, bf16[64,64,128]{2,1,0:T(8,128)(2,1)S(1)} %get-tuple-element.83.tile.grad, bf16[4,64,128]{2,1,0:T(8,128)(2,1)S(1)} %collective-permute-done.12.col_first.first, ...), custom_call_target="tpu_custom_call" | custom-call | flops 603979776 | bytes 5451780 | tf_op jit(solution)/shard_map/input_grad/pallas_call | solution.py:31
  87.1 3.1 %collective-permute-done.27.row_second = bf16[10,64,128]{2,1,0:T(8,128)(2,1)S(1)} collective-permute-done((bf16[10,64,128]{2,1,0:T(8,128)(2,1)S(1)}, bf16[10,64,128]{2,1,0:T(8,128)(2,1)S(1)}, u32[]{:S(2)}, u32[]{:S(2)}) %collective-permute-start.27) | collective-permute-done | bytes 163872 | tf_op jit(solution)/shard_map/ppermute | solution.py:90
  90.2 1.0 collective-permute-done.21.refs_3_
  91.1 0.2 collective-permute-done.20.refs_2_
  91.3 4.4 %collective-permute-done.19.refs_1_ = bf16[16,64,128]{2,1,0:T(8,128)(2,1)S(1)} collective-permute-done((bf16[16,64,128]{2,1,0:T(8,128)(2,1)S(1)}, bf16[16,64,128]{2,1,0:T(8,128)(2,1)S(1)}, u32[]{:S(2)}, u32[]{:S(2)}) %collective-permute-start.19) | collective-permute-done | bytes 262176 | tf_op jit(solution)/shard_map/ppermute | solution.py:370
  95.7 0.9 turn.3
  96.6 1.4 %collective-permute-start.28 = (bf16[32,64,128]{2,1,0:T(8,128)(2,1)S(1)}, bf16[32,64,128]{2,1,0:T(8,128)(2,1)S(1)}, u32[]{:S(2)}, u32[]{:S(2)}) collective-permute-start(bf16[32,64,128]{2,1,0:T(8,128)(2,1)S(1)} %get-tuple-element.111), channel_id=1, source_target_pairs={{0,4},{4,0},{8,12},{12,8},{16,20},{20,16},{24,28},{28,24},{1,5},{5... | collective-permute-start | bytes 1572872 | tf_op jit(solution)/shard_map/ppermute | solution.py:381
  98.1 0.1 collective-permute-start.29
  98.1 1.5 %input_grad_ends.1 = bf16[64,64,128]{2,1,0:T(8,128)(2,1)} custom-call(s32[1]{0:T(128)} %bitcast.row_odd, bf16[10,64,128]{2,1,0:T(8,128)(2,1)S(1)} %collective-permute-done.26.row_first, bf16[10,64,128]{2,1,0:T(8,128)(2,1)S(1)} %collective-permute-done.27.row_second, bf16[3,3,64,64]{3,2,1,0:T(8,128)(2,1)S(1)} %copy-done.4, ...), custom_call_target="tpu_custom_call", output_to_operand_aliasing={{}: (5, {})} | custom-call | bytes 3547140 | tf_op jit(solution)/shard_map/input_grad_ends/pallas_call | solution.py:31
  99.6 0.1 collective-permute-done.29.other
  99.7 0.8 unpack.1
  100.6 1.6 %join.1 = bf16[64,64,128]{2,1,0:T(8,128)(2,1)} custom-call(s32[1]{0:T(128)} %bitcast.row_odd, bf16[32,64,128]{2,1,0:T(8,128)(2,1)S(1)} %get-tuple-element.110.keep, bf16[32,64,128]{2,1,0:T(8,128)(2,1)S(1)} %collective-permute-done.28.got, bf16[16,64,128]{2,1,0:T(8,128)(2,1)S(1)} %get-tuple-element.96.refs_0_, ...), custom_call_target="tpu_custom_call" | custom-call | bytes 3145732 | tf_op jit(solution)/shard_map/join/pallas_call | solution.py:31
  (25 shorter events, 0.1 us)
Async XLA Ops:
  0.6 1.2 %copy-start = (bf16[64,64,128]{2,1,0:T(8,128)(2,1)S(1)}, bf16[64,64,128]{2,1,0:T(8,128)(2,1)}, u32[]{:S(2)}) copy-start(bf16[64,64,128]{2,1,0:T(8,128)(2,1)} %cot.5) | copy-start | bytes 3145732
  1.9 1.2 %copy-start.2 = (bf16[64,64,128]{2,1,0:T(8,128)(2,1)S(1)}, bf16[64,64,128]{2,1,0:T(8,128)(2,1)}, u32[]{:S(2)}) copy-start(bf16[64,64,128]{2,1,0:T(8,128)(2,1)} %x.1) | copy-start | bytes 3145732
  3.1 44.3 %copy-start.1 = (bf16[64,64,128]{2,1,0:T(8,128)(2,1)S(1)}, bf16[64,64,128]{2,1,0:T(8,128)(2,1)}, u32[]{:S(2)}) copy-start(bf16[64,64,128]{2,1,0:T(8,128)(2,1)} %cot.5) | copy-start | bytes 3145732
  4.0 15.8 %collective-permute-start.6 = (bf16[16,64,128]{2,1,0:T(8,128)(2,1)S(1)}, bf16[16,64,128]{2,1,0:T(8,128)(2,1)S(1)}, u32[]{:S(2)}, u32[]{:S(2)}) collective-permute-start(bf16[16,64,128]{2,1,0:T(8,128)(2,1)S(1)} %get-tuple-element.67), channel_id=1, source_target_pairs={{0,24},{4,28},{8,16},{12,20},{16,8},{20,12},{24,0},{28,4},{1,25},{... | collective-permute-start | bytes 786440 | tf_op jit(solution)/shard_map/ppermute | solution.py:360
  5.5 14.4 %collective-permute-start.4 = (bf16[16,64,128]{2,1,0:T(8,128)(2,1)S(1)}, bf16[16,64,128]{2,1,0:T(8,128)(2,1)S(1)}, u32[]{:S(2)}, u32[]{:S(2)}) collective-permute-start(bf16[16,64,128]{2,1,0:T(8,128)(2,1)S(1)} %get-tuple-element.65), channel_id=1, source_target_pairs={{0,16},{4,20},{8,24},{12,28},{16,0},{20,4},{24,8},{28,12},{1,17},{... | collective-permute-start | bytes 786440 | tf_op jit(solution)/shard_map/ppermute | solution.py:360
  7.0 14.3 %collective-permute-start.2 = (bf16[16,64,128]{2,1,0:T(8,128)(2,1)S(1)}, bf16[16,64,128]{2,1,0:T(8,128)(2,1)S(1)}, u32[]{:S(2)}, u32[]{:S(2)}) collective-permute-start(bf16[16,64,128]{2,1,0:T(8,128)(2,1)S(1)} %get-tuple-element.63), channel_id=1, source_target_pairs={{0,8},{4,12},{8,0},{12,4},{16,24},{20,28},{24,16},{28,20},{1,9},{5... | collective-permute-start | bytes 786440 | tf_op jit(solution)/shard_map/ppermute | solution.py:360
  7.6 5.1 %collective-permute-start = (bf16[4,64,128]{2,1,0:T(8,128)(2,1)S(1)}, bf16[4,64,128]{2,1,0:T(8,128)(2,1)S(1)}, u32[]{:S(2)}, u32[]{:S(2)}) collective-permute-start(bf16[4,64,128]{2,1,0:T(8,128)(2,1)S(1)} %get-tuple-element.61), channel_id=1, source_target_pairs={{0,1},{2,3},{1,0},{3,2},{4,5},{6,7},{5,4},{7,6},{8,9},{10,11},{9,8... | collective-permute-start | bytes 196616 | tf_op jit(solution)/shard_map/ppermute | solution.py:90
  8.0 6.8 %collective-permute-start.8 = (bf16[4,64,128]{2,1,0:T(8,128)(2,1)S(1)}, bf16[4,64,128]{2,1,0:T(8,128)(2,1)S(1)}, u32[]{:S(2)}, u32[]{:S(2)}) collective-permute-start(bf16[4,64,128]{2,1,0:T(8,128)(2,1)S(1)} %get-tuple-element.72), channel_id=1, source_target_pairs={{1,2},{2,1},{5,6},{6,5},{9,10},{10,9},{13,14},{14,13},{17,18},{18,... | collective-permute-start | bytes 196616 | tf_op jit(solution)/shard_map/ppermute | solution.py:90
  14.9 8.3 %collective-permute-start.9 = (bf16[10,64,128]{2,1,0:T(8,128)(2,1)S(1)}, bf16[10,64,128]{2,1,0:T(8,128)(2,1)S(1)}, u32[]{:S(2)}, u32[]{:S(2)}) collective-permute-start(bf16[10,64,128]{2,1,0:T(8,128)(2,1)S(1)} %get-tuple-element.73), channel_id=1, source_target_pairs={{0,4},{8,12},{16,20},{24,28},{4,0},{12,8},{20,16},{28,24},{1,5},{9... | collective-permute-start | bytes 491528 | tf_op jit(solution)/shard_map/ppermute | solution.py:90
  15.0 26.7 %collective-permute-start.1 = (bf16[16,64,128]{2,1,0:T(8,128)(2,1)S(1)}, bf16[16,64,128]{2,1,0:T(8,128)(2,1)S(1)}, u32[]{:S(2)}, u32[]{:S(2)}) collective-permute-start(bf16[16,64,128]{2,1,0:T(8,128)(2,1)S(1)} %get-tuple-element.62), channel_id=1, source_target_pairs={{0,0},{1,8},{2,16},{3,24},{4,4},{5,12},{6,20},{7,28},{8,1},{9,9},{... | collective-permute-start | bytes 786440 | tf_op jit(solution)/shard_map/ppermute | solution.py:370
  19.8 21.9 %collective-permute-start.7 = (bf16[16,64,128]{2,1,0:T(8,128)(2,1)S(1)}, bf16[16,64,128]{2,1,0:T(8,128)(2,1)S(1)}, u32[]{:S(2)}, u32[]{:S(2)}) collective-permute-start(bf16[16,64,128]{2,1,0:T(8,128)(2,1)S(1)} %collective-permute-done.6), channel_id=1, source_target_pairs={{0,3},{1,11},{2,19},{3,27},{4,7},{5,15},{6,23},{7,31},{8,2},{9,10}... | collective-permute-start | bytes 786440 | tf_op jit(solution)/shard_map/ppermute | solution.py:370
  19.9 24.6 %collective-permute-start.5 = (bf16[16,64,128]{2,1,0:T(8,128)(2,1)S(1)}, bf16[16,64,128]{2,1,0:T(8,128)(2,1)S(1)}, u32[]{:S(2)}, u32[]{:S(2)}) collective-permute-start(bf16[16,64,128]{2,1,0:T(8,128)(2,1)S(1)} %collective-permute-done.4), channel_id=1, source_target_pairs={{0,2},{1,10},{2,18},{3,26},{4,6},{5,14},{6,22},{7,30},{8,3},{9,11}... | collective-permute-start | bytes 786440 | tf_op jit(solution)/shard_map/ppermute | solution.py:370
  21.3 23.2 %collective-permute-start.3 = (bf16[16,64,128]{2,1,0:T(8,128)(2,1)S(1)}, bf16[16,64,128]{2,1,0:T(8,128)(2,1)S(1)}, u32[]{:S(2)}, u32[]{:S(2)}) collective-permute-start(bf16[16,64,128]{2,1,0:T(8,128)(2,1)S(1)} %collective-permute-done.2), channel_id=1, source_target_pairs={{0,1},{1,9},{2,17},{3,25},{4,5},{5,13},{6,21},{7,29},{8,0},{9,8},{... | collective-permute-start | bytes 786440 | tf_op jit(solution)/shard_map/ppermute | solution.py:370
  23.2 13.2 %collective-permute-start.10 = (bf16[10,64,128]{2,1,0:T(8,128)(2,1)S(1)}, bf16[10,64,128]{2,1,0:T(8,128)(2,1)S(1)}, u32[]{:S(2)}, u32[]{:S(2)}) collective-permute-start(bf16[10,64,128]{2,1,0:T(8,128)(2,1)S(1)} %get-tuple-element.75), channel_id=1, source_target_pairs={{4,8},{12,16},{20,24},{8,4},{16,12},{24,20},{5,9},{13,17},{21,25},... | collective-permute-start | bytes 491528 | tf_op jit(solution)/shard_map/ppermute | solution.py:90
  36.5 0.9 copy-start.3
  37.4 0.7 copy-start.5
  45.4 2.0 %collective-permute-start.11 = (bf16[32,64,128]{2,1,0:T(8,128)(2,1)S(1)}, bf16[32,64,128]{2,1,0:T(8,128)(2,1)S(1)}, u32[]{:S(2)}, u32[]{:S(2)}) collective-permute-start(bf16[32,64,128]{2,1,0:T(8,128)(2,1)S(1)} %get-tuple-element.82), channel_id=1, source_target_pairs={{0,4},{4,0},{8,12},{12,8},{16,20},{20,16},{24,28},{28,24},{1,5},{5... | collective-permute-start | bytes 1572872 | tf_op jit(solution)/shard_map/ppermute | solution.py:381
  45.5 8.7 %collective-permute-start.15 = (bf16[16,64,128]{2,1,0:T(8,128)(2,1)S(1)}, bf16[16,64,128]{2,1,0:T(8,128)(2,1)S(1)}, u32[]{:S(2)}, u32[]{:S(2)}) collective-permute-start(bf16[16,64,128]{2,1,0:T(8,128)(2,1)S(1)} %get-tuple-element.92.refs_1_), channel_id=1, source_target_pairs={{0,8},{4,12},{8,0},{12,4},{16,24},{20,28},{24,16},{28,20},{1,9},{5... | collective-permute-start | bytes 786440 | tf_op jit(solution)/shard_map/ppermute | solution.py:360
  45.6 14.8 %collective-permute-start.17 = (bf16[16,64,128]{2,1,0:T(8,128)(2,1)S(1)}, bf16[16,64,128]{2,1,0:T(8,128)(2,1)S(1)}, u32[]{:S(2)}, u32[]{:S(2)}) collective-permute-start(bf16[16,64,128]{2,1,0:T(8,128)(2,1)S(1)} %get-tuple-element.94.refs_2_), channel_id=1, source_target_pairs={{0,16},{4,20},{8,24},{12,28},{16,0},{20,4},{24,8},{28,12},{1,17},{... | collective-permute-start | bytes 786440 | tf_op jit(solution)/shard_map/ppermute | solution.py:360
  49.5 34.4 %copy-start.4 = (bf16[3,3,64,64]{3,2,1,0:T(8,128)(2,1)S(1)}, bf16[3,3,64,64]{3,2,1,0:T(8,128)(2,1)}, u32[]{:S(2)}) copy-start(bf16[3,3,64,64]{3,2,1,0:T(8,128)(2,1)} %weight.3) | copy-start | bytes 221188
  51.3 1.7 %collective-permute-start.14 = (f32[160,128]{1,0:T(8,128)S(1)}, f32[160,128]{1,0:T(8,128)S(1)}, u32[]{:S(2)}, u32[]{:S(2)}) collective-permute-start(f32[160,128]{1,0:T(8,128)S(1)} %get-tuple-element.91), channel_id=1, source_target_pairs={{0,4},{4,0},{8,12},{12,8},{16,20},{20,16},{24,28},{28,24},{1,5},{5... | collective-permute-start | bytes 245768 | tf_op jit(solution)/shard_map/ppermute | solution.py:381
  51.5 15.6 %collective-permute-start.22 = (bf16[16,64,128]{2,1,0:T(8,128)(2,1)S(1)}, bf16[16,64,128]{2,1,0:T(8,128)(2,1)S(1)}, u32[]{:S(2)}, u32[]{:S(2)}) collective-permute-start(bf16[16,64,128]{2,1,0:T(8,128)(2,1)S(1)} %get-tuple-element.99.refs_3_), channel_id=1, source_target_pairs={{0,24},{4,28},{8,16},{12,20},{16,8},{20,12},{24,0},{28,4},{1,25},{... | collective-permute-start | bytes 786440 | tf_op jit(solution)/shard_map/ppermute | solution.py:360
  54.2 6.1 %collective-permute-start.16 = (f32[160,128]{1,0:T(8,128)S(1)}, f32[160,128]{1,0:T(8,128)S(1)}, u32[]{:S(2)}, u32[]{:S(2)}) collective-permute-start(f32[160,128]{1,0:T(8,128)S(1)} %add.24), channel_id=1, source_target_pairs={{0,1},{1,0},{2,3},{3,2},{4,5},{5,4},{6,7},{7,6},{8,9},{9,8},{10,11... | collective-permute-start | bytes 245768 | tf_op jit(solution)/shard_map/ppermute | solution.py:471
  56.3 6.3 %collective-permute-start.12 = (bf16[4,64,128]{2,1,0:T(8,128)(2,1)S(1)}, bf16[4,64,128]{2,1,0:T(8,128)(2,1)S(1)}, u32[]{:S(2)}, u32[]{:S(2)}) collective-permute-start(bf16[4,64,128]{2,1,0:T(8,128)(2,1)S(1)} %get-tuple-element.84), channel_id=1, source_target_pairs={{0,1},{2,3},{1,0},{3,2},{4,5},{6,7},{5,4},{7,6},{8,9},{10,11},{9,8... | collective-permute-start | bytes 196616 | tf_op jit(solution)/shard_map/ppermute | solution.py:90
  56.4 7.8 %collective-permute-start.13 = (bf16[4,64,128]{2,1,0:T(8,128)(2,1)S(1)}, bf16[4,64,128]{2,1,0:T(8,128)(2,1)S(1)}, u32[]{:S(2)}, u32[]{:S(2)}) collective-permute-start(bf16[4,64,128]{2,1,0:T(8,128)(2,1)S(1)} %get-tuple-element.85), channel_id=1, source_target_pairs={{1,2},{2,1},{5,6},{6,5},{9,10},{10,9},{13,14},{14,13},{17,18},{18,... | collective-permute-start | bytes 196616 | tf_op jit(solution)/shard_map/ppermute | solution.py:90
  60.4 5.5 %collective-permute-start.18 = (f32[160,128]{1,0:T(8,128)S(1)}, f32[160,128]{1,0:T(8,128)S(1)}, u32[]{:S(2)}, u32[]{:S(2)}) collective-permute-start(f32[160,128]{1,0:T(8,128)S(1)} %add.25), channel_id=1, source_target_pairs={{0,2},{1,3},{2,0},{3,1},{4,6},{5,7},{6,4},{7,5},{8,10},{9,11},{10,... | collective-permute-start | bytes 245768 | tf_op jit(solution)/shard_map/ppermute | solution.py:400
  64.2 12.9 %collective-permute-start.26 = (bf16[10,64,128]{2,1,0:T(8,128)(2,1)S(1)}, bf16[10,64,128]{2,1,0:T(8,128)(2,1)S(1)}, u32[]{:S(2)}, u32[]{:S(2)}) collective-permute-start(bf16[10,64,128]{2,1,0:T(8,128)(2,1)S(1)} %get-tuple-element.103), channel_id=1, source_target_pairs={{0,4},{8,12},{16,20},{24,28},{4,0},{12,8},{20,16},{28,24},{1,5},{9... | collective-permute-start | bytes 491528 | tf_op jit(solution)/shard_map/ppermute | solution.py:90
  65.9 8.2 %collective-permute-start.24 = (f32[160,128]{1,0:T(8,128)S(1)}, f32[160,128]{1,0:T(8,128)S(1)}, u32[]{:S(2)}, u32[]{:S(2)}) collective-permute-start(f32[160,128]{1,0:T(8,128)S(1)} %add.26), channel_id=1, source_target_pairs={{0,8},{4,12},{8,0},{12,4},{16,24},{20,28},{24,16},{28,20},{1,9},{5... | collective-permute-start | bytes 245768 | tf_op jit(solution)/shard_map/ppermute | solution.py:400
  67.0 23.1 %collective-permute-start.23 = (bf16[16,64,128]{2,1,0:T(8,128)(2,1)S(1)}, bf16[16,64,128]{2,1,0:T(8,128)(2,1)S(1)}, u32[]{:S(2)}, u32[]{:S(2)}) collective-permute-start(bf16[16,64,128]{2,1,0:T(8,128)(2,1)S(1)} %collective-permute-done.22), channel_id=1, source_target_pairs={{0,3},{1,11},{2,19},{3,27},{4,7},{5,15},{6,23},{7,31},{8,2},{9,10}... | collective-permute-start | bytes 786440 | tf_op jit(solution)/shard_map/ppermute | solution.py:370
  67.5 23.6 %collective-permute-start.21 = (bf16[16,64,128]{2,1,0:T(8,128)(2,1)S(1)}, bf16[16,64,128]{2,1,0:T(8,128)(2,1)S(1)}, u32[]{:S(2)}, u32[]{:S(2)}) collective-permute-start(bf16[16,64,128]{2,1,0:T(8,128)(2,1)S(1)} %collective-permute-done.17), channel_id=1, source_target_pairs={{0,2},{1,10},{2,18},{3,26},{4,6},{5,14},{6,22},{7,30},{8,3},{9,11}... | collective-permute-start | bytes 786440 | tf_op jit(solution)/shard_map/ppermute | solution.py:370
  70.5 20.8 %collective-permute-start.20 = (bf16[16,64,128]{2,1,0:T(8,128)(2,1)S(1)}, bf16[16,64,128]{2,1,0:T(8,128)(2,1)S(1)}, u32[]{:S(2)}, u32[]{:S(2)}) collective-permute-start(bf16[16,64,128]{2,1,0:T(8,128)(2,1)S(1)} %collective-permute-done.15), channel_id=1, source_target_pairs={{0,1},{1,9},{2,17},{3,25},{4,5},{5,13},{6,21},{7,29},{8,0},{9,8},{... | collective-permute-start | bytes 786440 | tf_op jit(solution)/shard_map/ppermute | solution.py:370
  74.1 21.6 %collective-permute-start.19 = (bf16[16,64,128]{2,1,0:T(8,128)(2,1)S(1)}, bf16[16,64,128]{2,1,0:T(8,128)(2,1)S(1)}, u32[]{:S(2)}, u32[]{:S(2)}) collective-permute-start(bf16[16,64,128]{2,1,0:T(8,128)(2,1)S(1)} %get-tuple-element.96.refs_0_), channel_id=1, source_target_pairs={{0,0},{1,8},{2,16},{3,24},{4,4},{5,12},{6,20},{7,28},{8,1},{9,9},{... | collective-permute-start | bytes 786440 | tf_op jit(solution)/shard_map/ppermute | solution.py:370
  77.1 4.7 %collective-permute-start.25 = (f32[160,128]{1,0:T(8,128)S(1)}, f32[160,128]{1,0:T(8,128)S(1)}, u32[]{:S(2)}, u32[]{:S(2)}) collective-permute-start(f32[160,128]{1,0:T(8,128)S(1)} %add.27), channel_id=1, source_target_pairs={{0,16},{4,20},{8,24},{12,28},{16,0},{20,4},{24,8},{28,12},{1,17},{... | collective-permute-start | bytes 245768 | tf_op jit(solution)/shard_map/ppermute | solution.py:400
  81.8 8.3 %collective-permute-start.27 = (bf16[10,64,128]{2,1,0:T(8,128)(2,1)S(1)}, bf16[10,64,128]{2,1,0:T(8,128)(2,1)S(1)}, u32[]{:S(2)}, u32[]{:S(2)}) collective-permute-start(bf16[10,64,128]{2,1,0:T(8,128)(2,1)S(1)} %get-tuple-element.105), channel_id=1, source_target_pairs={{4,8},{12,16},{20,24},{8,4},{16,12},{24,20},{5,9},{13,17},{21,25},... | collective-permute-start | bytes 491528 | tf_op jit(solution)/shard_map/ppermute | solution.py:90
  96.6 3.9 %collective-permute-start.28 = (bf16[32,64,128]{2,1,0:T(8,128)(2,1)S(1)}, bf16[32,64,128]{2,1,0:T(8,128)(2,1)S(1)}, u32[]{:S(2)}, u32[]{:S(2)}) collective-permute-start(bf16[32,64,128]{2,1,0:T(8,128)(2,1)S(1)} %get-tuple-element.111), channel_id=1, source_target_pairs={{0,4},{4,0},{8,12},{12,8},{16,20},{20,16},{24,28},{28,24},{1,5},{5... | collective-permute-start | bytes 1572872 | tf_op jit(solution)/shard_map/ppermute | solution.py:381
  98.1 1.7 %collective-permute-start.29 = (f32[160,128]{1,0:T(8,128)S(1)}, f32[160,128]{1,0:T(8,128)S(1)}, u32[]{:S(2)}, u32[]{:S(2)}) collective-permute-start(f32[160,128]{1,0:T(8,128)S(1)} %add.28.mine), channel_id=1, source_target_pairs={{0,4},{4,0},{8,12},{12,8},{16,20},{20,16},{24,28},{28,24},{1,5},{5... | collective-permute-start | bytes 245768 | tf_op jit(solution)/shard_map/ppermute | solution.py:381

commit v8 on v6

--- a/solution.py
+++ b/solution.py
@@ -16,8 +16,6 @@
 def call(
     kernel, out_shape, *args, scratch=(), flops=0, in_hbm=(), out_hbm=0, aliases=None, name=None
 ):
-    out_bytes = sum(o.size * o.dtype.itemsize for o in jax.tree.leaves(out_shape))
-    in_bytes = sum(a.size * a.dtype.itemsize for a in args)
     in_specs = [
         pl.BlockSpec(memory_space=pltpu.SMEM if a.dtype == jnp.int32 else pltpu.VMEM) for a in args
     ]
@@ -38,7 +36,7 @@
         name=name,
         compiler_params=pltpu.CompilerParams(vmem_limit_bytes=VMEM_LIMIT),
         cost_estimate=pl.CostEstimate(
-            flops=flops, bytes_accessed=in_bytes + out_bytes, transcendentals=0
+            flops=flops, bytes_accessed=0, transcendentals=0
         ),
     )(*args)
 

time: 104 us -> 104 us (level)
  no operation moved by 1% of the time
where the time goes in v8:
time: 104 us; the launch traced here: 102 us
  starting transfers between devices  42.1 us (40%)
  waiting for transfers between devices  35.8 us (34%)
  Pallas kernels  19 us (18%)
  local copies, waits for them, and re-layouts  4.11 us (4%)
    pallas_call x12, Pallas kernels, call(): pl.pallas_call(kernel, out_shape=out_shape, in_specs=in_specs, out_specs=...  19 us
    ppermute x8, waiting for transfers between devices, exchanged(): return lax.ppermute(x, axis, pairs + [(j, i) for i, j in pairs])  18.6 us
    ppermute x8, starting transfers between devices, cross(): return lax.ppermute(piece, ('row', 'col'), owners)  17.1 us
    ppermute x8, starting transfers between devices, exchanged(): return lax.ppermute(x, axis, pairs + [(j, i) for i, j in pairs])  13.5 us
    ppermute x3, waiting for transfers between devices, summed(): lax.ppermute(part, axis, [(i, i ^ reach) for i in range(size)])  7.55 us
    ppermute x8, waiting for transfers between devices, cross(): return lax.ppermute(piece, ('row', 'col'), owners)  6.83 us
    ppermute x6, starting transfers between devices, detour(): lax.ppermute(piece, 'row', [(r, r ^ 2 * far) for r in range(lax.axis_size...  5.43 us
    unnamed x10, local copies, waits for them, and re-layouts  3.36 us
  transfers between devices with their start and end apart: 30, of which 13 were waited for; matrix products, arithmetic and copies ran while one was open for 1% of the time, Pallas kernels for 14%

profile of v8, /device:TPU:12, one launch (start us, length us, event | category | flops | bytes accessed | tf_op | source)
XLA Modules:
  0.0 102.0 jit_solution(11168120764872507344)
XLA Ops:
  0.7 1.2 %copy-done = bf16[64,64,128]{2,1,0:T(8,128)(2,1)S(1)} copy-done((bf16[64,64,128]{2,1,0:T(8,128)(2,1)S(1)}, bf16[64,64,128]{2,1,0:T(8,128)(2,1)}, u32[]{:S(2)}) %copy-start) | copy-done | bytes 1048600
  1.9 1.2 %copy-done.2 = bf16[64,64,128]{2,1,0:T(8,128)(2,1)S(1)} copy-done((bf16[64,64,128]{2,1,0:T(8,128)(2,1)S(1)}, bf16[64,64,128]{2,1,0:T(8,128)(2,1)}, u32[]{:S(2)}) %copy-start.2) | copy-done | bytes 1048600
  3.1 0.9 open.1
  4.0 1.5 %collective-permute-start.6 = (bf16[16,64,128]{2,1,0:T(8,128)(2,1)S(1)}, bf16[16,64,128]{2,1,0:T(8,128)(2,1)}, u32[]{:S(2)}, u32[]{:S(2)}) collective-permute-start(bf16[16,64,128]{2,1,0:T(8,128)(2,1)S(1)} %get-tuple-element.67), channel_id=1, source_target_pairs={{0,24},{4,28},{8,16},{12,20},{16,8},{20,12},{24,0},{28,4},{1,25},{... | collective-permute-start | bytes 786440 | tf_op jit(solution)/shard_map/ppermute | solution.py:355
  5.5 1.5 %collective-permute-start.4 = (bf16[16,64,128]{2,1,0:T(8,128)(2,1)S(1)}, bf16[16,64,128]{2,1,0:T(8,128)(2,1)}, u32[]{:S(2)}, u32[]{:S(2)}) collective-permute-start(bf16[16,64,128]{2,1,0:T(8,128)(2,1)S(1)} %get-tuple-element.65), channel_id=1, source_target_pairs={{0,16},{4,20},{8,24},{12,28},{16,0},{20,4},{24,8},{28,12},{1,17},{... | collective-permute-start | bytes 786440 | tf_op jit(solution)/shard_map/ppermute | solution.py:355
  7.0 0.5 collective-permute-start.2
  7.6 0.4 collective-permute-start
  8.0 4.6 %collective-permute-start.8 = (bf16[4,64,128]{2,1,0:T(8,128)(2,1)S(1)}, bf16[4,64,128]{2,1,0:T(8,128)(2,1)S(1)}, u32[]{:S(2)}, u32[]{:S(2)}) collective-permute-start(bf16[4,64,128]{2,1,0:T(8,128)(2,1)S(1)} %get-tuple-element.72), channel_id=1, source_target_pairs={{1,2},{2,1},{5,6},{6,5},{9,10},{10,9},{13,14},{14,13},{17,18},{18,... | collective-permute-start | bytes 196616 | tf_op jit(solution)/shard_map/ppermute | solution.py:88
  12.6 0.0 collective-permute-done.first.refs_2_
  12.6 2.2 %collective-permute-done.8.second.refs_3_ = bf16[4,64,128]{2,1,0:T(8,128)(2,1)S(1)} collective-permute-done((bf16[4,64,128]{2,1,0:T(8,128)(2,1)S(1)}, bf16[4,64,128]{2,1,0:T(8,128)(2,1)S(1)}, u32[]{:S(2)}, u32[]{:S(2)}) %collective-permute-start.8) | collective-permute-done | bytes 65568 | tf_op jit(solution)/shard_map/ppermute | solution.py:88
  14.8 0.7 messages.2
  15.6 4.8 %collective-permute-start.1 = (bf16[16,64,128]{2,1,0:T(8,128)(2,1)}, bf16[16,64,128]{2,1,0:T(8,128)(2,1)S(1)}, u32[]{:S(2)}, u32[]{:S(2)}) collective-permute-start(bf16[16,64,128]{2,1,0:T(8,128)(2,1)} %get-tuple-element.62), channel_id=1, source_target_pairs={{0,0},{1,8},{2,16},{3,24},{4,4},{5,12},{6,20},{7,28},{8,1},{9,9},{... | collective-permute-start | bytes 786440 | tf_op jit(solution)/shard_map/ppermute | solution.py:365
  20.4 0.0 collective-permute-done.6
  20.4 0.1 collective-permute-start.7
  20.4 0.0 collective-permute-done.4
  20.4 1.4 %collective-permute-start.5 = (bf16[16,64,128]{2,1,0:T(8,128)(2,1)}, bf16[16,64,128]{2,1,0:T(8,128)(2,1)S(1)}, u32[]{:S(2)}, u32[]{:S(2)}) collective-permute-start(bf16[16,64,128]{2,1,0:T(8,128)(2,1)} %collective-permute-done.4), channel_id=1, source_target_pairs={{0,2},{1,10},{2,18},{3,26},{4,6},{5,14},{6,22},{7,30},{8,3},{9,11}... | collective-permute-start | bytes 786440 | tf_op jit(solution)/shard_map/ppermute | solution.py:365
  21.9 1.4 %collective-permute-start.3 = (bf16[16,64,128]{2,1,0:T(8,128)(2,1)}, bf16[16,64,128]{2,1,0:T(8,128)(2,1)S(1)}, u32[]{:S(2)}, u32[]{:S(2)}) collective-permute-start(bf16[16,64,128]{2,1,0:T(8,128)(2,1)} %collective-permute-done.2), channel_id=1, source_target_pairs={{0,1},{1,9},{2,17},{3,25},{4,5},{5,13},{6,21},{7,29},{8,0},{9,8},{... | collective-permute-start | bytes 786440 | tf_op jit(solution)/shard_map/ppermute | solution.py:365
  23.2 1.9 %collective-permute-start.10 = (bf16[10,64,128]{2,1,0:T(8,128)(2,1)}, bf16[10,64,128]{2,1,0:T(8,128)(2,1)}, u32[]{:S(2)}, u32[]{:S(2)}) collective-permute-start(bf16[10,64,128]{2,1,0:T(8,128)(2,1)} %get-tuple-element.75), channel_id=1, source_target_pairs={{4,8},{12,16},{20,24},{8,4},{16,12},{24,20},{5,9},{13,17},{21,25},... | collective-permute-start | bytes 491528 | tf_op jit(solution)/shard_map/ppermute | solution.py:88
  25.2 0.7 copy.9.refs_5_
  25.9 11.5 %collective-permute-done.10.refs_1_ = bf16[10,64,128]{2,1,0:T(8,128)(2,1)} collective-permute-done((bf16[10,64,128]{2,1,0:T(8,128)(2,1)}, bf16[10,64,128]{2,1,0:T(8,128)(2,1)}, u32[]{:S(2)}, u32[]{:S(2)}) %collective-permute-start.10) | collective-permute-done | bytes 163872 | tf_op jit(solution)/shard_map/ppermute | solution.py:88
  37.4 0.9 copy-done.3
  38.3 4.5 %forward.1 = (f32[8,128]{1,0:T(8,128)}, bf16[80,192,128]{2,1,0:T(8,128)(2,1)S(1)}, f32[64,64,128]{2,1,0:T(8,128)S(1)}, bf16[16,64,128]{2,1,0:T(8,128)(2,1)S(1)},...) custom-call(s32[1]{0:T(128)} %bitcast.row_odd, ...), custom_call_target="tpu_custom_call" | custom-call | flops 603979776 | tf_op jit(solution)/shard_map/forward/pallas_call | solution.py:29
  42.9 2.4 %collective-permute-done.5.refs_2_ = bf16[16,64,128]{2,1,0:T(8,128)(2,1)S(1)} collective-permute-done((bf16[16,64,128]{2,1,0:T(8,128)(2,1)}, bf16[16,64,128]{2,1,0:T(8,128)(2,1)S(1)}, u32[]{:S(2)}, u32[]{:S(2)}) %collective-permute-start.5) | collective-permute-done | bytes 262176 | tf_op jit(solution)/shard_map/ppermute | solution.py:365
  45.3 0.0 collective-permute-done.3.refs_1_
  45.3 0.9 turn.2
  46.2 0.1 collective-permute-start.11
  46.3 0.0 collective-permute-start.15
  46.4 0.3 collective-permute-start.17
  46.7 1.5 %collective-permute-done.11.got = bf16[32,64,128]{2,1,0:T(8,128)(2,1)S(1)} collective-permute-done((bf16[32,64,128]{2,1,0:T(8,128)(2,1)S(1)}, bf16[32,64,128]{2,1,0:T(8,128)(2,1)S(1)}, u32[]{:S(2)}, u32[]{:S(2)}) %collective-permute-start.11) | collective-permute-done | bytes 524320 | tf_op jit(solution)/shard_map/ppermute | solution.py:376
  48.2 2.1 %grad_pre.1 = (f32[8,128]{1,0:T(8,128)}, bf16[64,64,128]{2,1,0:T(8,128)(2,1)S(1)}, bf16[8,64,128]{2,1,0:T(8,128)(2,1)S(1)}, bf16[8,64,128]{2,1,0:T(8,128)(2,1)S(...) custom-call(s32[1]{0:T(128)} %bitcast.row_odd, ...), custom_call_target="tpu_custom_call" | custom-call | tf_op jit(solution)/shard_map/grad_pre/pallas_call | solution.py:29
  50.3 1.8 %weight_terms.1 = (f32[8,128]{1,0:T(8,128)}, f32[160,128]{1,0:T(8,128)S(1)}, f32[160,128]{1,0:T(8,128)S(1)}) custom-call(s32[1]{0:T(128)} %bitcast.row_odd, bf16[64,64,128]{2,1,0:T(8,128)(2,1)S(1)} %get-tuple-element.83.tile.grad, bf16[80,192,128]{2,1,0:T(8,128)(2,1)S(1)} %get-tuple-element.89.stack), custom_call_target="tpu_custom_call" | custom-call | flops 603979776 | tf_op jit(solution)/shard_map/weight_terms/pallas_call | solution.py:29
  52.1 0.1 collective-permute-start.14
  52.2 1.5 %collective-permute-start.22 = (bf16[16,64,128]{2,1,0:T(8,128)(2,1)S(1)}, bf16[16,64,128]{2,1,0:T(8,128)(2,1)S(1)}, u32[]{:S(2)}, u32[]{:S(2)}) collective-permute-start(bf16[16,64,128]{2,1,0:T(8,128)(2,1)S(1)} %get-tuple-element.99.refs_3_), channel_id=1, source_target_pairs={{0,24},{4,28},{8,16},{12,20},{16,8},{20,12},{24,0},{28,4},{1,25},{... | collective-permute-start | bytes 786440 | tf_op jit(solution)/shard_map/ppermute | solution.py:355
  53.8 1.2 %collective-permute-done.15 = bf16[16,64,128]{2,1,0:T(8,128)(2,1)S(1)} collective-permute-done((bf16[16,64,128]{2,1,0:T(8,128)(2,1)S(1)}, bf16[16,64,128]{2,1,0:T(8,128)(2,1)S(1)}, u32[]{:S(2)}, u32[]{:S(2)}) %collective-permute-start.15) | collective-permute-done | bytes 262176 | tf_op jit(solution)/shard_map/ppermute | solution.py:355
  55.0 2.1 %collective-permute-start.16 = (f32[160,128]{1,0:T(8,128)S(1)}, f32[160,128]{1,0:T(8,128)S(1)}, u32[]{:S(2)}, u32[]{:S(2)}) collective-permute-start(f32[160,128]{1,0:T(8,128)S(1)} %add.24), channel_id=1, source_target_pairs={{0,1},{1,0},{2,3},{3,2},{4,5},{5,4},{6,7},{7,6},{8,9},{9,8},{10,11... | collective-permute-start | bytes 245768 | tf_op jit(solution)/shard_map/ppermute | solution.py:466
  57.1 0.0 collective-permute-start.12
  57.1 4.3 %collective-permute-start.13 = (bf16[4,64,128]{2,1,0:T(8,128)(2,1)S(1)}, bf16[4,64,128]{2,1,0:T(8,128)(2,1)S(1)}, u32[]{:S(2)}, u32[]{:S(2)}) collective-permute-start(bf16[4,64,128]{2,1,0:T(8,128)(2,1)S(1)} %get-tuple-element.85), channel_id=1, source_target_pairs={{1,2},{2,1},{5,6},{6,5},{9,10},{10,9},{13,14},{14,13},{17,18},{18,... | collective-permute-start | bytes 196616 | tf_op jit(solution)/shard_map/ppermute | solution.py:88
  61.4 0.0 collective-permute-done.16
  61.5 0.0 collective-permute-done.17
  61.5 2.2 %collective-permute-start.18 = (f32[160,128]{1,0:T(8,128)S(1)}, f32[160,128]{1,0:T(8,128)S(1)}, u32[]{:S(2)}, u32[]{:S(2)}) collective-permute-start(f32[160,128]{1,0:T(8,128)S(1)} %add.25), channel_id=1, source_target_pairs={{0,2},{1,3},{2,0},{3,1},{4,6},{5,7},{6,4},{7,5},{8,10},{9,11},{10,... | collective-permute-start | bytes 245768 | tf_op jit(solution)/shard_map/ppermute | solution.py:395
  63.7 0.7 collective-permute-done.13.col_second.second
  64.4 0.1 messages.3
  64.4 0.1 collective-permute-start.26
  64.5 2.4 %collective-permute-done.18 = f32[160,128]{1,0:T(8,128)S(1)} collective-permute-done((f32[160,128]{1,0:T(8,128)S(1)}, f32[160,128]{1,0:T(8,128)S(1)}, u32[]{:S(2)}, u32[]{:S(2)}) %collective-permute-start.18) | collective-permute-done | bytes 81952 | tf_op jit(solution)/shard_map/ppermute | solution.py:395
  66.9 0.9 collective-permute-start.24
  67.8 0.7 collective-permute-start.23
  68.5 2.8 %collective-permute-start.21 = (bf16[16,64,128]{2,1,0:T(8,128)(2,1)S(1)}, bf16[16,64,128]{2,1,0:T(8,128)(2,1)S(1)}, u32[]{:S(2)}, u32[]{:S(2)}) collective-permute-start(bf16[16,64,128]{2,1,0:T(8,128)(2,1)S(1)} %collective-permute-done.17), channel_id=1, source_target_pairs={{0,2},{1,10},{2,18},{3,26},{4,6},{5,14},{6,22},{7,30},{8,3},{9,11}... | collective-permute-start | bytes 786440 | tf_op jit(solution)/shard_map/ppermute | solution.py:365
  71.3 2.2 %collective-permute-start.20 = (bf16[16,64,128]{2,1,0:T(8,128)(2,1)S(1)}, bf16[16,64,128]{2,1,0:T(8,128)(2,1)S(1)}, u32[]{:S(2)}, u32[]{:S(2)}) collective-permute-start(bf16[16,64,128]{2,1,0:T(8,128)(2,1)S(1)} %collective-permute-done.15), channel_id=1, source_target_pairs={{0,1},{1,9},{2,17},{3,25},{4,5},{5,13},{6,21},{7,29},{8,0},{9,8},{... | collective-permute-start | bytes 786440 | tf_op jit(solution)/shard_map/ppermute | solution.py:365
  73.5 0.6 collective-permute-done.24
  74.1 3.8 %collective-permute-start.19 = (bf16[16,64,128]{2,1,0:T(8,128)(2,1)S(1)}, bf16[16,64,128]{2,1,0:T(8,128)(2,1)S(1)}, u32[]{:S(2)}, u32[]{:S(2)}) collective-permute-start(bf16[16,64,128]{2,1,0:T(8,128)(2,1)S(1)} %get-tuple-element.96.refs_0_), channel_id=1, source_target_pairs={{0,0},{1,8},{2,16},{3,24},{4,4},{5,12},{6,20},{7,28},{8,1},{9,9},{... | collective-permute-start | bytes 786440 | tf_op jit(solution)/shard_map/ppermute | solution.py:365
  77.9 0.1 collective-permute-start.25
  78.0 4.6 %collective-permute-done.25 = f32[160,128]{1,0:T(8,128)S(1)} collective-permute-done((f32[160,128]{1,0:T(8,128)S(1)}, f32[160,128]{1,0:T(8,128)S(1)}, u32[]{:S(2)}, u32[]{:S(2)}) %collective-permute-start.25) | collective-permute-done | bytes 81952 | tf_op jit(solution)/shard_map/ppermute | solution.py:395
  82.6 2.1 %collective-permute-start.27 = (bf16[10,64,128]{2,1,0:T(8,128)(2,1)S(1)}, bf16[10,64,128]{2,1,0:T(8,128)(2,1)S(1)}, u32[]{:S(2)}, u32[]{:S(2)}) collective-permute-start(bf16[10,64,128]{2,1,0:T(8,128)(2,1)S(1)} %get-tuple-element.105), channel_id=1, source_target_pairs={{4,8},{12,16},{20,24},{8,4},{16,12},{24,20},{5,9},{13,17},{21,25},... | collective-permute-start | bytes 491528 | tf_op jit(solution)/shard_map/ppermute | solution.py:88
  84.7 3.2 %input_grad.1 = (f32[8,128]{1,0:T(8,128)S(1)}, bf16[64,64,128]{2,1,0:T(8,128)(2,1)}, f32[2,64,16,128]{3,2,1,0:T(8,128)S(1)}) custom-call(s32[1]{0:T(128)} %bitcast.1.col_odd, bf16[64,64,128]{2,1,0:T(8,128)(2,1)S(1)} %get-tuple-element.83.tile.grad, bf16[4,64,128]{2,1,0:T(8,128)(2,1)S(1)} %collective-permute-done.12.col_first.first, ...), custom_call_target="tpu_custom_call" | custom-call | flops 603979776 | tf_op jit(solution)/shard_map/input_grad/pallas_call | solution.py:29
  87.9 4.2 %collective-permute-done.27.row_second = bf16[10,64,128]{2,1,0:T(8,128)(2,1)S(1)} collective-permute-done((bf16[10,64,128]{2,1,0:T(8,128)(2,1)S(1)}, bf16[10,64,128]{2,1,0:T(8,128)(2,1)S(1)}, u32[]{:S(2)}, u32[]{:S(2)}) %collective-permute-start.27) | collective-permute-done | bytes 163872 | tf_op jit(solution)/shard_map/ppermute | solution.py:88
  92.1 0.2 collective-permute-done.21.refs_3_
  92.3 4.2 %collective-permute-done.19.refs_1_ = bf16[16,64,128]{2,1,0:T(8,128)(2,1)S(1)} collective-permute-done((bf16[16,64,128]{2,1,0:T(8,128)(2,1)S(1)}, bf16[16,64,128]{2,1,0:T(8,128)(2,1)S(1)}, u32[]{:S(2)}, u32[]{:S(2)}) %collective-permute-start.19) | collective-permute-done | bytes 262176 | tf_op jit(solution)/shard_map/ppermute | solution.py:365
  96.5 0.9 turn.3
  97.4 0.1 collective-permute-start.28
  97.5 0.5 collective-permute-start.29
  98.0 1.5 %input_grad_ends.1 = bf16[64,64,128]{2,1,0:T(8,128)(2,1)} custom-call(s32[1]{0:T(128)} %bitcast.row_odd, bf16[10,64,128]{2,1,0:T(8,128)(2,1)S(1)} %collective-permute-done.26.row_first, bf16[10,64,128]{2,1,0:T(8,128)(2,1)S(1)} %collective-permute-done.27.row_second, bf16[3,3,64,64]{3,2,1,0:T(8,128)(2,1)S(1)} %copy-done.4, ...), custom_call_target="tpu_custom_call", output_to_operand_aliasing={{}: (5, {})} | custom-call | tf_op jit(solution)/shard_map/input_grad_ends/pallas_call | solution.py:29
  99.5 0.1 collective-permute-done.29.other
  99.5 0.8 unpack.1
  100.4 1.6 %join.1 = bf16[64,64,128]{2,1,0:T(8,128)(2,1)} custom-call(s32[1]{0:T(128)} %bitcast.row_odd, bf16[32,64,128]{2,1,0:T(8,128)(2,1)S(1)} %get-tuple-element.110.keep, bf16[32,64,128]{2,1,0:T(8,128)(2,1)S(1)} %collective-permute-done.28.got, bf16[16,64,128]{2,1,0:T(8,128)(2,1)S(1)} %get-tuple-element.96.refs_0_, ...), custom_call_target="tpu_custom_call" | custom-call | tf_op jit(solution)/shard_map/join/pallas_call | solution.py:29
  (24 shorter events, 0.1 us)
Async XLA Ops:
  0.6 1.2 %copy-start = (bf16[64,64,128]{2,1,0:T(8,128)(2,1)S(1)}, bf16[64,64,128]{2,1,0:T(8,128)(2,1)}, u32[]{:S(2)}) copy-start(bf16[64,64,128]{2,1,0:T(8,128)(2,1)} %cot.5) | copy-start | bytes 3145732
  1.9 1.2 %copy-start.2 = (bf16[64,64,128]{2,1,0:T(8,128)(2,1)S(1)}, bf16[64,64,128]{2,1,0:T(8,128)(2,1)}, u32[]{:S(2)}) copy-start(bf16[64,64,128]{2,1,0:T(8,128)(2,1)} %x.1) | copy-start | bytes 3145732
  3.1 45.1 %copy-start.1 = (bf16[64,64,128]{2,1,0:T(8,128)(2,1)S(1)}, bf16[64,64,128]{2,1,0:T(8,128)(2,1)}, u32[]{:S(2)}) copy-start(bf16[64,64,128]{2,1,0:T(8,128)(2,1)} %cot.5) | copy-start | bytes 3145732
  4.0 16.4 %collective-permute-start.6 = (bf16[16,64,128]{2,1,0:T(8,128)(2,1)S(1)}, bf16[16,64,128]{2,1,0:T(8,128)(2,1)}, u32[]{:S(2)}, u32[]{:S(2)}) collective-permute-start(bf16[16,64,128]{2,1,0:T(8,128)(2,1)S(1)} %get-tuple-element.67), channel_id=1, source_target_pairs={{0,24},{4,28},{8,16},{12,20},{16,8},{20,12},{24,0},{28,4},{1,25},{... | collective-permute-start | bytes 786440 | tf_op jit(solution)/shard_map/ppermute | solution.py:355
  5.5 14.9 %collective-permute-start.4 = (bf16[16,64,128]{2,1,0:T(8,128)(2,1)S(1)}, bf16[16,64,128]{2,1,0:T(8,128)(2,1)}, u32[]{:S(2)}, u32[]{:S(2)}) collective-permute-start(bf16[16,64,128]{2,1,0:T(8,128)(2,1)S(1)} %get-tuple-element.65), channel_id=1, source_target_pairs={{0,16},{4,20},{8,24},{12,28},{16,0},{20,4},{24,8},{28,12},{1,17},{... | collective-permute-start | bytes 786440 | tf_op jit(solution)/shard_map/ppermute | solution.py:355
  7.0 14.9 %collective-permute-start.2 = (bf16[16,64,128]{2,1,0:T(8,128)(2,1)S(1)}, bf16[16,64,128]{2,1,0:T(8,128)(2,1)}, u32[]{:S(2)}, u32[]{:S(2)}) collective-permute-start(bf16[16,64,128]{2,1,0:T(8,128)(2,1)S(1)} %get-tuple-element.63), channel_id=1, source_target_pairs={{0,8},{4,12},{8,0},{12,4},{16,24},{20,28},{24,16},{28,20},{1,9},{5... | collective-permute-start | bytes 786440 | tf_op jit(solution)/shard_map/ppermute | solution.py:355
  7.6 5.1 %collective-permute-start = (bf16[4,64,128]{2,1,0:T(8,128)(2,1)S(1)}, bf16[4,64,128]{2,1,0:T(8,128)(2,1)S(1)}, u32[]{:S(2)}, u32[]{:S(2)}) collective-permute-start(bf16[4,64,128]{2,1,0:T(8,128)(2,1)S(1)} %get-tuple-element.61), channel_id=1, source_target_pairs={{0,1},{2,3},{1,0},{3,2},{4,5},{6,7},{5,4},{7,6},{8,9},{10,11},{9,8... | collective-permute-start | bytes 196616 | tf_op jit(solution)/shard_map/ppermute | solution.py:88
  8.0 6.8 %collective-permute-start.8 = (bf16[4,64,128]{2,1,0:T(8,128)(2,1)S(1)}, bf16[4,64,128]{2,1,0:T(8,128)(2,1)S(1)}, u32[]{:S(2)}, u32[]{:S(2)}) collective-permute-start(bf16[4,64,128]{2,1,0:T(8,128)(2,1)S(1)} %get-tuple-element.72), channel_id=1, source_target_pairs={{1,2},{2,1},{5,6},{6,5},{9,10},{10,9},{13,14},{14,13},{17,18},{18,... | collective-permute-start | bytes 196616 | tf_op jit(solution)/shard_map/ppermute | solution.py:88
  15.6 7.7 %collective-permute-start.9 = (bf16[10,64,128]{2,1,0:T(8,128)(2,1)S(1)}, bf16[10,64,128]{2,1,0:T(8,128)(2,1)S(1)}, u32[]{:S(2)}, u32[]{:S(2)}) collective-permute-start(bf16[10,64,128]{2,1,0:T(8,128)(2,1)S(1)} %get-tuple-element.73), channel_id=1, source_target_pairs={{0,4},{8,12},{16,20},{24,28},{4,0},{12,8},{20,16},{28,24},{1,5},{9... | collective-permute-start | bytes 491528 | tf_op jit(solution)/shard_map/ppermute | solution.py:88
  15.6 27.3 %collective-permute-start.1 = (bf16[16,64,128]{2,1,0:T(8,128)(2,1)}, bf16[16,64,128]{2,1,0:T(8,128)(2,1)S(1)}, u32[]{:S(2)}, u32[]{:S(2)}) collective-permute-start(bf16[16,64,128]{2,1,0:T(8,128)(2,1)} %get-tuple-element.62), channel_id=1, source_target_pairs={{0,0},{1,8},{2,16},{3,24},{4,4},{5,12},{6,20},{7,28},{8,1},{9,9},{... | collective-permute-start | bytes 786440 | tf_op jit(solution)/shard_map/ppermute | solution.py:365
  20.4 22.5 %collective-permute-start.7 = (bf16[16,64,128]{2,1,0:T(8,128)(2,1)}, bf16[16,64,128]{2,1,0:T(8,128)(2,1)S(1)}, u32[]{:S(2)}, u32[]{:S(2)}) collective-permute-start(bf16[16,64,128]{2,1,0:T(8,128)(2,1)} %collective-permute-done.6), channel_id=1, source_target_pairs={{0,3},{1,11},{2,19},{3,27},{4,7},{5,15},{6,23},{7,31},{8,2},{9,10}... | collective-permute-start | bytes 786440 | tf_op jit(solution)/shard_map/ppermute | solution.py:365
  20.4 24.8 %collective-permute-start.5 = (bf16[16,64,128]{2,1,0:T(8,128)(2,1)}, bf16[16,64,128]{2,1,0:T(8,128)(2,1)S(1)}, u32[]{:S(2)}, u32[]{:S(2)}) collective-permute-start(bf16[16,64,128]{2,1,0:T(8,128)(2,1)} %collective-permute-done.4), channel_id=1, source_target_pairs={{0,2},{1,10},{2,18},{3,26},{4,6},{5,14},{6,22},{7,30},{8,3},{9,11}... | collective-permute-start | bytes 786440 | tf_op jit(solution)/shard_map/ppermute | solution.py:365
  21.9 23.4 %collective-permute-start.3 = (bf16[16,64,128]{2,1,0:T(8,128)(2,1)}, bf16[16,64,128]{2,1,0:T(8,128)(2,1)S(1)}, u32[]{:S(2)}, u32[]{:S(2)}) collective-permute-start(bf16[16,64,128]{2,1,0:T(8,128)(2,1)} %collective-permute-done.2), channel_id=1, source_target_pairs={{0,1},{1,9},{2,17},{3,25},{4,5},{5,13},{6,21},{7,29},{8,0},{9,8},{... | collective-permute-start | bytes 786440 | tf_op jit(solution)/shard_map/ppermute | solution.py:365
  23.2 14.2 %collective-permute-start.10 = (bf16[10,64,128]{2,1,0:T(8,128)(2,1)}, bf16[10,64,128]{2,1,0:T(8,128)(2,1)}, u32[]{:S(2)}, u32[]{:S(2)}) collective-permute-start(bf16[10,64,128]{2,1,0:T(8,128)(2,1)} %get-tuple-element.75), channel_id=1, source_target_pairs={{4,8},{12,16},{20,24},{8,4},{16,12},{24,20},{5,9},{13,17},{21,25},... | collective-permute-start | bytes 491528 | tf_op jit(solution)/shard_map/ppermute | solution.py:88
  37.4 0.9 copy-start.3
  46.2 2.0 %collective-permute-start.11 = (bf16[32,64,128]{2,1,0:T(8,128)(2,1)S(1)}, bf16[32,64,128]{2,1,0:T(8,128)(2,1)S(1)}, u32[]{:S(2)}, u32[]{:S(2)}) collective-permute-start(bf16[32,64,128]{2,1,0:T(8,128)(2,1)S(1)} %get-tuple-element.82), channel_id=1, source_target_pairs={{0,4},{4,0},{8,12},{12,8},{16,20},{20,16},{24,28},{28,24},{1,5},{5... | collective-permute-start | bytes 1572872 | tf_op jit(solution)/shard_map/ppermute | solution.py:376
  46.3 8.7 %collective-permute-start.15 = (bf16[16,64,128]{2,1,0:T(8,128)(2,1)S(1)}, bf16[16,64,128]{2,1,0:T(8,128)(2,1)S(1)}, u32[]{:S(2)}, u32[]{:S(2)}) collective-permute-start(bf16[16,64,128]{2,1,0:T(8,128)(2,1)S(1)} %get-tuple-element.92.refs_1_), channel_id=1, source_target_pairs={{0,8},{4,12},{8,0},{12,4},{16,24},{20,28},{24,16},{28,20},{1,9},{5... | collective-permute-start | bytes 786440 | tf_op jit(solution)/shard_map/ppermute | solution.py:355
  46.4 15.1 %collective-permute-start.17 = (bf16[16,64,128]{2,1,0:T(8,128)(2,1)S(1)}, bf16[16,64,128]{2,1,0:T(8,128)(2,1)S(1)}, u32[]{:S(2)}, u32[]{:S(2)}) collective-permute-start(bf16[16,64,128]{2,1,0:T(8,128)(2,1)S(1)} %get-tuple-element.94.refs_2_), channel_id=1, source_target_pairs={{0,16},{4,20},{8,24},{12,28},{16,0},{20,4},{24,8},{28,12},{1,17},{... | collective-permute-start | bytes 786440 | tf_op jit(solution)/shard_map/ppermute | solution.py:355
  50.3 34.4 %copy-start.4 = (bf16[3,3,64,64]{3,2,1,0:T(8,128)(2,1)S(1)}, bf16[3,3,64,64]{3,2,1,0:T(8,128)(2,1)}, u32[]{:S(2)}) copy-start(bf16[3,3,64,64]{3,2,1,0:T(8,128)(2,1)} %weight.3) | copy-start | bytes 221188
  52.1 1.7 %collective-permute-start.14 = (f32[160,128]{1,0:T(8,128)S(1)}, f32[160,128]{1,0:T(8,128)S(1)}, u32[]{:S(2)}, u32[]{:S(2)}) collective-permute-start(f32[160,128]{1,0:T(8,128)S(1)} %get-tuple-element.91), channel_id=1, source_target_pairs={{0,4},{4,0},{8,12},{12,8},{16,20},{20,16},{24,28},{28,24},{1,5},{5... | collective-permute-start | bytes 245768 | tf_op jit(solution)/shard_map/ppermute | solution.py:376
  52.2 15.6 %collective-permute-start.22 = (bf16[16,64,128]{2,1,0:T(8,128)(2,1)S(1)}, bf16[16,64,128]{2,1,0:T(8,128)(2,1)S(1)}, u32[]{:S(2)}, u32[]{:S(2)}) collective-permute-start(bf16[16,64,128]{2,1,0:T(8,128)(2,1)S(1)} %get-tuple-element.99.refs_3_), channel_id=1, source_target_pairs={{0,24},{4,28},{8,16},{12,20},{16,8},{20,12},{24,0},{28,4},{1,25},{... | collective-permute-start | bytes 786440 | tf_op jit(solution)/shard_map/ppermute | solution.py:355
  55.0 6.4 %collective-permute-start.16 = (f32[160,128]{1,0:T(8,128)S(1)}, f32[160,128]{1,0:T(8,128)S(1)}, u32[]{:S(2)}, u32[]{:S(2)}) collective-permute-start(f32[160,128]{1,0:T(8,128)S(1)} %add.24), channel_id=1, source_target_pairs={{0,1},{1,0},{2,3},{3,2},{4,5},{5,4},{6,7},{7,6},{8,9},{9,8},{10,11... | collective-permute-start | bytes 245768 | tf_op jit(solution)/shard_map/ppermute | solution.py:466
  57.1 6.6 %collective-permute-start.12 = (bf16[4,64,128]{2,1,0:T(8,128)(2,1)S(1)}, bf16[4,64,128]{2,1,0:T(8,128)(2,1)S(1)}, u32[]{:S(2)}, u32[]{:S(2)}) collective-permute-start(bf16[4,64,128]{2,1,0:T(8,128)(2,1)S(1)} %get-tuple-element.84), channel_id=1, source_target_pairs={{0,1},{2,3},{1,0},{3,2},{4,5},{6,7},{5,4},{7,6},{8,9},{10,11},{9,8... | collective-permute-start | bytes 196616 | tf_op jit(solution)/shard_map/ppermute | solution.py:88
  57.1 7.3 %collective-permute-start.13 = (bf16[4,64,128]{2,1,0:T(8,128)(2,1)S(1)}, bf16[4,64,128]{2,1,0:T(8,128)(2,1)S(1)}, u32[]{:S(2)}, u32[]{:S(2)}) collective-permute-start(bf16[4,64,128]{2,1,0:T(8,128)(2,1)S(1)} %get-tuple-element.85), channel_id=1, source_target_pairs={{1,2},{2,1},{5,6},{6,5},{9,10},{10,9},{13,14},{14,13},{17,18},{18,... | collective-permute-start | bytes 196616 | tf_op jit(solution)/shard_map/ppermute | solution.py:88
  61.5 5.4 %collective-permute-start.18 = (f32[160,128]{1,0:T(8,128)S(1)}, f32[160,128]{1,0:T(8,128)S(1)}, u32[]{:S(2)}, u32[]{:S(2)}) collective-permute-start(f32[160,128]{1,0:T(8,128)S(1)} %add.25), channel_id=1, source_target_pairs={{0,2},{1,3},{2,0},{3,1},{4,6},{5,7},{6,4},{7,5},{8,10},{9,11},{10,... | collective-permute-start | bytes 245768 | tf_op jit(solution)/shard_map/ppermute | solution.py:395
  64.4 13.4 %collective-permute-start.26 = (bf16[10,64,128]{2,1,0:T(8,128)(2,1)S(1)}, bf16[10,64,128]{2,1,0:T(8,128)(2,1)S(1)}, u32[]{:S(2)}, u32[]{:S(2)}) collective-permute-start(bf16[10,64,128]{2,1,0:T(8,128)(2,1)S(1)} %get-tuple-element.103), channel_id=1, source_target_pairs={{0,4},{8,12},{16,20},{24,28},{4,0},{12,8},{20,16},{28,24},{1,5},{9... | collective-permute-start | bytes 491528 | tf_op jit(solution)/shard_map/ppermute | solution.py:88
  66.9 7.2 %collective-permute-start.24 = (f32[160,128]{1,0:T(8,128)S(1)}, f32[160,128]{1,0:T(8,128)S(1)}, u32[]{:S(2)}, u32[]{:S(2)}) collective-permute-start(f32[160,128]{1,0:T(8,128)S(1)} %add.26), channel_id=1, source_target_pairs={{0,8},{4,12},{8,0},{12,4},{16,24},{20,28},{24,16},{28,20},{1,9},{5... | collective-permute-start | bytes 245768 | tf_op jit(solution)/shard_map/ppermute | solution.py:395
  67.8 24.3 %collective-permute-start.23 = (bf16[16,64,128]{2,1,0:T(8,128)(2,1)S(1)}, bf16[16,64,128]{2,1,0:T(8,128)(2,1)S(1)}, u32[]{:S(2)}, u32[]{:S(2)}) collective-permute-start(bf16[16,64,128]{2,1,0:T(8,128)(2,1)S(1)} %collective-permute-done.22), channel_id=1, source_target_pairs={{0,3},{1,11},{2,19},{3,27},{4,7},{5,15},{6,23},{7,31},{8,2},{9,10}... | collective-permute-start | bytes 786440 | tf_op jit(solution)/shard_map/ppermute | solution.py:365
  68.5 23.8 %collective-permute-start.21 = (bf16[16,64,128]{2,1,0:T(8,128)(2,1)S(1)}, bf16[16,64,128]{2,1,0:T(8,128)(2,1)S(1)}, u32[]{:S(2)}, u32[]{:S(2)}) collective-permute-start(bf16[16,64,128]{2,1,0:T(8,128)(2,1)S(1)} %collective-permute-done.17), channel_id=1, source_target_pairs={{0,2},{1,10},{2,18},{3,26},{4,6},{5,14},{6,22},{7,30},{8,3},{9,11}... | collective-permute-start | bytes 786440 | tf_op jit(solution)/shard_map/ppermute | solution.py:365
  71.3 21.0 %collective-permute-start.20 = (bf16[16,64,128]{2,1,0:T(8,128)(2,1)S(1)}, bf16[16,64,128]{2,1,0:T(8,128)(2,1)S(1)}, u32[]{:S(2)}, u32[]{:S(2)}) collective-permute-start(bf16[16,64,128]{2,1,0:T(8,128)(2,1)S(1)} %collective-permute-done.15), channel_id=1, source_target_pairs={{0,1},{1,9},{2,17},{3,25},{4,5},{5,13},{6,21},{7,29},{8,0},{9,8},{... | collective-permute-start | bytes 786440 | tf_op jit(solution)/shard_map/ppermute | solution.py:365
  74.1 22.4 %collective-permute-start.19 = (bf16[16,64,128]{2,1,0:T(8,128)(2,1)S(1)}, bf16[16,64,128]{2,1,0:T(8,128)(2,1)S(1)}, u32[]{:S(2)}, u32[]{:S(2)}) collective-permute-start(bf16[16,64,128]{2,1,0:T(8,128)(2,1)S(1)} %get-tuple-element.96.refs_0_), channel_id=1, source_target_pairs={{0,0},{1,8},{2,16},{3,24},{4,4},{5,12},{6,20},{7,28},{8,1},{9,9},{... | collective-permute-start | bytes 786440 | tf_op jit(solution)/shard_map/ppermute | solution.py:365
  77.9 4.7 %collective-permute-start.25 = (f32[160,128]{1,0:T(8,128)S(1)}, f32[160,128]{1,0:T(8,128)S(1)}, u32[]{:S(2)}, u32[]{:S(2)}) collective-permute-start(f32[160,128]{1,0:T(8,128)S(1)} %add.27), channel_id=1, source_target_pairs={{0,16},{4,20},{8,24},{12,28},{16,0},{20,4},{24,8},{28,12},{1,17},{... | collective-permute-start | bytes 245768 | tf_op jit(solution)/shard_map/ppermute | solution.py:395
  82.6 9.5 %collective-permute-start.27 = (bf16[10,64,128]{2,1,0:T(8,128)(2,1)S(1)}, bf16[10,64,128]{2,1,0:T(8,128)(2,1)S(1)}, u32[]{:S(2)}, u32[]{:S(2)}) collective-permute-start(bf16[10,64,128]{2,1,0:T(8,128)(2,1)S(1)} %get-tuple-element.105), channel_id=1, source_target_pairs={{4,8},{12,16},{20,24},{8,4},{16,12},{24,20},{5,9},{13,17},{21,25},... | collective-permute-start | bytes 491528 | tf_op jit(solution)/shard_map/ppermute | solution.py:88
  97.4 2.9 %collective-permute-start.28 = (bf16[32,64,128]{2,1,0:T(8,128)(2,1)S(1)}, bf16[32,64,128]{2,1,0:T(8,128)(2,1)S(1)}, u32[]{:S(2)}, u32[]{:S(2)}) collective-permute-start(bf16[32,64,128]{2,1,0:T(8,128)(2,1)S(1)} %get-tuple-element.111), channel_id=1, source_target_pairs={{0,4},{4,0},{8,12},{12,8},{16,20},{20,16},{24,28},{28,24},{1,5},{5... | collective-permute-start | bytes 1572872 | tf_op jit(solution)/shard_map/ppermute | solution.py:376
  97.5 2.0 %collective-permute-start.29 = (f32[160,128]{1,0:T(8,128)S(1)}, f32[160,128]{1,0:T(8,128)S(1)}, u32[]{:S(2)}, u32[]{:S(2)}) collective-permute-start(f32[160,128]{1,0:T(8,128)S(1)} %add.28.mine), channel_id=1, source_target_pairs={{0,4},{4,0},{8,12},{12,8},{16,20},{20,16},{24,28},{28,24},{1,5},{5... | collective-permute-start | bytes 245768 | tf_op jit(solution)/shard_map/ppermute | solution.py:376
